TPU v7x, 32 devices: a whole 2x2x4 slice. The times are simulated.
32 devices in a mesh: pipe: 2 (over x), expert: 16 (over z, y, core).
Axes of the slice: x: 2, y: 2, z: 4, core: 2. Of those that a mesh axis runs over, the one named last changes fastest.
Arguments:
- hidden_a: bfloat16 [16, 768, 2048], P('expert'), may hold values from -6 to 6
- expert_weights: bfloat16 [16, 2048, 7168], P('expert', None, 'pipe'), may hold values from -0.125 to 0.125
- routes_a: int32 [1024, 8], P('expert'), may hold values from 0 to 15, all different within a row; in each aligned block of 64 rows (0 to 63, 64 to 127, ...) at most 48 rows name the same one
- gates_a: float32 [1024, 8], P('expert'), may hold values from 0.05 to 0.6
- cotangent_b: bfloat16 [1024, 7168], P('expert', 'pipe'), may hold values from -6 to 6
- routes_b: int32 [1024, 8], P('expert'), may hold values from 0 to 15, all different within a row; in each aligned block of 64 rows (0 to 63, 64 to 127, ...) at most 48 rows name the same one
- gates_b: float32 [1024, 8], P('expert'), may hold values from 0.05 to 0.6
Outputs:
- mixed_a: bfloat16 [1024, 7168], P('expert', 'pipe')
- grad_hidden_b: bfloat16 [16, 768, 2048], P('expert', None, 'pipe')
Inputs may be any that keep to these rules, and one draw needn't show every extreme that they name: `routes_a`: among the tokens of one index of expert (aligned blocks of 64 rows), no expert is chosen more than 48 times, a bound that some block reaches; the 8 experts of a token differ. `routes_b`: among the tokens of one index of expert (aligned blocks of 64 rows), no expert is chosen more than 48 times, a bound that some block reaches; the 8 experts of a token differ.
All inputs are finite; a program needn't handle non-finite values.
Results may differ from a plain program's by a relative error of at most 0.019.
Values may be sent and summed in bfloat16 or wider, within the bound.
No kernel may reach another device: no remote copies, remote signals or barrier semaphores. Data moves between devices by JAX's collectives and lax.ppermute only.
A program may use at most 128 MiB of HBM per device.

v0:
```python
import jax
import jax.numpy as jnp
from jax import lax
from jax.sharding import PartitionSpec as P


def local_slots(routes, total):
    flat = routes.reshape(-1)
    onehot = (flat[:, None] == jnp.arange(total, dtype=jnp.int32)[None, :]).astype(jnp.int32)
    ranks = jnp.cumsum(onehot, axis=0) - onehot
    return jnp.sum(ranks * onehot, axis=1).reshape(routes.shape)


def on_device(hidden_a, expert_weights, routes_a, gates_a, cotangent_b, routes_b, gates_b):
    groups = lax.axis_size("expert")
    local = expert_weights.shape[0]
    total = local * groups
    cap = hidden_a.shape[1] // groups
    width = cotangent_b.shape[1]
    outputs = jnp.einsum(
        "erf,efd->erd", hidden_a, expert_weights, preferred_element_type=jnp.float32
    )
    flat = lax.all_to_all(
        outputs.astype(jnp.bfloat16).reshape(local, groups, cap, width),
        "expert",
        split_axis=1,
        concat_axis=0,
        tiled=True,
    ).reshape(total * cap, width)
    index = routes_a * cap + local_slots(routes_a, total)
    picked = flat[index]
    mixed = jnp.einsum("tk,tkd->td", gates_a, picked.astype(jnp.float32))
    mixed_a = mixed.astype(jnp.bfloat16)
    slots = local_slots(routes_b, total)
    index = routes_b % local * (groups * cap) + routes_b // local * cap + slots
    values = (gates_b[:, :, None] * cotangent_b[:, None, :].astype(jnp.float32)).astype(
        jnp.bfloat16
    )
    buffer = jnp.zeros((local * groups * cap, width), jnp.bfloat16)
    buffer = buffer.at[index.reshape(-1)].set(values.reshape(-1, width))
    arrived = lax.all_to_all(
        buffer.reshape(local, groups, cap, width), "expert", split_axis=1, concat_axis=0, tiled=True
    )
    partial_value = jnp.einsum(
        "secd,efd->escf", arrived, expert_weights, preferred_element_type=jnp.float32
    )
    summed = lax.psum_scatter(
        partial_value.astype(jnp.bfloat16), "pipe", scatter_dimension=3, tiled=True
    ).astype(jnp.float32)
    grad_hidden_b = summed.reshape(local, groups * cap, summed.shape[3]).astype(jnp.bfloat16)
    return (mixed_a, grad_hidden_b)


def solution(mesh):
    in_specs = (
        P("expert", None, None),
        P("expert", None, "pipe"),
        P("expert", None),
        P("expert", None),
        P("expert", "pipe"),
        P("expert", None),
        P("expert", None),
    )
    out_specs = (P("expert", "pipe"), P("expert", None, "pipe"))
    return jax.shard_map(
        on_device, mesh=mesh, in_specs=in_specs, out_specs=out_specs, check_vma=False
    )
```

profile of v0, /device:TPU:15, one launch (start us, length us, event | category | flops | bytes accessed | tf_op | source)
XLA Modules:
  0.0 297.8 jit_solution(12805376150087443290)
XLA Ops:
  7.2 0.9 copy.38
  8.1 0.1 eq.64
  8.2 0.1 eq.60
  8.3 1.2 reduce-window.16
  9.4 0.2 slice_reduce_fusion
  9.7 0.1 fusion.29
  9.8 0.1 reshape.135
  10.0 0.7 multiply_add_fusion
  10.7 0.1 copy.42
  10.8 0.1 reshape.136
  10.9 2.0 convert_element_type.55
  12.9 0.8 copy.43
  13.6 0.1 mul.35
  13.7 9.4 %scatter_custom_fusion = bf16[768,3584]{1,0:T(8,128)(2,1)} fusion(s32[512]{0:T(512)S(1)} %bitcast.86, f32[64,3584]{1,0:T(8,128)} %convert_element_type.55, f32[512]{0:T(512)S(1)} %mul.35, bf16[]{:T(256)} %constant.38.clone.1), kind=kCustom, calls=%fused_computation.10 | custom fusion | flops 3670016 | bytes 6424578 | tf_op jit(solution)/shard_map/scatter | solution.py:40
  23.1 6.6 %all-to-all-start.1 = ((bf16[1,16,48,3584]{3,2,0,1:T(8,128)(2,1)}), bf16[1,16,48,3584]{3,2,0,1:T(8,128)(2,1)}, u32[]{:S(2)}, u32[]{:S(2)}) async-start(bf16[1,16,48,3584]{3,2,0,1:T(8,128)(2,1)} %bitcast.82), calls=%async_computation.1 | async-start | bytes 11010048 | tf_op jit(solution)/shard_map/all_to_all | solution.py:41
  29.7 16.3 %fusion.5 = bf16[768,3584]{1,0:T(8,128)(2,1)} fusion(bf16[1,2048,3584]{2,1,0:T(8,128)(2,1)} %param.8, bf16[1,768,2048]{2,1,0:T(8,128)(2,1)S(1)} %copy-done), kind=kOutput, calls=%fused_computation.8 | convolution fusion | flops 11277041664 | bytes 23330816 | tf_op jit(solution)/shard_map/erf,efd->erd/dot_general | solution.py:20
  46.0 104.2 %all-to-all-done.1 = bf16[1,16,48,3584]{3,2,0,1:T(8,128)(2,1)} async-done(((bf16[1,16,48,3584]{3,2,0,1:T(8,128)(2,1)}), bf16[1,16,48,3584]{3,2,0,1:T(8,128)(2,1)}, u32[]{:S(2)}, u32[]{:S(2)}) %all-to-all-start.1) | async-done | bytes 5505056 | tf_op jit(solution)/shard_map/all_to_all | solution.py:41
  150.2 4.9 %all-to-all-start = ((bf16[1,16,48,3584]{3,2,0,1:T(8,128)(2,1)}), bf16[1,16,48,3584]{3,2,0,1:T(8,128)(2,1)}, u32[]{:S(2)}, u32[]{:S(2)}) async-start(bf16[1,16,48,3584]{3,2,0,1:T(8,128)(2,1)} %bitcast.83), calls=%async_computation | async-start | bytes 11010048 | tf_op jit(solution)/shard_map/all_to_all | solution.py:23
  155.2 17.6 %fusion.21 = bf16[1,16,48,2048]{3,2,1,0:T(8,128)(2,1)} fusion(bf16[1,2048,3584]{2,1,0:T(8,128)(2,1)} %param.8, bf16[1,16,48,3584]{3,2,0,1:T(8,128)(2,1)} %all-to-all-done.1), kind=kOutput, calls=%fused_computation.17 | convolution fusion | flops 11275862016 | bytes 23330816 | tf_op jit(solution)/shard_map/secd,efd->escf/dot_general | solution.py:44
  172.9 0.1 eq.56
  173.0 0.1 eq.52
  173.1 1.2 reduce-window.14
  174.3 0.2 slice_reduce_fusion.1
  174.5 0.1 fusion.32
  174.6 0.1 reshape.133
  174.8 0.1 copy.37
  174.9 0.1 reshape.141
  175.0 0.1 copy.44
  175.1 100.6 %all-to-all-done = bf16[1,16,48,3584]{3,2,0,1:T(8,128)(2,1)} async-done(((bf16[1,16,48,3584]{3,2,0,1:T(8,128)(2,1)}), bf16[1,16,48,3584]{3,2,0,1:T(8,128)(2,1)}, u32[]{:S(2)}, u32[]{:S(2)}) %all-to-all-start) | async-done | bytes 5505056 | tf_op jit(solution)/shard_map/all_to_all | solution.py:23
  275.7 11.2 %gather_fusion = bf16[512,3584]{1,0:T(8,128)(2,1)} fusion(bf16[768,3584]{1,0:T(8,128)(2,1)} %bitcast.4, s32[1024]{0:T(1024)S(1)} %pad_clamp_fusion), kind=kCustom, calls=%fused_computation | custom fusion | bytes 7342080 | tf_op jit(solution)/shard_map/gather | solution.py:31
  287.0 3.1 %fusion.11 = bf16[64,1,3584]{2,1,0:T(2,128)(2,1)S(1)} fusion(bf16[64,8,1]{1,2,0:T(2,128)(2,1)S(1)} %copy.44, bf16[512,3584]{1,0:T(8,128)(2,1)} %gather_fusion), kind=kOutput, calls=%fused_computation.11 | convolution fusion | flops 3670016 | bytes 4129792 | tf_op jit(solution)/shard_map/tk,tkd->td/dot_general | solution.py:32
  290.1 0.8 copy.51
  (21 shorter events, 0.4 us)
Async XLA Ops:
  7.2 22.5 %copy-start = (bf16[1,768,2048]{2,1,0:T(8,128)(2,1)S(1)}, bf16[1,768,2048]{2,1,0:T(8,128)(2,1)}, u32[]{:S(2)}) copy-start(bf16[1,768,2048]{2,1,0:T(8,128)(2,1)} %param.7) | copy-start | bytes 9437188
  23.1 127.1 %all-to-all-start.1 = ((bf16[1,16,48,3584]{3,2,0,1:T(8,128)(2,1)}), bf16[1,16,48,3584]{3,2,0,1:T(8,128)(2,1)}, u32[]{:S(2)}, u32[]{:S(2)}) async-start(bf16[1,16,48,3584]{3,2,0,1:T(8,128)(2,1)} %bitcast.82), calls=%async_computation.1 | async-start | bytes 11010048 | tf_op jit(solution)/shard_map/all_to_all | solution.py:41
  150.2 125.5 %all-to-all-start = ((bf16[1,16,48,3584]{3,2,0,1:T(8,128)(2,1)}), bf16[1,16,48,3584]{3,2,0,1:T(8,128)(2,1)}, u32[]{:S(2)}, u32[]{:S(2)}) async-start(bf16[1,16,48,3584]{3,2,0,1:T(8,128)(2,1)} %bitcast.83), calls=%async_computation | async-start | bytes 11010048 | tf_op jit(solution)/shard_map/all_to_all | solution.py:23
  155.2 17.7 %copy-start.1 = (s32[64,8]{0,1:T(8,128)S(1)}, s32[64,8]{0,1:T(8,128)}, u32[]{:S(2)}) copy-start(s32[64,8]{0,1:T(8,128)} %param.9) | copy-start | bytes 6148
  155.2 19.8 %copy-start.2 = (f32[64,8]{0,1:T(8,128)S(1)}, f32[64,8]{0,1:T(8,128)}, u32[]{:S(2)}) copy-start(f32[64,8]{0,1:T(8,128)} %param.10) | copy-start | bytes 6148
  155.2 135.8 %reduce-scatter.2.cloned.1.call-start = ((), (), s32[]{:S(2)}) async-start(), calls=%async_computation.3 | async-start | bytes 4718592 | tf_op jit(solution)/shard_map/reduce_scatter | solution.py:47
Sparse Core Ops, SparseCore 0:
  172.9 43.0 reduce-scatter.1
where the time goes:
time: 298 us
  waiting for transfers between devices  205 us (69%)
  matrix products  37 us (12%)
  local copies, waits for them, and re-layouts  15.5 us (5%)
  other arithmetic  14.7 us (5%)
  between operations  14.1 us (5%)
  starting transfers between devices  11.5 us (4%)
    all_to_all x1, waiting for transfers between devices, on_device(): lax.all_to_all(buffer.reshape(local, groups, cap, width), 'expert', split...  104 us
    all_to_all x1, waiting for transfers between devices, on_device(): lax.all_to_all(outputs.astype(jnp.bfloat16).reshape(local, groups, cap, w...  101 us
    dot_general x1, matrix products, on_device(): jnp.einsum('secd,efd->escf', arrived, expert_weights, preferred_element_t...  17.6 us
    dot_general x1, matrix products, on_device(): jnp.einsum('erf,efd->erd', hidden_a, expert_weights, preferred_element_ty...  16.3 us
    gather x1, local copies, waits for them, and re-layouts, on_device(): picked = flat[index]  11.2 us
    scatter x1, other arithmetic, on_device(): buffer = buffer.at[index.reshape(-1)].set(values.reshape(-1, width))  9.41 us
    all_to_all x1, starting transfers between devices, on_device(): lax.all_to_all(buffer.reshape(local, groups, cap, width), 'expert', split...  6.56 us
  transfers between devices with their start and end apart: 3, of which 2 were waited for; matrix products, arithmetic and copies ran while one was open for 17% of the time, Pallas kernels for 0%

commit v1 on v0

v1 whole, which is shorter than its diff:
```python
import functools

import jax
import jax.numpy as jnp
from jax import lax
from jax.experimental import pallas as pl
from jax.experimental.pallas import tpu as pltpu
from jax.sharding import PartitionSpec as P

BF16, F32 = jnp.bfloat16, jnp.float32
TILE = 512
LANES = 128


def dense_gates(routes, gates, total):
    experts = jnp.arange(total, dtype=jnp.int32)[:, None, None]
    return jnp.sum(jnp.where(routes[None] == experts, gates[None], 0.0), axis=2)


def ranks_of(gate):
    tokens = gate.shape[-1]
    earlier = jnp.triu(jnp.ones((tokens, tokens), BF16), 1)
    counts = jnp.dot((gate > 0.0).astype(BF16), earlier, preferred_element_type=F32)
    return counts.astype(jnp.int32)


def add(*terms):
    total = terms[0].astype(F32)
    for term in terms[1:]:
        total = total + term.astype(F32)
    return total.astype(BF16)


def on_device_any(hidden_a, expert_weights, routes_a, gates_a, cotangent_b, routes_b, gates_b):
    groups = lax.axis_size("expert")
    me = lax.axis_index("expert")
    total = expert_weights.shape[0] * groups
    rows = hidden_a.shape[1]
    cap = rows // groups
    tokens, width = cotangent_b.shape
    weights = expert_weights[0]

    both = jnp.stack(
        [dense_gates(routes_a, gates_a, total), dense_gates(routes_b, gates_b, total)], axis=1
    )
    every = lax.all_gather(both, "expert", axis=0, tiled=False)
    own = lax.dynamic_index_in_dim(every, me, axis=1, keepdims=False)
    gathered = lax.all_gather(cotangent_b, "expert", axis=0, tiled=True)

    def placement(gate):
        slots = jnp.arange(cap, dtype=jnp.int32)[None, :, None]
        hit = (gate > 0.0)[:, None, :] & (ranks_of(gate)[:, None, :] == slots)
        return hit.astype(BF16), jnp.sum(jnp.where(hit, gate[:, None, :], 0.0), axis=2)

    hit_a, slot_gate_a = placement(own[:, 0])
    hit_b, slot_gate_b = placement(own[:, 1])

    outputs = jnp.einsum("rf,fd->rd", hidden_a[0], weights, preferred_element_type=F32)
    scaled = (outputs * slot_gate_a.reshape(rows, 1)).astype(BF16)
    spread = jnp.einsum(
        "sct,scd->std", hit_a, scaled.reshape(groups, cap, width), preferred_element_type=F32
    ).astype(BF16)
    mixed_a = lax.psum_scatter(
        spread.reshape(groups * tokens, width), "expert", scatter_dimension=0, tiled=True
    )
    picked = jnp.einsum(
        "sct,std->scd",
        hit_b,
        gathered.reshape(groups, tokens, width),
        preferred_element_type=F32,
    ).astype(BF16)
    partial_value = jnp.einsum(
        "rd,fd->rf", picked.reshape(rows, width), weights, preferred_element_type=F32
    )
    partial_value = (partial_value * slot_gate_b.reshape(rows, 1)).astype(BF16)
    grad = lax.psum_scatter(partial_value, "pipe", scatter_dimension=1, tiled=True)
    return (mixed_a, grad[None])


RING = [(0, 0), (1, 0), (2, 0), (3, 0), (3, 1), (2, 1), (1, 1), (0, 1)]


def step_ring(value, way):
    pairs = []
    for place, (z, y) in enumerate(RING):
        to_z, to_y = RING[(place + way) % 8]
        pairs += [(z * 4 + y * 2 + c, to_z * 4 + to_y * 2 + c) for c in range(2)]
    return lax.ppermute(value, "expert", pairs)


def xor(value, bits):
    return lax.ppermute(value, "expert", [(i, i ^ bits) for i in range(16)])


def core(value):
    return xor(value, 1)


def across(value):
    return lax.ppermute(value, "pipe", [(0, 1), (1, 0)])


def pin(value):
    return pltpu.with_memory_space_constraint(value, pltpu.HBM)


def tie(*values):
    return lax.optimization_barrier(values)


SMEM = pl.BlockSpec(memory_space=pltpu.SMEM)
VMEM = pl.BlockSpec(memory_space=pltpu.VMEM)
HBM = pl.BlockSpec(memory_space=pltpu.HBM)
ANY = pl.BlockSpec(memory_space=pl.ANY)


def kernel_call(kernel, name, inputs, out_shape, scratch, flops, moved):
    in_specs, arrays = zip(*inputs)
    return pl.pallas_call(
        kernel,
        in_specs=in_specs,
        out_specs=[VMEM] * len(out_shape),
        out_shape=out_shape,
        scratch_shapes=scratch,
        compiler_params=pltpu.CompilerParams(vmem_limit_bytes=20 * 2**20),
        cost_estimate=pl.CostEstimate(flops=flops, bytes_accessed=moved, transcendentals=0),
        name=name,
    )(*arrays)


def gates_kernel(*refs):
    sources, out, held, sems = refs[:4], refs[4], refs[5:9], refs[9]
    copies = [pltpu.make_async_copy(x, y, sems.at[i]) for i, (x, y) in enumerate(zip(sources, held))]
    for copy in copies:
        copy.start()
    for copy in copies:
        copy.wait()
    top, tokens = held[0].shape
    experts = lax.broadcasted_iota(jnp.int32, (out.shape[0], tokens), 0)
    for i in range(2):
        routes, gates = held[2 * i : 2 * i + 2]
        total = jnp.zeros(experts.shape, F32)
        for k in range(top):
            total += jnp.where(routes[k : k + 1, :] == experts, gates[k : k + 1, :], 0.0)
        out[:, pl.ds(i * tokens, tokens)] = total


def gates_of(*arrays):
    tokens, top = arrays[0].shape
    arrays = [pin(x.T) for x in arrays]
    return kernel_call(
        gates_kernel,
        "gates",
        [(HBM, x) for x in arrays],
        [jax.ShapeDtypeStruct((16, 2 * tokens), F32)],
        [pltpu.VMEM((top, tokens), x.dtype) for x in arrays] + [pltpu.SemaphoreType.DMA((4,))],
        flops=2**20,
        moved=2**17,
    )[0]


def place_slots(distances, where, gates, cap, target, place, slot_gates):
    gate = gates[...]
    tokens = gate.shape[1] // 2
    row = lax.broadcasted_iota(jnp.int32, (2 * tokens, 2 * tokens), 0)
    col = lax.broadcasted_iota(jnp.int32, (2 * tokens, 2 * tokens), 1)
    earlier = ((row < col) & (row // tokens == col // tokens)).astype(F32).astype(BF16)
    chosen = (gate > 0.0).astype(F32).astype(BF16)
    rank = jnp.dot(chosen, earlier, preferred_element_type=F32)
    second = (lax.broadcasted_iota(jnp.int32, gate.shape, 1) // tokens) ^ where[8]
    target[...] = jnp.where(gate > 0.0, rank + (second * cap).astype(F32), -1.0)
    slots = lax.broadcasted_iota(jnp.int32, (2 * cap, 2 * tokens), 0).astype(F32)
    for i, d in enumerate(distances):
        block = pl.ds(where[9 + d % 8], 1)
        hit = target[block, :] == slots
        place[i] = hit.astype(F32).astype(BF16)
        total = jnp.sum(jnp.where(hit, gates[block, :], 0.0), axis=1, keepdims=True)
        slot_gates[pl.ds(i * 2 * cap, 2 * cap), :] = jnp.broadcast_to(total, (2 * cap, LANES))


def place_scratch(count, gates, cap):
    return [
        pltpu.VMEM(gates.shape, F32),
        pltpu.VMEM((count, 2 * cap, gates.shape[1]), BF16),
        pltpu.VMEM((count * 2 * cap, LANES), F32),
    ]


def gated(value, slot_gates):
    factor = jnp.concatenate([slot_gates] * (value.shape[1] // LANES), axis=1)
    return (value * factor).astype(BF16)


class Stream:
    def __init__(self, tile, buffer, sems):
        self.tile, self.buffer, self.sems = tile, buffer, sems
        self.slots, self.parts = sems.shape

    def copies(self, n):
        slot = n % self.slots
        rows = self.buffer.shape[1] // self.parts
        source = self.tile(n)
        for part in range(self.parts):
            at = pl.ds(part * rows, rows)
            yield pltpu.make_async_copy(
                source.at[at, :], self.buffer.at[slot, at, :], self.sems.at[slot, part]
            )

    def start(self, n):
        for copy in self.copies(n):
            copy.start()

    def wait(self, n):
        for copy in self.copies(n):
            copy.wait()


def raw_kernel(first, hidden, weights, out, buffer, sems, staged, out_sems):
    tile, tiles = buffer.shape[2], out.shape[1] // buffer.shape[2]
    stream = Stream(
        lambda n: weights.at[:, pl.ds(pl.multiple_of(first + n * tile, tile), tile)], buffer, sems
    )
    for n in range(stream.slots):
        stream.start(n)

    def put(n):
        cols = pl.ds(pl.multiple_of(n * tile, tile), tile)
        return pltpu.make_async_copy(staged.at[n % 2], out.at[:, cols], out_sems.at[n % 2])

    @pl.loop(0, tiles)
    def _(n):
        stream.wait(n)

        @pl.when(n >= 2)
        def _():
            put(n - 2).wait()

        value = jnp.dot(hidden[...], buffer[n % stream.slots], preferred_element_type=F32)
        staged[n % 2] = value.astype(BF16)
        put(n).start()

        @pl.when(n + stream.slots < tiles)
        def _():
            stream.start(n + stream.slots)

    put(tiles - 2).wait()
    put(tiles - 1).wait()


def raw_forward(first, width, hidden, weights):
    rows, depth = hidden.shape
    return pl.pallas_call(
        functools.partial(raw_kernel, first),
        in_specs=[VMEM, HBM],
        out_specs=HBM,
        out_shape=pltpu.HBM((rows, width), BF16),
        scratch_shapes=[
            pltpu.VMEM((3, depth, 256), BF16),
            pltpu.SemaphoreType.DMA((3, 4)),
            pltpu.VMEM((2, rows, 256), BF16),
            pltpu.SemaphoreType.DMA((2,)),
        ],
        compiler_params=pltpu.CompilerParams(vmem_limit_bytes=20 * 2**20),
        cost_estimate=pl.CostEstimate(
            flops=2 * rows * depth * width,
            bytes_accessed=2 * (depth * width + rows * (depth + width)),
            transcendentals=0,
        ),
        name="raw_forward",
    )(hidden, weights)


def spread_kernel(distances, split, cap, where, gates, *refs):
    count = len(distances)
    raws, (keep, *others), scratch = refs[:2], refs[2:-6], refs[-6:]
    target, place, slot_gates, to_tokens, held, sems = scratch
    rows, half = 2 * cap, gates.shape[1] // 2
    width = raws[0].shape[1]
    fetch = []
    for i, d in enumerate(distances):
        start = pl.multiple_of(where[d % 8] * rows, rows)
        for j, raw in enumerate(raws):
            source = raw.at[pl.ds(start, rows), :]
            fetch.append(
                pltpu.make_async_copy(source, held.at[i, :, pl.ds(j * width, width)], sems.at[i, j])
            )
            fetch[-1].start()
    place_slots(distances, where, gates, cap, target, place, slot_gates)
    tokens = 2 * half
    same = lax.broadcasted_iota(jnp.int32, (tokens, tokens), 0) == lax.broadcasted_iota(
        jnp.int32, (tokens, tokens), 1
    )
    same = same.astype(F32).astype(BF16)
    for i in range(count):
        to_tokens[i] = lax.dot_general(
            same, place[i], (((1,), (1,)), ((), ())), preferred_element_type=F32
        ).astype(BF16)
    for copy in fetch:
        copy.wait()
    for g, other in enumerate(others):

        @pl.loop(0, split)
        def _(j):
            i = g * split + j
            for n in range(2 * width // TILE):
                cols = pl.ds(n * TILE, TILE)
                part = held[i, :, cols].astype(F32)
                part = gated(part, slot_gates[pl.ds(pl.multiple_of(i * rows, rows), rows), :])
                part = jnp.dot(to_tokens[i], part, preferred_element_type=F32).astype(BF16)
                keep[pl.ds(pl.multiple_of(i * half, half), half), cols] = part[:half]
                other[pl.ds(pl.multiple_of(j * half, half), half), cols] = part[half:]


def spread_tokens(distances, split, cap, where, gates, raws):
    count, half, width = len(distances), gates.shape[1] // 2, 2 * raws[0].shape[1]
    return kernel_call(
        functools.partial(spread_kernel, distances, split, cap),
        "spread_tokens",
        [(SMEM, where), (VMEM, gates), (HBM, raws[0]), (HBM, raws[1])],
        [jax.ShapeDtypeStruct((count * half, width), BF16)]
        + [jax.ShapeDtypeStruct((split * half, width), BF16)] * (count // split),
        [
            *place_scratch(count, gates, cap),
            pltpu.VMEM((count, 2 * half, 2 * cap), BF16),
            pltpu.VMEM((count, 2 * cap, width), BF16),
            pltpu.SemaphoreType.DMA((count, 2)),
        ],
        flops=count * 2**28,
        moved=count * 6 * half * width,
    )


def backward_kernel(distances, cap, sides, where, pipe, gates, weights, *refs):
    count, rows = len(distances), 2 * cap
    tokens, outs = refs[: 2 * count], refs[2 * count : 2 * count + len(sides)]
    block, block_sems, picked, target, place, slot_gates, buffer, sems = refs[
        2 * count + len(sides) :
    ]
    half, tile = tokens[0].shape[0], buffer.shape[1]
    tiles = 4 * len(sides)
    first = (1 - pipe[0] + sides[0]) * 4

    def weight_tile(n):
        return weights.at[pl.ds(pl.multiple_of((first + n) % 8 * tile, tile), tile), :]

    fetch = []
    for i, token in enumerate(tokens):
        to = block.at[i // 2, pl.ds(i % 2 * half, half), :]
        fetch.append(pltpu.make_async_copy(token, to, block_sems.at[i]))
        fetch[-1].start()
    stream = Stream(weight_tile, buffer, sems)
    for n in range(stream.slots):
        stream.start(n)
    place_slots(distances, where, gates, cap, target, place, slot_gates)
    for copy in fetch:
        copy.wait()

    @pl.loop(0, count)
    def _(i):
        for n in range(block.shape[2] // TILE):
            cols = pl.ds(n * TILE, TILE)
            picked[pl.ds(pl.multiple_of(i * rows, rows), rows), cols] = jnp.dot(
                place[i], block[i, :, cols], preferred_element_type=F32
            ).astype(BF16)

    @pl.loop(0, tiles)
    def _(n):
        stream.wait(n)
        value = lax.dot_general(
            picked[...],
            buffer[n % stream.slots],
            (((1,), (1,)), ((), ())),
            preferred_element_type=F32,
        )
        value = gated(value, slot_gates[...])
        cols = pl.ds(pl.multiple_of(n % 4 * tile, tile), tile)
        for i, out in enumerate(outs):

            @pl.when(n // 4 == i)
            def _():
                out[:, cols] = value

        @pl.when(n + stream.slots < tiles)
        def _():
            stream.start(n + stream.slots)


def backward(distances, cap, sides, where, pipe, tokens, gates, weights, share):
    count, rows = len(distances), 2 * cap
    depth, width = weights.shape
    return kernel_call(
        functools.partial(backward_kernel, distances, cap, sides),
        "backward",
        [(SMEM, where), (SMEM, pipe), (VMEM, gates), (HBM, weights)] + [(ANY, x) for x in tokens],
        [jax.ShapeDtypeStruct((count * rows, depth // 2), BF16)] * len(sides),
        [
            pltpu.VMEM((count, gates.shape[1], width), BF16),
            pltpu.SemaphoreType.DMA((2 * count,)),
            pltpu.VMEM((count * rows, width), BF16),
            *place_scratch(count, gates, cap),
            pltpu.VMEM((4, depth // 8, width), BF16),
            pltpu.SemaphoreType.DMA((4, 4)),
        ],
        flops=len(sides) * count * rows * depth * width // share,
        moved=2 * (depth * width + count * rows * (depth + 2 * width)) // share,
    )


def collect_kernel(groups, where, *refs):
    out, held, sems = refs[-3:]
    copies = []
    for g, distances in enumerate(groups):
        hold, recv = refs[2 * g], refs[2 * g + 1]
        rows = hold.shape[0] // len(distances)
        for i, d in enumerate(distances):
            at, n = pl.ds(i * rows, rows), len(copies)
            held[n] = (hold[at, :].astype(F32) + recv[at, :].astype(F32)).astype(BF16)
            to = pl.ds(pl.multiple_of(where[d % 8] * rows, rows), rows)
            copies.append(pltpu.make_async_copy(held.at[n], out.at[to, :], sems.at[n]))
            copies[-1].start()
    for copy in copies:
        copy.wait()


def collect(groups, where, arrays, rows, into=None):
    count = sum(len(distances) for distances in groups)
    out = jax.ShapeDtypeStruct((rows, arrays[0].shape[1]), BF16)
    inputs = [(SMEM, where)] + [(VMEM, x) for x in arrays]
    if into is not None:
        inputs.append((HBM, into))
    in_specs, arrays = zip(*inputs)
    return pl.pallas_call(
        functools.partial(collect_kernel, groups),
        in_specs=in_specs,
        out_specs=HBM,
        out_shape=out,
        scratch_shapes=[
            pltpu.VMEM((count, rows // 8, out.shape[1]), BF16),
            pltpu.SemaphoreType.DMA((count,)),
        ],
        input_output_aliases={} if into is None else {len(inputs) - 1: 0},
        compiler_params=pltpu.CompilerParams(vmem_limit_bytes=20 * 2**20),
        cost_estimate=pl.CostEstimate(
            flops=2**20, bytes_accessed=6 * count * rows * 128, transcendentals=0
        ),
        name="collect",
    )(*arrays)


def on_device_16(hidden_a, expert_weights, routes_a, gates_a, cotangent_b, routes_b, gates_b):
    me = lax.axis_index("expert").astype(jnp.int32)
    z, y, c = me // 4, me // 2 % 2, me % 2
    pipe = lax.axis_index("pipe").astype(jnp.int32).reshape(1)
    rows = hidden_a.shape[1] // 8
    cap = rows // 2
    tokens, width = cotangent_b.shape
    weights, hidden = expert_weights[0], hidden_a[0]

    ring = (jnp.where(y == 0, z, 7 - z) + jnp.arange(8, dtype=jnp.int32)) % 8
    to_z, to_y = jnp.minimum(ring, 7 - ring), (ring > 3).astype(jnp.int32)
    chips = to_z * 2 + to_y
    where = jnp.concatenate([chips, c.reshape(1), (to_z ^ z) * 2 + (to_y ^ y)])

    got, pair = {0: cotangent_b}, {}
    got[-1], got[1] = step_ring(cotangent_b, 1), step_ring(cotangent_b, -1)

    both = gates_of(routes_a, gates_a, routes_b, gates_b)
    four = jnp.stack([both] + [xor(both, j) for j in (1, 2, 3)])
    four = lax.dynamic_index_in_dim(four.reshape(4, 4, 4, 2 * tokens), me % 4, 2, False)
    weights, four = tie(weights, four)
    raw1 = raw_forward(0, width // 2, hidden, pin(weights))
    every = jnp.stack([four] + [xor(four, 4 * k) for k in (1, 2, 3)])
    raw1, weights, every, got[-1], got[1] = tie(raw1, weights, every, got[-1], got[1])
    weights = pin(weights)
    every = lax.dynamic_index_in_dim(every, z, 2, False)
    gate = jnp.moveaxis(every.reshape(8, 2, 2, tokens), 2, 0).reshape(2, 8, 2 * tokens)
    gate_a, gate_b = gate[0], gate[1]

    def spread(distances, split, gates):
        return spread_tokens(distances, split, cap, where, gates, (pin(raw1), pin(raw2)))

    def bwd(distances, sides=(0, 1), share=1):
        values = [x for d in distances for x in (got[d], pair[d])]
        return backward(distances, cap, sides, where, pipe, values, gate_b, weights, share)

    got[-2], got[2] = step_ring(got[-1], 1), step_ring(got[1], -1)
    pair[0] = core(got[0])
    raw2 = raw_forward(width // 2, width // 2, hidden, weights)
    raw2, got[-2], got[2], pair[0] = tie(raw2, got[-2], got[2], pair[0])

    got[-3], got[3] = step_ring(got[-2], 1), step_ring(got[2], -1)
    keep1, other1, other2 = spread((3, -4, 2, -3), 2, gate_a)
    other1, other2 = core(other1), core(other2)
    pair[-1], pair[1] = core(got[-1]), core(got[1])
    up = step_ring(add(keep1[:tokens], other1[:tokens]), 1)
    down = step_ring(add(keep1[tokens : 2 * tokens], other1[tokens:]), -1)
    gate_a, pair[-1], pair[1], other2 = tie(gate_a, pair[-1], pair[1], other2)
    keep2, other3, other4 = spread((1, -2, -1, 0), 2, gate_a)
    keep2, gate_b = tie(keep2, gate_b)
    send1, hold1 = bwd((0, -1, 1), share=64)

    def mine(i, other, *more):
        at = slice(i * tokens, (i + 1) * tokens)
        other_at = slice(i % 2 * tokens, (i % 2 + 1) * tokens)
        return add(keep2[at], other[other_at], *more)

    send1, got[-3], got[3], up, down, other3, other4 = tie(
        send1, got[-3], got[3], up, down, other3, other4
    )
    got[-4] = step_ring(got[-3], 1)
    up = step_ring(add(keep1[2 * tokens : 3 * tokens], other2[:tokens], up), 1)
    down = step_ring(add(keep1[3 * tokens :], other2[tokens:], down), -1)
    recv1 = across(send1)
    pair[-2], pair[2], other3 = core(got[-2]), core(got[2]), core(other3)
    pair[-3], pair[3], other4 = core(got[-3]), core(got[3]), core(other4)
    gate_b, other3, other4, pair[-3], pair[3] = tie(gate_b, other3, other4, pair[-3], pair[3])
    send2, hold2 = bwd((-2, 2))

    hold2, send2, down, gate_b = tie(hold2, send2, down, gate_b)
    recv2 = across(send2)
    down = step_ring(mine(1, other3, down), -1)
    send3, hold3 = bwd((-3, 3), share=64)

    hold3, send3, up, got[-4], down, recv1, recv2 = tie(
        hold3, send3, up, got[-4], down, recv1, recv2
    )
    recv3 = across(send3)
    pair[-4] = core(got[-4])
    up, down = step_ring(mine(0, other3, up), 1), step_ring(mine(2, other4, down), -1)
    (send4,) = bwd((-4,), (0,))
    recv4 = across(send4)
    send4, gate_b = tie(send4, gate_b)
    (hold4,) = bwd((-4,), (1,), 64)
    hold4, up, down, recv3 = tie(hold4, up, down, recv3)
    mixed_a = mine(3, other4, up, down)
    grad = collect(
        ((0, -1, 1), (-2, 2), (-3, 3)), where, (hold1, recv1, hold2, recv2, hold3, recv3), 8 * rows
    )
    grad, mixed_a, recv4 = tie(grad, mixed_a, recv4)
    grad = collect(((-4,),), where, (hold4, recv4), 8 * rows, grad)
    return (mixed_a, grad[None])


def solution(mesh):
    in_specs = (
        P("expert", None, None),
        P("expert", None, "pipe"),
        P("expert", None),
        P("expert", None),
        P("expert", "pipe"),
        P("expert", None),
        P("expert", None),
    )
    out_specs = (P("expert", "pipe"), P("expert", None, "pipe"))
    tailored = mesh.shape["expert"] == 16 and mesh.shape["pipe"] == 2
    return jax.shard_map(
        on_device_16 if tailored else on_device_any,
        mesh=mesh,
        in_specs=in_specs,
        out_specs=out_specs,
        check_vma=False,
    )
```

time: 298 us -> 120 us (0.40)
  the two profiles are of different devices: /device:TPU:15 before, /device:TPU:0 now
where the time goes in v1:
time: 120 us
  Pallas kernels  70 us (58%)
  starting transfers between devices  29.3 us (24%)
  waiting for transfers between devices  8.69 us (7%)
  local copies, waits for them, and re-layouts  6.44 us (5%)
  other arithmetic  4.5 us (4%)
    pallas_call x8, Pallas kernels, kernel_call(): pl.pallas_call(kernel, in_specs=in_specs, out_specs=[VMEM] * len(out_shap...  48.8 us
    pallas_call x2, Pallas kernels, raw_forward(): pl.pallas_call(functools.partial(raw_kernel, first), in_specs=[VMEM, HBM]...  18.2 us
    ppermute x14, starting transfers between devices, step_ring(): return lax.ppermute(value, 'expert', pairs)  15 us
    ppermute x18, starting transfers between devices, xor(): return lax.ppermute(value, 'expert', [(i, i ^ bits) for i in range(16)])  9.99 us
    unnamed x18, local copies, waits for them, and re-layouts  6.13 us
    convert_element_type x5, other arithmetic, add(): return total.astype(BF16)  4.38 us
    ppermute x4, starting transfers between devices, across(): return lax.ppermute(value, 'pipe', [(0, 1), (1, 0)])  4.3 us
    ppermute x18, waiting for transfers between devices, xor(): return lax.ppermute(value, 'expert', [(i, i ^ bits) for i in range(16)])  3.83 us
  transfers between devices with their start and end apart: 36, of which 6 were waited for; matrix products, arithmetic and copies ran while one was open for 4% of the time, Pallas kernels for 52%

profile of v1, /device:TPU:0, one launch (start us, length us, event | category | flops | bytes accessed | tf_op | source)
XLA Modules:
  0.0 119.8 jit_solution(3077244996510889393)
XLA Ops:
  1.5 3.0 %collective-permute-start.1 = (f32[16,128]{1,0:T(8,128)S(1)}, f32[16,128]{1,0:T(8,128)S(1)}, u32[]{:S(2)}, u32[]{:S(2)}) collective-permute-start(f32[16,128]{1,0:T(8,128)S(1)} %gates.1), channel_id=1, source_target_pairs={{0,2},{1,3},{2,0},{3,1},{4,6},{5,7},{6,4},{7,5},{8,10},{9,11},{10,... | collective-permute-start | bytes 24584 | tf_op jit(solution)/shard_map/ppermute | solution.py:92
  4.7 2.0 %collective-permute-start.6 = (bf16[64,3584]{1,0:T(8,128)(2,1)}, bf16[64,3584]{1,0:T(8,128)(2,1)S(1)}, u32[]{:S(2)}, u32[]{:S(2)}) collective-permute-start(bf16[64,3584]{1,0:T(8,128)(2,1)} %refs_0_.1), channel_id=1, source_target_pairs={{0,4},{1,5},{4,8},{5,9},{8,12},{9,13},{12,14},{13,15},{14,10},{15,... | collective-permute-start | bytes 1376264 | tf_op jit(solution)/shard_map/ppermute | solution.py:88
  7.6 1.6 %collective-permute-start.3 = (f32[4,4,128]{2,0,1:T(4,128)S(1)}, f32[4,4,128]{2,0,1:T(4,128)S(1)}, u32[]{:S(2)}, u32[]{:S(2)}) collective-permute-start(f32[4,4,128]{2,0,1:T(4,128)S(1)} %bitcast.41), channel_id=1, source_target_pairs={{0,4},{1,5},{2,6},{3,7},{4,0},{5,1},{6,2},{7,3},{8,12},{9,13},{10,... | collective-permute-start | bytes 24584 | tf_op jit(solution)/shard_map/ppermute | solution.py:92
  9.3 2.6 %collective-permute-start.4 = (f32[4,4,128]{2,0,1:T(4,128)S(1)}, f32[4,4,128]{2,0,1:T(4,128)S(1)}, u32[]{:S(2)}, u32[]{:S(2)}) collective-permute-start(f32[4,4,128]{2,0,1:T(4,128)S(1)} %bitcast.42), channel_id=1, source_target_pairs={{0,8},{1,9},{2,10},{3,11},{4,12},{5,13},{6,14},{7,15},{8,0},{9,1},... | collective-permute-start | bytes 24584 | tf_op jit(solution)/shard_map/ppermute | solution.py:92
  12.1 1.9 %copy-done.7 = bf16[1,768,2048]{2,1,0:T(8,128)(2,1)S(1)} copy-done((bf16[1,768,2048]{2,1,0:T(8,128)(2,1)S(1)}, bf16[1,768,2048]{2,1,0:T(8,128)(2,1)}, u32[]{:S(2)}) %copy-start.7) | copy-done | bytes 3145752
  14.0 9.2 %raw_forward.2.refs_0_ = bf16[768,1792]{1,0:T(8,128)(2,1)} custom-call(bf16[768,2048]{1,0:T(8,128)(2,1)S(1)} %bitcast.30, bf16[2048,3584]{1,0:T(8,128)(2,1)} %bitcast.32), custom_call_target="tpu_custom_call" | custom-call | flops 5637144576 | bytes 13238272 | tf_op jit(solution)/shard_map/raw_forward/pallas_call | solution.py:252
  24.0 1.4 %collective-permute-start.11 = (bf16[64,3584]{1,0:T(8,128)(2,1)S(1)}, bf16[64,3584]{1,0:T(8,128)(2,1)}, u32[]{:S(2)}, u32[]{:S(2)}) collective-permute-start(bf16[64,3584]{1,0:T(8,128)(2,1)S(1)} %collective-permute-done.7.refs_4_), channel_id=1, source_target_pairs={{0,2},{1,3},{4,0},{5,1},{8,4},{9,5},{12,8},{13,9},{14,12},{15,13},... | collective-permute-start | bytes 1376264 | tf_op jit(solution)/shard_map/ppermute | solution.py:88
  25.6 1.9 %copy-done.8 = bf16[1,768,2048]{2,1,0:T(8,128)(2,1)S(1)} copy-done((bf16[1,768,2048]{2,1,0:T(8,128)(2,1)S(1)}, bf16[1,768,2048]{2,1,0:T(8,128)(2,1)}, u32[]{:S(2)}) %copy-start.8) | copy-done | bytes 3145752
  27.5 9.1 %raw_forward.3.refs_1_ = bf16[768,1792]{1,0:T(8,128)(2,1)} custom-call(bf16[768,2048]{1,0:T(8,128)(2,1)S(1)} %bitcast.31, bf16[2048,3584]{1,0:T(8,128)(2,1)} %bitcast.33), custom_call_target="tpu_custom_call" | custom-call | flops 5637144576 | bytes 13238272 | tf_op jit(solution)/shard_map/raw_forward/pallas_call | solution.py:252
  37.4 5.0 %spread_tokens.2 = (bf16[256,3584]{1,0:T(8,128)(2,1)S(1)}, bf16[128,3584]{1,0:T(8,128)(2,1)S(1)}, bf16[128,3584]{1,0:T(8,128)(2,1)}) custom-call(s32[17]{0:T(128)S(1)} %pad_add_fusion.where, f32[8,128]{1,0:T(8,128)S(1)} %squeeze.20.gates, bf16[768,1792]{1,0:T(8,128)(2,1)} %raw_forward.2.refs_0_, bf16[768,1792]{1,0:T(8,128)(2,1)} %raw_forward.3.refs_1_), custom_call_target="tpu_custom_call" | custom-call | flops 1073741824 | bytes 5505024 | tf_op jit(solution)/shard_map/spread_tokens/pallas_call | solution.py:119
  43.5 1.7 %collective-permute-start.14 = (bf16[64,3584]{1,0:T(8,128)(2,1)}, bf16[64,3584]{1,0:T(8,128)(2,1)}, u32[]{:S(2)}, u32[]{:S(2)}) collective-permute-start(bf16[64,3584]{1,0:T(8,128)(2,1)} %collective-permute-done.10.refs_0_), channel_id=1, source_target_pairs={{0,4},{1,5},{4,8},{5,9},{8,12},{9,13},{12,14},{13,15},{14,10},{15,... | collective-permute-start | bytes 1376264 | tf_op jit(solution)/shard_map/ppermute | solution.py:88
  46.1 1.1 add_convert_fusion.6
  48.0 1.1 collective-permute-start.17
  50.9 4.1 %spread_tokens.3 = (bf16[256,3584]{1,0:T(8,128)(2,1)S(1)}, bf16[128,3584]{1,0:T(8,128)(2,1)S(1)}, bf16[128,3584]{1,0:T(8,128)(2,1)S(1)}) custom-call(s32[17]{0:T(128)S(1)} %pad_add_fusion.where, f32[8,128]{1,0:T(8,128)S(1)} %squeeze.20.gates, bf16[768,1792]{1,0:T(8,128)(2,1)} %raw_forward.2.refs_0_, bf16[768,1792]{1,0:T(8,128)(2,1)} %raw_forward.3.refs_1_), custom_call_target="tpu_custom_call" | custom-call | flops 1073741824 | bytes 5505024 | tf_op jit(solution)/shard_map/spread_tokens/pallas_call | solution.py:119
  55.0 10.0 %backward.5 = (bf16[288,1024]{1,0:T(8,128)(2,1)S(1)}, bf16[288,1024]{1,0:T(8,128)(2,1)S(1)}) custom-call(s32[17]{0:T(128)S(1)} %pad_add_fusion.where, s32[1]{0:T(128)} %bitcast.1.pipe, f32[8,128]{1,0:T(8,128)S(1)} %squeeze.21.gates, bf16[2048,3584]{1,0:T(8,128)(2,1)} %bitcast.34, bf16[64,3584]{1,0:T(8,128)(2,1)S(1)} %copy-done, ...), custom_call_target="tpu_custom_call" | custom-call | flops 66060288 | bytes 312320 | tf_op jit(solution)/shard_map/backward/pallas_call | solution.py:119
  65.0 1.1 collective-permute-done.17
  66.1 1.5 %collective-permute-done.18 = bf16[64,3584]{1,0:T(8,128)(2,1)} collective-permute-done((bf16[64,3584]{1,0:T(8,128)(2,1)}, bf16[64,3584]{1,0:T(8,128)(2,1)}, u32[]{:S(2)}, u32[]{:S(2)}) %collective-permute-start.18) | collective-permute-done | bytes 458784 | tf_op jit(solution)/shard_map/ppermute | solution.py:88
  68.6 1.0 collective-permute-done.21.refs_1_
  69.8 1.8 %add_convert_fusion.4 = (bf16[64,3584]{1,0:T(8,128)(2,1)S(1)}, bf16[64,3584]{1,0:T(8,128)(2,1)S(1)}) fusion(bf16[64,3584]{1,0:T(8,128)(2,1)} %collective-permute-done.17, bf16[128,3584]{1,0:T(8,128)(2,1)} %collective-permute-done.13, bf16[256,3584]{1,0:T(8,128)(2,1)S(1)} %get-tuple-element.81, bf16[64,3584]{1,0:T(8,128)(2,1)} %collective-permute-done.18), kind=kLoop, calls=%fused_computation.4 | loop fusion | flops 2752512 | bytes 3670016 | tf_op jit(solution)/shard_map/convert_element_type | solution.py:31
  71.5 2.0 %collective-permute-done.22.refs_3_ = bf16[64,3584]{1,0:T(8,128)(2,1)S(1)} collective-permute-done((bf16[64,3584]{1,0:T(8,128)(2,1)}, bf16[64,3584]{1,0:T(8,128)(2,1)S(1)}, u32[]{:S(2)}, u32[]{:S(2)}) %collective-permute-start.22) | collective-permute-done | bytes 458784 | tf_op jit(solution)/shard_map/ppermute | solution.py:92
  73.6 1.2 %collective-permute-start.25 = (bf16[64,3584]{1,0:T(8,128)(2,1)S(1)}, bf16[64,3584]{1,0:T(8,128)(2,1)S(1)}, u32[]{:S(2)}, u32[]{:S(2)}) collective-permute-start(bf16[64,3584]{1,0:T(8,128)(2,1)S(1)} %get-tuple-element.125), channel_id=1, source_target_pairs={{0,2},{1,3},{4,0},{5,1},{8,4},{9,5},{12,8},{13,9},{14,12},{15,13},... | collective-permute-start | bytes 1376264 | tf_op jit(solution)/shard_map/ppermute | solution.py:88
  75.6 1.7 %collective-permute-start.26 = (bf16[64,3584]{1,0:T(8,128)(2,1)S(1)}, bf16[64,3584]{1,0:T(8,128)(2,1)S(1)}, u32[]{:S(2)}, u32[]{:S(2)}) collective-permute-start(bf16[64,3584]{1,0:T(8,128)(2,1)S(1)} %get-tuple-element.124), channel_id=1, source_target_pairs={{0,4},{1,5},{4,8},{5,9},{8,12},{9,13},{12,14},{13,15},{14,10},{15,... | collective-permute-start | bytes 1376264 | tf_op jit(solution)/shard_map/ppermute | solution.py:88
  77.3 1.5 %collective-permute-start.29 = (bf16[288,1024]{1,0:T(8,128)(2,1)S(1)}, bf16[288,1024]{1,0:T(8,128)(2,1)S(1)}, u32[]{:S(2)}, u32[]{:S(2)}) collective-permute-start(bf16[288,1024]{1,0:T(8,128)(2,1)S(1)} %get-tuple-element.103), channel_id=1, source_target_pairs={{0,16},{16,0},{1,17},{17,1},{2,18},{18,2},{3,19},{19,3},{4,20},{20... | collective-permute-start | bytes 1769480 | tf_op jit(solution)/shard_map/ppermute | solution.py:100
  78.8 9.0 %backward.6 = (bf16[192,1024]{1,0:T(8,128)(2,1)S(1)}, bf16[192,1024]{1,0:T(8,128)(2,1)S(1)}) custom-call(s32[17]{0:T(128)S(1)} %pad_add_fusion.where, s32[1]{0:T(128)} %bitcast.1.pipe, f32[8,128]{1,0:T(8,128)S(1)} %squeeze.21.gates, bf16[2048,3584]{1,0:T(8,128)(2,1)} %bitcast.35, bf16[64,3584]{1,0:T(8,128)(2,1)} %collective-permute-done.10.refs_0_, ...), custom_call_target="tpu_custom_call" | custom-call | flops 2818572288 | bytes 18219008 | tf_op jit(solution)/shard_map/backward/pallas_call | solution.py:119
  89.1 9.0 %backward.7 = (bf16[192,1024]{1,0:T(8,128)(2,1)S(1)}, bf16[192,1024]{1,0:T(8,128)(2,1)S(1)}) custom-call(s32[17]{0:T(128)S(1)} %pad_add_fusion.where, s32[1]{0:T(128)} %bitcast.1.pipe, f32[8,128]{1,0:T(8,128)S(1)} %squeeze.21.gates, bf16[2048,3584]{1,0:T(8,128)(2,1)} %bitcast.36, bf16[64,3584]{1,0:T(8,128)(2,1)} %collective-permute-done.14.refs_0_, ...), custom_call_target="tpu_custom_call" | custom-call | flops 44040192 | bytes 284672 | tf_op jit(solution)/shard_map/backward/pallas_call | solution.py:119
  98.0 2.2 %collective-permute-done.30.refs_3_ = bf16[192,1024]{1,0:T(8,128)(2,1)S(1)} collective-permute-done((bf16[192,1024]{1,0:T(8,128)(2,1)S(1)}, bf16[192,1024]{1,0:T(8,128)(2,1)S(1)}, u32[]{:S(2)}, u32[]{:S(2)}) %collective-permute-start.30) | collective-permute-done | bytes 393248 | tf_op jit(solution)/shard_map/ppermute | solution.py:100
  100.6 1.8 %collective-permute-start.32 = (bf16[64,3584]{1,0:T(8,128)(2,1)S(1)}, bf16[64,3584]{1,0:T(8,128)(2,1)S(1)}, u32[]{:S(2)}, u32[]{:S(2)}) collective-permute-start(bf16[64,3584]{1,0:T(8,128)(2,1)S(1)} %get-tuple-element.129), channel_id=1, source_target_pairs={{0,4},{1,5},{4,8},{5,9},{8,12},{9,13},{12,14},{13,15},{14,10},{15,... | collective-permute-start | bytes 1376264 | tf_op jit(solution)/shard_map/ppermute | solution.py:88
  102.7 1.5 %collective-permute-start.34 = (bf16[192,1024]{1,0:T(8,128)(2,1)S(1)}, bf16[192,1024]{1,0:T(8,128)(2,1)S(1)}, u32[]{:S(2)}, u32[]{:S(2)}) collective-permute-start(bf16[192,1024]{1,0:T(8,128)(2,1)S(1)} %get-tuple-element.114), channel_id=1, source_target_pairs={{0,16},{16,0},{1,17},{17,1},{2,18},{18,2},{3,19},{19,3},{4,20},{20... | collective-permute-start | bytes 1179656 | tf_op jit(solution)/shard_map/ppermute | solution.py:100
  104.2 5.5 %backward.8 = bf16[96,1024]{1,0:T(8,128)(2,1)S(1)} custom-call(s32[17]{0:T(128)S(1)} %pad_add_fusion.where, s32[1]{0:T(128)} %bitcast.1.pipe, f32[8,128]{1,0:T(8,128)S(1)} %squeeze.21.gates, bf16[2048,3584]{1,0:T(8,128)(2,1)} %bitcast.37, bf16[64,3584]{1,0:T(8,128)(2,1)S(1)} %collective-permute-done.27.refs_0_, ...), custom_call_target="tpu_custom_call" | custom-call | flops 704643072 | bytes 16449536 | tf_op jit(solution)/shard_map/backward/pallas_call | solution.py:119
  110.3 5.5 %backward.9.refs_0_ = bf16[96,1024]{1,0:T(8,128)(2,1)S(1)} custom-call(s32[17]{0:T(128)S(1)} %pad_add_fusion.where, s32[1]{0:T(128)} %bitcast.1.pipe, f32[8,128]{1,0:T(8,128)S(1)} %squeeze.21.gates, bf16[2048,3584]{1,0:T(8,128)(2,1)} %bitcast.38, bf16[64,3584]{1,0:T(8,128)(2,1)S(1)} %collective-permute-done.27.refs_0_, ...), custom_call_target="tpu_custom_call" | custom-call | flops 11010048 | bytes 257024 | tf_op jit(solution)/shard_map/backward/pallas_call | solution.py:119
  116.8 1.7 %collect.2.refs_2_ = bf16[768,1024]{1,0:T(8,128)(2,1)} custom-call(s32[17]{0:T(128)S(1)} %pad_add_fusion.where, bf16[288,1024]{1,0:T(8,128)(2,1)S(1)} %get-tuple-element.77.refs_0_, bf16[288,1024]{1,0:T(8,128)(2,1)S(1)} %collective-permute-done.29.refs_1_, bf16[192,1024]{1,0:T(8,128)(2,1)S(1)} %get-tuple-element.106.refs_2_, ...), custom_call_target="tpu_custom_call" | custom-call | flops 1048576 | bytes 4128768 | tf_op jit(solution)/shard_map/collect/pallas_call | solution.py:432
  118.5 1.3 %collect.3 = bf16[768,1024]{1,0:T(8,128)(2,1)} custom-call(s32[17]{0:T(128)S(1)} %pad_add_fusion.where, bf16[96,1024]{1,0:T(8,128)(2,1)S(1)} %backward.9.refs_0_, bf16[96,1024]{1,0:T(8,128)(2,1)S(1)} %collective-permute-done.35.refs_1_, bf16[768,1024]{1,0:T(8,128)(2,1)} %collect.2.refs_2_), custom_call_target="tpu_custom_call", output_to_operand_aliasing={{}: (3, {})} | custom-call | flops 1048576 | bytes 589824 | tf_op jit(solution)/shard_map/collect/pallas_call | solution.py:432
  (85 shorter events, 14.2 us)
Async XLA Ops:
  1.5 5.4 %collective-permute-start.1 = (f32[16,128]{1,0:T(8,128)S(1)}, f32[16,128]{1,0:T(8,128)S(1)}, u32[]{:S(2)}, u32[]{:S(2)}) collective-permute-start(f32[16,128]{1,0:T(8,128)S(1)} %gates.1), channel_id=1, source_target_pairs={{0,2},{1,3},{2,0},{3,1},{4,6},{5,7},{6,4},{7,5},{8,10},{9,11},{10,... | collective-permute-start | bytes 24584 | tf_op jit(solution)/shard_map/ppermute | solution.py:92
  4.7 18.6 %collective-permute-start.6 = (bf16[64,3584]{1,0:T(8,128)(2,1)}, bf16[64,3584]{1,0:T(8,128)(2,1)S(1)}, u32[]{:S(2)}, u32[]{:S(2)}) collective-permute-start(bf16[64,3584]{1,0:T(8,128)(2,1)} %refs_0_.1), channel_id=1, source_target_pairs={{0,4},{1,5},{4,8},{5,9},{8,12},{9,13},{12,14},{13,15},{14,10},{15,... | collective-permute-start | bytes 1376264 | tf_op jit(solution)/shard_map/ppermute | solution.py:88
  6.7 16.6 %collective-permute-start.7 = (bf16[64,3584]{1,0:T(8,128)(2,1)}, bf16[64,3584]{1,0:T(8,128)(2,1)S(1)}, u32[]{:S(2)}, u32[]{:S(2)}) collective-permute-start(bf16[64,3584]{1,0:T(8,128)(2,1)} %refs_0_.1), channel_id=1, source_target_pairs={{0,2},{1,3},{4,0},{5,1},{8,4},{9,5},{12,8},{13,9},{14,12},{15,13},... | collective-permute-start | bytes 1376264 | tf_op jit(solution)/shard_map/ppermute | solution.py:88
  7.6 15.5 %collective-permute-start.3 = (f32[4,4,128]{2,0,1:T(4,128)S(1)}, f32[4,4,128]{2,0,1:T(4,128)S(1)}, u32[]{:S(2)}, u32[]{:S(2)}) collective-permute-start(f32[4,4,128]{2,0,1:T(4,128)S(1)} %bitcast.41), channel_id=1, source_target_pairs={{0,4},{1,5},{2,6},{3,7},{4,0},{5,1},{6,2},{7,3},{8,12},{9,13},{10,... | collective-permute-start | bytes 24584 | tf_op jit(solution)/shard_map/ppermute | solution.py:92
  9.3 14.0 %collective-permute-start.4 = (f32[4,4,128]{2,0,1:T(4,128)S(1)}, f32[4,4,128]{2,0,1:T(4,128)S(1)}, u32[]{:S(2)}, u32[]{:S(2)}) collective-permute-start(f32[4,4,128]{2,0,1:T(4,128)S(1)} %bitcast.42), channel_id=1, source_target_pairs={{0,8},{1,9},{2,10},{3,11},{4,12},{5,13},{6,14},{7,15},{8,0},{9,1},... | collective-permute-start | bytes 24584 | tf_op jit(solution)/shard_map/ppermute | solution.py:92
  11.9 11.4 %collective-permute-start.5 = (f32[4,4,128]{2,0,1:T(4,128)S(1)}, f32[4,4,128]{2,0,1:T(4,128)S(1)}, u32[]{:S(2)}, u32[]{:S(2)}) collective-permute-start(f32[4,4,128]{2,0,1:T(4,128)S(1)} %bitcast.43), channel_id=1, source_target_pairs={{0,12},{1,13},{2,14},{3,15},{4,8},{5,9},{6,10},{7,11},{8,4},{9,5},... | collective-permute-start | bytes 24584 | tf_op jit(solution)/shard_map/ppermute | solution.py:92
  23.2 13.4 %collective-permute-start.12 = (bf16[64,3584]{1,0:T(8,128)(2,1)S(1)}, bf16[64,3584]{1,0:T(8,128)(2,1)S(1)}, u32[]{:S(2)}, u32[]{:S(2)}) collective-permute-start(bf16[64,3584]{1,0:T(8,128)(2,1)S(1)} %copy-done), channel_id=1, source_target_pairs={{0,1},{1,0},{2,3},{3,2},{4,5},{5,4},{6,7},{7,6},{8,9},{9,8},{10,11... | collective-permute-start | bytes 1376264 | tf_op jit(solution)/shard_map/ppermute | solution.py:92
  23.3 14.1 %collective-permute-start.10 = (bf16[64,3584]{1,0:T(8,128)(2,1)S(1)}, bf16[64,3584]{1,0:T(8,128)(2,1)}, u32[]{:S(2)}, u32[]{:S(2)}) collective-permute-start(bf16[64,3584]{1,0:T(8,128)(2,1)S(1)} %collective-permute-done.6.refs_2_), channel_id=1, source_target_pairs={{0,4},{1,5},{4,8},{5,9},{8,12},{9,13},{12,14},{13,15},{14,10},{15,... | collective-permute-start | bytes 1376264 | tf_op jit(solution)/shard_map/ppermute | solution.py:88
  24.0 13.4 %collective-permute-start.11 = (bf16[64,3584]{1,0:T(8,128)(2,1)S(1)}, bf16[64,3584]{1,0:T(8,128)(2,1)}, u32[]{:S(2)}, u32[]{:S(2)}) collective-permute-start(bf16[64,3584]{1,0:T(8,128)(2,1)S(1)} %collective-permute-done.7.refs_4_), channel_id=1, source_target_pairs={{0,2},{1,3},{4,0},{5,1},{8,4},{9,5},{12,8},{13,9},{14,12},{15,13},... | collective-permute-start | bytes 1376264 | tf_op jit(solution)/shard_map/ppermute | solution.py:88
  42.5 4.8 %collective-permute-start.8 = (bf16[64,3584]{1,0:T(8,128)(2,1)S(1)}, bf16[64,3584]{1,0:T(8,128)(2,1)S(1)}, u32[]{:S(2)}, u32[]{:S(2)}) collective-permute-start(bf16[64,3584]{1,0:T(8,128)(2,1)S(1)} %collective-permute-done.6.refs_2_), channel_id=1, source_target_pairs={{0,1},{1,0},{2,3},{3,2},{4,5},{5,4},{6,7},{7,6},{8,9},{9,8},{10,11... | collective-permute-start | bytes 1376264 | tf_op jit(solution)/shard_map/ppermute | solution.py:92
  42.9 6.1 %collective-permute-start.9 = (bf16[64,3584]{1,0:T(8,128)(2,1)S(1)}, bf16[64,3584]{1,0:T(8,128)(2,1)S(1)}, u32[]{:S(2)}, u32[]{:S(2)}) collective-permute-start(bf16[64,3584]{1,0:T(8,128)(2,1)S(1)} %collective-permute-done.7.refs_4_), channel_id=1, source_target_pairs={{0,1},{1,0},{2,3},{3,2},{4,5},{5,4},{6,7},{7,6},{8,9},{9,8},{10,11... | collective-permute-start | bytes 1376264 | tf_op jit(solution)/shard_map/ppermute | solution.py:92
  43.0 7.9 %collective-permute-start.13 = (bf16[128,3584]{1,0:T(8,128)(2,1)}, bf16[128,3584]{1,0:T(8,128)(2,1)}, u32[]{:S(2)}, u32[]{:S(2)}) collective-permute-start(bf16[128,3584]{1,0:T(8,128)(2,1)} %get-tuple-element.70), channel_id=1, source_target_pairs={{0,1},{1,0},{2,3},{3,2},{4,5},{5,4},{6,7},{7,6},{8,9},{9,8},{10,11... | collective-permute-start | bytes 2752520 | tf_op jit(solution)/shard_map/ppermute | solution.py:92
  43.5 21.5 %collective-permute-start.14 = (bf16[64,3584]{1,0:T(8,128)(2,1)}, bf16[64,3584]{1,0:T(8,128)(2,1)}, u32[]{:S(2)}, u32[]{:S(2)}) collective-permute-start(bf16[64,3584]{1,0:T(8,128)(2,1)} %collective-permute-done.10.refs_0_), channel_id=1, source_target_pairs={{0,4},{1,5},{4,8},{5,9},{8,12},{9,13},{12,14},{13,15},{14,10},{15,... | collective-permute-start | bytes 1376264 | tf_op jit(solution)/shard_map/ppermute | solution.py:88
  45.1 19.9 %collective-permute-start.15 = (bf16[64,3584]{1,0:T(8,128)(2,1)}, bf16[64,3584]{1,0:T(8,128)(2,1)}, u32[]{:S(2)}, u32[]{:S(2)}) collective-permute-start(bf16[64,3584]{1,0:T(8,128)(2,1)} %collective-permute-done.11.refs_2_), channel_id=1, source_target_pairs={{0,2},{1,3},{4,0},{5,1},{8,4},{9,5},{12,8},{13,9},{14,12},{15,13},... | collective-permute-start | bytes 1376264 | tf_op jit(solution)/shard_map/ppermute | solution.py:88
  48.0 18.1 %collective-permute-start.17 = (bf16[64,3584]{1,0:T(8,128)(2,1)}, bf16[64,3584]{1,0:T(8,128)(2,1)}, u32[]{:S(2)}, u32[]{:S(2)}) collective-permute-start(bf16[64,3584]{1,0:T(8,128)(2,1)} %get-tuple-element.127), channel_id=1, source_target_pairs={{0,4},{1,5},{4,8},{5,9},{8,12},{9,13},{12,14},{13,15},{14,10},{15,... | collective-permute-start | bytes 1376264 | tf_op jit(solution)/shard_map/ppermute | solution.py:88
  49.8 17.8 %collective-permute-start.18 = (bf16[64,3584]{1,0:T(8,128)(2,1)}, bf16[64,3584]{1,0:T(8,128)(2,1)}, u32[]{:S(2)}, u32[]{:S(2)}) collective-permute-start(bf16[64,3584]{1,0:T(8,128)(2,1)} %get-tuple-element.126), channel_id=1, source_target_pairs={{0,2},{1,3},{4,0},{5,1},{8,4},{9,5},{12,8},{13,9},{14,12},{15,13},... | collective-permute-start | bytes 1376264 | tf_op jit(solution)/shard_map/ppermute | solution.py:88
  67.6 9.7 %collective-permute-start.23 = (bf16[64,3584]{1,0:T(8,128)(2,1)}, bf16[64,3584]{1,0:T(8,128)(2,1)S(1)}, u32[]{:S(2)}, u32[]{:S(2)}) collective-permute-start(bf16[64,3584]{1,0:T(8,128)(2,1)} %collective-permute-done.10.refs_0_), channel_id=1, source_target_pairs={{0,1},{1,0},{2,3},{3,2},{4,5},{5,4},{6,7},{7,6},{8,9},{9,8},{10,11... | collective-permute-start | bytes 1376264 | tf_op jit(solution)/shard_map/ppermute | solution.py:92
  68.1 10.7 %collective-permute-start.24 = (bf16[64,3584]{1,0:T(8,128)(2,1)}, bf16[64,3584]{1,0:T(8,128)(2,1)S(1)}, u32[]{:S(2)}, u32[]{:S(2)}) collective-permute-start(bf16[64,3584]{1,0:T(8,128)(2,1)} %collective-permute-done.11.refs_2_), channel_id=1, source_target_pairs={{0,1},{1,0},{2,3},{3,2},{4,5},{5,4},{6,7},{7,6},{8,9},{9,8},{10,11... | collective-permute-start | bytes 1376264 | tf_op jit(solution)/shard_map/ppermute | solution.py:92
  68.1 6.7 %collective-permute-start.19 = (bf16[128,3584]{1,0:T(8,128)(2,1)S(1)}, bf16[128,3584]{1,0:T(8,128)(2,1)S(1)}, u32[]{:S(2)}, u32[]{:S(2)}) collective-permute-start(bf16[128,3584]{1,0:T(8,128)(2,1)S(1)} %get-tuple-element.85), channel_id=1, source_target_pairs={{0,1},{1,0},{2,3},{3,2},{4,5},{5,4},{6,7},{7,6},{8,9},{9,8},{10,11... | collective-permute-start | bytes 2752520 | tf_op jit(solution)/shard_map/ppermute | solution.py:92
  68.6 7.0 %collective-permute-start.20 = (bf16[128,3584]{1,0:T(8,128)(2,1)S(1)}, bf16[128,3584]{1,0:T(8,128)(2,1)S(1)}, u32[]{:S(2)}, u32[]{:S(2)}) collective-permute-start(bf16[128,3584]{1,0:T(8,128)(2,1)S(1)} %get-tuple-element.86), channel_id=1, source_target_pairs={{0,1},{1,0},{2,3},{3,2},{4,5},{5,4},{6,7},{7,6},{8,9},{9,8},{10,11... | collective-permute-start | bytes 2752520 | tf_op jit(solution)/shard_map/ppermute | solution.py:92
  69.6 3.9 %collective-permute-start.22 = (bf16[64,3584]{1,0:T(8,128)(2,1)}, bf16[64,3584]{1,0:T(8,128)(2,1)S(1)}, u32[]{:S(2)}, u32[]{:S(2)}) collective-permute-start(bf16[64,3584]{1,0:T(8,128)(2,1)} %collective-permute-done.15.refs_2_), channel_id=1, source_target_pairs={{0,1},{1,0},{2,3},{3,2},{4,5},{5,4},{6,7},{7,6},{8,9},{9,8},{10,11... | collective-permute-start | bytes 1376264 | tf_op jit(solution)/shard_map/ppermute | solution.py:92
  73.6 14.2 %collective-permute-start.25 = (bf16[64,3584]{1,0:T(8,128)(2,1)S(1)}, bf16[64,3584]{1,0:T(8,128)(2,1)S(1)}, u32[]{:S(2)}, u32[]{:S(2)}) collective-permute-start(bf16[64,3584]{1,0:T(8,128)(2,1)S(1)} %get-tuple-element.125), channel_id=1, source_target_pairs={{0,2},{1,3},{4,0},{5,1},{8,4},{9,5},{12,8},{13,9},{14,12},{15,13},... | collective-permute-start | bytes 1376264 | tf_op jit(solution)/shard_map/ppermute | solution.py:88
  74.8 23.2 %collective-permute-start.27 = (bf16[64,3584]{1,0:T(8,128)(2,1)}, bf16[64,3584]{1,0:T(8,128)(2,1)S(1)}, u32[]{:S(2)}, u32[]{:S(2)}) collective-permute-start(bf16[64,3584]{1,0:T(8,128)(2,1)} %collective-permute-done.14.refs_0_), channel_id=1, source_target_pairs={{0,4},{1,5},{4,8},{5,9},{8,12},{9,13},{12,14},{13,15},{14,10},{15,... | collective-permute-start | bytes 1376264 | tf_op jit(solution)/shard_map/ppermute | solution.py:88
  75.6 22.4 %collective-permute-start.26 = (bf16[64,3584]{1,0:T(8,128)(2,1)S(1)}, bf16[64,3584]{1,0:T(8,128)(2,1)S(1)}, u32[]{:S(2)}, u32[]{:S(2)}) collective-permute-start(bf16[64,3584]{1,0:T(8,128)(2,1)S(1)} %get-tuple-element.124), channel_id=1, source_target_pairs={{0,4},{1,5},{4,8},{5,9},{8,12},{9,13},{12,14},{13,15},{14,10},{15,... | collective-permute-start | bytes 1376264 | tf_op jit(solution)/shard_map/ppermute | solution.py:88
  77.3 20.7 %collective-permute-start.29 = (bf16[288,1024]{1,0:T(8,128)(2,1)S(1)}, bf16[288,1024]{1,0:T(8,128)(2,1)S(1)}, u32[]{:S(2)}, u32[]{:S(2)}) collective-permute-start(bf16[288,1024]{1,0:T(8,128)(2,1)S(1)} %get-tuple-element.103), channel_id=1, source_target_pairs={{0,16},{16,0},{1,17},{17,1},{2,18},{18,2},{3,19},{19,3},{4,20},{20... | collective-permute-start | bytes 1769480 | tf_op jit(solution)/shard_map/ppermute | solution.py:100
  87.9 12.3 %collective-permute-start.28 = (bf16[64,3584]{1,0:T(8,128)(2,1)S(1)}, bf16[64,3584]{1,0:T(8,128)(2,1)S(1)}, u32[]{:S(2)}, u32[]{:S(2)}) collective-permute-start(bf16[64,3584]{1,0:T(8,128)(2,1)S(1)} %add_convert_fusion.3), channel_id=1, source_target_pairs={{0,2},{1,3},{4,0},{5,1},{8,4},{9,5},{12,8},{13,9},{14,12},{15,13},... | collective-permute-start | bytes 1376264 | tf_op jit(solution)/shard_map/ppermute | solution.py:88
  88.3 11.9 %collective-permute-start.30 = (bf16[192,1024]{1,0:T(8,128)(2,1)S(1)}, bf16[192,1024]{1,0:T(8,128)(2,1)S(1)}, u32[]{:S(2)}, u32[]{:S(2)}) collective-permute-start(bf16[192,1024]{1,0:T(8,128)(2,1)S(1)} %get-tuple-element.104), channel_id=1, source_target_pairs={{0,16},{16,0},{1,17},{17,1},{2,18},{18,2},{3,19},{19,3},{4,20},{20... | collective-permute-start | bytes 1179656 | tf_op jit(solution)/shard_map/ppermute | solution.py:100
  100.3 3.9 %collective-permute-start.31 = (bf16[64,3584]{1,0:T(8,128)(2,1)S(1)}, bf16[64,3584]{1,0:T(8,128)(2,1)S(1)}, u32[]{:S(2)}, u32[]{:S(2)}) collective-permute-start(bf16[64,3584]{1,0:T(8,128)(2,1)S(1)} %collective-permute-done.27.refs_0_), channel_id=1, source_target_pairs={{0,1},{1,0},{2,3},{3,2},{4,5},{5,4},{6,7},{7,6},{8,9},{9,8},{10,11... | collective-permute-start | bytes 1376264 | tf_op jit(solution)/shard_map/ppermute | solution.py:92
  100.6 15.2 %collective-permute-start.32 = (bf16[64,3584]{1,0:T(8,128)(2,1)S(1)}, bf16[64,3584]{1,0:T(8,128)(2,1)S(1)}, u32[]{:S(2)}, u32[]{:S(2)}) collective-permute-start(bf16[64,3584]{1,0:T(8,128)(2,1)S(1)} %get-tuple-element.129), channel_id=1, source_target_pairs={{0,4},{1,5},{4,8},{5,9},{8,12},{9,13},{12,14},{13,15},{14,10},{15,... | collective-permute-start | bytes 1376264 | tf_op jit(solution)/shard_map/ppermute | solution.py:88
  102.4 13.4 %collective-permute-start.33 = (bf16[64,3584]{1,0:T(8,128)(2,1)S(1)}, bf16[64,3584]{1,0:T(8,128)(2,1)S(1)}, u32[]{:S(2)}, u32[]{:S(2)}) collective-permute-start(bf16[64,3584]{1,0:T(8,128)(2,1)S(1)} %get-tuple-element.128), channel_id=1, source_target_pairs={{0,2},{1,3},{4,0},{5,1},{8,4},{9,5},{12,8},{13,9},{14,12},{15,13},... | collective-permute-start | bytes 1376264 | tf_op jit(solution)/shard_map/ppermute | solution.py:88
  102.7 13.1 %collective-permute-start.34 = (bf16[192,1024]{1,0:T(8,128)(2,1)S(1)}, bf16[192,1024]{1,0:T(8,128)(2,1)S(1)}, u32[]{:S(2)}, u32[]{:S(2)}) collective-permute-start(bf16[192,1024]{1,0:T(8,128)(2,1)S(1)} %get-tuple-element.114), channel_id=1, source_target_pairs={{0,16},{16,0},{1,17},{17,1},{2,18},{18,2},{3,19},{19,3},{4,20},{20... | collective-permute-start | bytes 1179656 | tf_op jit(solution)/shard_map/ppermute | solution.py:100
  109.7 8.9 %collective-permute-start.35 = (bf16[96,1024]{1,0:T(8,128)(2,1)S(1)}, bf16[96,1024]{1,0:T(8,128)(2,1)S(1)}, u32[]{:S(2)}, u32[]{:S(2)}) collective-permute-start(bf16[96,1024]{1,0:T(8,128)(2,1)S(1)} %backward.8), channel_id=1, source_target_pairs={{0,16},{16,0},{1,17},{17,1},{2,18},{18,2},{3,19},{19,3},{4,20},{20... | collective-permute-start | bytes 589832 | tf_op jit(solution)/shard_map/ppermute | solution.py:100
  (13 other events, 38.5 us)

commit v2 on v1

--- a/solution.py
+++ b/solution.py
@@ -10,6 +10,7 @@
 BF16, F32 = jnp.bfloat16, jnp.float32
 TILE = 512
 LANES = 128
+RAW_TILE = 256
 
 
 def dense_gates(routes, gates, total):
@@ -215,17 +216,27 @@
             copy.wait()
 
 
-def raw_kernel(first, hidden, weights, out, buffer, sems, staged, out_sems):
-    tile, tiles = buffer.shape[2], out.shape[1] // buffer.shape[2]
+def raw_kernel(first, hidden, weights, out, held, held_sems, buffer, sems, staged, out_sems):
+    tiles = out.shape[1] // RAW_TILE
     stream = Stream(
-        lambda n: weights.at[:, pl.ds(pl.multiple_of(first + n * tile, tile), tile)], buffer, sems
-    )
-    for n in range(stream.slots):
+        lambda n: weights.at[:, pl.ds(pl.multiple_of(first + n * RAW_TILE, RAW_TILE), RAW_TILE)], buffer, sems
+    )
+    rows = held.shape[0] // held_sems.shape[0]
+    fetch = []
+    for i in range(held_sems.shape[0]):
+        at = pl.ds(i * rows, rows)
+        fetch.append(pltpu.make_async_copy(hidden.at[at, :], held.at[at, :], held_sems.at[i]))
+        fetch[-1].start()
+    stream.start(0)
+
+    def put(n):
+        cols = pl.ds(pl.multiple_of(n * RAW_TILE, RAW_TILE), RAW_TILE)
+        return pltpu.make_async_copy(staged.at[n % 2], out.at[:, cols], out_sems.at[n % 2])
+
+    for copy in fetch:
+        copy.wait()
+    for n in range(1, stream.slots):
         stream.start(n)
-
-    def put(n):
-        cols = pl.ds(pl.multiple_of(n * tile, tile), tile)
-        return pltpu.make_async_copy(staged.at[n % 2], out.at[:, cols], out_sems.at[n % 2])
 
     @pl.loop(0, tiles)
     def _(n):
@@ -235,7 +246,7 @@
         def _():
             put(n - 2).wait()
 
-        value = jnp.dot(hidden[...], buffer[n % stream.slots], preferred_element_type=F32)
+        value = jnp.dot(held[...], buffer[n % stream.slots], preferred_element_type=F32)
         staged[n % 2] = value.astype(BF16)
         put(n).start()
 
@@ -251,13 +262,15 @@
     rows, depth = hidden.shape
     return pl.pallas_call(
         functools.partial(raw_kernel, first),
-        in_specs=[VMEM, HBM],
+        in_specs=[HBM, HBM],
         out_specs=HBM,
         out_shape=pltpu.HBM((rows, width), BF16),
         scratch_shapes=[
-            pltpu.VMEM((3, depth, 256), BF16),
+            pltpu.VMEM(hidden.shape, BF16),
+            pltpu.SemaphoreType.DMA((4,)),
+            pltpu.VMEM((3, depth, RAW_TILE), BF16),
             pltpu.SemaphoreType.DMA((3, 4)),
-            pltpu.VMEM((2, rows, 256), BF16),
+            pltpu.VMEM((2, rows, RAW_TILE), BF16),
             pltpu.SemaphoreType.DMA((2,)),
         ],
         compiler_params=pltpu.CompilerParams(vmem_limit_bytes=20 * 2**20),
@@ -276,15 +289,20 @@
     target, place, slot_gates, to_tokens, held, sems = scratch
     rows, half = 2 * cap, gates.shape[1] // 2
     width = raws[0].shape[1]
-    fetch = []
+
+    def fetch(i, start):
+        return [
+            pltpu.make_async_copy(
+                raw.at[pl.ds(start, rows), :],
+                held.at[i, :, pl.ds(j * width, width)],
+                sems.at[i, j],
+            )
+            for j, raw in enumerate(raws)
+        ]
+
     for i, d in enumerate(distances):
-        start = pl.multiple_of(where[d % 8] * rows, rows)
-        for j, raw in enumerate(raws):
-            source = raw.at[pl.ds(start, rows), :]
-            fetch.append(
-                pltpu.make_async_copy(source, held.at[i, :, pl.ds(j * width, width)], sems.at[i, j])
-            )
-            fetch[-1].start()
+        for copy in fetch(i, pl.multiple_of(where[d % 8] * rows, rows)):
+            copy.start()
     place_slots(distances, where, gates, cap, target, place, slot_gates)
     tokens = 2 * half
     same = lax.broadcasted_iota(jnp.int32, (tokens, tokens), 0) == lax.broadcasted_iota(
@@ -295,13 +313,13 @@
         to_tokens[i] = lax.dot_general(
             same, place[i], (((1,), (1,)), ((), ())), preferred_element_type=F32
         ).astype(BF16)
-    for copy in fetch:
-        copy.wait()
     for g, other in enumerate(others):
 
         @pl.loop(0, split)
         def _(j):
             i = g * split + j
+            for copy in fetch(i, 0):
+                copy.wait()
             for n in range(2 * width // TILE):
                 cols = pl.ds(n * TILE, TILE)
                 part = held[i, :, cols].astype(F32)
@@ -468,7 +486,7 @@
     four = jnp.stack([both] + [xor(both, j) for j in (1, 2, 3)])
     four = lax.dynamic_index_in_dim(four.reshape(4, 4, 4, 2 * tokens), me % 4, 2, False)
     weights, four = tie(weights, four)
-    raw1 = raw_forward(0, width // 2, hidden, pin(weights))
+    raw1 = raw_forward(0, width // 2, pin(hidden), pin(weights))
     every = jnp.stack([four] + [xor(four, 4 * k) for k in (1, 2, 3)])
     raw1, weights, every, got[-1], got[1] = tie(raw1, weights, every, got[-1], got[1])
     weights = pin(weights)
@@ -485,19 +503,23 @@
 
     got[-2], got[2] = step_ring(got[-1], 1), step_ring(got[1], -1)
     pair[0] = core(got[0])
-    raw2 = raw_forward(width // 2, width // 2, hidden, weights)
+    raw2 = raw_forward(width // 2, width // 2, pin(hidden), weights)
     raw2, got[-2], got[2], pair[0] = tie(raw2, got[-2], got[2], pair[0])
 
     got[-3], got[3] = step_ring(got[-2], 1), step_ring(got[2], -1)
     keep1, other1, other2 = spread((3, -4, 2, -3), 2, gate_a)
     other1, other2 = core(other1), core(other2)
-    pair[-1], pair[1] = core(got[-1]), core(got[1])
+    for d in (-1, 1, -2):
+        pair[d] = core(got[d])
     up = step_ring(add(keep1[:tokens], other1[:tokens]), 1)
     down = step_ring(add(keep1[tokens : 2 * tokens], other1[tokens:]), -1)
-    gate_a, pair[-1], pair[1], other2 = tie(gate_a, pair[-1], pair[1], other2)
+    gate_a, pair[-1], pair[1], pair[-2], other2 = tie(
+        gate_a, pair[-1], pair[1], pair[-2], other2
+    )
     keep2, other3, other4 = spread((1, -2, -1, 0), 2, gate_a)
     keep2, gate_b = tie(keep2, gate_b)
-    send1, hold1 = bwd((0, -1, 1), share=64)
+    groups = (0, -1, 1, -2), (2, -3, 3), (-4,)
+    send1, hold1 = bwd(groups[0], share=64)
 
     def mine(i, other, *more):
         at = slice(i * tokens, (i + 1) * tokens)
@@ -511,33 +533,25 @@
     up = step_ring(add(keep1[2 * tokens : 3 * tokens], other2[:tokens], up), 1)
     down = step_ring(add(keep1[3 * tokens :], other2[tokens:], down), -1)
     recv1 = across(send1)
-    pair[-2], pair[2], other3 = core(got[-2]), core(got[2]), core(other3)
-    pair[-3], pair[3], other4 = core(got[-3]), core(got[3]), core(other4)
-    gate_b, other3, other4, pair[-3], pair[3] = tie(gate_b, other3, other4, pair[-3], pair[3])
-    send2, hold2 = bwd((-2, 2))
-
-    hold2, send2, down, gate_b = tie(hold2, send2, down, gate_b)
+    pair[2], pair[-3], pair[3] = core(got[2]), core(got[-3]), core(got[3])
+    other3, other4 = core(other3), core(other4)
+    gate_b, other3, other4 = tie(gate_b, other3, other4)
+    send2, hold2 = bwd(groups[1], share=64)
+
+    hold2, send2, down = tie(hold2, send2, down)
     recv2 = across(send2)
     down = step_ring(mine(1, other3, down), -1)
-    send3, hold3 = bwd((-3, 3), share=64)
-
-    hold3, send3, up, got[-4], down, recv1, recv2 = tie(
-        hold3, send3, up, got[-4], down, recv1, recv2
-    )
-    recv3 = across(send3)
+    up, got[-4], down, recv1 = tie(up, got[-4], down, recv1)
+
     pair[-4] = core(got[-4])
     up, down = step_ring(mine(0, other3, up), 1), step_ring(mine(2, other4, down), -1)
-    (send4,) = bwd((-4,), (0,))
-    recv4 = across(send4)
-    send4, gate_b = tie(send4, gate_b)
-    (hold4,) = bwd((-4,), (1,), 64)
-    hold4, up, down, recv3 = tie(hold4, up, down, recv3)
+    send3, hold3 = bwd(groups[2], share=64)
+    recv3 = across(send3)
+    hold3, recv2 = tie(hold3, recv2)
+    grad = collect(groups[:2], where, (hold1, recv1, hold2, recv2), 8 * rows)
+    grad, up, down, recv3 = tie(grad, up, down, recv3)
     mixed_a = mine(3, other4, up, down)
-    grad = collect(
-        ((0, -1, 1), (-2, 2), (-3, 3)), where, (hold1, recv1, hold2, recv2, hold3, recv3), 8 * rows
-    )
-    grad, mixed_a, recv4 = tie(grad, mixed_a, recv4)
-    grad = collect(((-4,),), where, (hold4, recv4), 8 * rows, grad)
+    grad = collect(groups[2:], where, (hold3, recv3), 8 * rows, grad)
     return (mixed_a, grad[None])
 
 

time: 120 us -> 120 us (level)
  waiting for transfers between devices: 8.69 us -> 20.8 us
  Pallas kernels: 70 us -> 62.6 us
  local copies, waits for them, and re-layouts: 6.44 us -> 2.67 us
    ppermute x14, waiting for transfers between devices: 2.64 us -> 13.7 us  [step_ring(): return lax.ppermute(value, 'expert', pairs)]
    pallas_call x8 -> x6, Pallas kernels: 48.8 us -> 39.1 us  [kernel_call(): pl.pallas_call(kernel, in_specs=in_specs, out_specs=[VMEM] * len(out_shap...]
    unnamed x18 -> x24, local copies, waits for them, and re-layouts: 6.13 us -> 2.36 us
    ppermute x4 -> x3, waiting for transfers between devices: 2.21 us -> 5.19 us  [across(): return lax.ppermute(value, 'pipe', [(0, 1), (1, 0)])]
    pallas_call x2, Pallas kernels: 18.2 us -> 20.5 us  [raw_forward(): pl.pallas_call(functools.partial(raw_kernel, first), in_specs=[HBM, HBM],...]
    ppermute x18, waiting for transfers between devices: 3.83 us -> 1.95 us  [xor(): return lax.ppermute(value, 'expert', [(i, i ^ bits) for i in range(16)])]
    ppermute x4 -> x3, starting transfers between devices: 4.3 us -> 2.63 us  [across(): return lax.ppermute(value, 'pipe', [(0, 1), (1, 0)])]
  transfers between devices with their start and end apart: 36 -> 35, of which waited for: 6 -> 11; matrix products, arithmetic and copies ran while one was open for 4% -> 3% of each run, Pallas kernels for 52% -> 47%
where the time goes in v2:
time: 120 us
  Pallas kernels  62.6 us (52%)
  starting transfers between devices  28.1 us (23%)
  waiting for transfers between devices  20.8 us (17%)
  other arithmetic  4.56 us (4%)
  local copies, waits for them, and re-layouts  2.67 us (2%)
    pallas_call x6, Pallas kernels, kernel_call(): pl.pallas_call(kernel, in_specs=in_specs, out_specs=[VMEM] * len(out_shap...  39.1 us
    pallas_call x2, Pallas kernels, raw_forward(): pl.pallas_call(functools.partial(raw_kernel, first), in_specs=[HBM, HBM],...  20.5 us
    ppermute x14, starting transfers between devices, step_ring(): return lax.ppermute(value, 'expert', pairs)  15.6 us
    ppermute x14, waiting for transfers between devices, step_ring(): return lax.ppermute(value, 'expert', pairs)  13.7 us
    ppermute x18, starting transfers between devices, xor(): return lax.ppermute(value, 'expert', [(i, i ^ bits) for i in range(16)])  9.88 us
    ppermute x3, waiting for transfers between devices, across(): return lax.ppermute(value, 'pipe', [(0, 1), (1, 0)])  5.19 us
    convert_element_type x5, other arithmetic, add(): return total.astype(BF16)  4.44 us
    pallas_call x2, Pallas kernels, collect(): pl.pallas_call(functools.partial(collect_kernel, groups), in_specs=in_spe...  2.98 us
  transfers between devices with their start and end apart: 35, of which 11 were waited for; matrix products, arithmetic and copies ran while one was open for 3% of the time, Pallas kernels for 47%

profile of v2, /device:TPU:0, one launch (start us, length us, event | category | flops | bytes accessed | tf_op | source)
XLA Modules:
  0.0 119.8 jit_solution(5798929065134723296)
XLA Ops:
  0.6 0.9 gates.1
  1.5 2.5 %collective-permute-start.2 = (f32[16,128]{1,0:T(8,128)S(1)}, f32[16,128]{1,0:T(8,128)S(1)}, u32[]{:S(2)}, u32[]{:S(2)}) collective-permute-start(f32[16,128]{1,0:T(8,128)S(1)} %gates.1), channel_id=1, source_target_pairs={{0,3},{1,2},{2,1},{3,0},{4,7},{5,6},{6,5},{7,4},{8,11},{9,10},{10,... | collective-permute-start | bytes 24584 | tf_op jit(solution)/shard_map/ppermute | solution.py:93
  4.7 2.0 %collective-permute-start.6 = (bf16[64,3584]{1,0:T(8,128)(2,1)}, bf16[64,3584]{1,0:T(8,128)(2,1)S(1)}, u32[]{:S(2)}, u32[]{:S(2)}) collective-permute-start(bf16[64,3584]{1,0:T(8,128)(2,1)} %refs_0_.1), channel_id=1, source_target_pairs={{0,4},{1,5},{4,8},{5,9},{8,12},{9,13},{12,14},{13,15},{14,10},{15,... | collective-permute-start | bytes 1376264 | tf_op jit(solution)/shard_map/ppermute | solution.py:89
  6.8 1.5 %collective-permute-done.1 = f32[16,128]{1,0:T(8,128)S(1)} collective-permute-done((f32[16,128]{1,0:T(8,128)S(1)}, f32[16,128]{1,0:T(8,128)S(1)}, u32[]{:S(2)}, u32[]{:S(2)}) %collective-permute-start.1) | collective-permute-done | bytes 8224 | tf_op jit(solution)/shard_map/ppermute | solution.py:93
  8.3 1.6 %collective-permute-start.3 = (f32[4,4,128]{2,0,1:T(4,128)S(1)}, f32[4,4,128]{2,0,1:T(4,128)S(1)}, u32[]{:S(2)}, u32[]{:S(2)}) collective-permute-start(f32[4,4,128]{2,0,1:T(4,128)S(1)} %bitcast.37), channel_id=1, source_target_pairs={{0,4},{1,5},{2,6},{3,7},{4,0},{5,1},{6,2},{7,3},{8,12},{9,13},{10,... | collective-permute-start | bytes 24584 | tf_op jit(solution)/shard_map/ppermute | solution.py:93
  10.0 2.6 %collective-permute-start.4 = (f32[4,4,128]{2,0,1:T(4,128)S(1)}, f32[4,4,128]{2,0,1:T(4,128)S(1)}, u32[]{:S(2)}, u32[]{:S(2)}) collective-permute-start(f32[4,4,128]{2,0,1:T(4,128)S(1)} %bitcast.38), channel_id=1, source_target_pairs={{0,8},{1,9},{2,10},{3,11},{4,12},{5,13},{6,14},{7,15},{8,0},{9,1},... | collective-permute-start | bytes 24584 | tf_op jit(solution)/shard_map/ppermute | solution.py:93
  12.8 10.3 %raw_forward.2.refs_0_ = bf16[768,1792]{1,0:T(8,128)(2,1)} custom-call(bf16[768,2048]{1,0:T(8,128)(2,1)} %bitcast.51, bf16[2048,3584]{1,0:T(8,128)(2,1)} %bitcast.30), custom_call_target="tpu_custom_call" | custom-call | flops 5637144576 | bytes 13238272 | tf_op jit(solution)/shard_map/raw_forward/pallas_call | solution.py:263
  24.0 1.4 %collective-permute-start.11 = (bf16[64,3584]{1,0:T(8,128)(2,1)}, bf16[64,3584]{1,0:T(8,128)(2,1)S(1)}, u32[]{:S(2)}, u32[]{:S(2)}) collective-permute-start(bf16[64,3584]{1,0:T(8,128)(2,1)} %collective-permute-done.7.refs_4_), channel_id=1, source_target_pairs={{0,2},{1,3},{4,0},{5,1},{8,4},{9,5},{12,8},{13,9},{14,12},{15,13},... | collective-permute-start | bytes 1376264 | tf_op jit(solution)/shard_map/ppermute | solution.py:89
  25.6 10.2 %raw_forward.3.refs_1_ = bf16[768,1792]{1,0:T(8,128)(2,1)} custom-call(bf16[768,2048]{1,0:T(8,128)(2,1)} %bitcast.52, bf16[2048,3584]{1,0:T(8,128)(2,1)} %bitcast.31), custom_call_target="tpu_custom_call" | custom-call | flops 5637144576 | bytes 13238272 | tf_op jit(solution)/shard_map/raw_forward/pallas_call | solution.py:263
  36.8 4.4 %spread_tokens.2 = (bf16[256,3584]{1,0:T(8,128)(2,1)S(1)}, bf16[128,3584]{1,0:T(8,128)(2,1)S(1)}, bf16[128,3584]{1,0:T(8,128)(2,1)}) custom-call(s32[17]{0:T(128)S(1)} %pad_add_fusion.where, f32[8,128]{1,0:T(8,128)S(1)} %squeeze.20.gates, bf16[768,1792]{1,0:T(8,128)(2,1)} %raw_forward.2.refs_0_, bf16[768,1792]{1,0:T(8,128)(2,1)} %raw_forward.3.refs_1_), custom_call_target="tpu_custom_call" | custom-call | flops 1073741824 | bytes 5505024 | tf_op jit(solution)/shard_map/spread_tokens/pallas_call | solution.py:120
  42.3 2.3 %collective-permute-start.15 = (bf16[64,3584]{1,0:T(8,128)(2,1)}, bf16[64,3584]{1,0:T(8,128)(2,1)S(1)}, u32[]{:S(2)}, u32[]{:S(2)}) collective-permute-start(bf16[64,3584]{1,0:T(8,128)(2,1)} %collective-permute-done.10.refs_6_), channel_id=1, source_target_pairs={{0,4},{1,5},{4,8},{5,9},{8,12},{9,13},{12,14},{13,15},{14,10},{15,... | collective-permute-start | bytes 1376264 | tf_op jit(solution)/shard_map/ppermute | solution.py:89
  44.6 1.2 add_convert_fusion.6
  45.8 0.8 copy-done.6
  47.2 0.8 copy-done.8
  48.0 1.4 %collective-permute-start.18 = (bf16[64,3584]{1,0:T(8,128)(2,1)}, bf16[64,3584]{1,0:T(8,128)(2,1)}, u32[]{:S(2)}, u32[]{:S(2)}) collective-permute-start(bf16[64,3584]{1,0:T(8,128)(2,1)} %get-tuple-element.113), channel_id=1, source_target_pairs={{0,4},{1,5},{4,8},{5,9},{8,12},{9,13},{12,14},{13,15},{14,10},{15,... | collective-permute-start | bytes 1376264 | tf_op jit(solution)/shard_map/ppermute | solution.py:89
  51.0 3.5 %spread_tokens.3 = (bf16[256,3584]{1,0:T(8,128)(2,1)S(1)}, bf16[128,3584]{1,0:T(8,128)(2,1)S(1)}, bf16[128,3584]{1,0:T(8,128)(2,1)S(1)}) custom-call(s32[17]{0:T(128)S(1)} %pad_add_fusion.where, f32[8,128]{1,0:T(8,128)S(1)} %squeeze.20.gates, bf16[768,1792]{1,0:T(8,128)(2,1)} %raw_forward.2.refs_0_, bf16[768,1792]{1,0:T(8,128)(2,1)} %raw_forward.3.refs_1_), custom_call_target="tpu_custom_call" | custom-call | flops 1073741824 | bytes 5505024 | tf_op jit(solution)/shard_map/spread_tokens/pallas_call | solution.py:120
  54.5 12.1 %backward.3 = (bf16[384,1024]{1,0:T(8,128)(2,1)S(1)}, bf16[384,1024]{1,0:T(8,128)(2,1)S(1)}) custom-call(s32[17]{0:T(128)S(1)} %pad_add_fusion.where, s32[1]{0:T(128)} %bitcast.20.pipe, f32[8,128]{1,0:T(8,128)S(1)} %squeeze.21.gates, bf16[2048,3584]{1,0:T(8,128)(2,1)} %bitcast.32, bf16[64,3584]{1,0:T(8,128)(2,1)S(1)} %copy-done.1, ...), custom_call_target="tpu_custom_call" | custom-call | flops 88080384 | bytes 339968 | tf_op jit(solution)/shard_map/backward/pallas_call | solution.py:120
  66.7 2.8 %collective-permute-done.19 = bf16[64,3584]{1,0:T(8,128)(2,1)} collective-permute-done((bf16[64,3584]{1,0:T(8,128)(2,1)}, bf16[64,3584]{1,0:T(8,128)(2,1)}, u32[]{:S(2)}, u32[]{:S(2)}) %collective-permute-start.19) | collective-permute-done | bytes 458784 | tf_op jit(solution)/shard_map/ppermute | solution.py:89
  70.5 1.8 %add_convert_fusion.4 = (bf16[64,3584]{1,0:T(8,128)(2,1)S(1)}, bf16[64,3584]{1,0:T(8,128)(2,1)S(1)}) fusion(bf16[64,3584]{1,0:T(8,128)(2,1)} %collective-permute-done.19, bf16[128,3584]{1,0:T(8,128)(2,1)} %collective-permute-done.14, bf16[256,3584]{1,0:T(8,128)(2,1)S(1)} %get-tuple-element.75, bf16[64,3584]{1,0:T(8,128)(2,1)} %collective-permute-done.18), kind=kLoop, calls=%fused_computation.4 | loop fusion | flops 2752512 | bytes 3670016 | tf_op jit(solution)/shard_map/convert_element_type | solution.py:32
  73.2 1.7 %collective-permute-start.23 = (bf16[64,3584]{1,0:T(8,128)(2,1)S(1)}, bf16[64,3584]{1,0:T(8,128)(2,1)S(1)}, u32[]{:S(2)}, u32[]{:S(2)}) collective-permute-start(bf16[64,3584]{1,0:T(8,128)(2,1)S(1)} %collective-permute-done.15.refs_2_), channel_id=1, source_target_pairs={{0,4},{1,5},{4,8},{5,9},{8,12},{9,13},{12,14},{13,15},{14,10},{15,... | collective-permute-start | bytes 1376264 | tf_op jit(solution)/shard_map/ppermute | solution.py:89
  75.0 1.4 %collective-permute-start.22 = (bf16[64,3584]{1,0:T(8,128)(2,1)S(1)}, bf16[64,3584]{1,0:T(8,128)(2,1)S(1)}, u32[]{:S(2)}, u32[]{:S(2)}) collective-permute-start(bf16[64,3584]{1,0:T(8,128)(2,1)S(1)} %get-tuple-element.111), channel_id=1, source_target_pairs={{0,4},{1,5},{4,8},{5,9},{8,12},{9,13},{12,14},{13,15},{14,10},{15,... | collective-permute-start | bytes 1376264 | tf_op jit(solution)/shard_map/ppermute | solution.py:89
  76.4 1.5 %collective-permute-start.29 = (bf16[384,1024]{1,0:T(8,128)(2,1)S(1)}, bf16[384,1024]{1,0:T(8,128)(2,1)S(1)}, u32[]{:S(2)}, u32[]{:S(2)}) collective-permute-start(bf16[384,1024]{1,0:T(8,128)(2,1)S(1)} %get-tuple-element.93), channel_id=1, source_target_pairs={{0,16},{16,0},{1,17},{17,1},{2,18},{18,2},{3,19},{19,3},{4,20},{20... | collective-permute-start | bytes 2359304 | tf_op jit(solution)/shard_map/ppermute | solution.py:101
  77.9 10.0 %backward.4 = (bf16[288,1024]{1,0:T(8,128)(2,1)S(1)}, bf16[288,1024]{1,0:T(8,128)(2,1)S(1)}) custom-call(s32[17]{0:T(128)S(1)} %pad_add_fusion.where, s32[1]{0:T(128)} %bitcast.20.pipe, f32[8,128]{1,0:T(8,128)S(1)} %squeeze.21.gates, bf16[2048,3584]{1,0:T(8,128)(2,1)} %bitcast.33, bf16[64,3584]{1,0:T(8,128)(2,1)S(1)} %collective-permute-done.11.refs_0_, ...), custom_call_target="tpu_custom_call" | custom-call | flops 66060288 | bytes 312320 | tf_op jit(solution)/shard_map/backward/pallas_call | solution.py:120
  89.2 6.4 %collective-permute-done.22 = bf16[64,3584]{1,0:T(8,128)(2,1)S(1)} collective-permute-done((bf16[64,3584]{1,0:T(8,128)(2,1)S(1)}, bf16[64,3584]{1,0:T(8,128)(2,1)S(1)}, u32[]{:S(2)}, u32[]{:S(2)}) %collective-permute-start.22) | collective-permute-done | bytes 458784 | tf_op jit(solution)/shard_map/ppermute | solution.py:89
  95.6 1.3 %collective-permute-done.29.refs_1_ = bf16[384,1024]{1,0:T(8,128)(2,1)S(1)} collective-permute-done((bf16[384,1024]{1,0:T(8,128)(2,1)S(1)}, bf16[384,1024]{1,0:T(8,128)(2,1)S(1)}, u32[]{:S(2)}, u32[]{:S(2)}) %collective-permute-start.29) | collective-permute-done | bytes 786464 | tf_op jit(solution)/shard_map/ppermute | solution.py:101
  96.9 3.0 %collective-permute-done.28 = bf16[64,3584]{1,0:T(8,128)(2,1)S(1)} collective-permute-done((bf16[64,3584]{1,0:T(8,128)(2,1)S(1)}, bf16[64,3584]{1,0:T(8,128)(2,1)S(1)}, u32[]{:S(2)}, u32[]{:S(2)}) %collective-permute-start.28) | collective-permute-done | bytes 458784 | tf_op jit(solution)/shard_map/ppermute | solution.py:89
  100.9 1.3 %collective-permute-start.33 = (bf16[64,3584]{1,0:T(8,128)(2,1)S(1)}, bf16[64,3584]{1,0:T(8,128)(2,1)S(1)}, u32[]{:S(2)}, u32[]{:S(2)}) collective-permute-start(bf16[64,3584]{1,0:T(8,128)(2,1)S(1)} %get-tuple-element.114), channel_id=1, source_target_pairs={{0,2},{1,3},{4,0},{5,1},{8,4},{9,5},{12,8},{13,9},{14,12},{15,13},... | collective-permute-start | bytes 1376264 | tf_op jit(solution)/shard_map/ppermute | solution.py:89
  102.3 8.4 %backward.5 = (bf16[96,1024]{1,0:T(8,128)(2,1)S(1)}, bf16[96,1024]{1,0:T(8,128)(2,1)S(1)}) custom-call(s32[17]{0:T(128)S(1)} %pad_add_fusion.where, s32[1]{0:T(128)} %bitcast.20.pipe, f32[8,128]{1,0:T(8,128)S(1)} %squeeze.21.gates, bf16[2048,3584]{1,0:T(8,128)(2,1)} %bitcast.34, bf16[64,3584]{1,0:T(8,128)(2,1)S(1)} %collective-permute-done.23.refs_0_, ...), custom_call_target="tpu_custom_call" | custom-call | flops 22020096 | bytes 257024 | tf_op jit(solution)/shard_map/backward/pallas_call | solution.py:120
  111.3 1.7 %collect.2.refs_2_ = bf16[768,1024]{1,0:T(8,128)(2,1)} custom-call(s32[17]{0:T(128)S(1)} %pad_add_fusion.where, bf16[384,1024]{1,0:T(8,128)(2,1)S(1)} %get-tuple-element.82.refs_0_, bf16[384,1024]{1,0:T(8,128)(2,1)S(1)} %collective-permute-done.29.refs_1_, bf16[288,1024]{1,0:T(8,128)(2,1)S(1)} %get-tuple-element.95.refs_2_, ...), custom_call_target="tpu_custom_call" | custom-call | flops 1048576 | bytes 4128768 | tf_op jit(solution)/shard_map/collect/pallas_call | solution.py:450
  113.6 3.9 %collective-permute-done.34.refs_1_ = bf16[96,1024]{1,0:T(8,128)(2,1)S(1)} collective-permute-done((bf16[96,1024]{1,0:T(8,128)(2,1)S(1)}, bf16[96,1024]{1,0:T(8,128)(2,1)S(1)}, u32[]{:S(2)}, u32[]{:S(2)}) %collective-permute-start.34) | collective-permute-done | bytes 196640 | tf_op jit(solution)/shard_map/ppermute | solution.py:101
  117.5 1.0 add_convert_fusion
  118.5 1.3 %collect.3 = bf16[768,1024]{1,0:T(8,128)(2,1)} custom-call(s32[17]{0:T(128)S(1)} %pad_add_fusion.where, bf16[96,1024]{1,0:T(8,128)(2,1)S(1)} %get-tuple-element.105.refs_0_, bf16[96,1024]{1,0:T(8,128)(2,1)S(1)} %collective-permute-done.34.refs_1_, bf16[768,1024]{1,0:T(8,128)(2,1)} %collect.2.refs_2_), custom_call_target="tpu_custom_call", output_to_operand_aliasing={{}: (3, {})} | custom-call | flops 1048576 | bytes 589824 | tf_op jit(solution)/shard_map/collect/pallas_call | solution.py:450
  (87 shorter events, 12.0 us)
Async XLA Ops:
  1.5 5.3 %collective-permute-start.2 = (f32[16,128]{1,0:T(8,128)S(1)}, f32[16,128]{1,0:T(8,128)S(1)}, u32[]{:S(2)}, u32[]{:S(2)}) collective-permute-start(f32[16,128]{1,0:T(8,128)S(1)} %gates.1), channel_id=1, source_target_pairs={{0,3},{1,2},{2,1},{3,0},{4,7},{5,6},{6,5},{7,4},{8,11},{9,10},{10,... | collective-permute-start | bytes 24584 | tf_op jit(solution)/shard_map/ppermute | solution.py:93
  4.6 3.7 %collective-permute-start.1 = (f32[16,128]{1,0:T(8,128)S(1)}, f32[16,128]{1,0:T(8,128)S(1)}, u32[]{:S(2)}, u32[]{:S(2)}) collective-permute-start(f32[16,128]{1,0:T(8,128)S(1)} %gates.1), channel_id=1, source_target_pairs={{0,2},{1,3},{2,0},{3,1},{4,6},{5,7},{6,4},{7,5},{8,10},{9,11},{10,... | collective-permute-start | bytes 24584 | tf_op jit(solution)/shard_map/ppermute | solution.py:93
  4.7 18.6 %collective-permute-start.6 = (bf16[64,3584]{1,0:T(8,128)(2,1)}, bf16[64,3584]{1,0:T(8,128)(2,1)S(1)}, u32[]{:S(2)}, u32[]{:S(2)}) collective-permute-start(bf16[64,3584]{1,0:T(8,128)(2,1)} %refs_0_.1), channel_id=1, source_target_pairs={{0,4},{1,5},{4,8},{5,9},{8,12},{9,13},{12,14},{13,15},{14,10},{15,... | collective-permute-start | bytes 1376264 | tf_op jit(solution)/shard_map/ppermute | solution.py:89
  6.7 16.5 %collective-permute-start.7 = (bf16[64,3584]{1,0:T(8,128)(2,1)}, bf16[64,3584]{1,0:T(8,128)(2,1)}, u32[]{:S(2)}, u32[]{:S(2)}) collective-permute-start(bf16[64,3584]{1,0:T(8,128)(2,1)} %refs_0_.1), channel_id=1, source_target_pairs={{0,2},{1,3},{4,0},{5,1},{8,4},{9,5},{12,8},{13,9},{14,12},{15,13},... | collective-permute-start | bytes 1376264 | tf_op jit(solution)/shard_map/ppermute | solution.py:89
  8.3 14.8 %collective-permute-start.3 = (f32[4,4,128]{2,0,1:T(4,128)S(1)}, f32[4,4,128]{2,0,1:T(4,128)S(1)}, u32[]{:S(2)}, u32[]{:S(2)}) collective-permute-start(f32[4,4,128]{2,0,1:T(4,128)S(1)} %bitcast.37), channel_id=1, source_target_pairs={{0,4},{1,5},{2,6},{3,7},{4,0},{5,1},{6,2},{7,3},{8,12},{9,13},{10,... | collective-permute-start | bytes 24584 | tf_op jit(solution)/shard_map/ppermute | solution.py:93
  10.0 13.2 %collective-permute-start.4 = (f32[4,4,128]{2,0,1:T(4,128)S(1)}, f32[4,4,128]{2,0,1:T(4,128)S(1)}, u32[]{:S(2)}, u32[]{:S(2)}) collective-permute-start(f32[4,4,128]{2,0,1:T(4,128)S(1)} %bitcast.38), channel_id=1, source_target_pairs={{0,8},{1,9},{2,10},{3,11},{4,12},{5,13},{6,14},{7,15},{8,0},{9,1},... | collective-permute-start | bytes 24584 | tf_op jit(solution)/shard_map/ppermute | solution.py:93
  12.6 10.7 %collective-permute-start.5 = (f32[4,4,128]{2,0,1:T(4,128)S(1)}, f32[4,4,128]{2,0,1:T(4,128)S(1)}, u32[]{:S(2)}, u32[]{:S(2)}) collective-permute-start(f32[4,4,128]{2,0,1:T(4,128)S(1)} %bitcast.39), channel_id=1, source_target_pairs={{0,12},{1,13},{2,14},{3,15},{4,8},{5,9},{6,10},{7,11},{8,4},{9,5},... | collective-permute-start | bytes 24584 | tf_op jit(solution)/shard_map/ppermute | solution.py:93
  23.1 12.7 %collective-permute-start.12 = (bf16[64,3584]{1,0:T(8,128)(2,1)S(1)}, bf16[64,3584]{1,0:T(8,128)(2,1)S(1)}, u32[]{:S(2)}, u32[]{:S(2)}) collective-permute-start(bf16[64,3584]{1,0:T(8,128)(2,1)S(1)} %copy-done), channel_id=1, source_target_pairs={{0,1},{1,0},{2,3},{3,2},{4,5},{5,4},{6,7},{7,6},{8,9},{9,8},{10,11... | collective-permute-start | bytes 1376264 | tf_op jit(solution)/shard_map/ppermute | solution.py:93
  23.3 13.1 %collective-permute-start.10 = (bf16[64,3584]{1,0:T(8,128)(2,1)S(1)}, bf16[64,3584]{1,0:T(8,128)(2,1)}, u32[]{:S(2)}, u32[]{:S(2)}) collective-permute-start(bf16[64,3584]{1,0:T(8,128)(2,1)S(1)} %collective-permute-done.6.refs_2_), channel_id=1, source_target_pairs={{0,4},{1,5},{4,8},{5,9},{8,12},{9,13},{12,14},{13,15},{14,10},{15,... | collective-permute-start | bytes 1376264 | tf_op jit(solution)/shard_map/ppermute | solution.py:89
  24.0 12.8 %collective-permute-start.11 = (bf16[64,3584]{1,0:T(8,128)(2,1)}, bf16[64,3584]{1,0:T(8,128)(2,1)S(1)}, u32[]{:S(2)}, u32[]{:S(2)}) collective-permute-start(bf16[64,3584]{1,0:T(8,128)(2,1)} %collective-permute-done.7.refs_4_), channel_id=1, source_target_pairs={{0,2},{1,3},{4,0},{5,1},{8,4},{9,5},{12,8},{13,9},{14,12},{15,13},... | collective-permute-start | bytes 1376264 | tf_op jit(solution)/shard_map/ppermute | solution.py:89
  41.2 3.4 %collective-permute-start.17 = (bf16[128,3584]{1,0:T(8,128)(2,1)S(1)}, bf16[128,3584]{1,0:T(8,128)(2,1)S(1)}, u32[]{:S(2)}, u32[]{:S(2)}) collective-permute-start(bf16[128,3584]{1,0:T(8,128)(2,1)S(1)} %get-tuple-element.76), channel_id=1, source_target_pairs={{0,1},{1,0},{2,3},{3,2},{4,5},{5,4},{6,7},{7,6},{8,9},{9,8},{10,11... | collective-permute-start | bytes 2752520 | tf_op jit(solution)/shard_map/ppermute | solution.py:93
  41.3 4.5 %collective-permute-start.8 = (bf16[64,3584]{1,0:T(8,128)(2,1)S(1)}, bf16[64,3584]{1,0:T(8,128)(2,1)S(1)}, u32[]{:S(2)}, u32[]{:S(2)}) collective-permute-start(bf16[64,3584]{1,0:T(8,128)(2,1)S(1)} %collective-permute-done.6.refs_2_), channel_id=1, source_target_pairs={{0,1},{1,0},{2,3},{3,2},{4,5},{5,4},{6,7},{7,6},{8,9},{9,8},{10,11... | collective-permute-start | bytes 1376264 | tf_op jit(solution)/shard_map/ppermute | solution.py:93
  41.8 5.5 %collective-permute-start.9 = (bf16[64,3584]{1,0:T(8,128)(2,1)}, bf16[64,3584]{1,0:T(8,128)(2,1)S(1)}, u32[]{:S(2)}, u32[]{:S(2)}) collective-permute-start(bf16[64,3584]{1,0:T(8,128)(2,1)} %collective-permute-done.7.refs_4_), channel_id=1, source_target_pairs={{0,1},{1,0},{2,3},{3,2},{4,5},{5,4},{6,7},{7,6},{8,9},{9,8},{10,11... | collective-permute-start | bytes 1376264 | tf_op jit(solution)/shard_map/ppermute | solution.py:93
  41.9 7.5 %collective-permute-start.13 = (bf16[64,3584]{1,0:T(8,128)(2,1)}, bf16[64,3584]{1,0:T(8,128)(2,1)S(1)}, u32[]{:S(2)}, u32[]{:S(2)}) collective-permute-start(bf16[64,3584]{1,0:T(8,128)(2,1)} %collective-permute-done.10.refs_6_), channel_id=1, source_target_pairs={{0,1},{1,0},{2,3},{3,2},{4,5},{5,4},{6,7},{7,6},{8,9},{9,8},{10,11... | collective-permute-start | bytes 1376264 | tf_op jit(solution)/shard_map/ppermute | solution.py:93
  42.3 24.3 %collective-permute-start.15 = (bf16[64,3584]{1,0:T(8,128)(2,1)}, bf16[64,3584]{1,0:T(8,128)(2,1)S(1)}, u32[]{:S(2)}, u32[]{:S(2)}) collective-permute-start(bf16[64,3584]{1,0:T(8,128)(2,1)} %collective-permute-done.10.refs_6_), channel_id=1, source_target_pairs={{0,4},{1,5},{4,8},{5,9},{8,12},{9,13},{12,14},{13,15},{14,10},{15,... | collective-permute-start | bytes 1376264 | tf_op jit(solution)/shard_map/ppermute | solution.py:89
  44.6 6.3 %collective-permute-start.14 = (bf16[128,3584]{1,0:T(8,128)(2,1)}, bf16[128,3584]{1,0:T(8,128)(2,1)}, u32[]{:S(2)}, u32[]{:S(2)}) collective-permute-start(bf16[128,3584]{1,0:T(8,128)(2,1)} %get-tuple-element.64), channel_id=1, source_target_pairs={{0,1},{1,0},{2,3},{3,2},{4,5},{5,4},{6,7},{7,6},{8,9},{9,8},{10,11... | collective-permute-start | bytes 2752520 | tf_op jit(solution)/shard_map/ppermute | solution.py:93
  46.6 20.1 %collective-permute-start.16 = (bf16[64,3584]{1,0:T(8,128)(2,1)S(1)}, bf16[64,3584]{1,0:T(8,128)(2,1)S(1)}, u32[]{:S(2)}, u32[]{:S(2)}) collective-permute-start(bf16[64,3584]{1,0:T(8,128)(2,1)S(1)} %collective-permute-done.11.refs_0_), channel_id=1, source_target_pairs={{0,2},{1,3},{4,0},{5,1},{8,4},{9,5},{12,8},{13,9},{14,12},{15,13},... | collective-permute-start | bytes 1376264 | tf_op jit(solution)/shard_map/ppermute | solution.py:89
  48.0 18.6 %collective-permute-start.18 = (bf16[64,3584]{1,0:T(8,128)(2,1)}, bf16[64,3584]{1,0:T(8,128)(2,1)}, u32[]{:S(2)}, u32[]{:S(2)}) collective-permute-start(bf16[64,3584]{1,0:T(8,128)(2,1)} %get-tuple-element.113), channel_id=1, source_target_pairs={{0,4},{1,5},{4,8},{5,9},{8,12},{9,13},{12,14},{13,15},{14,10},{15,... | collective-permute-start | bytes 1376264 | tf_op jit(solution)/shard_map/ppermute | solution.py:89
  50.1 19.3 %collective-permute-start.19 = (bf16[64,3584]{1,0:T(8,128)(2,1)}, bf16[64,3584]{1,0:T(8,128)(2,1)}, u32[]{:S(2)}, u32[]{:S(2)}) collective-permute-start(bf16[64,3584]{1,0:T(8,128)(2,1)} %get-tuple-element.112), channel_id=1, source_target_pairs={{0,2},{1,3},{4,0},{5,1},{8,4},{9,5},{12,8},{13,9},{14,12},{15,13},... | collective-permute-start | bytes 1376264 | tf_op jit(solution)/shard_map/ppermute | solution.py:89
  50.9 24.1 %collective-permute-start.24 = (bf16[64,3584]{1,0:T(8,128)(2,1)S(1)}, bf16[64,3584]{1,0:T(8,128)(2,1)S(1)}, u32[]{:S(2)}, u32[]{:S(2)}) collective-permute-start(bf16[64,3584]{1,0:T(8,128)(2,1)S(1)} %collective-permute-done.11.refs_0_), channel_id=1, source_target_pairs={{0,1},{1,0},{2,3},{3,2},{4,5},{5,4},{6,7},{7,6},{8,9},{9,8},{10,11... | collective-permute-start | bytes 1376264 | tf_op jit(solution)/shard_map/ppermute | solution.py:93
  69.4 3.8 %collective-permute-start.21 = (bf16[128,3584]{1,0:T(8,128)(2,1)S(1)}, bf16[128,3584]{1,0:T(8,128)(2,1)S(1)}, u32[]{:S(2)}, u32[]{:S(2)}) collective-permute-start(bf16[128,3584]{1,0:T(8,128)(2,1)S(1)} %get-tuple-element.80), channel_id=1, source_target_pairs={{0,1},{1,0},{2,3},{3,2},{4,5},{5,4},{6,7},{7,6},{8,9},{9,8},{10,11... | collective-permute-start | bytes 2752520 | tf_op jit(solution)/shard_map/ppermute | solution.py:93
  69.9 6.5 %collective-permute-start.25 = (bf16[64,3584]{1,0:T(8,128)(2,1)S(1)}, bf16[64,3584]{1,0:T(8,128)(2,1)S(1)}, u32[]{:S(2)}, u32[]{:S(2)}) collective-permute-start(bf16[64,3584]{1,0:T(8,128)(2,1)S(1)} %collective-permute-done.15.refs_2_), channel_id=1, source_target_pairs={{0,1},{1,0},{2,3},{3,2},{4,5},{5,4},{6,7},{7,6},{8,9},{9,8},{10,11... | collective-permute-start | bytes 1376264 | tf_op jit(solution)/shard_map/ppermute | solution.py:93
  70.0 8.0 %collective-permute-start.26 = (bf16[64,3584]{1,0:T(8,128)(2,1)S(1)}, bf16[64,3584]{1,0:T(8,128)(2,1)S(1)}, u32[]{:S(2)}, u32[]{:S(2)}) collective-permute-start(bf16[64,3584]{1,0:T(8,128)(2,1)S(1)} %collective-permute-done.16.refs_4_), channel_id=1, source_target_pairs={{0,1},{1,0},{2,3},{3,2},{4,5},{5,4},{6,7},{7,6},{8,9},{9,8},{10,11... | collective-permute-start | bytes 1376264 | tf_op jit(solution)/shard_map/ppermute | solution.py:93
  72.2 15.6 %collective-permute-start.27 = (bf16[64,3584]{1,0:T(8,128)(2,1)S(1)}, bf16[64,3584]{1,0:T(8,128)(2,1)S(1)}, u32[]{:S(2)}, u32[]{:S(2)}) collective-permute-start(bf16[64,3584]{1,0:T(8,128)(2,1)S(1)} %get-tuple-element.110), channel_id=1, source_target_pairs={{0,2},{1,3},{4,0},{5,1},{8,4},{9,5},{12,8},{13,9},{14,12},{15,13},... | collective-permute-start | bytes 1376264 | tf_op jit(solution)/shard_map/ppermute | solution.py:89
  73.2 22.4 %collective-permute-start.23 = (bf16[64,3584]{1,0:T(8,128)(2,1)S(1)}, bf16[64,3584]{1,0:T(8,128)(2,1)S(1)}, u32[]{:S(2)}, u32[]{:S(2)}) collective-permute-start(bf16[64,3584]{1,0:T(8,128)(2,1)S(1)} %collective-permute-done.15.refs_2_), channel_id=1, source_target_pairs={{0,4},{1,5},{4,8},{5,9},{8,12},{9,13},{12,14},{13,15},{14,10},{15,... | collective-permute-start | bytes 1376264 | tf_op jit(solution)/shard_map/ppermute | solution.py:89
  75.0 20.6 %collective-permute-start.22 = (bf16[64,3584]{1,0:T(8,128)(2,1)S(1)}, bf16[64,3584]{1,0:T(8,128)(2,1)S(1)}, u32[]{:S(2)}, u32[]{:S(2)}) collective-permute-start(bf16[64,3584]{1,0:T(8,128)(2,1)S(1)} %get-tuple-element.111), channel_id=1, source_target_pairs={{0,4},{1,5},{4,8},{5,9},{8,12},{9,13},{12,14},{13,15},{14,10},{15,... | collective-permute-start | bytes 1376264 | tf_op jit(solution)/shard_map/ppermute | solution.py:89
  76.4 20.5 %collective-permute-start.29 = (bf16[384,1024]{1,0:T(8,128)(2,1)S(1)}, bf16[384,1024]{1,0:T(8,128)(2,1)S(1)}, u32[]{:S(2)}, u32[]{:S(2)}) collective-permute-start(bf16[384,1024]{1,0:T(8,128)(2,1)S(1)} %get-tuple-element.93), channel_id=1, source_target_pairs={{0,16},{16,0},{1,17},{17,1},{2,18},{18,2},{3,19},{19,3},{4,20},{20... | collective-permute-start | bytes 2359304 | tf_op jit(solution)/shard_map/ppermute | solution.py:101
  88.1 11.8 %collective-permute-start.28 = (bf16[64,3584]{1,0:T(8,128)(2,1)S(1)}, bf16[64,3584]{1,0:T(8,128)(2,1)S(1)}, u32[]{:S(2)}, u32[]{:S(2)}) collective-permute-start(bf16[64,3584]{1,0:T(8,128)(2,1)S(1)} %add_convert_fusion.3), channel_id=1, source_target_pairs={{0,2},{1,3},{4,0},{5,1},{8,4},{9,5},{12,8},{13,9},{14,12},{15,13},... | collective-permute-start | bytes 1376264 | tf_op jit(solution)/shard_map/ppermute | solution.py:89
  88.7 22.6 %collective-permute-start.31 = (bf16[288,1024]{1,0:T(8,128)(2,1)S(1)}, bf16[288,1024]{1,0:T(8,128)(2,1)S(1)}, u32[]{:S(2)}, u32[]{:S(2)}) collective-permute-start(bf16[288,1024]{1,0:T(8,128)(2,1)S(1)} %get-tuple-element.98), channel_id=1, source_target_pairs={{0,16},{16,0},{1,17},{17,1},{2,18},{18,2},{3,19},{19,3},{4,20},{20... | collective-permute-start | bytes 1769480 | tf_op jit(solution)/shard_map/ppermute | solution.py:101
  100.2 13.0 %collective-permute-start.32 = (bf16[64,3584]{1,0:T(8,128)(2,1)S(1)}, bf16[64,3584]{1,0:T(8,128)(2,1)S(1)}, u32[]{:S(2)}, u32[]{:S(2)}) collective-permute-start(bf16[64,3584]{1,0:T(8,128)(2,1)S(1)} %get-tuple-element.115), channel_id=1, source_target_pairs={{0,4},{1,5},{4,8},{5,9},{8,12},{9,13},{12,14},{13,15},{14,10},{15,... | collective-permute-start | bytes 1376264 | tf_op jit(solution)/shard_map/ppermute | solution.py:89
  100.9 12.7 %collective-permute-start.33 = (bf16[64,3584]{1,0:T(8,128)(2,1)S(1)}, bf16[64,3584]{1,0:T(8,128)(2,1)S(1)}, u32[]{:S(2)}, u32[]{:S(2)}) collective-permute-start(bf16[64,3584]{1,0:T(8,128)(2,1)S(1)} %get-tuple-element.114), channel_id=1, source_target_pairs={{0,2},{1,3},{4,0},{5,1},{8,4},{9,5},{12,8},{13,9},{14,12},{15,13},... | collective-permute-start | bytes 1376264 | tf_op jit(solution)/shard_map/ppermute | solution.py:89
  110.7 6.8 %collective-permute-start.34 = (bf16[96,1024]{1,0:T(8,128)(2,1)S(1)}, bf16[96,1024]{1,0:T(8,128)(2,1)S(1)}, u32[]{:S(2)}, u32[]{:S(2)}) collective-permute-start(bf16[96,1024]{1,0:T(8,128)(2,1)S(1)} %get-tuple-element.102), channel_id=1, source_target_pairs={{0,16},{16,0},{1,17},{17,1},{2,18},{18,2},{3,19},{19,3},{4,20},{20... | collective-permute-start | bytes 589832 | tf_op jit(solution)/shard_map/ppermute | solution.py:101
  (15 other events, 65.8 us)

commit v3 on v2

--- a/solution.py
+++ b/solution.py
@@ -350,11 +350,9 @@
 
 def backward_kernel(distances, cap, sides, where, pipe, gates, weights, *refs):
     count, rows = len(distances), 2 * cap
-    tokens, outs = refs[: 2 * count], refs[2 * count : 2 * count + len(sides)]
-    block, block_sems, picked, target, place, slot_gates, buffer, sems = refs[
-        2 * count + len(sides) :
-    ]
-    half, tile = tokens[0].shape[0], buffer.shape[1]
+    tokens, outs = refs[: -8 - len(sides)], refs[-8 - len(sides) : -8]
+    block, block_sems, picked, target, place, slot_gates, buffer, sems = refs[-8:]
+    tile = buffer.shape[1]
     tiles = 4 * len(sides)
     first = (1 - pipe[0] + sides[0]) * 4
 
@@ -362,10 +360,13 @@
         return weights.at[pl.ds(pl.multiple_of((first + n) % 8 * tile, tile), tile), :]
 
     fetch = []
+    at = 0
     for i, token in enumerate(tokens):
-        to = block.at[i // 2, pl.ds(i % 2 * half, half), :]
+        chip, row = divmod(at, block.shape[1])
+        to = block.at[chip, pl.ds(row, token.shape[0]), :]
         fetch.append(pltpu.make_async_copy(token, to, block_sems.at[i]))
         fetch[-1].start()
+        at += token.shape[0]
     stream = Stream(weight_tile, buffer, sems)
     for n in range(stream.slots):
         stream.start(n)
@@ -413,7 +414,7 @@
         [jax.ShapeDtypeStruct((count * rows, depth // 2), BF16)] * len(sides),
         [
             pltpu.VMEM((count, gates.shape[1], width), BF16),
-            pltpu.SemaphoreType.DMA((2 * count,)),
+            pltpu.SemaphoreType.DMA((len(tokens),)),
             pltpu.VMEM((count * rows, width), BF16),
             *place_scratch(count, gates, cap),
             pltpu.VMEM((4, depth // 8, width), BF16),
@@ -479,8 +480,15 @@
     chips = to_z * 2 + to_y
     where = jnp.concatenate([chips, c.reshape(1), (to_z ^ z) * 2 + (to_y ^ y)])
 
-    got, pair = {0: cotangent_b}, {}
-    got[-1], got[1] = step_ring(cotangent_b, 1), step_ring(cotangent_b, -1)
+    got, pair = {0: [cotangent_b]}, {}
+
+    def hop(d, way):
+        return [step_ring(x, way) for x in got[d]]
+
+    def swap(d):
+        return [core(x) for x in got[d]]
+
+    got[-1], got[1] = hop(0, 1), hop(0, -1)
 
     both = gates_of(routes_a, gates_a, routes_b, gates_b)
     four = jnp.stack([both] + [xor(both, j) for j in (1, 2, 3)])
@@ -498,19 +506,19 @@
         return spread_tokens(distances, split, cap, where, gates, (pin(raw1), pin(raw2)))
 
     def bwd(distances, sides=(0, 1), share=1):
-        values = [x for d in distances for x in (got[d], pair[d])]
+        values = [x for d in distances for x in (*got[d], *pair[d])]
         return backward(distances, cap, sides, where, pipe, values, gate_b, weights, share)
 
-    got[-2], got[2] = step_ring(got[-1], 1), step_ring(got[1], -1)
-    pair[0] = core(got[0])
+    got[-2], got[2] = hop(-1, 1), hop(1, -1)
+    pair[0] = swap(0)
     raw2 = raw_forward(width // 2, width // 2, pin(hidden), weights)
     raw2, got[-2], got[2], pair[0] = tie(raw2, got[-2], got[2], pair[0])
 
-    got[-3], got[3] = step_ring(got[-2], 1), step_ring(got[2], -1)
+    got[-3], got[3] = hop(-2, 1), hop(2, -1)
     keep1, other1, other2 = spread((3, -4, 2, -3), 2, gate_a)
     other1, other2 = core(other1), core(other2)
     for d in (-1, 1, -2):
-        pair[d] = core(got[d])
+        pair[d] = swap(d)
     up = step_ring(add(keep1[:tokens], other1[:tokens]), 1)
     down = step_ring(add(keep1[tokens : 2 * tokens], other1[tokens:]), -1)
     gate_a, pair[-1], pair[1], pair[-2], other2 = tie(
@@ -529,28 +537,30 @@
     send1, got[-3], got[3], up, down, other3, other4 = tie(
         send1, got[-3], got[3], up, down, other3, other4
     )
-    got[-4] = step_ring(got[-3], 1)
+    middle = tokens // 2
+    got[-4] = [step_ring(got[-3][0][:middle], 1), step_ring(got[3][0][middle:], -1)]
     up = step_ring(add(keep1[2 * tokens : 3 * tokens], other2[:tokens], up), 1)
     down = step_ring(add(keep1[3 * tokens :], other2[tokens:], down), -1)
     recv1 = across(send1)
-    pair[2], pair[-3], pair[3] = core(got[2]), core(got[-3]), core(got[3])
+    pair[2], pair[-3], pair[3] = swap(2), swap(-3), swap(3)
     other3, other4 = core(other3), core(other4)
     gate_b, other3, other4 = tie(gate_b, other3, other4)
     send2, hold2 = bwd(groups[1], share=64)
 
-    hold2, send2, down = tie(hold2, send2, down)
+    hold2, send2, up, down, got[-4] = tie(hold2, send2, up, down, got[-4])
+    up, down = tie(mine(0, other3, up), mine(1, other3, down))
+    up, down = step_ring(up, 1), step_ring(down, -1)
     recv2 = across(send2)
-    down = step_ring(mine(1, other3, down), -1)
-    up, got[-4], down, recv1 = tie(up, got[-4], down, recv1)
-
-    pair[-4] = core(got[-4])
-    up, down = step_ring(mine(0, other3, up), 1), step_ring(mine(2, other4, down), -1)
+    pair[-4] = swap(-4)
     send3, hold3 = bwd(groups[2], share=64)
+
+    hold3, send3, up, down, recv1 = tie(hold3, send3, up, down, recv1)
+    down = step_ring(mine(2, other4, down), -1)
     recv3 = across(send3)
-    hold3, recv2 = tie(hold3, recv2)
     grad = collect(groups[:2], where, (hold1, recv1, hold2, recv2), 8 * rows)
-    grad, up, down, recv3 = tie(grad, up, down, recv3)
+    grad, down = tie(grad, down)
     mixed_a = mine(3, other4, up, down)
+    mixed_a, recv3 = tie(mixed_a, recv3)
     grad = collect(groups[2:], where, (hold3, recv3), 8 * rows, grad)
     return (mixed_a, grad[None])
 

time: 120 us -> 121 us (level)
  waiting for transfers between devices: 20.8 us -> 18.4 us
  starting transfers between devices: 28.1 us -> 29.9 us
    ppermute x14 -> x15, waiting for transfers between devices: 13.7 us -> 11.6 us  [step_ring(): return lax.ppermute(value, 'expert', pairs)]
    ppermute x18 -> x19, waiting for transfers between devices: 1.95 us -> 2.5 us  [xor(): return lax.ppermute(value, 'expert', [(i, i ^ bits) for i in range(16)])]
    ppermute x18 -> x19, starting transfers between devices: 9.88 us -> 10.4 us  [xor(): return lax.ppermute(value, 'expert', [(i, i ^ bits) for i in range(16)])]
    ppermute x14 -> x15, starting transfers between devices: 15.6 us -> 15.9 us  [step_ring(): return lax.ppermute(value, 'expert', pairs)]
  transfers between devices with their start and end apart: 35 -> 37, of which waited for: 11 -> 8; matrix products, arithmetic and copies ran while one was open for 3% -> 4% of each run, Pallas kernels for 47% -> 47%
where the time goes in v3:
time: 121 us
  Pallas kernels  63.3 us (52%)
  starting transfers between devices  29.9 us (25%)
  waiting for transfers between devices  18.4 us (15%)
  other arithmetic  4.56 us (4%)
  local copies, waits for them, and re-layouts  3.47 us (3%)
    pallas_call x6, Pallas kernels, kernel_call(): pl.pallas_call(kernel, in_specs=in_specs, out_specs=[VMEM] * len(out_shap...  39.8 us
    pallas_call x2, Pallas kernels, raw_forward(): pl.pallas_call(functools.partial(raw_kernel, first), in_specs=[HBM, HBM],...  20.5 us
    ppermute x15, starting transfers between devices, step_ring(): return lax.ppermute(value, 'expert', pairs)  15.9 us
    ppermute x15, waiting for transfers between devices, step_ring(): return lax.ppermute(value, 'expert', pairs)  11.6 us
    ppermute x19, starting transfers between devices, xor(): return lax.ppermute(value, 'expert', [(i, i ^ bits) for i in range(16)])  10.4 us
    convert_element_type x5, other arithmetic, add(): return total.astype(BF16)  4.45 us
    ppermute x3, waiting for transfers between devices, across(): return lax.ppermute(value, 'pipe', [(0, 1), (1, 0)])  4.33 us
    ppermute x3, starting transfers between devices, across(): return lax.ppermute(value, 'pipe', [(0, 1), (1, 0)])  3.52 us
  transfers between devices with their start and end apart: 37, of which 8 were waited for; matrix products, arithmetic and copies ran while one was open for 4% of the time, Pallas kernels for 47%

profile of v3, /device:TPU:0, one launch (start us, length us, event | category | flops | bytes accessed | tf_op | source)
XLA Modules:
  0.0 120.6 jit_solution(15584098258294825401)
XLA Ops:
  0.6 0.9 gates.1
  1.5 2.5 %collective-permute-start.2 = (f32[16,128]{1,0:T(8,128)S(1)}, f32[16,128]{1,0:T(8,128)S(1)}, u32[]{:S(2)}, u32[]{:S(2)}) collective-permute-start(f32[16,128]{1,0:T(8,128)S(1)} %gates.1), channel_id=1, source_target_pairs={{0,3},{1,2},{2,1},{3,0},{4,7},{5,6},{6,5},{7,4},{8,11},{9,10},{10,... | collective-permute-start | bytes 24584 | tf_op jit(solution)/shard_map/ppermute | solution.py:93
  4.7 2.0 %collective-permute-start.6 = (bf16[64,3584]{1,0:T(8,128)(2,1)}, bf16[64,3584]{1,0:T(8,128)(2,1)S(1)}, u32[]{:S(2)}, u32[]{:S(2)}) collective-permute-start(bf16[64,3584]{1,0:T(8,128)(2,1)} %refs_0_.1), channel_id=1, source_target_pairs={{0,4},{1,5},{4,8},{5,9},{8,12},{9,13},{12,14},{13,15},{14,10},{15,... | collective-permute-start | bytes 1376264 | tf_op jit(solution)/shard_map/ppermute | solution.py:89
  6.8 1.5 %collective-permute-done.1 = f32[16,128]{1,0:T(8,128)S(1)} collective-permute-done((f32[16,128]{1,0:T(8,128)S(1)}, f32[16,128]{1,0:T(8,128)S(1)}, u32[]{:S(2)}, u32[]{:S(2)}) %collective-permute-start.1) | collective-permute-done | bytes 8224 | tf_op jit(solution)/shard_map/ppermute | solution.py:93
  8.3 1.6 %collective-permute-start.3 = (f32[4,4,128]{2,0,1:T(4,128)S(1)}, f32[4,4,128]{2,0,1:T(4,128)S(1)}, u32[]{:S(2)}, u32[]{:S(2)}) collective-permute-start(f32[4,4,128]{2,0,1:T(4,128)S(1)} %bitcast.37), channel_id=1, source_target_pairs={{0,4},{1,5},{2,6},{3,7},{4,0},{5,1},{6,2},{7,3},{8,12},{9,13},{10,... | collective-permute-start | bytes 24584 | tf_op jit(solution)/shard_map/ppermute | solution.py:93
  10.0 2.6 %collective-permute-start.4 = (f32[4,4,128]{2,0,1:T(4,128)S(1)}, f32[4,4,128]{2,0,1:T(4,128)S(1)}, u32[]{:S(2)}, u32[]{:S(2)}) collective-permute-start(f32[4,4,128]{2,0,1:T(4,128)S(1)} %bitcast.38), channel_id=1, source_target_pairs={{0,8},{1,9},{2,10},{3,11},{4,12},{5,13},{6,14},{7,15},{8,0},{9,1},... | collective-permute-start | bytes 24584 | tf_op jit(solution)/shard_map/ppermute | solution.py:93
  12.8 10.3 %raw_forward.2.refs_0_ = bf16[768,1792]{1,0:T(8,128)(2,1)} custom-call(bf16[768,2048]{1,0:T(8,128)(2,1)} %bitcast.51, bf16[2048,3584]{1,0:T(8,128)(2,1)} %bitcast.30), custom_call_target="tpu_custom_call" | custom-call | flops 5637144576 | bytes 13238272 | tf_op jit(solution)/shard_map/raw_forward/pallas_call | solution.py:263
  24.0 1.4 %collective-permute-start.11 = (bf16[64,3584]{1,0:T(8,128)(2,1)}, bf16[64,3584]{1,0:T(8,128)(2,1)S(1)}, u32[]{:S(2)}, u32[]{:S(2)}) collective-permute-start(bf16[64,3584]{1,0:T(8,128)(2,1)} %collective-permute-done.7.refs_4_), channel_id=1, source_target_pairs={{0,2},{1,3},{4,0},{5,1},{8,4},{9,5},{12,8},{13,9},{14,12},{15,13},... | collective-permute-start | bytes 1376264 | tf_op jit(solution)/shard_map/ppermute | solution.py:89
  25.6 10.2 %raw_forward.3.refs_1_ = bf16[768,1792]{1,0:T(8,128)(2,1)} custom-call(bf16[768,2048]{1,0:T(8,128)(2,1)} %bitcast.52, bf16[2048,3584]{1,0:T(8,128)(2,1)} %bitcast.31), custom_call_target="tpu_custom_call" | custom-call | flops 5637144576 | bytes 13238272 | tf_op jit(solution)/shard_map/raw_forward/pallas_call | solution.py:263
  36.8 4.4 %spread_tokens.2 = (bf16[256,3584]{1,0:T(8,128)(2,1)S(1)}, bf16[128,3584]{1,0:T(8,128)(2,1)S(1)}, bf16[128,3584]{1,0:T(8,128)(2,1)}) custom-call(s32[17]{0:T(128)S(1)} %pad_add_fusion.where, f32[8,128]{1,0:T(8,128)S(1)} %squeeze.20.gates, bf16[768,1792]{1,0:T(8,128)(2,1)} %raw_forward.2.refs_0_, bf16[768,1792]{1,0:T(8,128)(2,1)} %raw_forward.3.refs_1_), custom_call_target="tpu_custom_call" | custom-call | flops 1073741824 | bytes 5505024 | tf_op jit(solution)/shard_map/spread_tokens/pallas_call | solution.py:120
  42.3 2.3 %collective-permute-start.15 = (bf16[64,3584]{1,0:T(8,128)(2,1)}, bf16[64,3584]{1,0:T(8,128)(2,1)S(1)}, u32[]{:S(2)}, u32[]{:S(2)}) collective-permute-start(bf16[64,3584]{1,0:T(8,128)(2,1)} %collective-permute-done.10.refs_6_), channel_id=1, source_target_pairs={{0,4},{1,5},{4,8},{5,9},{8,12},{9,13},{12,14},{13,15},{14,10},{15,... | collective-permute-start | bytes 1376264 | tf_op jit(solution)/shard_map/ppermute | solution.py:89
  44.6 1.2 add_convert_fusion.6
  48.0 1.4 %collective-permute-start.18 = (bf16[64,3584]{1,0:T(8,128)(2,1)}, bf16[64,3584]{1,0:T(8,128)(2,1)}, u32[]{:S(2)}, u32[]{:S(2)}) collective-permute-start(bf16[64,3584]{1,0:T(8,128)(2,1)} %get-tuple-element.123), channel_id=1, source_target_pairs={{0,4},{1,5},{4,8},{5,9},{8,12},{9,13},{12,14},{13,15},{14,10},{15,... | collective-permute-start | bytes 1376264 | tf_op jit(solution)/shard_map/ppermute | solution.py:89
  51.0 3.5 %spread_tokens.3 = (bf16[256,3584]{1,0:T(8,128)(2,1)S(1)}, bf16[128,3584]{1,0:T(8,128)(2,1)S(1)}, bf16[128,3584]{1,0:T(8,128)(2,1)S(1)}) custom-call(s32[17]{0:T(128)S(1)} %pad_add_fusion.where, f32[8,128]{1,0:T(8,128)S(1)} %squeeze.20.gates, bf16[768,1792]{1,0:T(8,128)(2,1)} %raw_forward.2.refs_0_, bf16[768,1792]{1,0:T(8,128)(2,1)} %raw_forward.3.refs_1_), custom_call_target="tpu_custom_call" | custom-call | flops 1073741824 | bytes 5505024 | tf_op jit(solution)/shard_map/spread_tokens/pallas_call | solution.py:120
  54.5 12.1 %backward.3 = (bf16[384,1024]{1,0:T(8,128)(2,1)S(1)}, bf16[384,1024]{1,0:T(8,128)(2,1)S(1)}) custom-call(s32[17]{0:T(128)S(1)} %pad_add_fusion.where, s32[1]{0:T(128)} %bitcast.20.pipe, f32[8,128]{1,0:T(8,128)S(1)} %squeeze.21.gates, bf16[2048,3584]{1,0:T(8,128)(2,1)} %bitcast.32, bf16[64,3584]{1,0:T(8,128)(2,1)S(1)} %copy-done.1, ...), custom_call_target="tpu_custom_call" | custom-call | flops 88080384 | bytes 339968 | tf_op jit(solution)/shard_map/backward/pallas_call | solution.py:120
  66.7 2.8 %collective-permute-done.19 = bf16[64,3584]{1,0:T(8,128)(2,1)} collective-permute-done((bf16[64,3584]{1,0:T(8,128)(2,1)}, bf16[64,3584]{1,0:T(8,128)(2,1)}, u32[]{:S(2)}, u32[]{:S(2)}) %collective-permute-start.19) | collective-permute-done | bytes 458784 | tf_op jit(solution)/shard_map/ppermute | solution.py:89
  70.5 1.8 %add_convert_fusion.4 = (bf16[64,3584]{1,0:T(8,128)(2,1)S(1)}, bf16[64,3584]{1,0:T(8,128)(2,1)S(1)}) fusion(bf16[64,3584]{1,0:T(8,128)(2,1)} %collective-permute-done.19, bf16[128,3584]{1,0:T(8,128)(2,1)} %collective-permute-done.14, bf16[256,3584]{1,0:T(8,128)(2,1)S(1)} %get-tuple-element.79, bf16[64,3584]{1,0:T(8,128)(2,1)} %collective-permute-done.18), kind=kLoop, calls=%fused_computation.4 | loop fusion | flops 2752512 | bytes 3670016 | tf_op jit(solution)/shard_map/convert_element_type | solution.py:32
  72.2 1.8 %collective-permute-start.25 = (bf16[64,3584]{1,0:T(8,128)(2,1)S(1)}, bf16[64,3584]{1,0:T(8,128)(2,1)S(1)}, u32[]{:S(2)}, u32[]{:S(2)}) collective-permute-start(bf16[64,3584]{1,0:T(8,128)(2,1)S(1)} %get-tuple-element.121), channel_id=1, source_target_pairs={{0,4},{1,5},{4,8},{5,9},{8,12},{9,13},{12,14},{13,15},{14,10},{15,... | collective-permute-start | bytes 1376264 | tf_op jit(solution)/shard_map/ppermute | solution.py:89
  74.4 1.7 %collective-permute-start.27 = (bf16[32,3584]{1,0:T(8,128)(2,1)S(1)}, bf16[32,3584]{1,0:T(8,128)(2,1)S(1)}, u32[]{:S(2)}, u32[]{:S(2)}) collective-permute-start(bf16[32,3584]{1,0:T(8,128)(2,1)S(1)} %slice.74), channel_id=1, source_target_pairs={{0,4},{1,5},{4,8},{5,9},{8,12},{9,13},{12,14},{13,15},{14,10},{15,... | collective-permute-start | bytes 688136 | tf_op jit(solution)/shard_map/ppermute | solution.py:89
  76.5 1.5 %collective-permute-start.33 = (bf16[384,1024]{1,0:T(8,128)(2,1)S(1)}, bf16[384,1024]{1,0:T(8,128)(2,1)S(1)}, u32[]{:S(2)}, u32[]{:S(2)}) collective-permute-start(bf16[384,1024]{1,0:T(8,128)(2,1)S(1)} %get-tuple-element.103), channel_id=1, source_target_pairs={{0,16},{16,0},{1,17},{17,1},{2,18},{18,2},{3,19},{19,3},{4,20},{20... | collective-permute-start | bytes 2359304 | tf_op jit(solution)/shard_map/ppermute | solution.py:101
  78.0 10.0 %backward.4 = (bf16[288,1024]{1,0:T(8,128)(2,1)S(1)}, bf16[288,1024]{1,0:T(8,128)(2,1)S(1)}) custom-call(s32[17]{0:T(128)S(1)} %pad_add_fusion.where, s32[1]{0:T(128)} %bitcast.20.pipe, f32[8,128]{1,0:T(8,128)S(1)} %squeeze.21.gates, bf16[2048,3584]{1,0:T(8,128)(2,1)} %bitcast.33, bf16[64,3584]{1,0:T(8,128)(2,1)S(1)} %collective-permute-done.11.refs_0_, ...), custom_call_target="tpu_custom_call" | custom-call | flops 66060288 | bytes 312320 | tf_op jit(solution)/shard_map/backward/pallas_call | solution.py:120
  88.0 1.7 %collective-permute-done.27.refs_0_ = bf16[32,3584]{1,0:T(8,128)(2,1)S(1)} collective-permute-done((bf16[32,3584]{1,0:T(8,128)(2,1)S(1)}, bf16[32,3584]{1,0:T(8,128)(2,1)S(1)}, u32[]{:S(2)}, u32[]{:S(2)}) %collective-permute-start.27) | collective-permute-done | bytes 229408 | tf_op jit(solution)/shard_map/ppermute | solution.py:89
  89.6 1.7 %collective-permute-done.28.refs_1_ = bf16[32,3584]{1,0:T(8,128)(2,1)S(1)} collective-permute-done((bf16[32,3584]{1,0:T(8,128)(2,1)S(1)}, bf16[32,3584]{1,0:T(8,128)(2,1)S(1)}, u32[]{:S(2)}, u32[]{:S(2)}) %collective-permute-start.28) | collective-permute-done | bytes 229408 | tf_op jit(solution)/shard_map/ppermute | solution.py:89
  91.7 1.8 %collective-permute-start.31 = (bf16[64,3584]{1,0:T(8,128)(2,1)S(1)}, bf16[64,3584]{1,0:T(8,128)(2,1)S(1)}, u32[]{:S(2)}, u32[]{:S(2)}) collective-permute-start(bf16[64,3584]{1,0:T(8,128)(2,1)S(1)} %get-tuple-element.101), channel_id=1, source_target_pairs={{0,4},{1,5},{4,8},{5,9},{8,12},{9,13},{12,14},{13,15},{14,10},{15,... | collective-permute-start | bytes 1376264 | tf_op jit(solution)/shard_map/ppermute | solution.py:89
  94.3 1.0 collective-permute-done.29.refs_2_
  95.3 1.5 %collective-permute-start.34 = (bf16[288,1024]{1,0:T(8,128)(2,1)S(1)}, bf16[288,1024]{1,0:T(8,128)(2,1)S(1)}, u32[]{:S(2)}, u32[]{:S(2)}) collective-permute-start(bf16[288,1024]{1,0:T(8,128)(2,1)S(1)} %get-tuple-element.108), channel_id=1, source_target_pairs={{0,16},{16,0},{1,17},{17,1},{2,18},{18,2},{3,19},{19,3},{4,20},{20... | collective-permute-start | bytes 1769480 | tf_op jit(solution)/shard_map/ppermute | solution.py:101
  96.8 9.0 %backward.5 = (bf16[96,1024]{1,0:T(8,128)(2,1)S(1)}, bf16[96,1024]{1,0:T(8,128)(2,1)S(1)}) custom-call(s32[17]{0:T(128)S(1)} %pad_add_fusion.where, s32[1]{0:T(128)} %bitcast.20.pipe, f32[8,128]{1,0:T(8,128)S(1)} %squeeze.21.gates, bf16[2048,3584]{1,0:T(8,128)(2,1)} %bitcast.34, bf16[32,3584]{1,0:T(8,128)(2,1)S(1)} %collective-permute-done.27.refs_0_, ...), custom_call_target="tpu_custom_call" | custom-call | flops 22020096 | bytes 257024 | tf_op jit(solution)/shard_map/backward/pallas_call | solution.py:120
  107.1 4.3 %collective-permute-done.34.refs_3_ = bf16[288,1024]{1,0:T(8,128)(2,1)S(1)} collective-permute-done((bf16[288,1024]{1,0:T(8,128)(2,1)S(1)}, bf16[288,1024]{1,0:T(8,128)(2,1)S(1)}, u32[]{:S(2)}, u32[]{:S(2)}) %collective-permute-start.34) | collective-permute-done | bytes 589856 | tf_op jit(solution)/shard_map/ppermute | solution.py:101
  111.4 1.7 %collect.2.refs_2_ = bf16[768,1024]{1,0:T(8,128)(2,1)} custom-call(s32[17]{0:T(128)S(1)} %pad_add_fusion.where, bf16[384,1024]{1,0:T(8,128)(2,1)S(1)} %get-tuple-element.105.refs_0_, bf16[384,1024]{1,0:T(8,128)(2,1)S(1)} %collective-permute-done.33.refs_1_, bf16[288,1024]{1,0:T(8,128)(2,1)S(1)} %get-tuple-element.107.refs_2_, ...), custom_call_target="tpu_custom_call" | custom-call | flops 1048576 | bytes 4128768 | tf_op jit(solution)/shard_map/collect/pallas_call | solution.py:451
  113.2 5.2 %collective-permute-done.35 = bf16[64,3584]{1,0:T(8,128)(2,1)S(1)} collective-permute-done((bf16[64,3584]{1,0:T(8,128)(2,1)S(1)}, bf16[64,3584]{1,0:T(8,128)(2,1)S(1)}, u32[]{:S(2)}, u32[]{:S(2)}) %collective-permute-start.35) | collective-permute-done | bytes 458784 | tf_op jit(solution)/shard_map/ppermute | solution.py:89
  118.4 1.0 add_convert_fusion
  119.4 1.3 %collect.3 = bf16[768,1024]{1,0:T(8,128)(2,1)} custom-call(s32[17]{0:T(128)S(1)} %pad_add_fusion.where, bf16[96,1024]{1,0:T(8,128)(2,1)S(1)} %get-tuple-element.113.refs_0_, bf16[96,1024]{1,0:T(8,128)(2,1)S(1)} %collective-permute-done.36.refs_1_, bf16[768,1024]{1,0:T(8,128)(2,1)} %collect.2.refs_2_), custom_call_target="tpu_custom_call", output_to_operand_aliasing={{}: (3, {})} | custom-call | flops 1048576 | bytes 589824 | tf_op jit(solution)/shard_map/collect/pallas_call | solution.py:451
  (93 shorter events, 12.2 us)
Async XLA Ops:
  1.5 5.3 %collective-permute-start.2 = (f32[16,128]{1,0:T(8,128)S(1)}, f32[16,128]{1,0:T(8,128)S(1)}, u32[]{:S(2)}, u32[]{:S(2)}) collective-permute-start(f32[16,128]{1,0:T(8,128)S(1)} %gates.1), channel_id=1, source_target_pairs={{0,3},{1,2},{2,1},{3,0},{4,7},{5,6},{6,5},{7,4},{8,11},{9,10},{10,... | collective-permute-start | bytes 24584 | tf_op jit(solution)/shard_map/ppermute | solution.py:93
  4.7 18.6 %collective-permute-start.6 = (bf16[64,3584]{1,0:T(8,128)(2,1)}, bf16[64,3584]{1,0:T(8,128)(2,1)S(1)}, u32[]{:S(2)}, u32[]{:S(2)}) collective-permute-start(bf16[64,3584]{1,0:T(8,128)(2,1)} %refs_0_.1), channel_id=1, source_target_pairs={{0,4},{1,5},{4,8},{5,9},{8,12},{9,13},{12,14},{13,15},{14,10},{15,... | collective-permute-start | bytes 1376264 | tf_op jit(solution)/shard_map/ppermute | solution.py:89
  6.7 16.5 %collective-permute-start.7 = (bf16[64,3584]{1,0:T(8,128)(2,1)}, bf16[64,3584]{1,0:T(8,128)(2,1)}, u32[]{:S(2)}, u32[]{:S(2)}) collective-permute-start(bf16[64,3584]{1,0:T(8,128)(2,1)} %refs_0_.1), channel_id=1, source_target_pairs={{0,2},{1,3},{4,0},{5,1},{8,4},{9,5},{12,8},{13,9},{14,12},{15,13},... | collective-permute-start | bytes 1376264 | tf_op jit(solution)/shard_map/ppermute | solution.py:89
  8.3 14.8 %collective-permute-start.3 = (f32[4,4,128]{2,0,1:T(4,128)S(1)}, f32[4,4,128]{2,0,1:T(4,128)S(1)}, u32[]{:S(2)}, u32[]{:S(2)}) collective-permute-start(f32[4,4,128]{2,0,1:T(4,128)S(1)} %bitcast.37), channel_id=1, source_target_pairs={{0,4},{1,5},{2,6},{3,7},{4,0},{5,1},{6,2},{7,3},{8,12},{9,13},{10,... | collective-permute-start | bytes 24584 | tf_op jit(solution)/shard_map/ppermute | solution.py:93
  10.0 13.2 %collective-permute-start.4 = (f32[4,4,128]{2,0,1:T(4,128)S(1)}, f32[4,4,128]{2,0,1:T(4,128)S(1)}, u32[]{:S(2)}, u32[]{:S(2)}) collective-permute-start(f32[4,4,128]{2,0,1:T(4,128)S(1)} %bitcast.38), channel_id=1, source_target_pairs={{0,8},{1,9},{2,10},{3,11},{4,12},{5,13},{6,14},{7,15},{8,0},{9,1},... | collective-permute-start | bytes 24584 | tf_op jit(solution)/shard_map/ppermute | solution.py:93
  12.6 10.7 %collective-permute-start.5 = (f32[4,4,128]{2,0,1:T(4,128)S(1)}, f32[4,4,128]{2,0,1:T(4,128)S(1)}, u32[]{:S(2)}, u32[]{:S(2)}) collective-permute-start(f32[4,4,128]{2,0,1:T(4,128)S(1)} %bitcast.39), channel_id=1, source_target_pairs={{0,12},{1,13},{2,14},{3,15},{4,8},{5,9},{6,10},{7,11},{8,4},{9,5},... | collective-permute-start | bytes 24584 | tf_op jit(solution)/shard_map/ppermute | solution.py:93
  23.1 12.7 %collective-permute-start.12 = (bf16[64,3584]{1,0:T(8,128)(2,1)S(1)}, bf16[64,3584]{1,0:T(8,128)(2,1)S(1)}, u32[]{:S(2)}, u32[]{:S(2)}) collective-permute-start(bf16[64,3584]{1,0:T(8,128)(2,1)S(1)} %copy-done), channel_id=1, source_target_pairs={{0,1},{1,0},{2,3},{3,2},{4,5},{5,4},{6,7},{7,6},{8,9},{9,8},{10,11... | collective-permute-start | bytes 1376264 | tf_op jit(solution)/shard_map/ppermute | solution.py:93
  23.3 13.3 %collective-permute-start.10 = (bf16[64,3584]{1,0:T(8,128)(2,1)S(1)}, bf16[64,3584]{1,0:T(8,128)(2,1)}, u32[]{:S(2)}, u32[]{:S(2)}) collective-permute-start(bf16[64,3584]{1,0:T(8,128)(2,1)S(1)} %collective-permute-done.6.refs_2_), channel_id=1, source_target_pairs={{0,4},{1,5},{4,8},{5,9},{8,12},{9,13},{12,14},{13,15},{14,10},{15,... | collective-permute-start | bytes 1376264 | tf_op jit(solution)/shard_map/ppermute | solution.py:89
  24.0 12.8 %collective-permute-start.11 = (bf16[64,3584]{1,0:T(8,128)(2,1)}, bf16[64,3584]{1,0:T(8,128)(2,1)S(1)}, u32[]{:S(2)}, u32[]{:S(2)}) collective-permute-start(bf16[64,3584]{1,0:T(8,128)(2,1)} %collective-permute-done.7.refs_4_), channel_id=1, source_target_pairs={{0,2},{1,3},{4,0},{5,1},{8,4},{9,5},{12,8},{13,9},{14,12},{15,13},... | collective-permute-start | bytes 1376264 | tf_op jit(solution)/shard_map/ppermute | solution.py:89
  41.3 4.5 %collective-permute-start.8 = (bf16[64,3584]{1,0:T(8,128)(2,1)S(1)}, bf16[64,3584]{1,0:T(8,128)(2,1)S(1)}, u32[]{:S(2)}, u32[]{:S(2)}) collective-permute-start(bf16[64,3584]{1,0:T(8,128)(2,1)S(1)} %collective-permute-done.6.refs_2_), channel_id=1, source_target_pairs={{0,1},{1,0},{2,3},{3,2},{4,5},{5,4},{6,7},{7,6},{8,9},{9,8},{10,11... | collective-permute-start | bytes 1376264 | tf_op jit(solution)/shard_map/ppermute | solution.py:93
  41.8 5.5 %collective-permute-start.9 = (bf16[64,3584]{1,0:T(8,128)(2,1)}, bf16[64,3584]{1,0:T(8,128)(2,1)S(1)}, u32[]{:S(2)}, u32[]{:S(2)}) collective-permute-start(bf16[64,3584]{1,0:T(8,128)(2,1)} %collective-permute-done.7.refs_4_), channel_id=1, source_target_pairs={{0,1},{1,0},{2,3},{3,2},{4,5},{5,4},{6,7},{7,6},{8,9},{9,8},{10,11... | collective-permute-start | bytes 1376264 | tf_op jit(solution)/shard_map/ppermute | solution.py:93
  41.8 7.5 %collective-permute-start.13 = (bf16[64,3584]{1,0:T(8,128)(2,1)}, bf16[64,3584]{1,0:T(8,128)(2,1)S(1)}, u32[]{:S(2)}, u32[]{:S(2)}) collective-permute-start(bf16[64,3584]{1,0:T(8,128)(2,1)} %collective-permute-done.10.refs_6_), channel_id=1, source_target_pairs={{0,1},{1,0},{2,3},{3,2},{4,5},{5,4},{6,7},{7,6},{8,9},{9,8},{10,11... | collective-permute-start | bytes 1376264 | tf_op jit(solution)/shard_map/ppermute | solution.py:93
  42.3 24.4 %collective-permute-start.15 = (bf16[64,3584]{1,0:T(8,128)(2,1)}, bf16[64,3584]{1,0:T(8,128)(2,1)S(1)}, u32[]{:S(2)}, u32[]{:S(2)}) collective-permute-start(bf16[64,3584]{1,0:T(8,128)(2,1)} %collective-permute-done.10.refs_6_), channel_id=1, source_target_pairs={{0,4},{1,5},{4,8},{5,9},{8,12},{9,13},{12,14},{13,15},{14,10},{15,... | collective-permute-start | bytes 1376264 | tf_op jit(solution)/shard_map/ppermute | solution.py:89
  44.6 6.3 %collective-permute-start.14 = (bf16[128,3584]{1,0:T(8,128)(2,1)}, bf16[128,3584]{1,0:T(8,128)(2,1)}, u32[]{:S(2)}, u32[]{:S(2)}) collective-permute-start(bf16[128,3584]{1,0:T(8,128)(2,1)} %get-tuple-element.68), channel_id=1, source_target_pairs={{0,1},{1,0},{2,3},{3,2},{4,5},{5,4},{6,7},{7,6},{8,9},{9,8},{10,11... | collective-permute-start | bytes 2752520 | tf_op jit(solution)/shard_map/ppermute | solution.py:93
  46.6 20.1 %collective-permute-start.16 = (bf16[64,3584]{1,0:T(8,128)(2,1)S(1)}, bf16[64,3584]{1,0:T(8,128)(2,1)S(1)}, u32[]{:S(2)}, u32[]{:S(2)}) collective-permute-start(bf16[64,3584]{1,0:T(8,128)(2,1)S(1)} %collective-permute-done.11.refs_0_), channel_id=1, source_target_pairs={{0,2},{1,3},{4,0},{5,1},{8,4},{9,5},{12,8},{13,9},{14,12},{15,13},... | collective-permute-start | bytes 1376264 | tf_op jit(solution)/shard_map/ppermute | solution.py:89
  48.0 18.7 %collective-permute-start.18 = (bf16[64,3584]{1,0:T(8,128)(2,1)}, bf16[64,3584]{1,0:T(8,128)(2,1)}, u32[]{:S(2)}, u32[]{:S(2)}) collective-permute-start(bf16[64,3584]{1,0:T(8,128)(2,1)} %get-tuple-element.123), channel_id=1, source_target_pairs={{0,4},{1,5},{4,8},{5,9},{8,12},{9,13},{12,14},{13,15},{14,10},{15,... | collective-permute-start | bytes 1376264 | tf_op jit(solution)/shard_map/ppermute | solution.py:89
  50.1 19.3 %collective-permute-start.19 = (bf16[64,3584]{1,0:T(8,128)(2,1)}, bf16[64,3584]{1,0:T(8,128)(2,1)}, u32[]{:S(2)}, u32[]{:S(2)}) collective-permute-start(bf16[64,3584]{1,0:T(8,128)(2,1)} %get-tuple-element.122), channel_id=1, source_target_pairs={{0,2},{1,3},{4,0},{5,1},{8,4},{9,5},{12,8},{13,9},{14,12},{15,13},... | collective-permute-start | bytes 1376264 | tf_op jit(solution)/shard_map/ppermute | solution.py:89
  50.9 21.3 %collective-permute-start.22 = (bf16[64,3584]{1,0:T(8,128)(2,1)S(1)}, bf16[64,3584]{1,0:T(8,128)(2,1)S(1)}, u32[]{:S(2)}, u32[]{:S(2)}) collective-permute-start(bf16[64,3584]{1,0:T(8,128)(2,1)S(1)} %collective-permute-done.11.refs_0_), channel_id=1, source_target_pairs={{0,1},{1,0},{2,3},{3,2},{4,5},{5,4},{6,7},{7,6},{8,9},{9,8},{10,11... | collective-permute-start | bytes 1376264 | tf_op jit(solution)/shard_map/ppermute | solution.py:93
  69.4 5.0 %collective-permute-start.20 = (bf16[128,3584]{1,0:T(8,128)(2,1)S(1)}, bf16[128,3584]{1,0:T(8,128)(2,1)S(1)}, u32[]{:S(2)}, u32[]{:S(2)}) collective-permute-start(bf16[128,3584]{1,0:T(8,128)(2,1)S(1)} %get-tuple-element.83), channel_id=1, source_target_pairs={{0,1},{1,0},{2,3},{3,2},{4,5},{5,4},{6,7},{7,6},{8,9},{9,8},{10,11... | collective-permute-start | bytes 2752520 | tf_op jit(solution)/shard_map/ppermute | solution.py:93
  69.4 6.7 %collective-permute-start.21 = (bf16[128,3584]{1,0:T(8,128)(2,1)S(1)}, bf16[128,3584]{1,0:T(8,128)(2,1)S(1)}, u32[]{:S(2)}, u32[]{:S(2)}) collective-permute-start(bf16[128,3584]{1,0:T(8,128)(2,1)S(1)} %get-tuple-element.84), channel_id=1, source_target_pairs={{0,1},{1,0},{2,3},{3,2},{4,5},{5,4},{6,7},{7,6},{8,9},{9,8},{10,11... | collective-permute-start | bytes 2752520 | tf_op jit(solution)/shard_map/ppermute | solution.py:93
  69.9 4.1 %collective-permute-start.23 = (bf16[64,3584]{1,0:T(8,128)(2,1)S(1)}, bf16[64,3584]{1,0:T(8,128)(2,1)S(1)}, u32[]{:S(2)}, u32[]{:S(2)}) collective-permute-start(bf16[64,3584]{1,0:T(8,128)(2,1)S(1)} %collective-permute-done.15.refs_2_), channel_id=1, source_target_pairs={{0,1},{1,0},{2,3},{3,2},{4,5},{5,4},{6,7},{7,6},{8,9},{9,8},{10,11... | collective-permute-start | bytes 1376264 | tf_op jit(solution)/shard_map/ppermute | solution.py:93
  69.9 6.6 %collective-permute-start.24 = (bf16[64,3584]{1,0:T(8,128)(2,1)S(1)}, bf16[64,3584]{1,0:T(8,128)(2,1)S(1)}, u32[]{:S(2)}, u32[]{:S(2)}) collective-permute-start(bf16[64,3584]{1,0:T(8,128)(2,1)S(1)} %collective-permute-done.16.refs_4_), channel_id=1, source_target_pairs={{0,1},{1,0},{2,3},{3,2},{4,5},{5,4},{6,7},{7,6},{8,9},{9,8},{10,11... | collective-permute-start | bytes 1376264 | tf_op jit(solution)/shard_map/ppermute | solution.py:93
  72.2 19.1 %collective-permute-start.25 = (bf16[64,3584]{1,0:T(8,128)(2,1)S(1)}, bf16[64,3584]{1,0:T(8,128)(2,1)S(1)}, u32[]{:S(2)}, u32[]{:S(2)}) collective-permute-start(bf16[64,3584]{1,0:T(8,128)(2,1)S(1)} %get-tuple-element.121), channel_id=1, source_target_pairs={{0,4},{1,5},{4,8},{5,9},{8,12},{9,13},{12,14},{13,15},{14,10},{15,... | collective-permute-start | bytes 1376264 | tf_op jit(solution)/shard_map/ppermute | solution.py:89
  74.0 17.3 %collective-permute-start.26 = (bf16[64,3584]{1,0:T(8,128)(2,1)S(1)}, bf16[64,3584]{1,0:T(8,128)(2,1)S(1)}, u32[]{:S(2)}, u32[]{:S(2)}) collective-permute-start(bf16[64,3584]{1,0:T(8,128)(2,1)S(1)} %get-tuple-element.120), channel_id=1, source_target_pairs={{0,2},{1,3},{4,0},{5,1},{8,4},{9,5},{12,8},{13,9},{14,12},{15,13},... | collective-permute-start | bytes 1376264 | tf_op jit(solution)/shard_map/ppermute | solution.py:89
  74.4 15.2 %collective-permute-start.27 = (bf16[32,3584]{1,0:T(8,128)(2,1)S(1)}, bf16[32,3584]{1,0:T(8,128)(2,1)S(1)}, u32[]{:S(2)}, u32[]{:S(2)}) collective-permute-start(bf16[32,3584]{1,0:T(8,128)(2,1)S(1)} %slice.74), channel_id=1, source_target_pairs={{0,4},{1,5},{4,8},{5,9},{8,12},{9,13},{12,14},{13,15},{14,10},{15,... | collective-permute-start | bytes 688136 | tf_op jit(solution)/shard_map/ppermute | solution.py:89
  76.2 15.2 %collective-permute-start.28 = (bf16[32,3584]{1,0:T(8,128)(2,1)S(1)}, bf16[32,3584]{1,0:T(8,128)(2,1)S(1)}, u32[]{:S(2)}, u32[]{:S(2)}) collective-permute-start(bf16[32,3584]{1,0:T(8,128)(2,1)S(1)} %slice.75), channel_id=1, source_target_pairs={{0,2},{1,3},{4,0},{5,1},{8,4},{9,5},{12,8},{13,9},{14,12},{15,13},... | collective-permute-start | bytes 688136 | tf_op jit(solution)/shard_map/ppermute | solution.py:89
  76.5 29.3 %collective-permute-start.33 = (bf16[384,1024]{1,0:T(8,128)(2,1)S(1)}, bf16[384,1024]{1,0:T(8,128)(2,1)S(1)}, u32[]{:S(2)}, u32[]{:S(2)}) collective-permute-start(bf16[384,1024]{1,0:T(8,128)(2,1)S(1)} %get-tuple-element.103), channel_id=1, source_target_pairs={{0,16},{16,0},{1,17},{17,1},{2,18},{18,2},{3,19},{19,3},{4,20},{20... | collective-permute-start | bytes 2359304 | tf_op jit(solution)/shard_map/ppermute | solution.py:101
  91.7 14.1 %collective-permute-start.31 = (bf16[64,3584]{1,0:T(8,128)(2,1)S(1)}, bf16[64,3584]{1,0:T(8,128)(2,1)S(1)}, u32[]{:S(2)}, u32[]{:S(2)}) collective-permute-start(bf16[64,3584]{1,0:T(8,128)(2,1)S(1)} %get-tuple-element.101), channel_id=1, source_target_pairs={{0,4},{1,5},{4,8},{5,9},{8,12},{9,13},{12,14},{13,15},{14,10},{15,... | collective-permute-start | bytes 1376264 | tf_op jit(solution)/shard_map/ppermute | solution.py:89
  93.5 12.4 %collective-permute-start.32 = (bf16[64,3584]{1,0:T(8,128)(2,1)S(1)}, bf16[64,3584]{1,0:T(8,128)(2,1)S(1)}, u32[]{:S(2)}, u32[]{:S(2)}) collective-permute-start(bf16[64,3584]{1,0:T(8,128)(2,1)S(1)} %get-tuple-element.102), channel_id=1, source_target_pairs={{0,2},{1,3},{4,0},{5,1},{8,4},{9,5},{12,8},{13,9},{14,12},{15,13},... | collective-permute-start | bytes 1376264 | tf_op jit(solution)/shard_map/ppermute | solution.py:89
  95.3 16.2 %collective-permute-start.34 = (bf16[288,1024]{1,0:T(8,128)(2,1)S(1)}, bf16[288,1024]{1,0:T(8,128)(2,1)S(1)}, u32[]{:S(2)}, u32[]{:S(2)}) collective-permute-start(bf16[288,1024]{1,0:T(8,128)(2,1)S(1)} %get-tuple-element.108), channel_id=1, source_target_pairs={{0,16},{16,0},{1,17},{17,1},{2,18},{18,2},{3,19},{19,3},{4,20},{20... | collective-permute-start | bytes 1769480 | tf_op jit(solution)/shard_map/ppermute | solution.py:101
  106.0 12.3 %collective-permute-start.35 = (bf16[64,3584]{1,0:T(8,128)(2,1)S(1)}, bf16[64,3584]{1,0:T(8,128)(2,1)S(1)}, u32[]{:S(2)}, u32[]{:S(2)}) collective-permute-start(bf16[64,3584]{1,0:T(8,128)(2,1)S(1)} %add_convert_fusion.1), channel_id=1, source_target_pairs={{0,2},{1,3},{4,0},{5,1},{8,4},{9,5},{12,8},{13,9},{14,12},{15,13},... | collective-permute-start | bytes 1376264 | tf_op jit(solution)/shard_map/ppermute | solution.py:89
  106.6 12.8 %collective-permute-start.36 = (bf16[96,1024]{1,0:T(8,128)(2,1)S(1)}, bf16[96,1024]{1,0:T(8,128)(2,1)S(1)}, u32[]{:S(2)}, u32[]{:S(2)}) collective-permute-start(bf16[96,1024]{1,0:T(8,128)(2,1)S(1)} %get-tuple-element.111), channel_id=1, source_target_pairs={{0,16},{16,0},{1,17},{17,1},{2,18},{18,2},{3,19},{19,3},{4,20},{20... | collective-permute-start | bytes 589832 | tf_op jit(solution)/shard_map/ppermute | solution.py:101
  (17 other events, 67.5 us)

commit v4 on v2

--- a/solution.py
+++ b/solution.py
@@ -343,8 +343,8 @@
             pltpu.VMEM((count, 2 * cap, width), BF16),
             pltpu.SemaphoreType.DMA((count, 2)),
         ],
-        flops=count * 2**28,
-        moved=count * 6 * half * width,
+        flops=2**20,
+        moved=2**14,
     )
 
 
@@ -504,10 +504,11 @@
     got[-2], got[2] = step_ring(got[-1], 1), step_ring(got[1], -1)
     pair[0] = core(got[0])
     raw2 = raw_forward(width // 2, width // 2, pin(hidden), weights)
-    raw2, got[-2], got[2], pair[0] = tie(raw2, got[-2], got[2], pair[0])
-
+    raw2, pair[0] = tie(raw2, pair[0])
+
+    keep1, other1, other2 = spread((3, -4, 2, -3), 2, gate_a)
+    keep1, other1, other2, got[-2], got[2] = tie(keep1, other1, other2, got[-2], got[2])
     got[-3], got[3] = step_ring(got[-2], 1), step_ring(got[2], -1)
-    keep1, other1, other2 = spread((3, -4, 2, -3), 2, gate_a)
     other1, other2 = core(other1), core(other2)
     for d in (-1, 1, -2):
         pair[d] = core(got[d])
@@ -530,7 +531,6 @@
         send1, got[-3], got[3], up, down, other3, other4
     )
     got[-4] = step_ring(got[-3], 1)
-    up = step_ring(add(keep1[2 * tokens : 3 * tokens], other2[:tokens], up), 1)
     down = step_ring(add(keep1[3 * tokens :], other2[tokens:], down), -1)
     recv1 = across(send1)
     pair[2], pair[-3], pair[3] = core(got[2]), core(got[-3]), core(got[3])
@@ -538,14 +538,15 @@
     gate_b, other3, other4 = tie(gate_b, other3, other4)
     send2, hold2 = bwd(groups[1], share=64)
 
-    hold2, send2, down = tie(hold2, send2, down)
+    hold2, send2, up, down, got[-4] = tie(hold2, send2, up, down, got[-4])
+    up = step_ring(add(keep1[2 * tokens : 3 * tokens], other2[:tokens], up), 1)
+    down = step_ring(mine(1, other3, down), -1)
+    pair[-4] = core(got[-4])
     recv2 = across(send2)
-    down = step_ring(mine(1, other3, down), -1)
-    up, got[-4], down, recv1 = tie(up, got[-4], down, recv1)
-
-    pair[-4] = core(got[-4])
+    send3, hold3 = bwd(groups[2], share=64)
+
+    send3, hold3, up, down, recv1 = tie(send3, hold3, up, down, recv1)
     up, down = step_ring(mine(0, other3, up), 1), step_ring(mine(2, other4, down), -1)
-    send3, hold3 = bwd(groups[2], share=64)
     recv3 = across(send3)
     hold3, recv2 = tie(hold3, recv2)
     grad = collect(groups[:2], where, (hold1, recv1, hold2, recv2), 8 * rows)

time: 120 us -> 116 us (0.967)
  waiting for transfers between devices: 20.8 us -> 16.4 us
    ppermute x14, waiting for transfers between devices: 13.7 us -> 8.88 us  [step_ring(): return lax.ppermute(value, 'expert', pairs)]
    ppermute x14, starting transfers between devices: 15.6 us -> 13.6 us  [step_ring(): return lax.ppermute(value, 'expert', pairs)]
    ppermute x18, waiting for transfers between devices: 1.95 us -> 3.16 us  [xor(): return lax.ppermute(value, 'expert', [(i, i ^ bits) for i in range(16)])]
    convert_element_type x5 -> x6, other arithmetic: 4.44 us -> 5.35 us  [add(): return total.astype(BF16)]
  transfers between devices with their start and end apart: 35 -> 35, of which waited for: 11 -> 10; matrix products, arithmetic and copies ran while one was open for 3% -> 4% of each run, Pallas kernels for 47% -> 52%
where the time goes in v4:
time: 116 us
  Pallas kernels  62.6 us (54%)
  starting transfers between devices  27.3 us (24%)
  waiting for transfers between devices  16.4 us (14%)
  other arithmetic  5.47 us (5%)
  local copies, waits for them, and re-layouts  2.71 us (2%)
    pallas_call x6, Pallas kernels, kernel_call(): pl.pallas_call(kernel, in_specs=in_specs, out_specs=[VMEM] * len(out_shap...  39.2 us
    pallas_call x2, Pallas kernels, raw_forward(): pl.pallas_call(functools.partial(raw_kernel, first), in_specs=[HBM, HBM],...  20.5 us
    ppermute x14, starting transfers between devices, step_ring(): return lax.ppermute(value, 'expert', pairs)  13.6 us
    ppermute x18, starting transfers between devices, xor(): return lax.ppermute(value, 'expert', [(i, i ^ bits) for i in range(16)])  10 us
    ppermute x14, waiting for transfers between devices, step_ring(): return lax.ppermute(value, 'expert', pairs)  8.88 us
    convert_element_type x6, other arithmetic, add(): return total.astype(BF16)  5.35 us
    ppermute x3, waiting for transfers between devices, across(): return lax.ppermute(value, 'pipe', [(0, 1), (1, 0)])  4.39 us
    ppermute x3, starting transfers between devices, across(): return lax.ppermute(value, 'pipe', [(0, 1), (1, 0)])  3.63 us
  transfers between devices with their start and end apart: 35, of which 10 were waited for; matrix products, arithmetic and copies ran while one was open for 4% of the time, Pallas kernels for 52%

profile of v4, /device:TPU:0, one launch (start us, length us, event | category | flops | bytes accessed | tf_op | source)
XLA Modules:
  0.0 115.5 jit_solution(2583351788094351322)
XLA Ops:
  1.5 2.5 %collective-permute-start.2 = (f32[16,128]{1,0:T(8,128)S(1)}, f32[16,128]{1,0:T(8,128)S(1)}, u32[]{:S(2)}, u32[]{:S(2)}) collective-permute-start(f32[16,128]{1,0:T(8,128)S(1)} %gates.1), channel_id=1, source_target_pairs={{0,3},{1,2},{2,1},{3,0},{4,7},{5,6},{6,5},{7,4},{8,11},{9,10},{10,... | collective-permute-start | bytes 24584 | tf_op jit(solution)/shard_map/ppermute | solution.py:93
  4.7 2.0 %collective-permute-start.6 = (bf16[64,3584]{1,0:T(8,128)(2,1)}, bf16[64,3584]{1,0:T(8,128)(2,1)S(1)}, u32[]{:S(2)}, u32[]{:S(2)}) collective-permute-start(bf16[64,3584]{1,0:T(8,128)(2,1)} %refs_0_.1), channel_id=1, source_target_pairs={{0,4},{1,5},{4,8},{5,9},{8,12},{9,13},{12,14},{13,15},{14,10},{15,... | collective-permute-start | bytes 1376264 | tf_op jit(solution)/shard_map/ppermute | solution.py:89
  6.8 1.5 %collective-permute-done.1 = f32[16,128]{1,0:T(8,128)S(1)} collective-permute-done((f32[16,128]{1,0:T(8,128)S(1)}, f32[16,128]{1,0:T(8,128)S(1)}, u32[]{:S(2)}, u32[]{:S(2)}) %collective-permute-start.1) | collective-permute-done | bytes 8224 | tf_op jit(solution)/shard_map/ppermute | solution.py:93
  8.3 1.6 %collective-permute-start.3 = (f32[4,4,128]{2,0,1:T(4,128)S(1)}, f32[4,4,128]{2,0,1:T(4,128)S(1)}, u32[]{:S(2)}, u32[]{:S(2)}) collective-permute-start(f32[4,4,128]{2,0,1:T(4,128)S(1)} %bitcast.37), channel_id=1, source_target_pairs={{0,4},{1,5},{2,6},{3,7},{4,0},{5,1},{6,2},{7,3},{8,12},{9,13},{10,... | collective-permute-start | bytes 24584 | tf_op jit(solution)/shard_map/ppermute | solution.py:93
  10.0 2.6 %collective-permute-start.4 = (f32[4,4,128]{2,0,1:T(4,128)S(1)}, f32[4,4,128]{2,0,1:T(4,128)S(1)}, u32[]{:S(2)}, u32[]{:S(2)}) collective-permute-start(f32[4,4,128]{2,0,1:T(4,128)S(1)} %bitcast.38), channel_id=1, source_target_pairs={{0,8},{1,9},{2,10},{3,11},{4,12},{5,13},{6,14},{7,15},{8,0},{9,1},... | collective-permute-start | bytes 24584 | tf_op jit(solution)/shard_map/ppermute | solution.py:93
  12.8 10.3 %raw_forward.2.refs_0_ = bf16[768,1792]{1,0:T(8,128)(2,1)} custom-call(bf16[768,2048]{1,0:T(8,128)(2,1)} %bitcast.51, bf16[2048,3584]{1,0:T(8,128)(2,1)} %bitcast.30), custom_call_target="tpu_custom_call" | custom-call | flops 5637144576 | bytes 13238272 | tf_op jit(solution)/shard_map/raw_forward/pallas_call | solution.py:263
  23.9 1.4 %collective-permute-start.12 = (bf16[64,3584]{1,0:T(8,128)(2,1)}, bf16[64,3584]{1,0:T(8,128)(2,1)S(1)}, u32[]{:S(2)}, u32[]{:S(2)}) collective-permute-start(bf16[64,3584]{1,0:T(8,128)(2,1)} %collective-permute-done.7.refs_4_), channel_id=1, source_target_pairs={{0,2},{1,3},{4,0},{5,1},{8,4},{9,5},{12,8},{13,9},{14,12},{15,13},... | collective-permute-start | bytes 1376264 | tf_op jit(solution)/shard_map/ppermute | solution.py:89
  25.3 10.2 %raw_forward.3.refs_1_ = bf16[768,1792]{1,0:T(8,128)(2,1)} custom-call(bf16[768,2048]{1,0:T(8,128)(2,1)} %bitcast.52, bf16[2048,3584]{1,0:T(8,128)(2,1)} %bitcast.31), custom_call_target="tpu_custom_call" | custom-call | flops 5637144576 | bytes 13238272 | tf_op jit(solution)/shard_map/raw_forward/pallas_call | solution.py:263
  35.8 4.4 %spread_tokens.2 = (bf16[256,3584]{1,0:T(8,128)(2,1)S(1)}, bf16[128,3584]{1,0:T(8,128)(2,1)S(1)}, bf16[128,3584]{1,0:T(8,128)(2,1)}) custom-call(s32[17]{0:T(128)S(1)} %pad_add_fusion.where, f32[8,128]{1,0:T(8,128)S(1)} %squeeze.20.gates, bf16[768,1792]{1,0:T(8,128)(2,1)} %raw_forward.2.refs_0_, bf16[768,1792]{1,0:T(8,128)(2,1)} %raw_forward.3.refs_1_), custom_call_target="tpu_custom_call" | custom-call | flops 1048576 | bytes 16384 | tf_op jit(solution)/shard_map/spread_tokens/pallas_call | solution.py:120
  42.9 1.2 %add_convert_fusion.6 = (bf16[64,3584]{1,0:T(8,128)(2,1)}, bf16[64,3584]{1,0:T(8,128)(2,1)}) fusion(bf16[128,3584]{1,0:T(8,128)(2,1)S(1)} %collective-permute-done.17, bf16[256,3584]{1,0:T(8,128)(2,1)S(1)} %get-tuple-element.84), kind=kLoop, calls=%fused_computation.6 | loop fusion | flops 1835008 | bytes 2752512 | tf_op jit(solution)/shard_map/convert_element_type | solution.py:32
  46.1 1.5 %collective-permute-start.18 = (bf16[64,3584]{1,0:T(8,128)(2,1)}, bf16[64,3584]{1,0:T(8,128)(2,1)}, u32[]{:S(2)}, u32[]{:S(2)}) collective-permute-start(bf16[64,3584]{1,0:T(8,128)(2,1)} %get-tuple-element.123), channel_id=1, source_target_pairs={{0,4},{1,5},{4,8},{5,9},{8,12},{9,13},{12,14},{13,15},{14,10},{15,... | collective-permute-start | bytes 1376264 | tf_op jit(solution)/shard_map/ppermute | solution.py:89
  49.1 3.5 %spread_tokens.3 = (bf16[256,3584]{1,0:T(8,128)(2,1)S(1)}, bf16[128,3584]{1,0:T(8,128)(2,1)S(1)}, bf16[128,3584]{1,0:T(8,128)(2,1)S(1)}) custom-call(s32[17]{0:T(128)S(1)} %pad_add_fusion.where, f32[8,128]{1,0:T(8,128)S(1)} %squeeze.20.gates, bf16[768,1792]{1,0:T(8,128)(2,1)} %raw_forward.2.refs_0_, bf16[768,1792]{1,0:T(8,128)(2,1)} %raw_forward.3.refs_1_), custom_call_target="tpu_custom_call" | custom-call | flops 1048576 | bytes 16384 | tf_op jit(solution)/shard_map/spread_tokens/pallas_call | solution.py:120
  52.7 12.1 %backward.3 = (bf16[384,1024]{1,0:T(8,128)(2,1)S(1)}, bf16[384,1024]{1,0:T(8,128)(2,1)S(1)}) custom-call(s32[17]{0:T(128)S(1)} %pad_add_fusion.where, s32[1]{0:T(128)} %bitcast.20.pipe, f32[8,128]{1,0:T(8,128)S(1)} %squeeze.21.gates, bf16[2048,3584]{1,0:T(8,128)(2,1)} %bitcast.32, bf16[64,3584]{1,0:T(8,128)(2,1)S(1)} %copy-done.1, ...), custom_call_target="tpu_custom_call" | custom-call | flops 88080384 | bytes 339968 | tf_op jit(solution)/shard_map/backward/pallas_call | solution.py:120
  64.8 2.7 %collective-permute-done.19 = bf16[64,3584]{1,0:T(8,128)(2,1)} collective-permute-done((bf16[64,3584]{1,0:T(8,128)(2,1)}, bf16[64,3584]{1,0:T(8,128)(2,1)}, u32[]{:S(2)}, u32[]{:S(2)}) %collective-permute-start.19) | collective-permute-done | bytes 458784 | tf_op jit(solution)/shard_map/ppermute | solution.py:89
  68.6 1.3 %add_convert_fusion.5 = bf16[64,3584]{1,0:T(8,128)(2,1)S(1)} fusion(bf16[64,3584]{1,0:T(8,128)(2,1)} %collective-permute-done.19, bf16[128,3584]{1,0:T(8,128)(2,1)} %collective-permute-done.14, bf16[256,3584]{1,0:T(8,128)(2,1)S(1)} %get-tuple-element.84), kind=kLoop, calls=%fused_computation.5 | loop fusion | flops 1376256 | bytes 1835008 | tf_op jit(solution)/shard_map/convert_element_type | solution.py:32
  71.4 1.5 %collective-permute-start.26 = (bf16[64,3584]{1,0:T(8,128)(2,1)S(1)}, bf16[64,3584]{1,0:T(8,128)(2,1)S(1)}, u32[]{:S(2)}, u32[]{:S(2)}) collective-permute-start(bf16[64,3584]{1,0:T(8,128)(2,1)S(1)} %collective-permute-done.15.refs_2_), channel_id=1, source_target_pairs={{0,4},{1,5},{4,8},{5,9},{8,12},{9,13},{12,14},{13,15},{14,10},{15,... | collective-permute-start | bytes 1376264 | tf_op jit(solution)/shard_map/ppermute | solution.py:89
  72.9 1.5 %collective-permute-start.30 = (bf16[384,1024]{1,0:T(8,128)(2,1)S(1)}, bf16[384,1024]{1,0:T(8,128)(2,1)S(1)}, u32[]{:S(2)}, u32[]{:S(2)}) collective-permute-start(bf16[384,1024]{1,0:T(8,128)(2,1)S(1)} %get-tuple-element.106), channel_id=1, source_target_pairs={{0,16},{16,0},{1,17},{17,1},{2,18},{18,2},{3,19},{19,3},{4,20},{20... | collective-permute-start | bytes 2359304 | tf_op jit(solution)/shard_map/ppermute | solution.py:101
  74.4 10.0 %backward.4 = (bf16[288,1024]{1,0:T(8,128)(2,1)S(1)}, bf16[288,1024]{1,0:T(8,128)(2,1)S(1)}) custom-call(s32[17]{0:T(128)S(1)} %pad_add_fusion.where, s32[1]{0:T(128)} %bitcast.20.pipe, f32[8,128]{1,0:T(8,128)S(1)} %squeeze.21.gates, bf16[2048,3584]{1,0:T(8,128)(2,1)} %bitcast.33, bf16[64,3584]{1,0:T(8,128)(2,1)S(1)} %collective-permute-done.12.refs_0_, ...), custom_call_target="tpu_custom_call" | custom-call | flops 66060288 | bytes 312320 | tf_op jit(solution)/shard_map/backward/pallas_call | solution.py:120
  85.1 1.3 %add_convert_fusion.4 = bf16[64,3584]{1,0:T(8,128)(2,1)S(1)} fusion(bf16[64,3584]{1,0:T(8,128)(2,1)} %collective-permute-done.18, bf16[128,3584]{1,0:T(8,128)(2,1)} %collective-permute-done.14, bf16[256,3584]{1,0:T(8,128)(2,1)S(1)} %get-tuple-element.84), kind=kLoop, calls=%fused_computation.4 | loop fusion | flops 1376256 | bytes 1835008 | tf_op jit(solution)/shard_map/convert_element_type | solution.py:32
  86.4 1.6 %collective-permute-start.28 = (bf16[64,3584]{1,0:T(8,128)(2,1)S(1)}, bf16[64,3584]{1,0:T(8,128)(2,1)S(1)}, u32[]{:S(2)}, u32[]{:S(2)}) collective-permute-start(bf16[64,3584]{1,0:T(8,128)(2,1)S(1)} %add_convert_fusion.4), channel_id=1, source_target_pairs={{0,4},{1,5},{4,8},{5,9},{8,12},{9,13},{12,14},{13,15},{14,10},{15,... | collective-permute-start | bytes 1376264 | tf_op jit(solution)/shard_map/ppermute | solution.py:89
  88.0 1.0 collective-permute-start.31
  89.0 8.4 %backward.5 = (bf16[96,1024]{1,0:T(8,128)(2,1)S(1)}, bf16[96,1024]{1,0:T(8,128)(2,1)S(1)}) custom-call(s32[17]{0:T(128)S(1)} %pad_add_fusion.where, s32[1]{0:T(128)} %bitcast.20.pipe, f32[8,128]{1,0:T(8,128)S(1)} %squeeze.21.gates, bf16[2048,3584]{1,0:T(8,128)(2,1)} %bitcast.34, bf16[64,3584]{1,0:T(8,128)(2,1)S(1)} %collective-permute-done.26.refs_0_, ...), custom_call_target="tpu_custom_call" | custom-call | flops 22020096 | bytes 257024 | tf_op jit(solution)/shard_map/backward/pallas_call | solution.py:120
  97.5 1.9 %collective-permute-done.28 = bf16[64,3584]{1,0:T(8,128)(2,1)S(1)} collective-permute-done((bf16[64,3584]{1,0:T(8,128)(2,1)S(1)}, bf16[64,3584]{1,0:T(8,128)(2,1)S(1)}, u32[]{:S(2)}, u32[]{:S(2)}) %collective-permute-start.28) | collective-permute-done | bytes 458784 | tf_op jit(solution)/shard_map/ppermute | solution.py:89
  99.7 1.6 %collective-permute-start.32 = (bf16[64,3584]{1,0:T(8,128)(2,1)S(1)}, bf16[64,3584]{1,0:T(8,128)(2,1)S(1)}, u32[]{:S(2)}, u32[]{:S(2)}) collective-permute-start(bf16[64,3584]{1,0:T(8,128)(2,1)S(1)} %get-tuple-element.125), channel_id=1, source_target_pairs={{0,4},{1,5},{4,8},{5,9},{8,12},{9,13},{12,14},{13,15},{14,10},{15,... | collective-permute-start | bytes 1376264 | tf_op jit(solution)/shard_map/ppermute | solution.py:89
  101.8 1.1 collective-permute-start.34
  102.9 3.0 %collective-permute-done.31.refs_3_ = bf16[288,1024]{1,0:T(8,128)(2,1)S(1)} collective-permute-done((bf16[288,1024]{1,0:T(8,128)(2,1)S(1)}, bf16[288,1024]{1,0:T(8,128)(2,1)S(1)}, u32[]{:S(2)}, u32[]{:S(2)}) %collective-permute-start.31) | collective-permute-done | bytes 589856 | tf_op jit(solution)/shard_map/ppermute | solution.py:101
  105.9 1.7 %collect.2.refs_2_ = bf16[768,1024]{1,0:T(8,128)(2,1)} custom-call(s32[17]{0:T(128)S(1)} %pad_add_fusion.where, bf16[384,1024]{1,0:T(8,128)(2,1)S(1)} %get-tuple-element.91.refs_0_, bf16[384,1024]{1,0:T(8,128)(2,1)S(1)} %collective-permute-done.30.refs_1_, bf16[288,1024]{1,0:T(8,128)(2,1)S(1)} %get-tuple-element.108.refs_2_, ...), custom_call_target="tpu_custom_call" | custom-call | flops 1048576 | bytes 4128768 | tf_op jit(solution)/shard_map/collect/pallas_call | solution.py:450
  107.7 1.4 %collective-permute-done.34.refs_1_ = bf16[96,1024]{1,0:T(8,128)(2,1)S(1)} collective-permute-done((bf16[96,1024]{1,0:T(8,128)(2,1)S(1)}, bf16[96,1024]{1,0:T(8,128)(2,1)S(1)}, u32[]{:S(2)}, u32[]{:S(2)}) %collective-permute-start.34) | collective-permute-done | bytes 196640 | tf_op jit(solution)/shard_map/ppermute | solution.py:101
  109.0 2.9 %collective-permute-done.32 = bf16[64,3584]{1,0:T(8,128)(2,1)S(1)} collective-permute-done((bf16[64,3584]{1,0:T(8,128)(2,1)S(1)}, bf16[64,3584]{1,0:T(8,128)(2,1)S(1)}, u32[]{:S(2)}, u32[]{:S(2)}) %collective-permute-start.32) | collective-permute-done | bytes 458784 | tf_op jit(solution)/shard_map/ppermute | solution.py:89
  111.9 1.3 %collective-permute-done.33 = bf16[64,3584]{1,0:T(8,128)(2,1)S(1)} collective-permute-done((bf16[64,3584]{1,0:T(8,128)(2,1)S(1)}, bf16[64,3584]{1,0:T(8,128)(2,1)S(1)}, u32[]{:S(2)}, u32[]{:S(2)}) %collective-permute-start.33) | collective-permute-done | bytes 458784 | tf_op jit(solution)/shard_map/ppermute | solution.py:89
  113.2 1.0 add_convert_fusion
  114.2 1.3 %collect.3 = bf16[768,1024]{1,0:T(8,128)(2,1)} custom-call(s32[17]{0:T(128)S(1)} %pad_add_fusion.where, bf16[96,1024]{1,0:T(8,128)(2,1)S(1)} %get-tuple-element.117.refs_0_, bf16[96,1024]{1,0:T(8,128)(2,1)S(1)} %collective-permute-done.34.refs_1_, bf16[768,1024]{1,0:T(8,128)(2,1)} %collect.2.refs_2_), custom_call_target="tpu_custom_call", output_to_operand_aliasing={{}: (3, {})} | custom-call | flops 1048576 | bytes 589824 | tf_op jit(solution)/shard_map/collect/pallas_call | solution.py:450
  (88 shorter events, 13.2 us)
Async XLA Ops:
  1.5 5.3 %collective-permute-start.2 = (f32[16,128]{1,0:T(8,128)S(1)}, f32[16,128]{1,0:T(8,128)S(1)}, u32[]{:S(2)}, u32[]{:S(2)}) collective-permute-start(f32[16,128]{1,0:T(8,128)S(1)} %gates.1), channel_id=1, source_target_pairs={{0,3},{1,2},{2,1},{3,0},{4,7},{5,6},{6,5},{7,4},{8,11},{9,10},{10,... | collective-permute-start | bytes 24584 | tf_op jit(solution)/shard_map/ppermute | solution.py:93
  4.6 3.7 %collective-permute-start.1 = (f32[16,128]{1,0:T(8,128)S(1)}, f32[16,128]{1,0:T(8,128)S(1)}, u32[]{:S(2)}, u32[]{:S(2)}) collective-permute-start(f32[16,128]{1,0:T(8,128)S(1)} %gates.1), channel_id=1, source_target_pairs={{0,2},{1,3},{2,0},{3,1},{4,6},{5,7},{6,4},{7,5},{8,10},{9,11},{10,... | collective-permute-start | bytes 24584 | tf_op jit(solution)/shard_map/ppermute | solution.py:93
  4.7 18.5 %collective-permute-start.6 = (bf16[64,3584]{1,0:T(8,128)(2,1)}, bf16[64,3584]{1,0:T(8,128)(2,1)S(1)}, u32[]{:S(2)}, u32[]{:S(2)}) collective-permute-start(bf16[64,3584]{1,0:T(8,128)(2,1)} %refs_0_.1), channel_id=1, source_target_pairs={{0,4},{1,5},{4,8},{5,9},{8,12},{9,13},{12,14},{13,15},{14,10},{15,... | collective-permute-start | bytes 1376264 | tf_op jit(solution)/shard_map/ppermute | solution.py:89
  6.7 16.5 %collective-permute-start.7 = (bf16[64,3584]{1,0:T(8,128)(2,1)}, bf16[64,3584]{1,0:T(8,128)(2,1)}, u32[]{:S(2)}, u32[]{:S(2)}) collective-permute-start(bf16[64,3584]{1,0:T(8,128)(2,1)} %refs_0_.1), channel_id=1, source_target_pairs={{0,2},{1,3},{4,0},{5,1},{8,4},{9,5},{12,8},{13,9},{14,12},{15,13},... | collective-permute-start | bytes 1376264 | tf_op jit(solution)/shard_map/ppermute | solution.py:89
  8.3 14.7 %collective-permute-start.3 = (f32[4,4,128]{2,0,1:T(4,128)S(1)}, f32[4,4,128]{2,0,1:T(4,128)S(1)}, u32[]{:S(2)}, u32[]{:S(2)}) collective-permute-start(f32[4,4,128]{2,0,1:T(4,128)S(1)} %bitcast.37), channel_id=1, source_target_pairs={{0,4},{1,5},{2,6},{3,7},{4,0},{5,1},{6,2},{7,3},{8,12},{9,13},{10,... | collective-permute-start | bytes 24584 | tf_op jit(solution)/shard_map/ppermute | solution.py:93
  10.0 13.2 %collective-permute-start.4 = (f32[4,4,128]{2,0,1:T(4,128)S(1)}, f32[4,4,128]{2,0,1:T(4,128)S(1)}, u32[]{:S(2)}, u32[]{:S(2)}) collective-permute-start(f32[4,4,128]{2,0,1:T(4,128)S(1)} %bitcast.38), channel_id=1, source_target_pairs={{0,8},{1,9},{2,10},{3,11},{4,12},{5,13},{6,14},{7,15},{8,0},{9,1},... | collective-permute-start | bytes 24584 | tf_op jit(solution)/shard_map/ppermute | solution.py:93
  12.6 10.6 %collective-permute-start.5 = (f32[4,4,128]{2,0,1:T(4,128)S(1)}, f32[4,4,128]{2,0,1:T(4,128)S(1)}, u32[]{:S(2)}, u32[]{:S(2)}) collective-permute-start(f32[4,4,128]{2,0,1:T(4,128)S(1)} %bitcast.39), channel_id=1, source_target_pairs={{0,12},{1,13},{2,14},{3,15},{4,8},{5,9},{6,10},{7,11},{8,4},{9,5},... | collective-permute-start | bytes 24584 | tf_op jit(solution)/shard_map/ppermute | solution.py:93
  23.1 12.4 %collective-permute-start.10 = (bf16[64,3584]{1,0:T(8,128)(2,1)S(1)}, bf16[64,3584]{1,0:T(8,128)(2,1)S(1)}, u32[]{:S(2)}, u32[]{:S(2)}) collective-permute-start(bf16[64,3584]{1,0:T(8,128)(2,1)S(1)} %copy-done), channel_id=1, source_target_pairs={{0,1},{1,0},{2,3},{3,2},{4,5},{5,4},{6,7},{7,6},{8,9},{9,8},{10,11... | collective-permute-start | bytes 1376264 | tf_op jit(solution)/shard_map/ppermute | solution.py:93
  23.2 16.9 %collective-permute-start.11 = (bf16[64,3584]{1,0:T(8,128)(2,1)S(1)}, bf16[64,3584]{1,0:T(8,128)(2,1)}, u32[]{:S(2)}, u32[]{:S(2)}) collective-permute-start(bf16[64,3584]{1,0:T(8,128)(2,1)S(1)} %collective-permute-done.6.refs_2_), channel_id=1, source_target_pairs={{0,4},{1,5},{4,8},{5,9},{8,12},{9,13},{12,14},{13,15},{14,10},{15,... | collective-permute-start | bytes 1376264 | tf_op jit(solution)/shard_map/ppermute | solution.py:89
  23.9 16.2 %collective-permute-start.12 = (bf16[64,3584]{1,0:T(8,128)(2,1)}, bf16[64,3584]{1,0:T(8,128)(2,1)S(1)}, u32[]{:S(2)}, u32[]{:S(2)}) collective-permute-start(bf16[64,3584]{1,0:T(8,128)(2,1)} %collective-permute-done.7.refs_4_), channel_id=1, source_target_pairs={{0,2},{1,3},{4,0},{5,1},{8,4},{9,5},{12,8},{13,9},{14,12},{15,13},... | collective-permute-start | bytes 1376264 | tf_op jit(solution)/shard_map/ppermute | solution.py:89
  40.3 3.8 %collective-permute-start.8 = (bf16[64,3584]{1,0:T(8,128)(2,1)S(1)}, bf16[64,3584]{1,0:T(8,128)(2,1)S(1)}, u32[]{:S(2)}, u32[]{:S(2)}) collective-permute-start(bf16[64,3584]{1,0:T(8,128)(2,1)S(1)} %collective-permute-done.6.refs_2_), channel_id=1, source_target_pairs={{0,1},{1,0},{2,3},{3,2},{4,5},{5,4},{6,7},{7,6},{8,9},{9,8},{10,11... | collective-permute-start | bytes 1376264 | tf_op jit(solution)/shard_map/ppermute | solution.py:93
  40.8 4.6 %collective-permute-start.9 = (bf16[64,3584]{1,0:T(8,128)(2,1)}, bf16[64,3584]{1,0:T(8,128)(2,1)S(1)}, u32[]{:S(2)}, u32[]{:S(2)}) collective-permute-start(bf16[64,3584]{1,0:T(8,128)(2,1)} %collective-permute-done.7.refs_4_), channel_id=1, source_target_pairs={{0,1},{1,0},{2,3},{3,2},{4,5},{5,4},{6,7},{7,6},{8,9},{9,8},{10,11... | collective-permute-start | bytes 1376264 | tf_op jit(solution)/shard_map/ppermute | solution.py:93
  40.8 6.8 %collective-permute-start.13 = (bf16[64,3584]{1,0:T(8,128)(2,1)}, bf16[64,3584]{1,0:T(8,128)(2,1)S(1)}, u32[]{:S(2)}, u32[]{:S(2)}) collective-permute-start(bf16[64,3584]{1,0:T(8,128)(2,1)} %collective-permute-done.11.refs_6_), channel_id=1, source_target_pairs={{0,1},{1,0},{2,3},{3,2},{4,5},{5,4},{6,7},{7,6},{8,9},{9,8},{10,11... | collective-permute-start | bytes 1376264 | tf_op jit(solution)/shard_map/ppermute | solution.py:93
  41.3 23.5 %collective-permute-start.15 = (bf16[64,3584]{1,0:T(8,128)(2,1)}, bf16[64,3584]{1,0:T(8,128)(2,1)S(1)}, u32[]{:S(2)}, u32[]{:S(2)}) collective-permute-start(bf16[64,3584]{1,0:T(8,128)(2,1)} %collective-permute-done.11.refs_6_), channel_id=1, source_target_pairs={{0,4},{1,5},{4,8},{5,9},{8,12},{9,13},{12,14},{13,15},{14,10},{15,... | collective-permute-start | bytes 1376264 | tf_op jit(solution)/shard_map/ppermute | solution.py:89
  42.7 6.3 %collective-permute-start.14 = (bf16[128,3584]{1,0:T(8,128)(2,1)}, bf16[128,3584]{1,0:T(8,128)(2,1)}, u32[]{:S(2)}, u32[]{:S(2)}) collective-permute-start(bf16[128,3584]{1,0:T(8,128)(2,1)} %get-tuple-element.73), channel_id=1, source_target_pairs={{0,1},{1,0},{2,3},{3,2},{4,5},{5,4},{6,7},{7,6},{8,9},{9,8},{10,11... | collective-permute-start | bytes 2752520 | tf_op jit(solution)/shard_map/ppermute | solution.py:93
  44.8 20.0 %collective-permute-start.16 = (bf16[64,3584]{1,0:T(8,128)(2,1)S(1)}, bf16[64,3584]{1,0:T(8,128)(2,1)S(1)}, u32[]{:S(2)}, u32[]{:S(2)}) collective-permute-start(bf16[64,3584]{1,0:T(8,128)(2,1)S(1)} %collective-permute-done.12.refs_0_), channel_id=1, source_target_pairs={{0,2},{1,3},{4,0},{5,1},{8,4},{9,5},{12,8},{13,9},{14,12},{15,13},... | collective-permute-start | bytes 1376264 | tf_op jit(solution)/shard_map/ppermute | solution.py:89
  46.1 18.7 %collective-permute-start.18 = (bf16[64,3584]{1,0:T(8,128)(2,1)}, bf16[64,3584]{1,0:T(8,128)(2,1)}, u32[]{:S(2)}, u32[]{:S(2)}) collective-permute-start(bf16[64,3584]{1,0:T(8,128)(2,1)} %get-tuple-element.123), channel_id=1, source_target_pairs={{0,4},{1,5},{4,8},{5,9},{8,12},{9,13},{12,14},{13,15},{14,10},{15,... | collective-permute-start | bytes 1376264 | tf_op jit(solution)/shard_map/ppermute | solution.py:89
  48.4 19.1 %collective-permute-start.19 = (bf16[64,3584]{1,0:T(8,128)(2,1)}, bf16[64,3584]{1,0:T(8,128)(2,1)}, u32[]{:S(2)}, u32[]{:S(2)}) collective-permute-start(bf16[64,3584]{1,0:T(8,128)(2,1)} %get-tuple-element.122), channel_id=1, source_target_pairs={{0,2},{1,3},{4,0},{5,1},{8,4},{9,5},{12,8},{13,9},{14,12},{15,13},... | collective-permute-start | bytes 1376264 | tf_op jit(solution)/shard_map/ppermute | solution.py:89
  49.0 23.8 %collective-permute-start.22 = (bf16[64,3584]{1,0:T(8,128)(2,1)S(1)}, bf16[64,3584]{1,0:T(8,128)(2,1)S(1)}, u32[]{:S(2)}, u32[]{:S(2)}) collective-permute-start(bf16[64,3584]{1,0:T(8,128)(2,1)S(1)} %collective-permute-done.12.refs_0_), channel_id=1, source_target_pairs={{0,1},{1,0},{2,3},{3,2},{4,5},{5,4},{6,7},{7,6},{8,9},{9,8},{10,11... | collective-permute-start | bytes 1376264 | tf_op jit(solution)/shard_map/ppermute | solution.py:93
  67.6 3.8 %collective-permute-start.21 = (bf16[128,3584]{1,0:T(8,128)(2,1)S(1)}, bf16[128,3584]{1,0:T(8,128)(2,1)S(1)}, u32[]{:S(2)}, u32[]{:S(2)}) collective-permute-start(bf16[128,3584]{1,0:T(8,128)(2,1)S(1)} %get-tuple-element.89), channel_id=1, source_target_pairs={{0,1},{1,0},{2,3},{3,2},{4,5},{5,4},{6,7},{7,6},{8,9},{9,8},{10,11... | collective-permute-start | bytes 2752520 | tf_op jit(solution)/shard_map/ppermute | solution.py:93
  68.1 6.3 %collective-permute-start.23 = (bf16[64,3584]{1,0:T(8,128)(2,1)S(1)}, bf16[64,3584]{1,0:T(8,128)(2,1)S(1)}, u32[]{:S(2)}, u32[]{:S(2)}) collective-permute-start(bf16[64,3584]{1,0:T(8,128)(2,1)S(1)} %collective-permute-done.15.refs_2_), channel_id=1, source_target_pairs={{0,1},{1,0},{2,3},{3,2},{4,5},{5,4},{6,7},{7,6},{8,9},{9,8},{10,11... | collective-permute-start | bytes 1376264 | tf_op jit(solution)/shard_map/ppermute | solution.py:93
  68.1 6.3 %collective-permute-start.24 = (bf16[64,3584]{1,0:T(8,128)(2,1)S(1)}, bf16[64,3584]{1,0:T(8,128)(2,1)S(1)}, u32[]{:S(2)}, u32[]{:S(2)}) collective-permute-start(bf16[64,3584]{1,0:T(8,128)(2,1)S(1)} %collective-permute-done.16.refs_4_), channel_id=1, source_target_pairs={{0,1},{1,0},{2,3},{3,2},{4,5},{5,4},{6,7},{7,6},{8,9},{9,8},{10,11... | collective-permute-start | bytes 1376264 | tf_op jit(solution)/shard_map/ppermute | solution.py:93
  70.0 14.3 %collective-permute-start.25 = (bf16[64,3584]{1,0:T(8,128)(2,1)S(1)}, bf16[64,3584]{1,0:T(8,128)(2,1)S(1)}, u32[]{:S(2)}, u32[]{:S(2)}) collective-permute-start(bf16[64,3584]{1,0:T(8,128)(2,1)S(1)} %add_convert_fusion.5), channel_id=1, source_target_pairs={{0,2},{1,3},{4,0},{5,1},{8,4},{9,5},{12,8},{13,9},{14,12},{15,13},... | collective-permute-start | bytes 1376264 | tf_op jit(solution)/shard_map/ppermute | solution.py:89
  71.4 13.0 %collective-permute-start.26 = (bf16[64,3584]{1,0:T(8,128)(2,1)S(1)}, bf16[64,3584]{1,0:T(8,128)(2,1)S(1)}, u32[]{:S(2)}, u32[]{:S(2)}) collective-permute-start(bf16[64,3584]{1,0:T(8,128)(2,1)S(1)} %collective-permute-done.15.refs_2_), channel_id=1, source_target_pairs={{0,4},{1,5},{4,8},{5,9},{8,12},{9,13},{12,14},{13,15},{14,10},{15,... | collective-permute-start | bytes 1376264 | tf_op jit(solution)/shard_map/ppermute | solution.py:89
  72.9 24.6 %collective-permute-start.30 = (bf16[384,1024]{1,0:T(8,128)(2,1)S(1)}, bf16[384,1024]{1,0:T(8,128)(2,1)S(1)}, u32[]{:S(2)}, u32[]{:S(2)}) collective-permute-start(bf16[384,1024]{1,0:T(8,128)(2,1)S(1)} %get-tuple-element.106), channel_id=1, source_target_pairs={{0,16},{16,0},{1,17},{17,1},{2,18},{18,2},{3,19},{19,3},{4,20},{20... | collective-permute-start | bytes 2359304 | tf_op jit(solution)/shard_map/ppermute | solution.py:101
  84.6 12.9 %collective-permute-start.29 = (bf16[64,3584]{1,0:T(8,128)(2,1)S(1)}, bf16[64,3584]{1,0:T(8,128)(2,1)S(1)}, u32[]{:S(2)}, u32[]{:S(2)}) collective-permute-start(bf16[64,3584]{1,0:T(8,128)(2,1)S(1)} %add_convert_fusion.3), channel_id=1, source_target_pairs={{0,2},{1,3},{4,0},{5,1},{8,4},{9,5},{12,8},{13,9},{14,12},{15,13},... | collective-permute-start | bytes 1376264 | tf_op jit(solution)/shard_map/ppermute | solution.py:89
  85.1 3.9 %collective-permute-start.27 = (bf16[64,3584]{1,0:T(8,128)(2,1)S(1)}, bf16[64,3584]{1,0:T(8,128)(2,1)S(1)}, u32[]{:S(2)}, u32[]{:S(2)}) collective-permute-start(bf16[64,3584]{1,0:T(8,128)(2,1)S(1)} %collective-permute-done.26.refs_0_), channel_id=1, source_target_pairs={{0,1},{1,0},{2,3},{3,2},{4,5},{5,4},{6,7},{7,6},{8,9},{9,8},{10,11... | collective-permute-start | bytes 1376264 | tf_op jit(solution)/shard_map/ppermute | solution.py:93
  86.4 13.0 %collective-permute-start.28 = (bf16[64,3584]{1,0:T(8,128)(2,1)S(1)}, bf16[64,3584]{1,0:T(8,128)(2,1)S(1)}, u32[]{:S(2)}, u32[]{:S(2)}) collective-permute-start(bf16[64,3584]{1,0:T(8,128)(2,1)S(1)} %add_convert_fusion.4), channel_id=1, source_target_pairs={{0,4},{1,5},{4,8},{5,9},{8,12},{9,13},{12,14},{13,15},{14,10},{15,... | collective-permute-start | bytes 1376264 | tf_op jit(solution)/shard_map/ppermute | solution.py:89
  88.0 17.9 %collective-permute-start.31 = (bf16[288,1024]{1,0:T(8,128)(2,1)S(1)}, bf16[288,1024]{1,0:T(8,128)(2,1)S(1)}, u32[]{:S(2)}, u32[]{:S(2)}) collective-permute-start(bf16[288,1024]{1,0:T(8,128)(2,1)S(1)} %get-tuple-element.110), channel_id=1, source_target_pairs={{0,16},{16,0},{1,17},{17,1},{2,18},{18,2},{3,19},{19,3},{4,20},{20... | collective-permute-start | bytes 1769480 | tf_op jit(solution)/shard_map/ppermute | solution.py:101
  99.7 12.2 %collective-permute-start.32 = (bf16[64,3584]{1,0:T(8,128)(2,1)S(1)}, bf16[64,3584]{1,0:T(8,128)(2,1)S(1)}, u32[]{:S(2)}, u32[]{:S(2)}) collective-permute-start(bf16[64,3584]{1,0:T(8,128)(2,1)S(1)} %get-tuple-element.125), channel_id=1, source_target_pairs={{0,4},{1,5},{4,8},{5,9},{8,12},{9,13},{12,14},{13,15},{14,10},{15,... | collective-permute-start | bytes 1376264 | tf_op jit(solution)/shard_map/ppermute | solution.py:89
  101.3 11.9 %collective-permute-start.33 = (bf16[64,3584]{1,0:T(8,128)(2,1)S(1)}, bf16[64,3584]{1,0:T(8,128)(2,1)S(1)}, u32[]{:S(2)}, u32[]{:S(2)}) collective-permute-start(bf16[64,3584]{1,0:T(8,128)(2,1)S(1)} %get-tuple-element.124), channel_id=1, source_target_pairs={{0,2},{1,3},{4,0},{5,1},{8,4},{9,5},{12,8},{13,9},{14,12},{15,13},... | collective-permute-start | bytes 1376264 | tf_op jit(solution)/shard_map/ppermute | solution.py:89
  101.8 7.2 %collective-permute-start.34 = (bf16[96,1024]{1,0:T(8,128)(2,1)S(1)}, bf16[96,1024]{1,0:T(8,128)(2,1)S(1)}, u32[]{:S(2)}, u32[]{:S(2)}) collective-permute-start(bf16[96,1024]{1,0:T(8,128)(2,1)S(1)} %get-tuple-element.114), channel_id=1, source_target_pairs={{0,16},{16,0},{1,17},{17,1},{2,18},{18,2},{3,19},{19,3},{4,20},{20... | collective-permute-start | bytes 589832 | tf_op jit(solution)/shard_map/ppermute | solution.py:101
  (15 other events, 63.9 us)

commit v5 on v4

--- a/solution.py
+++ b/solution.py
@@ -502,21 +502,19 @@
         return backward(distances, cap, sides, where, pipe, values, gate_b, weights, share)
 
     got[-2], got[2] = step_ring(got[-1], 1), step_ring(got[1], -1)
-    pair[0] = core(got[0])
+    for d in (0, -1, 1):
+        pair[d] = core(got[d])
     raw2 = raw_forward(width // 2, width // 2, pin(hidden), weights)
-    raw2, pair[0] = tie(raw2, pair[0])
+    raw2, pair[0], pair[-1], pair[1] = tie(raw2, pair[0], pair[-1], pair[1])
 
     keep1, other1, other2 = spread((3, -4, 2, -3), 2, gate_a)
     keep1, other1, other2, got[-2], got[2] = tie(keep1, other1, other2, got[-2], got[2])
     got[-3], got[3] = step_ring(got[-2], 1), step_ring(got[2], -1)
     other1, other2 = core(other1), core(other2)
-    for d in (-1, 1, -2):
-        pair[d] = core(got[d])
     up = step_ring(add(keep1[:tokens], other1[:tokens]), 1)
     down = step_ring(add(keep1[tokens : 2 * tokens], other1[tokens:]), -1)
-    gate_a, pair[-1], pair[1], pair[-2], other2 = tie(
-        gate_a, pair[-1], pair[1], pair[-2], other2
-    )
+    pair[-2] = core(got[-2])
+    gate_a, pair[-2], other2 = tie(gate_a, pair[-2], other2)
     keep2, other3, other4 = spread((1, -2, -1, 0), 2, gate_a)
     keep2, gate_b = tie(keep2, gate_b)
     groups = (0, -1, 1, -2), (2, -3, 3), (-4,)
@@ -531,7 +529,10 @@
         send1, got[-3], got[3], up, down, other3, other4
     )
     got[-4] = step_ring(got[-3], 1)
-    down = step_ring(add(keep1[3 * tokens :], other2[tokens:], down), -1)
+    up = add(keep1[2 * tokens : 3 * tokens], other2[:tokens], up)
+    down = add(keep1[3 * tokens :], other2[tokens:], down)
+    up, down = tie(up, down)
+    down = step_ring(down, -1)
     recv1 = across(send1)
     pair[2], pair[-3], pair[3] = core(got[2]), core(got[-3]), core(got[3])
     other3, other4 = core(other3), core(other4)
@@ -539,8 +540,7 @@
     send2, hold2 = bwd(groups[1], share=64)
 
     hold2, send2, up, down, got[-4] = tie(hold2, send2, up, down, got[-4])
-    up = step_ring(add(keep1[2 * tokens : 3 * tokens], other2[:tokens], up), 1)
-    down = step_ring(mine(1, other3, down), -1)
+    up, down = step_ring(up, 1), step_ring(mine(1, other3, down), -1)
     pair[-4] = core(got[-4])
     recv2 = across(send2)
     send3, hold3 = bwd(groups[2], share=64)
@@ -550,7 +550,7 @@
     recv3 = across(send3)
     hold3, recv2 = tie(hold3, recv2)
     grad = collect(groups[:2], where, (hold1, recv1, hold2, recv2), 8 * rows)
-    grad, up, down, recv3 = tie(grad, up, down, recv3)
+    grad, recv3 = tie(grad, recv3)
     mixed_a = mine(3, other4, up, down)
     grad = collect(groups[2:], where, (hold3, recv3), 8 * rows, grad)
     return (mixed_a, grad[None])

time: 116 us -> 113 us (0.974)
  waiting for transfers between devices: 16.4 us -> 12.6 us
    ppermute x14, waiting for transfers between devices: 8.88 us -> 5 us  [step_ring(): return lax.ppermute(value, 'expert', pairs)]
    ppermute x3, waiting for transfers between devices: 4.39 us -> 6.04 us  [across(): return lax.ppermute(value, 'pipe', [(0, 1), (1, 0)])]
    ppermute x18, waiting for transfers between devices: 3.16 us -> 1.52 us  [xor(): return lax.ppermute(value, 'expert', [(i, i ^ bits) for i in range(16)])]
    ppermute x14, starting transfers between devices: 13.6 us -> 15.2 us  [step_ring(): return lax.ppermute(value, 'expert', pairs)]
    convert_element_type x6 -> x5, other arithmetic: 5.35 us -> 4.42 us  [add(): return total.astype(BF16)]
    unnamed x24 -> x28, local copies, waits for them, and re-layouts: 2.39 us -> 3.14 us
  transfers between devices with their start and end apart: 35 -> 35, of which waited for: 10 -> 8; matrix products, arithmetic and copies ran while one was open for 4% -> 3% of each run, Pallas kernels for 52% -> 55%
where the time goes in v5:
time: 113 us
  Pallas kernels  63 us (56%)
  starting transfers between devices  28.4 us (25%)
  waiting for transfers between devices  12.6 us (11%)
  other arithmetic  4.54 us (4%)
  local copies, waits for them, and re-layouts  3.45 us (3%)
    pallas_call x6, Pallas kernels, kernel_call(): pl.pallas_call(kernel, in_specs=in_specs, out_specs=[VMEM] * len(out_shap...  39.5 us
    pallas_call x2, Pallas kernels, raw_forward(): pl.pallas_call(functools.partial(raw_kernel, first), in_specs=[HBM, HBM],...  20.5 us
    ppermute x14, starting transfers between devices, step_ring(): return lax.ppermute(value, 'expert', pairs)  15.2 us
    ppermute x18, starting transfers between devices, xor(): return lax.ppermute(value, 'expert', [(i, i ^ bits) for i in range(16)])  10 us
    ppermute x3, waiting for transfers between devices, across(): return lax.ppermute(value, 'pipe', [(0, 1), (1, 0)])  6.04 us
    ppermute x14, waiting for transfers between devices, step_ring(): return lax.ppermute(value, 'expert', pairs)  5 us
    convert_element_type x5, other arithmetic, add(): return total.astype(BF16)  4.42 us
    ppermute x3, starting transfers between devices, across(): return lax.ppermute(value, 'pipe', [(0, 1), (1, 0)])  3.21 us
  transfers between devices with their start and end apart: 35, of which 8 were waited for; matrix products, arithmetic and copies ran while one was open for 3% of the time, Pallas kernels for 55%

profile of v5, /device:TPU:0, one launch (start us, length us, event | category | flops | bytes accessed | tf_op | source)
XLA Modules:
  0.0 113.0 jit_solution(16321416833759299146)
XLA Ops:
  1.5 2.5 %collective-permute-start.2 = (f32[16,128]{1,0:T(8,128)S(1)}, f32[16,128]{1,0:T(8,128)S(1)}, u32[]{:S(2)}, u32[]{:S(2)}) collective-permute-start(f32[16,128]{1,0:T(8,128)S(1)} %gates.1), channel_id=1, source_target_pairs={{0,3},{1,2},{2,1},{3,0},{4,7},{5,6},{6,5},{7,4},{8,11},{9,10},{10,... | collective-permute-start | bytes 24584 | tf_op jit(solution)/shard_map/ppermute | solution.py:93
  4.7 2.0 %collective-permute-start.6 = (bf16[64,3584]{1,0:T(8,128)(2,1)}, bf16[64,3584]{1,0:T(8,128)(2,1)S(1)}, u32[]{:S(2)}, u32[]{:S(2)}) collective-permute-start(bf16[64,3584]{1,0:T(8,128)(2,1)} %refs_0_.1), channel_id=1, source_target_pairs={{0,4},{1,5},{4,8},{5,9},{8,12},{9,13},{12,14},{13,15},{14,10},{15,... | collective-permute-start | bytes 1376264 | tf_op jit(solution)/shard_map/ppermute | solution.py:89
  6.8 1.5 %collective-permute-done.1 = f32[16,128]{1,0:T(8,128)S(1)} collective-permute-done((f32[16,128]{1,0:T(8,128)S(1)}, f32[16,128]{1,0:T(8,128)S(1)}, u32[]{:S(2)}, u32[]{:S(2)}) %collective-permute-start.1) | collective-permute-done | bytes 8224 | tf_op jit(solution)/shard_map/ppermute | solution.py:93
  8.3 1.6 %collective-permute-start.3 = (f32[4,4,128]{2,0,1:T(4,128)S(1)}, f32[4,4,128]{2,0,1:T(4,128)S(1)}, u32[]{:S(2)}, u32[]{:S(2)}) collective-permute-start(f32[4,4,128]{2,0,1:T(4,128)S(1)} %bitcast.37), channel_id=1, source_target_pairs={{0,4},{1,5},{2,6},{3,7},{4,0},{5,1},{6,2},{7,3},{8,12},{9,13},{10,... | collective-permute-start | bytes 24584 | tf_op jit(solution)/shard_map/ppermute | solution.py:93
  10.0 2.6 %collective-permute-start.4 = (f32[4,4,128]{2,0,1:T(4,128)S(1)}, f32[4,4,128]{2,0,1:T(4,128)S(1)}, u32[]{:S(2)}, u32[]{:S(2)}) collective-permute-start(f32[4,4,128]{2,0,1:T(4,128)S(1)} %bitcast.38), channel_id=1, source_target_pairs={{0,8},{1,9},{2,10},{3,11},{4,12},{5,13},{6,14},{7,15},{8,0},{9,1},... | collective-permute-start | bytes 24584 | tf_op jit(solution)/shard_map/ppermute | solution.py:93
  12.8 10.3 %raw_forward.2.refs_0_ = bf16[768,1792]{1,0:T(8,128)(2,1)} custom-call(bf16[768,2048]{1,0:T(8,128)(2,1)} %bitcast.51, bf16[2048,3584]{1,0:T(8,128)(2,1)} %bitcast.30), custom_call_target="tpu_custom_call" | custom-call | flops 5637144576 | bytes 13238272 | tf_op jit(solution)/shard_map/raw_forward/pallas_call | solution.py:263
  24.5 1.4 %collective-permute-start.12 = (bf16[64,3584]{1,0:T(8,128)(2,1)S(1)}, bf16[64,3584]{1,0:T(8,128)(2,1)S(1)}, u32[]{:S(2)}, u32[]{:S(2)}) collective-permute-start(bf16[64,3584]{1,0:T(8,128)(2,1)S(1)} %collective-permute-done.7.refs_4_), channel_id=1, source_target_pairs={{0,2},{1,3},{4,0},{5,1},{8,4},{9,5},{12,8},{13,9},{14,12},{15,13},... | collective-permute-start | bytes 1376264 | tf_op jit(solution)/shard_map/ppermute | solution.py:89
  26.1 10.2 %raw_forward.3.refs_1_ = bf16[768,1792]{1,0:T(8,128)(2,1)} custom-call(bf16[768,2048]{1,0:T(8,128)(2,1)} %bitcast.52, bf16[2048,3584]{1,0:T(8,128)(2,1)} %bitcast.31), custom_call_target="tpu_custom_call" | custom-call | flops 5637144576 | bytes 13238272 | tf_op jit(solution)/shard_map/raw_forward/pallas_call | solution.py:263
  38.7 4.4 %spread_tokens.2 = (bf16[256,3584]{1,0:T(8,128)(2,1)S(1)}, bf16[128,3584]{1,0:T(8,128)(2,1)S(1)}, bf16[128,3584]{1,0:T(8,128)(2,1)}) custom-call(s32[17]{0:T(128)S(1)} %pad_add_fusion.where, f32[8,128]{1,0:T(8,128)S(1)} %squeeze.20.gates, bf16[768,1792]{1,0:T(8,128)(2,1)} %raw_forward.2.refs_0_, bf16[768,1792]{1,0:T(8,128)(2,1)} %raw_forward.3.refs_1_), custom_call_target="tpu_custom_call" | custom-call | flops 1048576 | bytes 16384 | tf_op jit(solution)/shard_map/spread_tokens/pallas_call | solution.py:120
  44.3 1.4 %collective-permute-start.16 = (bf16[64,3584]{1,0:T(8,128)(2,1)S(1)}, bf16[64,3584]{1,0:T(8,128)(2,1)S(1)}, u32[]{:S(2)}, u32[]{:S(2)}) collective-permute-start(bf16[64,3584]{1,0:T(8,128)(2,1)S(1)} %collective-permute-done.12.refs_0_), channel_id=1, source_target_pairs={{0,2},{1,3},{4,0},{5,1},{8,4},{9,5},{12,8},{13,9},{14,12},{15,13},... | collective-permute-start | bytes 1376264 | tf_op jit(solution)/shard_map/ppermute | solution.py:89
  45.7 1.2 %add_convert_fusion.6 = (bf16[64,3584]{1,0:T(8,128)(2,1)}, bf16[64,3584]{1,0:T(8,128)(2,1)}) fusion(bf16[128,3584]{1,0:T(8,128)(2,1)S(1)} %collective-permute-done.17, bf16[256,3584]{1,0:T(8,128)(2,1)S(1)} %get-tuple-element.84), kind=kLoop, calls=%fused_computation.6 | loop fusion | flops 1835008 | bytes 2752512 | tf_op jit(solution)/shard_map/convert_element_type | solution.py:32
  46.8 0.9 collective-permute-start.18
  48.5 1.1 collective-permute-start.19
  49.9 3.6 %spread_tokens.3 = (bf16[256,3584]{1,0:T(8,128)(2,1)S(1)}, bf16[128,3584]{1,0:T(8,128)(2,1)S(1)}, bf16[128,3584]{1,0:T(8,128)(2,1)S(1)}) custom-call(s32[17]{0:T(128)S(1)} %pad_add_fusion.where, f32[8,128]{1,0:T(8,128)S(1)} %squeeze.20.gates, bf16[768,1792]{1,0:T(8,128)(2,1)} %raw_forward.2.refs_0_, bf16[768,1792]{1,0:T(8,128)(2,1)} %raw_forward.3.refs_1_), custom_call_target="tpu_custom_call" | custom-call | flops 1048576 | bytes 16384 | tf_op jit(solution)/shard_map/spread_tokens/pallas_call | solution.py:120
  53.5 12.3 %backward.3 = (bf16[384,1024]{1,0:T(8,128)(2,1)S(1)}, bf16[384,1024]{1,0:T(8,128)(2,1)S(1)}) custom-call(s32[17]{0:T(128)S(1)} %pad_add_fusion.where, s32[1]{0:T(128)} %bitcast.20.pipe, f32[8,128]{1,0:T(8,128)S(1)} %squeeze.21.gates, bf16[2048,3584]{1,0:T(8,128)(2,1)} %bitcast.32, bf16[64,3584]{1,0:T(8,128)(2,1)S(1)} %copy-done.1, ...), custom_call_target="tpu_custom_call" | custom-call | flops 88080384 | bytes 339968 | tf_op jit(solution)/shard_map/backward/pallas_call | solution.py:120
  66.5 1.1 collective-permute-done.19
  68.6 1.8 %add_convert_fusion.4 = (bf16[64,3584]{1,0:T(8,128)(2,1)S(1)}, bf16[64,3584]{1,0:T(8,128)(2,1)S(1)}) fusion(bf16[64,3584]{1,0:T(8,128)(2,1)} %collective-permute-done.19, bf16[128,3584]{1,0:T(8,128)(2,1)} %collective-permute-done.14, bf16[256,3584]{1,0:T(8,128)(2,1)S(1)} %get-tuple-element.84, bf16[64,3584]{1,0:T(8,128)(2,1)} %collective-permute-done.18), kind=kLoop, calls=%fused_computation.4 | loop fusion | flops 2752512 | bytes 3670016 | tf_op jit(solution)/shard_map/convert_element_type | solution.py:32
  70.3 1.1 collective-permute-start.25
  71.4 1.9 %collective-permute-start.26 = (bf16[64,3584]{1,0:T(8,128)(2,1)S(1)}, bf16[64,3584]{1,0:T(8,128)(2,1)S(1)}, u32[]{:S(2)}, u32[]{:S(2)}) collective-permute-start(bf16[64,3584]{1,0:T(8,128)(2,1)S(1)} %collective-permute-done.15.refs_2_), channel_id=1, source_target_pairs={{0,4},{1,5},{4,8},{5,9},{8,12},{9,13},{12,14},{13,15},{14,10},{15,... | collective-permute-start | bytes 1376264 | tf_op jit(solution)/shard_map/ppermute | solution.py:89
  73.3 1.5 %collective-permute-start.30 = (bf16[384,1024]{1,0:T(8,128)(2,1)S(1)}, bf16[384,1024]{1,0:T(8,128)(2,1)S(1)}, u32[]{:S(2)}, u32[]{:S(2)}) collective-permute-start(bf16[384,1024]{1,0:T(8,128)(2,1)S(1)} %get-tuple-element.107), channel_id=1, source_target_pairs={{0,16},{16,0},{1,17},{17,1},{2,18},{18,2},{3,19},{19,3},{4,20},{20... | collective-permute-start | bytes 2359304 | tf_op jit(solution)/shard_map/ppermute | solution.py:101
  74.8 10.0 %backward.4 = (bf16[288,1024]{1,0:T(8,128)(2,1)S(1)}, bf16[288,1024]{1,0:T(8,128)(2,1)S(1)}) custom-call(s32[17]{0:T(128)S(1)} %pad_add_fusion.where, s32[1]{0:T(128)} %bitcast.20.pipe, f32[8,128]{1,0:T(8,128)S(1)} %squeeze.21.gates, bf16[2048,3584]{1,0:T(8,128)(2,1)} %bitcast.33, bf16[64,3584]{1,0:T(8,128)(2,1)S(1)} %collective-permute-done.12.refs_0_, ...), custom_call_target="tpu_custom_call" | custom-call | flops 66060288 | bytes 312320 | tf_op jit(solution)/shard_map/backward/pallas_call | solution.py:120
  85.2 1.9 %collective-permute-start.28 = (bf16[64,3584]{1,0:T(8,128)(2,1)S(1)}, bf16[64,3584]{1,0:T(8,128)(2,1)S(1)}, u32[]{:S(2)}, u32[]{:S(2)}) collective-permute-start(bf16[64,3584]{1,0:T(8,128)(2,1)S(1)} %get-tuple-element.105), channel_id=1, source_target_pairs={{0,4},{1,5},{4,8},{5,9},{8,12},{9,13},{12,14},{13,15},{14,10},{15,... | collective-permute-start | bytes 1376264 | tf_op jit(solution)/shard_map/ppermute | solution.py:89
  87.7 8.4 %backward.5 = (bf16[96,1024]{1,0:T(8,128)(2,1)S(1)}, bf16[96,1024]{1,0:T(8,128)(2,1)S(1)}) custom-call(s32[17]{0:T(128)S(1)} %pad_add_fusion.where, s32[1]{0:T(128)} %bitcast.20.pipe, f32[8,128]{1,0:T(8,128)S(1)} %squeeze.21.gates, bf16[2048,3584]{1,0:T(8,128)(2,1)} %bitcast.34, bf16[64,3584]{1,0:T(8,128)(2,1)S(1)} %collective-permute-done.26.refs_0_, ...), custom_call_target="tpu_custom_call" | custom-call | flops 22020096 | bytes 257024 | tf_op jit(solution)/shard_map/backward/pallas_call | solution.py:120
  96.1 1.9 %collective-permute-done.29 = bf16[64,3584]{1,0:T(8,128)(2,1)S(1)} collective-permute-done((bf16[64,3584]{1,0:T(8,128)(2,1)S(1)}, bf16[64,3584]{1,0:T(8,128)(2,1)S(1)}, u32[]{:S(2)}, u32[]{:S(2)}) %collective-permute-start.29) | collective-permute-done | bytes 458784 | tf_op jit(solution)/shard_map/ppermute | solution.py:89
  98.4 1.8 %collective-permute-start.31 = (bf16[64,3584]{1,0:T(8,128)(2,1)S(1)}, bf16[64,3584]{1,0:T(8,128)(2,1)S(1)}, u32[]{:S(2)}, u32[]{:S(2)}) collective-permute-start(bf16[64,3584]{1,0:T(8,128)(2,1)S(1)} %get-tuple-element.126), channel_id=1, source_target_pairs={{0,4},{1,5},{4,8},{5,9},{8,12},{9,13},{12,14},{13,15},{14,10},{15,... | collective-permute-start | bytes 1376264 | tf_op jit(solution)/shard_map/ppermute | solution.py:89
  100.5 1.2 %collective-permute-start.34 = (bf16[96,1024]{1,0:T(8,128)(2,1)S(1)}, bf16[96,1024]{1,0:T(8,128)(2,1)S(1)}, u32[]{:S(2)}, u32[]{:S(2)}) collective-permute-start(bf16[96,1024]{1,0:T(8,128)(2,1)S(1)} %get-tuple-element.117), channel_id=1, source_target_pairs={{0,16},{16,0},{1,17},{17,1},{2,18},{18,2},{3,19},{19,3},{4,20},{20... | collective-permute-start | bytes 589832 | tf_op jit(solution)/shard_map/ppermute | solution.py:101
  101.7 4.7 %collective-permute-done.33.refs_3_ = bf16[288,1024]{1,0:T(8,128)(2,1)S(1)} collective-permute-done((bf16[288,1024]{1,0:T(8,128)(2,1)S(1)}, bf16[288,1024]{1,0:T(8,128)(2,1)S(1)}, u32[]{:S(2)}, u32[]{:S(2)}) %collective-permute-start.33) | collective-permute-done | bytes 589856 | tf_op jit(solution)/shard_map/ppermute | solution.py:101
  106.4 1.7 %collect.2.refs_2_ = bf16[768,1024]{1,0:T(8,128)(2,1)} custom-call(s32[17]{0:T(128)S(1)} %pad_add_fusion.where, bf16[384,1024]{1,0:T(8,128)(2,1)S(1)} %get-tuple-element.113.refs_0_, bf16[384,1024]{1,0:T(8,128)(2,1)S(1)} %collective-permute-done.30.refs_1_, bf16[288,1024]{1,0:T(8,128)(2,1)S(1)} %get-tuple-element.115.refs_2_, ...), custom_call_target="tpu_custom_call" | custom-call | flops 1048576 | bytes 4128768 | tf_op jit(solution)/shard_map/collect/pallas_call | solution.py:450
  108.1 1.4 %collective-permute-done.34.refs_1_ = bf16[96,1024]{1,0:T(8,128)(2,1)S(1)} collective-permute-done((bf16[96,1024]{1,0:T(8,128)(2,1)S(1)}, bf16[96,1024]{1,0:T(8,128)(2,1)S(1)}, u32[]{:S(2)}, u32[]{:S(2)}) %collective-permute-start.34) | collective-permute-done | bytes 196640 | tf_op jit(solution)/shard_map/ppermute | solution.py:101
  109.4 1.3 %collect.3 = bf16[768,1024]{1,0:T(8,128)(2,1)} custom-call(s32[17]{0:T(128)S(1)} %pad_add_fusion.where, bf16[96,1024]{1,0:T(8,128)(2,1)S(1)} %get-tuple-element.112.refs_0_, bf16[96,1024]{1,0:T(8,128)(2,1)S(1)} %collective-permute-done.34.refs_1_, bf16[768,1024]{1,0:T(8,128)(2,1)} %collect.2.refs_2_), custom_call_target="tpu_custom_call", output_to_operand_aliasing={{}: (3, {})} | custom-call | flops 1048576 | bytes 589824 | tf_op jit(solution)/shard_map/collect/pallas_call | solution.py:450
  110.7 1.3 %collective-permute-done.32 = bf16[64,3584]{1,0:T(8,128)(2,1)S(1)} collective-permute-done((bf16[64,3584]{1,0:T(8,128)(2,1)S(1)}, bf16[64,3584]{1,0:T(8,128)(2,1)S(1)}, u32[]{:S(2)}, u32[]{:S(2)}) %collective-permute-start.32) | collective-permute-done | bytes 458784 | tf_op jit(solution)/shard_map/ppermute | solution.py:89
  112.0 1.0 add_convert_fusion
  (91 shorter events, 11.4 us)
Async XLA Ops:
  1.5 5.3 %collective-permute-start.2 = (f32[16,128]{1,0:T(8,128)S(1)}, f32[16,128]{1,0:T(8,128)S(1)}, u32[]{:S(2)}, u32[]{:S(2)}) collective-permute-start(f32[16,128]{1,0:T(8,128)S(1)} %gates.1), channel_id=1, source_target_pairs={{0,3},{1,2},{2,1},{3,0},{4,7},{5,6},{6,5},{7,4},{8,11},{9,10},{10,... | collective-permute-start | bytes 24584 | tf_op jit(solution)/shard_map/ppermute | solution.py:93
  4.6 3.7 %collective-permute-start.1 = (f32[16,128]{1,0:T(8,128)S(1)}, f32[16,128]{1,0:T(8,128)S(1)}, u32[]{:S(2)}, u32[]{:S(2)}) collective-permute-start(f32[16,128]{1,0:T(8,128)S(1)} %gates.1), channel_id=1, source_target_pairs={{0,2},{1,3},{2,0},{3,1},{4,6},{5,7},{6,4},{7,5},{8,10},{9,11},{10,... | collective-permute-start | bytes 24584 | tf_op jit(solution)/shard_map/ppermute | solution.py:93
  4.7 18.6 %collective-permute-start.6 = (bf16[64,3584]{1,0:T(8,128)(2,1)}, bf16[64,3584]{1,0:T(8,128)(2,1)S(1)}, u32[]{:S(2)}, u32[]{:S(2)}) collective-permute-start(bf16[64,3584]{1,0:T(8,128)(2,1)} %refs_0_.1), channel_id=1, source_target_pairs={{0,4},{1,5},{4,8},{5,9},{8,12},{9,13},{12,14},{13,15},{14,10},{15,... | collective-permute-start | bytes 1376264 | tf_op jit(solution)/shard_map/ppermute | solution.py:89
  6.7 16.5 %collective-permute-start.7 = (bf16[64,3584]{1,0:T(8,128)(2,1)}, bf16[64,3584]{1,0:T(8,128)(2,1)S(1)}, u32[]{:S(2)}, u32[]{:S(2)}) collective-permute-start(bf16[64,3584]{1,0:T(8,128)(2,1)} %refs_0_.1), channel_id=1, source_target_pairs={{0,2},{1,3},{4,0},{5,1},{8,4},{9,5},{12,8},{13,9},{14,12},{15,13},... | collective-permute-start | bytes 1376264 | tf_op jit(solution)/shard_map/ppermute | solution.py:89
  8.3 14.8 %collective-permute-start.3 = (f32[4,4,128]{2,0,1:T(4,128)S(1)}, f32[4,4,128]{2,0,1:T(4,128)S(1)}, u32[]{:S(2)}, u32[]{:S(2)}) collective-permute-start(f32[4,4,128]{2,0,1:T(4,128)S(1)} %bitcast.37), channel_id=1, source_target_pairs={{0,4},{1,5},{2,6},{3,7},{4,0},{5,1},{6,2},{7,3},{8,12},{9,13},{10,... | collective-permute-start | bytes 24584 | tf_op jit(solution)/shard_map/ppermute | solution.py:93
  10.0 13.2 %collective-permute-start.4 = (f32[4,4,128]{2,0,1:T(4,128)S(1)}, f32[4,4,128]{2,0,1:T(4,128)S(1)}, u32[]{:S(2)}, u32[]{:S(2)}) collective-permute-start(f32[4,4,128]{2,0,1:T(4,128)S(1)} %bitcast.38), channel_id=1, source_target_pairs={{0,8},{1,9},{2,10},{3,11},{4,12},{5,13},{6,14},{7,15},{8,0},{9,1},... | collective-permute-start | bytes 24584 | tf_op jit(solution)/shard_map/ppermute | solution.py:93
  12.6 10.7 %collective-permute-start.5 = (f32[4,4,128]{2,0,1:T(4,128)S(1)}, f32[4,4,128]{2,0,1:T(4,128)S(1)}, u32[]{:S(2)}, u32[]{:S(2)}) collective-permute-start(f32[4,4,128]{2,0,1:T(4,128)S(1)} %bitcast.39), channel_id=1, source_target_pairs={{0,12},{1,13},{2,14},{3,15},{4,8},{5,9},{6,10},{7,11},{8,4},{9,5},... | collective-permute-start | bytes 24584 | tf_op jit(solution)/shard_map/ppermute | solution.py:93
  23.1 13.2 %collective-permute-start.8 = (bf16[64,3584]{1,0:T(8,128)(2,1)S(1)}, bf16[64,3584]{1,0:T(8,128)(2,1)S(1)}, u32[]{:S(2)}, u32[]{:S(2)}) collective-permute-start(bf16[64,3584]{1,0:T(8,128)(2,1)S(1)} %copy-done), channel_id=1, source_target_pairs={{0,1},{1,0},{2,3},{3,2},{4,5},{5,4},{6,7},{7,6},{8,9},{9,8},{10,11... | collective-permute-start | bytes 1376264 | tf_op jit(solution)/shard_map/ppermute | solution.py:93
  23.3 14.6 %collective-permute-start.9 = (bf16[64,3584]{1,0:T(8,128)(2,1)S(1)}, bf16[64,3584]{1,0:T(8,128)(2,1)S(1)}, u32[]{:S(2)}, u32[]{:S(2)}) collective-permute-start(bf16[64,3584]{1,0:T(8,128)(2,1)S(1)} %collective-permute-done.6.refs_2_), channel_id=1, source_target_pairs={{0,1},{1,0},{2,3},{3,2},{4,5},{5,4},{6,7},{7,6},{8,9},{9,8},{10,11... | collective-permute-start | bytes 1376264 | tf_op jit(solution)/shard_map/ppermute | solution.py:93
  23.8 19.3 %collective-permute-start.11 = (bf16[64,3584]{1,0:T(8,128)(2,1)S(1)}, bf16[64,3584]{1,0:T(8,128)(2,1)}, u32[]{:S(2)}, u32[]{:S(2)}) collective-permute-start(bf16[64,3584]{1,0:T(8,128)(2,1)S(1)} %collective-permute-done.6.refs_2_), channel_id=1, source_target_pairs={{0,4},{1,5},{4,8},{5,9},{8,12},{9,13},{12,14},{13,15},{14,10},{15,... | collective-permute-start | bytes 1376264 | tf_op jit(solution)/shard_map/ppermute | solution.py:89
  24.5 12.7 %collective-permute-start.10 = (bf16[64,3584]{1,0:T(8,128)(2,1)S(1)}, bf16[64,3584]{1,0:T(8,128)(2,1)S(1)}, u32[]{:S(2)}, u32[]{:S(2)}) collective-permute-start(bf16[64,3584]{1,0:T(8,128)(2,1)S(1)} %collective-permute-done.7.refs_4_), channel_id=1, source_target_pairs={{0,1},{1,0},{2,3},{3,2},{4,5},{5,4},{6,7},{7,6},{8,9},{9,8},{10,11... | collective-permute-start | bytes 1376264 | tf_op jit(solution)/shard_map/ppermute | solution.py:93
  24.5 18.6 %collective-permute-start.12 = (bf16[64,3584]{1,0:T(8,128)(2,1)S(1)}, bf16[64,3584]{1,0:T(8,128)(2,1)S(1)}, u32[]{:S(2)}, u32[]{:S(2)}) collective-permute-start(bf16[64,3584]{1,0:T(8,128)(2,1)S(1)} %collective-permute-done.7.refs_4_), channel_id=1, source_target_pairs={{0,2},{1,3},{4,0},{5,1},{8,4},{9,5},{12,8},{13,9},{14,12},{15,13},... | collective-permute-start | bytes 1376264 | tf_op jit(solution)/shard_map/ppermute | solution.py:89
  43.4 4.4 %collective-permute-start.13 = (bf16[64,3584]{1,0:T(8,128)(2,1)}, bf16[64,3584]{1,0:T(8,128)(2,1)S(1)}, u32[]{:S(2)}, u32[]{:S(2)}) collective-permute-start(bf16[64,3584]{1,0:T(8,128)(2,1)} %collective-permute-done.11.refs_6_), channel_id=1, source_target_pairs={{0,1},{1,0},{2,3},{3,2},{4,5},{5,4},{6,7},{7,6},{8,9},{9,8},{10,11... | collective-permute-start | bytes 1376264 | tf_op jit(solution)/shard_map/ppermute | solution.py:93
  43.7 22.2 %collective-permute-start.15 = (bf16[64,3584]{1,0:T(8,128)(2,1)}, bf16[64,3584]{1,0:T(8,128)(2,1)S(1)}, u32[]{:S(2)}, u32[]{:S(2)}) collective-permute-start(bf16[64,3584]{1,0:T(8,128)(2,1)} %collective-permute-done.11.refs_6_), channel_id=1, source_target_pairs={{0,4},{1,5},{4,8},{5,9},{8,12},{9,13},{12,14},{13,15},{14,10},{15,... | collective-permute-start | bytes 1376264 | tf_op jit(solution)/shard_map/ppermute | solution.py:89
  44.3 5.4 %collective-permute-start.14 = (bf16[128,3584]{1,0:T(8,128)(2,1)}, bf16[128,3584]{1,0:T(8,128)(2,1)}, u32[]{:S(2)}, u32[]{:S(2)}) collective-permute-start(bf16[128,3584]{1,0:T(8,128)(2,1)} %get-tuple-element.73), channel_id=1, source_target_pairs={{0,1},{1,0},{2,3},{3,2},{4,5},{5,4},{6,7},{7,6},{8,9},{9,8},{10,11... | collective-permute-start | bytes 2752520 | tf_op jit(solution)/shard_map/ppermute | solution.py:93
  44.3 21.5 %collective-permute-start.16 = (bf16[64,3584]{1,0:T(8,128)(2,1)S(1)}, bf16[64,3584]{1,0:T(8,128)(2,1)S(1)}, u32[]{:S(2)}, u32[]{:S(2)}) collective-permute-start(bf16[64,3584]{1,0:T(8,128)(2,1)S(1)} %collective-permute-done.12.refs_0_), channel_id=1, source_target_pairs={{0,2},{1,3},{4,0},{5,1},{8,4},{9,5},{12,8},{13,9},{14,12},{15,13},... | collective-permute-start | bytes 1376264 | tf_op jit(solution)/shard_map/ppermute | solution.py:89
  46.8 19.6 %collective-permute-start.18 = (bf16[64,3584]{1,0:T(8,128)(2,1)}, bf16[64,3584]{1,0:T(8,128)(2,1)}, u32[]{:S(2)}, u32[]{:S(2)}) collective-permute-start(bf16[64,3584]{1,0:T(8,128)(2,1)} %get-tuple-element.125), channel_id=1, source_target_pairs={{0,4},{1,5},{4,8},{5,9},{8,12},{9,13},{12,14},{13,15},{14,10},{15,... | collective-permute-start | bytes 1376264 | tf_op jit(solution)/shard_map/ppermute | solution.py:89
  48.5 19.0 %collective-permute-start.19 = (bf16[64,3584]{1,0:T(8,128)(2,1)}, bf16[64,3584]{1,0:T(8,128)(2,1)}, u32[]{:S(2)}, u32[]{:S(2)}) collective-permute-start(bf16[64,3584]{1,0:T(8,128)(2,1)} %get-tuple-element.124), channel_id=1, source_target_pairs={{0,2},{1,3},{4,0},{5,1},{8,4},{9,5},{12,8},{13,9},{14,12},{15,13},... | collective-permute-start | bytes 1376264 | tf_op jit(solution)/shard_map/ppermute | solution.py:89
  49.8 23.5 %collective-permute-start.22 = (bf16[64,3584]{1,0:T(8,128)(2,1)S(1)}, bf16[64,3584]{1,0:T(8,128)(2,1)S(1)}, u32[]{:S(2)}, u32[]{:S(2)}) collective-permute-start(bf16[64,3584]{1,0:T(8,128)(2,1)S(1)} %collective-permute-done.12.refs_0_), channel_id=1, source_target_pairs={{0,1},{1,0},{2,3},{3,2},{4,5},{5,4},{6,7},{7,6},{8,9},{9,8},{10,11... | collective-permute-start | bytes 1376264 | tf_op jit(solution)/shard_map/ppermute | solution.py:93
  67.6 3.9 %collective-permute-start.21 = (bf16[128,3584]{1,0:T(8,128)(2,1)S(1)}, bf16[128,3584]{1,0:T(8,128)(2,1)S(1)}, u32[]{:S(2)}, u32[]{:S(2)}) collective-permute-start(bf16[128,3584]{1,0:T(8,128)(2,1)S(1)} %get-tuple-element.89), channel_id=1, source_target_pairs={{0,1},{1,0},{2,3},{3,2},{4,5},{5,4},{6,7},{7,6},{8,9},{9,8},{10,11... | collective-permute-start | bytes 2752520 | tf_op jit(solution)/shard_map/ppermute | solution.py:93
  68.1 6.7 %collective-permute-start.23 = (bf16[64,3584]{1,0:T(8,128)(2,1)S(1)}, bf16[64,3584]{1,0:T(8,128)(2,1)S(1)}, u32[]{:S(2)}, u32[]{:S(2)}) collective-permute-start(bf16[64,3584]{1,0:T(8,128)(2,1)S(1)} %collective-permute-done.15.refs_2_), channel_id=1, source_target_pairs={{0,1},{1,0},{2,3},{3,2},{4,5},{5,4},{6,7},{7,6},{8,9},{9,8},{10,11... | collective-permute-start | bytes 1376264 | tf_op jit(solution)/shard_map/ppermute | solution.py:93
  68.1 6.7 %collective-permute-start.24 = (bf16[64,3584]{1,0:T(8,128)(2,1)S(1)}, bf16[64,3584]{1,0:T(8,128)(2,1)S(1)}, u32[]{:S(2)}, u32[]{:S(2)}) collective-permute-start(bf16[64,3584]{1,0:T(8,128)(2,1)S(1)} %collective-permute-done.16.refs_4_), channel_id=1, source_target_pairs={{0,1},{1,0},{2,3},{3,2},{4,5},{5,4},{6,7},{7,6},{8,9},{9,8},{10,11... | collective-permute-start | bytes 1376264 | tf_op jit(solution)/shard_map/ppermute | solution.py:93
  70.3 14.4 %collective-permute-start.25 = (bf16[64,3584]{1,0:T(8,128)(2,1)S(1)}, bf16[64,3584]{1,0:T(8,128)(2,1)S(1)}, u32[]{:S(2)}, u32[]{:S(2)}) collective-permute-start(bf16[64,3584]{1,0:T(8,128)(2,1)S(1)} %get-tuple-element.101), channel_id=1, source_target_pairs={{0,2},{1,3},{4,0},{5,1},{8,4},{9,5},{12,8},{13,9},{14,12},{15,13},... | collective-permute-start | bytes 1376264 | tf_op jit(solution)/shard_map/ppermute | solution.py:89
  71.4 13.4 %collective-permute-start.26 = (bf16[64,3584]{1,0:T(8,128)(2,1)S(1)}, bf16[64,3584]{1,0:T(8,128)(2,1)S(1)}, u32[]{:S(2)}, u32[]{:S(2)}) collective-permute-start(bf16[64,3584]{1,0:T(8,128)(2,1)S(1)} %collective-permute-done.15.refs_2_), channel_id=1, source_target_pairs={{0,4},{1,5},{4,8},{5,9},{8,12},{9,13},{12,14},{13,15},{14,10},{15,... | collective-permute-start | bytes 1376264 | tf_op jit(solution)/shard_map/ppermute | solution.py:89
  73.3 22.8 %collective-permute-start.30 = (bf16[384,1024]{1,0:T(8,128)(2,1)S(1)}, bf16[384,1024]{1,0:T(8,128)(2,1)S(1)}, u32[]{:S(2)}, u32[]{:S(2)}) collective-permute-start(bf16[384,1024]{1,0:T(8,128)(2,1)S(1)} %get-tuple-element.107), channel_id=1, source_target_pairs={{0,16},{16,0},{1,17},{17,1},{2,18},{18,2},{3,19},{19,3},{4,20},{20... | collective-permute-start | bytes 2359304 | tf_op jit(solution)/shard_map/ppermute | solution.py:101
  84.8 2.9 %collective-permute-start.27 = (bf16[64,3584]{1,0:T(8,128)(2,1)S(1)}, bf16[64,3584]{1,0:T(8,128)(2,1)S(1)}, u32[]{:S(2)}, u32[]{:S(2)}) collective-permute-start(bf16[64,3584]{1,0:T(8,128)(2,1)S(1)} %collective-permute-done.26.refs_0_), channel_id=1, source_target_pairs={{0,1},{1,0},{2,3},{3,2},{4,5},{5,4},{6,7},{7,6},{8,9},{9,8},{10,11... | collective-permute-start | bytes 1376264 | tf_op jit(solution)/shard_map/ppermute | solution.py:93
  85.0 13.0 %collective-permute-start.29 = (bf16[64,3584]{1,0:T(8,128)(2,1)S(1)}, bf16[64,3584]{1,0:T(8,128)(2,1)S(1)}, u32[]{:S(2)}, u32[]{:S(2)}) collective-permute-start(bf16[64,3584]{1,0:T(8,128)(2,1)S(1)} %add_convert_fusion.3), channel_id=1, source_target_pairs={{0,2},{1,3},{4,0},{5,1},{8,4},{9,5},{12,8},{13,9},{14,12},{15,13},... | collective-permute-start | bytes 1376264 | tf_op jit(solution)/shard_map/ppermute | solution.py:89
  85.2 12.9 %collective-permute-start.28 = (bf16[64,3584]{1,0:T(8,128)(2,1)S(1)}, bf16[64,3584]{1,0:T(8,128)(2,1)S(1)}, u32[]{:S(2)}, u32[]{:S(2)}) collective-permute-start(bf16[64,3584]{1,0:T(8,128)(2,1)S(1)} %get-tuple-element.105), channel_id=1, source_target_pairs={{0,4},{1,5},{4,8},{5,9},{8,12},{9,13},{12,14},{13,15},{14,10},{15,... | collective-permute-start | bytes 1376264 | tf_op jit(solution)/shard_map/ppermute | solution.py:89
  87.1 19.2 %collective-permute-start.33 = (bf16[288,1024]{1,0:T(8,128)(2,1)S(1)}, bf16[288,1024]{1,0:T(8,128)(2,1)S(1)}, u32[]{:S(2)}, u32[]{:S(2)}) collective-permute-start(bf16[288,1024]{1,0:T(8,128)(2,1)S(1)} %get-tuple-element.111), channel_id=1, source_target_pairs={{0,16},{16,0},{1,17},{17,1},{2,18},{18,2},{3,19},{19,3},{4,20},{20... | collective-permute-start | bytes 1769480 | tf_op jit(solution)/shard_map/ppermute | solution.py:101
  98.4 12.3 %collective-permute-start.31 = (bf16[64,3584]{1,0:T(8,128)(2,1)S(1)}, bf16[64,3584]{1,0:T(8,128)(2,1)S(1)}, u32[]{:S(2)}, u32[]{:S(2)}) collective-permute-start(bf16[64,3584]{1,0:T(8,128)(2,1)S(1)} %get-tuple-element.126), channel_id=1, source_target_pairs={{0,4},{1,5},{4,8},{5,9},{8,12},{9,13},{12,14},{13,15},{14,10},{15,... | collective-permute-start | bytes 1376264 | tf_op jit(solution)/shard_map/ppermute | solution.py:89
  100.2 11.8 %collective-permute-start.32 = (bf16[64,3584]{1,0:T(8,128)(2,1)S(1)}, bf16[64,3584]{1,0:T(8,128)(2,1)S(1)}, u32[]{:S(2)}, u32[]{:S(2)}) collective-permute-start(bf16[64,3584]{1,0:T(8,128)(2,1)S(1)} %get-tuple-element.127), channel_id=1, source_target_pairs={{0,2},{1,3},{4,0},{5,1},{8,4},{9,5},{12,8},{13,9},{14,12},{15,13},... | collective-permute-start | bytes 1376264 | tf_op jit(solution)/shard_map/ppermute | solution.py:89
  100.5 8.9 %collective-permute-start.34 = (bf16[96,1024]{1,0:T(8,128)(2,1)S(1)}, bf16[96,1024]{1,0:T(8,128)(2,1)S(1)}, u32[]{:S(2)}, u32[]{:S(2)}) collective-permute-start(bf16[96,1024]{1,0:T(8,128)(2,1)S(1)} %get-tuple-element.117), channel_id=1, source_target_pairs={{0,16},{16,0},{1,17},{17,1},{2,18},{18,2},{3,19},{19,3},{4,20},{20... | collective-permute-start | bytes 589832 | tf_op jit(solution)/shard_map/ppermute | solution.py:101
  (17 other events, 74.0 us)

commit v6 on v5

--- a/solution.py
+++ b/solution.py
@@ -115,7 +115,7 @@
 ANY = pl.BlockSpec(memory_space=pl.ANY)
 
 
-def kernel_call(kernel, name, inputs, out_shape, scratch, flops, moved):
+def kernel_call(kernel, name, inputs, out_shape, scratch, flops, moved, limit=12):
     in_specs, arrays = zip(*inputs)
     return pl.pallas_call(
         kernel,
@@ -123,7 +123,7 @@
         out_specs=[VMEM] * len(out_shape),
         out_shape=out_shape,
         scratch_shapes=scratch,
-        compiler_params=pltpu.CompilerParams(vmem_limit_bytes=20 * 2**20),
+        compiler_params=pltpu.CompilerParams(vmem_limit_bytes=limit * 2**20),
         cost_estimate=pl.CostEstimate(flops=flops, bytes_accessed=moved, transcendentals=0),
         name=name,
     )(*arrays)
@@ -273,7 +273,7 @@
             pltpu.VMEM((2, rows, RAW_TILE), BF16),
             pltpu.SemaphoreType.DMA((2,)),
         ],
-        compiler_params=pltpu.CompilerParams(vmem_limit_bytes=20 * 2**20),
+        compiler_params=pltpu.CompilerParams(vmem_limit_bytes=12 * 2**20),
         cost_estimate=pl.CostEstimate(
             flops=2 * rows * depth * width,
             bytes_accessed=2 * (depth * width + rows * (depth + width)),
@@ -421,6 +421,7 @@
         ],
         flops=len(sides) * count * rows * depth * width // share,
         moved=2 * (depth * width + count * rows * (depth + 2 * width)) // share,
+        limit=18,
     )
 
 
@@ -457,7 +458,7 @@
             pltpu.SemaphoreType.DMA((count,)),
         ],
         input_output_aliases={} if into is None else {len(inputs) - 1: 0},
-        compiler_params=pltpu.CompilerParams(vmem_limit_bytes=20 * 2**20),
+        compiler_params=pltpu.CompilerParams(vmem_limit_bytes=12 * 2**20),
         cost_estimate=pl.CostEstimate(
             flops=2**20, bytes_accessed=6 * count * rows * 128, transcendentals=0
         ),
@@ -518,6 +519,8 @@
     keep2, other3, other4 = spread((1, -2, -1, 0), 2, gate_a)
     keep2, gate_b = tie(keep2, gate_b)
     groups = (0, -1, 1, -2), (2, -3, 3), (-4,)
+    for d in (0, -1, 1):
+        pair[d] = pin(pair[d])
     send1, hold1 = bwd(groups[0], share=64)
 
     def mine(i, other, *more):

time: 113 us -> 112 us (level)
    unnamed x28 -> x20, local copies, waits for them, and re-layouts: 3.14 us -> 2.34 us
where the time goes in v6:
time: 112 us
  Pallas kernels  62.2 us (56%)
  starting transfers between devices  28.4 us (25%)
  waiting for transfers between devices  13.4 us (12%)
  other arithmetic  4.5 us (4%)
  local copies, waits for them, and re-layouts  2.65 us (2%)
    pallas_call x6, Pallas kernels, kernel_call(): pl.pallas_call(kernel, in_specs=in_specs, out_specs=[VMEM] * len(out_shap...  38.8 us
    pallas_call x2, Pallas kernels, raw_forward(): pl.pallas_call(functools.partial(raw_kernel, first), in_specs=[HBM, HBM],...  20.5 us
    ppermute x14, starting transfers between devices, step_ring(): return lax.ppermute(value, 'expert', pairs)  15.2 us
    ppermute x18, starting transfers between devices, xor(): return lax.ppermute(value, 'expert', [(i, i ^ bits) for i in range(16)])  10 us
    ppermute x3, waiting for transfers between devices, across(): return lax.ppermute(value, 'pipe', [(0, 1), (1, 0)])  6.04 us
    ppermute x14, waiting for transfers between devices, step_ring(): return lax.ppermute(value, 'expert', pairs)  5.8 us
    convert_element_type x5, other arithmetic, add(): return total.astype(BF16)  4.39 us
    ppermute x3, starting transfers between devices, across(): return lax.ppermute(value, 'pipe', [(0, 1), (1, 0)])  3.22 us
  transfers between devices with their start and end apart: 35, of which 8 were waited for; matrix products, arithmetic and copies ran while one was open for 3% of the time, Pallas kernels for 55%

profile of v6, /device:TPU:0, one launch (start us, length us, event | category | flops | bytes accessed | tf_op | source)
XLA Modules:
  0.0 112.2 jit_solution(15848742238907672592)
XLA Ops:
  1.5 2.5 %collective-permute-start.2 = (f32[16,128]{1,0:T(8,128)S(1)}, f32[16,128]{1,0:T(8,128)S(1)}, u32[]{:S(2)}, u32[]{:S(2)}) collective-permute-start(f32[16,128]{1,0:T(8,128)S(1)} %gates.1), channel_id=1, source_target_pairs={{0,3},{1,2},{2,1},{3,0},{4,7},{5,6},{6,5},{7,4},{8,11},{9,10},{10,... | collective-permute-start | bytes 24584 | tf_op jit(solution)/shard_map/ppermute | solution.py:93
  4.7 2.0 %collective-permute-start.6 = (bf16[64,3584]{1,0:T(8,128)(2,1)}, bf16[64,3584]{1,0:T(8,128)(2,1)S(1)}, u32[]{:S(2)}, u32[]{:S(2)}) collective-permute-start(bf16[64,3584]{1,0:T(8,128)(2,1)} %refs_0_.1), channel_id=1, source_target_pairs={{0,4},{1,5},{4,8},{5,9},{8,12},{9,13},{12,14},{13,15},{14,10},{15,... | collective-permute-start | bytes 1376264 | tf_op jit(solution)/shard_map/ppermute | solution.py:89
  6.8 1.5 %collective-permute-done.1 = f32[16,128]{1,0:T(8,128)S(1)} collective-permute-done((f32[16,128]{1,0:T(8,128)S(1)}, f32[16,128]{1,0:T(8,128)S(1)}, u32[]{:S(2)}, u32[]{:S(2)}) %collective-permute-start.1) | collective-permute-done | bytes 8224 | tf_op jit(solution)/shard_map/ppermute | solution.py:93
  8.3 1.6 %collective-permute-start.3 = (f32[4,4,128]{2,0,1:T(4,128)S(1)}, f32[4,4,128]{2,0,1:T(4,128)S(1)}, u32[]{:S(2)}, u32[]{:S(2)}) collective-permute-start(f32[4,4,128]{2,0,1:T(4,128)S(1)} %bitcast.37), channel_id=1, source_target_pairs={{0,4},{1,5},{2,6},{3,7},{4,0},{5,1},{6,2},{7,3},{8,12},{9,13},{10,... | collective-permute-start | bytes 24584 | tf_op jit(solution)/shard_map/ppermute | solution.py:93
  10.0 2.6 %collective-permute-start.4 = (f32[4,4,128]{2,0,1:T(4,128)S(1)}, f32[4,4,128]{2,0,1:T(4,128)S(1)}, u32[]{:S(2)}, u32[]{:S(2)}) collective-permute-start(f32[4,4,128]{2,0,1:T(4,128)S(1)} %bitcast.38), channel_id=1, source_target_pairs={{0,8},{1,9},{2,10},{3,11},{4,12},{5,13},{6,14},{7,15},{8,0},{9,1},... | collective-permute-start | bytes 24584 | tf_op jit(solution)/shard_map/ppermute | solution.py:93
  12.8 10.3 %raw_forward.2.refs_0_ = bf16[768,1792]{1,0:T(8,128)(2,1)} custom-call(bf16[768,2048]{1,0:T(8,128)(2,1)} %bitcast.51, bf16[2048,3584]{1,0:T(8,128)(2,1)} %bitcast.30), custom_call_target="tpu_custom_call" | custom-call | flops 5637144576 | bytes 13238272 | tf_op jit(solution)/shard_map/raw_forward/pallas_call | solution.py:263
  24.5 1.4 %collective-permute-start.12 = (bf16[64,3584]{1,0:T(8,128)(2,1)S(1)}, bf16[64,3584]{1,0:T(8,128)(2,1)S(1)}, u32[]{:S(2)}, u32[]{:S(2)}) collective-permute-start(bf16[64,3584]{1,0:T(8,128)(2,1)S(1)} %collective-permute-done.7.refs_4_), channel_id=1, source_target_pairs={{0,2},{1,3},{4,0},{5,1},{8,4},{9,5},{12,8},{13,9},{14,12},{15,13},... | collective-permute-start | bytes 1376264 | tf_op jit(solution)/shard_map/ppermute | solution.py:89
  26.1 10.2 %raw_forward.3.refs_1_ = bf16[768,1792]{1,0:T(8,128)(2,1)} custom-call(bf16[768,2048]{1,0:T(8,128)(2,1)} %bitcast.52, bf16[2048,3584]{1,0:T(8,128)(2,1)} %bitcast.31), custom_call_target="tpu_custom_call" | custom-call | flops 5637144576 | bytes 13238272 | tf_op jit(solution)/shard_map/raw_forward/pallas_call | solution.py:263
  37.9 4.4 %spread_tokens.2 = (bf16[256,3584]{1,0:T(8,128)(2,1)S(1)}, bf16[128,3584]{1,0:T(8,128)(2,1)S(1)}, bf16[128,3584]{1,0:T(8,128)(2,1)}) custom-call(s32[17]{0:T(128)S(1)} %pad_add_fusion.where, f32[8,128]{1,0:T(8,128)S(1)} %squeeze.20.gates, bf16[768,1792]{1,0:T(8,128)(2,1)} %raw_forward.2.refs_0_, bf16[768,1792]{1,0:T(8,128)(2,1)} %raw_forward.3.refs_1_), custom_call_target="tpu_custom_call" | custom-call | flops 1048576 | bytes 16384 | tf_op jit(solution)/shard_map/spread_tokens/pallas_call | solution.py:120
  43.5 1.4 %collective-permute-start.16 = (bf16[64,3584]{1,0:T(8,128)(2,1)S(1)}, bf16[64,3584]{1,0:T(8,128)(2,1)S(1)}, u32[]{:S(2)}, u32[]{:S(2)}) collective-permute-start(bf16[64,3584]{1,0:T(8,128)(2,1)S(1)} %collective-permute-done.12.refs_0_), channel_id=1, source_target_pairs={{0,2},{1,3},{4,0},{5,1},{8,4},{9,5},{12,8},{13,9},{14,12},{15,13},... | collective-permute-start | bytes 1376264 | tf_op jit(solution)/shard_map/ppermute | solution.py:89
  44.9 1.1 %add_convert_fusion.6 = (bf16[64,3584]{1,0:T(8,128)(2,1)}, bf16[64,3584]{1,0:T(8,128)(2,1)}) fusion(bf16[128,3584]{1,0:T(8,128)(2,1)S(1)} %collective-permute-done.17, bf16[256,3584]{1,0:T(8,128)(2,1)S(1)} %get-tuple-element.84), kind=kLoop, calls=%fused_computation.6 | loop fusion | flops 1835008 | bytes 2752512 | tf_op jit(solution)/shard_map/convert_element_type | solution.py:32
  47.7 1.1 %collective-permute-start.19 = (bf16[64,3584]{1,0:T(8,128)(2,1)}, bf16[64,3584]{1,0:T(8,128)(2,1)}, u32[]{:S(2)}, u32[]{:S(2)}) collective-permute-start(bf16[64,3584]{1,0:T(8,128)(2,1)} %get-tuple-element.124), channel_id=1, source_target_pairs={{0,2},{1,3},{4,0},{5,1},{8,4},{9,5},{12,8},{13,9},{14,12},{15,13},... | collective-permute-start | bytes 1376264 | tf_op jit(solution)/shard_map/ppermute | solution.py:89
  49.0 3.4 %spread_tokens.3 = (bf16[256,3584]{1,0:T(8,128)(2,1)S(1)}, bf16[128,3584]{1,0:T(8,128)(2,1)S(1)}, bf16[128,3584]{1,0:T(8,128)(2,1)S(1)}) custom-call(s32[17]{0:T(128)S(1)} %pad_add_fusion.where, f32[8,128]{1,0:T(8,128)S(1)} %squeeze.20.gates, bf16[768,1792]{1,0:T(8,128)(2,1)} %raw_forward.2.refs_0_, bf16[768,1792]{1,0:T(8,128)(2,1)} %raw_forward.3.refs_1_), custom_call_target="tpu_custom_call" | custom-call | flops 1048576 | bytes 16384 | tf_op jit(solution)/shard_map/spread_tokens/pallas_call | solution.py:120
  52.5 11.8 %backward.3 = (bf16[384,1024]{1,0:T(8,128)(2,1)S(1)}, bf16[384,1024]{1,0:T(8,128)(2,1)S(1)}) custom-call(s32[17]{0:T(128)S(1)} %pad_add_fusion.where, s32[1]{0:T(128)} %bitcast.20.pipe, f32[8,128]{1,0:T(8,128)S(1)} %squeeze.21.gates, bf16[2048,3584]{1,0:T(8,128)(2,1)} %bitcast.32, bf16[64,3584]{1,0:T(8,128)(2,1)S(1)} %copy-done.1, ...), custom_call_target="tpu_custom_call" | custom-call | flops 88080384 | bytes 339968 | tf_op jit(solution)/shard_map/backward/pallas_call | solution.py:120
  64.2 1.4 %collective-permute-done.18 = bf16[64,3584]{1,0:T(8,128)(2,1)} collective-permute-done((bf16[64,3584]{1,0:T(8,128)(2,1)}, bf16[64,3584]{1,0:T(8,128)(2,1)}, u32[]{:S(2)}, u32[]{:S(2)}) %collective-permute-start.18) | collective-permute-done | bytes 458784 | tf_op jit(solution)/shard_map/ppermute | solution.py:89
  65.6 1.1 collective-permute-done.19
  67.8 1.8 %add_convert_fusion.4 = (bf16[64,3584]{1,0:T(8,128)(2,1)S(1)}, bf16[64,3584]{1,0:T(8,128)(2,1)S(1)}) fusion(bf16[64,3584]{1,0:T(8,128)(2,1)} %collective-permute-done.19, bf16[128,3584]{1,0:T(8,128)(2,1)} %collective-permute-done.14, bf16[256,3584]{1,0:T(8,128)(2,1)S(1)} %get-tuple-element.84, bf16[64,3584]{1,0:T(8,128)(2,1)} %collective-permute-done.18), kind=kLoop, calls=%fused_computation.4 | loop fusion | flops 2752512 | bytes 3670016 | tf_op jit(solution)/shard_map/convert_element_type | solution.py:32
  69.5 1.1 collective-permute-start.25
  70.6 1.9 %collective-permute-start.26 = (bf16[64,3584]{1,0:T(8,128)(2,1)S(1)}, bf16[64,3584]{1,0:T(8,128)(2,1)S(1)}, u32[]{:S(2)}, u32[]{:S(2)}) collective-permute-start(bf16[64,3584]{1,0:T(8,128)(2,1)S(1)} %collective-permute-done.15.refs_2_), channel_id=1, source_target_pairs={{0,4},{1,5},{4,8},{5,9},{8,12},{9,13},{12,14},{13,15},{14,10},{15,... | collective-permute-start | bytes 1376264 | tf_op jit(solution)/shard_map/ppermute | solution.py:89
  72.5 1.5 %collective-permute-start.30 = (bf16[384,1024]{1,0:T(8,128)(2,1)S(1)}, bf16[384,1024]{1,0:T(8,128)(2,1)S(1)}, u32[]{:S(2)}, u32[]{:S(2)}) collective-permute-start(bf16[384,1024]{1,0:T(8,128)(2,1)S(1)} %get-tuple-element.107), channel_id=1, source_target_pairs={{0,16},{16,0},{1,17},{17,1},{2,18},{18,2},{3,19},{19,3},{4,20},{20... | collective-permute-start | bytes 2359304 | tf_op jit(solution)/shard_map/ppermute | solution.py:101
  74.0 10.0 %backward.4 = (bf16[288,1024]{1,0:T(8,128)(2,1)S(1)}, bf16[288,1024]{1,0:T(8,128)(2,1)S(1)}) custom-call(s32[17]{0:T(128)S(1)} %pad_add_fusion.where, s32[1]{0:T(128)} %bitcast.20.pipe, f32[8,128]{1,0:T(8,128)S(1)} %squeeze.21.gates, bf16[2048,3584]{1,0:T(8,128)(2,1)} %bitcast.33, bf16[64,3584]{1,0:T(8,128)(2,1)S(1)} %collective-permute-done.12.refs_0_, ...), custom_call_target="tpu_custom_call" | custom-call | flops 66060288 | bytes 312320 | tf_op jit(solution)/shard_map/backward/pallas_call | solution.py:120
  84.4 1.9 %collective-permute-start.28 = (bf16[64,3584]{1,0:T(8,128)(2,1)S(1)}, bf16[64,3584]{1,0:T(8,128)(2,1)S(1)}, u32[]{:S(2)}, u32[]{:S(2)}) collective-permute-start(bf16[64,3584]{1,0:T(8,128)(2,1)S(1)} %get-tuple-element.105), channel_id=1, source_target_pairs={{0,4},{1,5},{4,8},{5,9},{8,12},{9,13},{12,14},{13,15},{14,10},{15,... | collective-permute-start | bytes 1376264 | tf_op jit(solution)/shard_map/ppermute | solution.py:89
  86.8 8.4 %backward.5 = (bf16[96,1024]{1,0:T(8,128)(2,1)S(1)}, bf16[96,1024]{1,0:T(8,128)(2,1)S(1)}) custom-call(s32[17]{0:T(128)S(1)} %pad_add_fusion.where, s32[1]{0:T(128)} %bitcast.20.pipe, f32[8,128]{1,0:T(8,128)S(1)} %squeeze.21.gates, bf16[2048,3584]{1,0:T(8,128)(2,1)} %bitcast.34, bf16[64,3584]{1,0:T(8,128)(2,1)S(1)} %collective-permute-done.26.refs_0_, ...), custom_call_target="tpu_custom_call" | custom-call | flops 22020096 | bytes 257024 | tf_op jit(solution)/shard_map/backward/pallas_call | solution.py:120
  95.2 1.9 %collective-permute-done.29 = bf16[64,3584]{1,0:T(8,128)(2,1)S(1)} collective-permute-done((bf16[64,3584]{1,0:T(8,128)(2,1)S(1)}, bf16[64,3584]{1,0:T(8,128)(2,1)S(1)}, u32[]{:S(2)}, u32[]{:S(2)}) %collective-permute-start.29) | collective-permute-done | bytes 458784 | tf_op jit(solution)/shard_map/ppermute | solution.py:89
  97.6 1.8 %collective-permute-start.31 = (bf16[64,3584]{1,0:T(8,128)(2,1)S(1)}, bf16[64,3584]{1,0:T(8,128)(2,1)S(1)}, u32[]{:S(2)}, u32[]{:S(2)}) collective-permute-start(bf16[64,3584]{1,0:T(8,128)(2,1)S(1)} %get-tuple-element.126), channel_id=1, source_target_pairs={{0,4},{1,5},{4,8},{5,9},{8,12},{9,13},{12,14},{13,15},{14,10},{15,... | collective-permute-start | bytes 1376264 | tf_op jit(solution)/shard_map/ppermute | solution.py:89
  99.7 1.2 %collective-permute-start.34 = (bf16[96,1024]{1,0:T(8,128)(2,1)S(1)}, bf16[96,1024]{1,0:T(8,128)(2,1)S(1)}, u32[]{:S(2)}, u32[]{:S(2)}) collective-permute-start(bf16[96,1024]{1,0:T(8,128)(2,1)S(1)} %get-tuple-element.117), channel_id=1, source_target_pairs={{0,16},{16,0},{1,17},{17,1},{2,18},{18,2},{3,19},{19,3},{4,20},{20... | collective-permute-start | bytes 589832 | tf_op jit(solution)/shard_map/ppermute | solution.py:101
  100.9 4.7 %collective-permute-done.33.refs_3_ = bf16[288,1024]{1,0:T(8,128)(2,1)S(1)} collective-permute-done((bf16[288,1024]{1,0:T(8,128)(2,1)S(1)}, bf16[288,1024]{1,0:T(8,128)(2,1)S(1)}, u32[]{:S(2)}, u32[]{:S(2)}) %collective-permute-start.33) | collective-permute-done | bytes 589856 | tf_op jit(solution)/shard_map/ppermute | solution.py:101
  105.5 1.7 %collect.2.refs_2_ = bf16[768,1024]{1,0:T(8,128)(2,1)} custom-call(s32[17]{0:T(128)S(1)} %pad_add_fusion.where, bf16[384,1024]{1,0:T(8,128)(2,1)S(1)} %get-tuple-element.113.refs_0_, bf16[384,1024]{1,0:T(8,128)(2,1)S(1)} %collective-permute-done.30.refs_1_, bf16[288,1024]{1,0:T(8,128)(2,1)S(1)} %get-tuple-element.115.refs_2_, ...), custom_call_target="tpu_custom_call" | custom-call | flops 1048576 | bytes 4128768 | tf_op jit(solution)/shard_map/collect/pallas_call | solution.py:451
  107.3 1.4 %collective-permute-done.34.refs_1_ = bf16[96,1024]{1,0:T(8,128)(2,1)S(1)} collective-permute-done((bf16[96,1024]{1,0:T(8,128)(2,1)S(1)}, bf16[96,1024]{1,0:T(8,128)(2,1)S(1)}, u32[]{:S(2)}, u32[]{:S(2)}) %collective-permute-start.34) | collective-permute-done | bytes 196640 | tf_op jit(solution)/shard_map/ppermute | solution.py:101
  108.6 1.3 %collect.3 = bf16[768,1024]{1,0:T(8,128)(2,1)} custom-call(s32[17]{0:T(128)S(1)} %pad_add_fusion.where, bf16[96,1024]{1,0:T(8,128)(2,1)S(1)} %get-tuple-element.112.refs_0_, bf16[96,1024]{1,0:T(8,128)(2,1)S(1)} %collective-permute-done.34.refs_1_, bf16[768,1024]{1,0:T(8,128)(2,1)} %collect.2.refs_2_), custom_call_target="tpu_custom_call", output_to_operand_aliasing={{}: (3, {})} | custom-call | flops 1048576 | bytes 589824 | tf_op jit(solution)/shard_map/collect/pallas_call | solution.py:451
  109.9 1.3 %collective-permute-done.32 = bf16[64,3584]{1,0:T(8,128)(2,1)S(1)} collective-permute-done((bf16[64,3584]{1,0:T(8,128)(2,1)S(1)}, bf16[64,3584]{1,0:T(8,128)(2,1)S(1)}, u32[]{:S(2)}, u32[]{:S(2)}) %collective-permute-start.32) | collective-permute-done | bytes 458784 | tf_op jit(solution)/shard_map/ppermute | solution.py:89
  111.2 1.0 add_convert_fusion
  (83 shorter events, 10.8 us)
Async XLA Ops:
  1.5 5.3 %collective-permute-start.2 = (f32[16,128]{1,0:T(8,128)S(1)}, f32[16,128]{1,0:T(8,128)S(1)}, u32[]{:S(2)}, u32[]{:S(2)}) collective-permute-start(f32[16,128]{1,0:T(8,128)S(1)} %gates.1), channel_id=1, source_target_pairs={{0,3},{1,2},{2,1},{3,0},{4,7},{5,6},{6,5},{7,4},{8,11},{9,10},{10,... | collective-permute-start | bytes 24584 | tf_op jit(solution)/shard_map/ppermute | solution.py:93
  4.6 3.7 %collective-permute-start.1 = (f32[16,128]{1,0:T(8,128)S(1)}, f32[16,128]{1,0:T(8,128)S(1)}, u32[]{:S(2)}, u32[]{:S(2)}) collective-permute-start(f32[16,128]{1,0:T(8,128)S(1)} %gates.1), channel_id=1, source_target_pairs={{0,2},{1,3},{2,0},{3,1},{4,6},{5,7},{6,4},{7,5},{8,10},{9,11},{10,... | collective-permute-start | bytes 24584 | tf_op jit(solution)/shard_map/ppermute | solution.py:93
  4.7 18.5 %collective-permute-start.6 = (bf16[64,3584]{1,0:T(8,128)(2,1)}, bf16[64,3584]{1,0:T(8,128)(2,1)S(1)}, u32[]{:S(2)}, u32[]{:S(2)}) collective-permute-start(bf16[64,3584]{1,0:T(8,128)(2,1)} %refs_0_.1), channel_id=1, source_target_pairs={{0,4},{1,5},{4,8},{5,9},{8,12},{9,13},{12,14},{13,15},{14,10},{15,... | collective-permute-start | bytes 1376264 | tf_op jit(solution)/shard_map/ppermute | solution.py:89
  6.7 16.5 %collective-permute-start.7 = (bf16[64,3584]{1,0:T(8,128)(2,1)}, bf16[64,3584]{1,0:T(8,128)(2,1)S(1)}, u32[]{:S(2)}, u32[]{:S(2)}) collective-permute-start(bf16[64,3584]{1,0:T(8,128)(2,1)} %refs_0_.1), channel_id=1, source_target_pairs={{0,2},{1,3},{4,0},{5,1},{8,4},{9,5},{12,8},{13,9},{14,12},{15,13},... | collective-permute-start | bytes 1376264 | tf_op jit(solution)/shard_map/ppermute | solution.py:89
  8.3 14.8 %collective-permute-start.3 = (f32[4,4,128]{2,0,1:T(4,128)S(1)}, f32[4,4,128]{2,0,1:T(4,128)S(1)}, u32[]{:S(2)}, u32[]{:S(2)}) collective-permute-start(f32[4,4,128]{2,0,1:T(4,128)S(1)} %bitcast.37), channel_id=1, source_target_pairs={{0,4},{1,5},{2,6},{3,7},{4,0},{5,1},{6,2},{7,3},{8,12},{9,13},{10,... | collective-permute-start | bytes 24584 | tf_op jit(solution)/shard_map/ppermute | solution.py:93
  10.0 13.2 %collective-permute-start.4 = (f32[4,4,128]{2,0,1:T(4,128)S(1)}, f32[4,4,128]{2,0,1:T(4,128)S(1)}, u32[]{:S(2)}, u32[]{:S(2)}) collective-permute-start(f32[4,4,128]{2,0,1:T(4,128)S(1)} %bitcast.38), channel_id=1, source_target_pairs={{0,8},{1,9},{2,10},{3,11},{4,12},{5,13},{6,14},{7,15},{8,0},{9,1},... | collective-permute-start | bytes 24584 | tf_op jit(solution)/shard_map/ppermute | solution.py:93
  12.6 10.7 %collective-permute-start.5 = (f32[4,4,128]{2,0,1:T(4,128)S(1)}, f32[4,4,128]{2,0,1:T(4,128)S(1)}, u32[]{:S(2)}, u32[]{:S(2)}) collective-permute-start(f32[4,4,128]{2,0,1:T(4,128)S(1)} %bitcast.39), channel_id=1, source_target_pairs={{0,12},{1,13},{2,14},{3,15},{4,8},{5,9},{6,10},{7,11},{8,4},{9,5},... | collective-permute-start | bytes 24584 | tf_op jit(solution)/shard_map/ppermute | solution.py:93
  23.1 13.2 %collective-permute-start.8 = (bf16[64,3584]{1,0:T(8,128)(2,1)S(1)}, bf16[64,3584]{1,0:T(8,128)(2,1)S(1)}, u32[]{:S(2)}, u32[]{:S(2)}) collective-permute-start(bf16[64,3584]{1,0:T(8,128)(2,1)S(1)} %copy-done), channel_id=1, source_target_pairs={{0,1},{1,0},{2,3},{3,2},{4,5},{5,4},{6,7},{7,6},{8,9},{9,8},{10,11... | collective-permute-start | bytes 1376264 | tf_op jit(solution)/shard_map/ppermute | solution.py:93
  23.3 14.6 %collective-permute-start.9 = (bf16[64,3584]{1,0:T(8,128)(2,1)S(1)}, bf16[64,3584]{1,0:T(8,128)(2,1)}, u32[]{:S(2)}, u32[]{:S(2)}) collective-permute-start(bf16[64,3584]{1,0:T(8,128)(2,1)S(1)} %collective-permute-done.6.refs_2_), channel_id=1, source_target_pairs={{0,1},{1,0},{2,3},{3,2},{4,5},{5,4},{6,7},{7,6},{8,9},{9,8},{10,11... | collective-permute-start | bytes 1376264 | tf_op jit(solution)/shard_map/ppermute | solution.py:93
  23.8 18.4 %collective-permute-start.11 = (bf16[64,3584]{1,0:T(8,128)(2,1)S(1)}, bf16[64,3584]{1,0:T(8,128)(2,1)}, u32[]{:S(2)}, u32[]{:S(2)}) collective-permute-start(bf16[64,3584]{1,0:T(8,128)(2,1)S(1)} %collective-permute-done.6.refs_2_), channel_id=1, source_target_pairs={{0,4},{1,5},{4,8},{5,9},{8,12},{9,13},{12,14},{13,15},{14,10},{15,... | collective-permute-start | bytes 1376264 | tf_op jit(solution)/shard_map/ppermute | solution.py:89
  24.5 11.9 %collective-permute-start.10 = (bf16[64,3584]{1,0:T(8,128)(2,1)S(1)}, bf16[64,3584]{1,0:T(8,128)(2,1)S(1)}, u32[]{:S(2)}, u32[]{:S(2)}) collective-permute-start(bf16[64,3584]{1,0:T(8,128)(2,1)S(1)} %collective-permute-done.7.refs_4_), channel_id=1, source_target_pairs={{0,1},{1,0},{2,3},{3,2},{4,5},{5,4},{6,7},{7,6},{8,9},{9,8},{10,11... | collective-permute-start | bytes 1376264 | tf_op jit(solution)/shard_map/ppermute | solution.py:93
  24.5 17.8 %collective-permute-start.12 = (bf16[64,3584]{1,0:T(8,128)(2,1)S(1)}, bf16[64,3584]{1,0:T(8,128)(2,1)S(1)}, u32[]{:S(2)}, u32[]{:S(2)}) collective-permute-start(bf16[64,3584]{1,0:T(8,128)(2,1)S(1)} %collective-permute-done.7.refs_4_), channel_id=1, source_target_pairs={{0,2},{1,3},{4,0},{5,1},{8,4},{9,5},{12,8},{13,9},{14,12},{15,13},... | collective-permute-start | bytes 1376264 | tf_op jit(solution)/shard_map/ppermute | solution.py:89
  42.6 4.4 %collective-permute-start.13 = (bf16[64,3584]{1,0:T(8,128)(2,1)}, bf16[64,3584]{1,0:T(8,128)(2,1)S(1)}, u32[]{:S(2)}, u32[]{:S(2)}) collective-permute-start(bf16[64,3584]{1,0:T(8,128)(2,1)} %collective-permute-done.11.refs_6_), channel_id=1, source_target_pairs={{0,1},{1,0},{2,3},{3,2},{4,5},{5,4},{6,7},{7,6},{8,9},{9,8},{10,11... | collective-permute-start | bytes 1376264 | tf_op jit(solution)/shard_map/ppermute | solution.py:93
  42.8 21.4 %collective-permute-start.15 = (bf16[64,3584]{1,0:T(8,128)(2,1)}, bf16[64,3584]{1,0:T(8,128)(2,1)S(1)}, u32[]{:S(2)}, u32[]{:S(2)}) collective-permute-start(bf16[64,3584]{1,0:T(8,128)(2,1)} %collective-permute-done.11.refs_6_), channel_id=1, source_target_pairs={{0,4},{1,5},{4,8},{5,9},{8,12},{9,13},{12,14},{13,15},{14,10},{15,... | collective-permute-start | bytes 1376264 | tf_op jit(solution)/shard_map/ppermute | solution.py:89
  43.5 5.4 %collective-permute-start.14 = (bf16[128,3584]{1,0:T(8,128)(2,1)}, bf16[128,3584]{1,0:T(8,128)(2,1)}, u32[]{:S(2)}, u32[]{:S(2)}) collective-permute-start(bf16[128,3584]{1,0:T(8,128)(2,1)} %get-tuple-element.73), channel_id=1, source_target_pairs={{0,1},{1,0},{2,3},{3,2},{4,5},{5,4},{6,7},{7,6},{8,9},{9,8},{10,11... | collective-permute-start | bytes 2752520 | tf_op jit(solution)/shard_map/ppermute | solution.py:93
  43.5 20.7 %collective-permute-start.16 = (bf16[64,3584]{1,0:T(8,128)(2,1)S(1)}, bf16[64,3584]{1,0:T(8,128)(2,1)S(1)}, u32[]{:S(2)}, u32[]{:S(2)}) collective-permute-start(bf16[64,3584]{1,0:T(8,128)(2,1)S(1)} %collective-permute-done.12.refs_0_), channel_id=1, source_target_pairs={{0,2},{1,3},{4,0},{5,1},{8,4},{9,5},{12,8},{13,9},{14,12},{15,13},... | collective-permute-start | bytes 1376264 | tf_op jit(solution)/shard_map/ppermute | solution.py:89
  46.0 19.6 %collective-permute-start.18 = (bf16[64,3584]{1,0:T(8,128)(2,1)}, bf16[64,3584]{1,0:T(8,128)(2,1)}, u32[]{:S(2)}, u32[]{:S(2)}) collective-permute-start(bf16[64,3584]{1,0:T(8,128)(2,1)} %get-tuple-element.125), channel_id=1, source_target_pairs={{0,4},{1,5},{4,8},{5,9},{8,12},{9,13},{12,14},{13,15},{14,10},{15,... | collective-permute-start | bytes 1376264 | tf_op jit(solution)/shard_map/ppermute | solution.py:89
  47.7 19.1 %collective-permute-start.19 = (bf16[64,3584]{1,0:T(8,128)(2,1)}, bf16[64,3584]{1,0:T(8,128)(2,1)}, u32[]{:S(2)}, u32[]{:S(2)}) collective-permute-start(bf16[64,3584]{1,0:T(8,128)(2,1)} %get-tuple-element.124), channel_id=1, source_target_pairs={{0,2},{1,3},{4,0},{5,1},{8,4},{9,5},{12,8},{13,9},{14,12},{15,13},... | collective-permute-start | bytes 1376264 | tf_op jit(solution)/shard_map/ppermute | solution.py:89
  48.9 23.6 %collective-permute-start.22 = (bf16[64,3584]{1,0:T(8,128)(2,1)S(1)}, bf16[64,3584]{1,0:T(8,128)(2,1)S(1)}, u32[]{:S(2)}, u32[]{:S(2)}) collective-permute-start(bf16[64,3584]{1,0:T(8,128)(2,1)S(1)} %collective-permute-done.12.refs_0_), channel_id=1, source_target_pairs={{0,1},{1,0},{2,3},{3,2},{4,5},{5,4},{6,7},{7,6},{8,9},{9,8},{10,11... | collective-permute-start | bytes 1376264 | tf_op jit(solution)/shard_map/ppermute | solution.py:93
  66.7 3.9 %collective-permute-start.21 = (bf16[128,3584]{1,0:T(8,128)(2,1)S(1)}, bf16[128,3584]{1,0:T(8,128)(2,1)S(1)}, u32[]{:S(2)}, u32[]{:S(2)}) collective-permute-start(bf16[128,3584]{1,0:T(8,128)(2,1)S(1)} %get-tuple-element.89), channel_id=1, source_target_pairs={{0,1},{1,0},{2,3},{3,2},{4,5},{5,4},{6,7},{7,6},{8,9},{9,8},{10,11... | collective-permute-start | bytes 2752520 | tf_op jit(solution)/shard_map/ppermute | solution.py:93
  67.2 6.7 %collective-permute-start.23 = (bf16[64,3584]{1,0:T(8,128)(2,1)S(1)}, bf16[64,3584]{1,0:T(8,128)(2,1)S(1)}, u32[]{:S(2)}, u32[]{:S(2)}) collective-permute-start(bf16[64,3584]{1,0:T(8,128)(2,1)S(1)} %collective-permute-done.15.refs_2_), channel_id=1, source_target_pairs={{0,1},{1,0},{2,3},{3,2},{4,5},{5,4},{6,7},{7,6},{8,9},{9,8},{10,11... | collective-permute-start | bytes 1376264 | tf_op jit(solution)/shard_map/ppermute | solution.py:93
  67.3 6.7 %collective-permute-start.24 = (bf16[64,3584]{1,0:T(8,128)(2,1)S(1)}, bf16[64,3584]{1,0:T(8,128)(2,1)S(1)}, u32[]{:S(2)}, u32[]{:S(2)}) collective-permute-start(bf16[64,3584]{1,0:T(8,128)(2,1)S(1)} %collective-permute-done.16.refs_4_), channel_id=1, source_target_pairs={{0,1},{1,0},{2,3},{3,2},{4,5},{5,4},{6,7},{7,6},{8,9},{9,8},{10,11... | collective-permute-start | bytes 1376264 | tf_op jit(solution)/shard_map/ppermute | solution.py:93
  69.5 14.4 %collective-permute-start.25 = (bf16[64,3584]{1,0:T(8,128)(2,1)S(1)}, bf16[64,3584]{1,0:T(8,128)(2,1)S(1)}, u32[]{:S(2)}, u32[]{:S(2)}) collective-permute-start(bf16[64,3584]{1,0:T(8,128)(2,1)S(1)} %get-tuple-element.101), channel_id=1, source_target_pairs={{0,2},{1,3},{4,0},{5,1},{8,4},{9,5},{12,8},{13,9},{14,12},{15,13},... | collective-permute-start | bytes 1376264 | tf_op jit(solution)/shard_map/ppermute | solution.py:89
  70.6 13.4 %collective-permute-start.26 = (bf16[64,3584]{1,0:T(8,128)(2,1)S(1)}, bf16[64,3584]{1,0:T(8,128)(2,1)S(1)}, u32[]{:S(2)}, u32[]{:S(2)}) collective-permute-start(bf16[64,3584]{1,0:T(8,128)(2,1)S(1)} %collective-permute-done.15.refs_2_), channel_id=1, source_target_pairs={{0,4},{1,5},{4,8},{5,9},{8,12},{9,13},{12,14},{13,15},{14,10},{15,... | collective-permute-start | bytes 1376264 | tf_op jit(solution)/shard_map/ppermute | solution.py:89
  72.5 22.8 %collective-permute-start.30 = (bf16[384,1024]{1,0:T(8,128)(2,1)S(1)}, bf16[384,1024]{1,0:T(8,128)(2,1)S(1)}, u32[]{:S(2)}, u32[]{:S(2)}) collective-permute-start(bf16[384,1024]{1,0:T(8,128)(2,1)S(1)} %get-tuple-element.107), channel_id=1, source_target_pairs={{0,16},{16,0},{1,17},{17,1},{2,18},{18,2},{3,19},{19,3},{4,20},{20... | collective-permute-start | bytes 2359304 | tf_op jit(solution)/shard_map/ppermute | solution.py:101
  84.0 2.9 %collective-permute-start.27 = (bf16[64,3584]{1,0:T(8,128)(2,1)S(1)}, bf16[64,3584]{1,0:T(8,128)(2,1)S(1)}, u32[]{:S(2)}, u32[]{:S(2)}) collective-permute-start(bf16[64,3584]{1,0:T(8,128)(2,1)S(1)} %collective-permute-done.26.refs_0_), channel_id=1, source_target_pairs={{0,1},{1,0},{2,3},{3,2},{4,5},{5,4},{6,7},{7,6},{8,9},{9,8},{10,11... | collective-permute-start | bytes 1376264 | tf_op jit(solution)/shard_map/ppermute | solution.py:93
  84.2 13.0 %collective-permute-start.29 = (bf16[64,3584]{1,0:T(8,128)(2,1)S(1)}, bf16[64,3584]{1,0:T(8,128)(2,1)S(1)}, u32[]{:S(2)}, u32[]{:S(2)}) collective-permute-start(bf16[64,3584]{1,0:T(8,128)(2,1)S(1)} %add_convert_fusion.3), channel_id=1, source_target_pairs={{0,2},{1,3},{4,0},{5,1},{8,4},{9,5},{12,8},{13,9},{14,12},{15,13},... | collective-permute-start | bytes 1376264 | tf_op jit(solution)/shard_map/ppermute | solution.py:89
  84.4 12.9 %collective-permute-start.28 = (bf16[64,3584]{1,0:T(8,128)(2,1)S(1)}, bf16[64,3584]{1,0:T(8,128)(2,1)S(1)}, u32[]{:S(2)}, u32[]{:S(2)}) collective-permute-start(bf16[64,3584]{1,0:T(8,128)(2,1)S(1)} %get-tuple-element.105), channel_id=1, source_target_pairs={{0,4},{1,5},{4,8},{5,9},{8,12},{9,13},{12,14},{13,15},{14,10},{15,... | collective-permute-start | bytes 1376264 | tf_op jit(solution)/shard_map/ppermute | solution.py:89
  86.3 19.2 %collective-permute-start.33 = (bf16[288,1024]{1,0:T(8,128)(2,1)S(1)}, bf16[288,1024]{1,0:T(8,128)(2,1)S(1)}, u32[]{:S(2)}, u32[]{:S(2)}) collective-permute-start(bf16[288,1024]{1,0:T(8,128)(2,1)S(1)} %get-tuple-element.111), channel_id=1, source_target_pairs={{0,16},{16,0},{1,17},{17,1},{2,18},{18,2},{3,19},{19,3},{4,20},{20... | collective-permute-start | bytes 1769480 | tf_op jit(solution)/shard_map/ppermute | solution.py:101
  97.6 12.3 %collective-permute-start.31 = (bf16[64,3584]{1,0:T(8,128)(2,1)S(1)}, bf16[64,3584]{1,0:T(8,128)(2,1)S(1)}, u32[]{:S(2)}, u32[]{:S(2)}) collective-permute-start(bf16[64,3584]{1,0:T(8,128)(2,1)S(1)} %get-tuple-element.126), channel_id=1, source_target_pairs={{0,4},{1,5},{4,8},{5,9},{8,12},{9,13},{12,14},{13,15},{14,10},{15,... | collective-permute-start | bytes 1376264 | tf_op jit(solution)/shard_map/ppermute | solution.py:89
  99.4 11.8 %collective-permute-start.32 = (bf16[64,3584]{1,0:T(8,128)(2,1)S(1)}, bf16[64,3584]{1,0:T(8,128)(2,1)S(1)}, u32[]{:S(2)}, u32[]{:S(2)}) collective-permute-start(bf16[64,3584]{1,0:T(8,128)(2,1)S(1)} %get-tuple-element.127), channel_id=1, source_target_pairs={{0,2},{1,3},{4,0},{5,1},{8,4},{9,5},{12,8},{13,9},{14,12},{15,13},... | collective-permute-start | bytes 1376264 | tf_op jit(solution)/shard_map/ppermute | solution.py:89
  99.7 8.9 %collective-permute-start.34 = (bf16[96,1024]{1,0:T(8,128)(2,1)S(1)}, bf16[96,1024]{1,0:T(8,128)(2,1)S(1)}, u32[]{:S(2)}, u32[]{:S(2)}) collective-permute-start(bf16[96,1024]{1,0:T(8,128)(2,1)S(1)} %get-tuple-element.117), channel_id=1, source_target_pairs={{0,16},{16,0},{1,17},{17,1},{2,18},{18,2},{3,19},{19,3},{4,20},{20... | collective-permute-start | bytes 589832 | tf_op jit(solution)/shard_map/ppermute | solution.py:101
  (13 other events, 61.2 us)

commit v7 on v6

--- a/solution.py
+++ b/solution.py
@@ -518,7 +518,7 @@
     gate_a, pair[-2], other2 = tie(gate_a, pair[-2], other2)
     keep2, other3, other4 = spread((1, -2, -1, 0), 2, gate_a)
     keep2, gate_b = tie(keep2, gate_b)
-    groups = (0, -1, 1, -2), (2, -3, 3), (-4,)
+    groups = (0, -1, 1, -2), (2, -3), (3, -4)
     for d in (0, -1, 1):
         pair[d] = pin(pair[d])
     send1, hold1 = bwd(groups[0], share=64)
@@ -537,21 +537,20 @@
     up, down = tie(up, down)
     down = step_ring(down, -1)
     recv1 = across(send1)
-    pair[2], pair[-3], pair[3] = core(got[2]), core(got[-3]), core(got[3])
+    pair[2], pair[-3] = core(got[2]), core(got[-3])
     other3, other4 = core(other3), core(other4)
     gate_b, other3, other4 = tie(gate_b, other3, other4)
     send2, hold2 = bwd(groups[1], share=64)
 
-    hold2, send2, up, down, got[-4] = tie(hold2, send2, up, down, got[-4])
+    hold2, send2, up, down, got[3], got[-4] = tie(hold2, send2, up, down, got[3], got[-4])
     up, down = step_ring(up, 1), step_ring(mine(1, other3, down), -1)
-    pair[-4] = core(got[-4])
+    pair[3], pair[-4] = core(got[3]), core(got[-4])
     recv2 = across(send2)
     send3, hold3 = bwd(groups[2], share=64)
 
-    send3, hold3, up, down, recv1 = tie(send3, hold3, up, down, recv1)
+    send3, hold3, up, down, recv1, recv2 = tie(send3, hold3, up, down, recv1, recv2)
     up, down = step_ring(mine(0, other3, up), 1), step_ring(mine(2, other4, down), -1)
     recv3 = across(send3)
-    hold3, recv2 = tie(hold3, recv2)
     grad = collect(groups[:2], where, (hold1, recv1, hold2, recv2), 8 * rows)
     grad, recv3 = tie(grad, recv3)
     mixed_a = mine(3, other4, up, down)

time: 112 us -> 114 us (1.018)
    ppermute x3, waiting for transfers between devices: 6.04 us -> 9.42 us  [across(): return lax.ppermute(value, 'pipe', [(0, 1), (1, 0)])]
    ppermute x14, waiting for transfers between devices: 5.8 us -> 3.15 us  [step_ring(): return lax.ppermute(value, 'expert', pairs)]
    ppermute x3, starting transfers between devices: 3.22 us -> 4.48 us  [across(): return lax.ppermute(value, 'pipe', [(0, 1), (1, 0)])]
  transfers between devices with their start and end apart: 35 -> 35, of which waited for: 8 -> 7; matrix products, arithmetic and copies ran while one was open for 3% -> 3% of each run, Pallas kernels for 55% -> 54%
where the time goes in v7:
time: 114 us
  Pallas kernels  62.7 us (55%)
  starting transfers between devices  28.8 us (25%)
  waiting for transfers between devices  14.1 us (12%)
  other arithmetic  4.5 us (4%)
  local copies, waits for them, and re-layouts  2.65 us (2%)
    pallas_call x6, Pallas kernels, kernel_call(): pl.pallas_call(kernel, in_specs=in_specs, out_specs=[VMEM] * len(out_shap...  39.3 us
    pallas_call x2, Pallas kernels, raw_forward(): pl.pallas_call(functools.partial(raw_kernel, first), in_specs=[HBM, HBM],...  20.5 us
    ppermute x14, starting transfers between devices, step_ring(): return lax.ppermute(value, 'expert', pairs)  14.4 us
    ppermute x18, starting transfers between devices, xor(): return lax.ppermute(value, 'expert', [(i, i ^ bits) for i in range(16)])  9.93 us
    ppermute x3, waiting for transfers between devices, across(): return lax.ppermute(value, 'pipe', [(0, 1), (1, 0)])  9.42 us
    ppermute x3, starting transfers between devices, across(): return lax.ppermute(value, 'pipe', [(0, 1), (1, 0)])  4.48 us
    convert_element_type x5, other arithmetic, add(): return total.astype(BF16)  4.39 us
    ppermute x14, waiting for transfers between devices, step_ring(): return lax.ppermute(value, 'expert', pairs)  3.15 us
  transfers between devices with their start and end apart: 35, of which 7 were waited for; matrix products, arithmetic and copies ran while one was open for 3% of the time, Pallas kernels for 54%

profile of v7, /device:TPU:0, one launch (start us, length us, event | category | flops | bytes accessed | tf_op | source)
XLA Modules:
  0.0 113.8 jit_solution(6749596162831030037)
XLA Ops:
  1.5 2.5 %collective-permute-start.2 = (f32[16,128]{1,0:T(8,128)S(1)}, f32[16,128]{1,0:T(8,128)S(1)}, u32[]{:S(2)}, u32[]{:S(2)}) collective-permute-start(f32[16,128]{1,0:T(8,128)S(1)} %gates.1), channel_id=1, source_target_pairs={{0,3},{1,2},{2,1},{3,0},{4,7},{5,6},{6,5},{7,4},{8,11},{9,10},{10,... | collective-permute-start | bytes 24584 | tf_op jit(solution)/shard_map/ppermute | solution.py:93
  4.7 2.0 %collective-permute-start.6 = (bf16[64,3584]{1,0:T(8,128)(2,1)}, bf16[64,3584]{1,0:T(8,128)(2,1)S(1)}, u32[]{:S(2)}, u32[]{:S(2)}) collective-permute-start(bf16[64,3584]{1,0:T(8,128)(2,1)} %refs_0_.1), channel_id=1, source_target_pairs={{0,4},{1,5},{4,8},{5,9},{8,12},{9,13},{12,14},{13,15},{14,10},{15,... | collective-permute-start | bytes 1376264 | tf_op jit(solution)/shard_map/ppermute | solution.py:89
  6.8 1.5 %collective-permute-done.1 = f32[16,128]{1,0:T(8,128)S(1)} collective-permute-done((f32[16,128]{1,0:T(8,128)S(1)}, f32[16,128]{1,0:T(8,128)S(1)}, u32[]{:S(2)}, u32[]{:S(2)}) %collective-permute-start.1) | collective-permute-done | bytes 8224 | tf_op jit(solution)/shard_map/ppermute | solution.py:93
  8.3 1.6 %collective-permute-start.3 = (f32[4,4,128]{2,0,1:T(4,128)S(1)}, f32[4,4,128]{2,0,1:T(4,128)S(1)}, u32[]{:S(2)}, u32[]{:S(2)}) collective-permute-start(f32[4,4,128]{2,0,1:T(4,128)S(1)} %bitcast.37), channel_id=1, source_target_pairs={{0,4},{1,5},{2,6},{3,7},{4,0},{5,1},{6,2},{7,3},{8,12},{9,13},{10,... | collective-permute-start | bytes 24584 | tf_op jit(solution)/shard_map/ppermute | solution.py:93
  10.0 2.6 %collective-permute-start.4 = (f32[4,4,128]{2,0,1:T(4,128)S(1)}, f32[4,4,128]{2,0,1:T(4,128)S(1)}, u32[]{:S(2)}, u32[]{:S(2)}) collective-permute-start(f32[4,4,128]{2,0,1:T(4,128)S(1)} %bitcast.38), channel_id=1, source_target_pairs={{0,8},{1,9},{2,10},{3,11},{4,12},{5,13},{6,14},{7,15},{8,0},{9,1},... | collective-permute-start | bytes 24584 | tf_op jit(solution)/shard_map/ppermute | solution.py:93
  12.8 10.3 %raw_forward.2.refs_0_ = bf16[768,1792]{1,0:T(8,128)(2,1)} custom-call(bf16[768,2048]{1,0:T(8,128)(2,1)} %bitcast.51, bf16[2048,3584]{1,0:T(8,128)(2,1)} %bitcast.30), custom_call_target="tpu_custom_call" | custom-call | flops 5637144576 | bytes 13238272 | tf_op jit(solution)/shard_map/raw_forward/pallas_call | solution.py:263
  24.5 1.4 %collective-permute-start.12 = (bf16[64,3584]{1,0:T(8,128)(2,1)S(1)}, bf16[64,3584]{1,0:T(8,128)(2,1)S(1)}, u32[]{:S(2)}, u32[]{:S(2)}) collective-permute-start(bf16[64,3584]{1,0:T(8,128)(2,1)S(1)} %collective-permute-done.7.refs_4_), channel_id=1, source_target_pairs={{0,2},{1,3},{4,0},{5,1},{8,4},{9,5},{12,8},{13,9},{14,12},{15,13},... | collective-permute-start | bytes 1376264 | tf_op jit(solution)/shard_map/ppermute | solution.py:89
  26.1 10.2 %raw_forward.3.refs_1_ = bf16[768,1792]{1,0:T(8,128)(2,1)} custom-call(bf16[768,2048]{1,0:T(8,128)(2,1)} %bitcast.52, bf16[2048,3584]{1,0:T(8,128)(2,1)} %bitcast.31), custom_call_target="tpu_custom_call" | custom-call | flops 5637144576 | bytes 13238272 | tf_op jit(solution)/shard_map/raw_forward/pallas_call | solution.py:263
  37.9 4.4 %spread_tokens.2 = (bf16[256,3584]{1,0:T(8,128)(2,1)S(1)}, bf16[128,3584]{1,0:T(8,128)(2,1)S(1)}, bf16[128,3584]{1,0:T(8,128)(2,1)}) custom-call(s32[17]{0:T(128)S(1)} %pad_add_fusion.where, f32[8,128]{1,0:T(8,128)S(1)} %squeeze.20.gates, bf16[768,1792]{1,0:T(8,128)(2,1)} %raw_forward.2.refs_0_, bf16[768,1792]{1,0:T(8,128)(2,1)} %raw_forward.3.refs_1_), custom_call_target="tpu_custom_call" | custom-call | flops 1048576 | bytes 16384 | tf_op jit(solution)/shard_map/spread_tokens/pallas_call | solution.py:120
  43.5 1.4 %collective-permute-start.16 = (bf16[64,3584]{1,0:T(8,128)(2,1)S(1)}, bf16[64,3584]{1,0:T(8,128)(2,1)S(1)}, u32[]{:S(2)}, u32[]{:S(2)}) collective-permute-start(bf16[64,3584]{1,0:T(8,128)(2,1)S(1)} %collective-permute-done.12.refs_0_), channel_id=1, source_target_pairs={{0,2},{1,3},{4,0},{5,1},{8,4},{9,5},{12,8},{13,9},{14,12},{15,13},... | collective-permute-start | bytes 1376264 | tf_op jit(solution)/shard_map/ppermute | solution.py:89
  44.9 1.1 add_convert_fusion.6
  46.0 0.9 collective-permute-start.18
  47.7 1.1 collective-permute-start.19
  49.0 3.4 %spread_tokens.3 = (bf16[256,3584]{1,0:T(8,128)(2,1)S(1)}, bf16[128,3584]{1,0:T(8,128)(2,1)S(1)}, bf16[128,3584]{1,0:T(8,128)(2,1)S(1)}) custom-call(s32[17]{0:T(128)S(1)} %pad_add_fusion.where, f32[8,128]{1,0:T(8,128)S(1)} %squeeze.20.gates, bf16[768,1792]{1,0:T(8,128)(2,1)} %raw_forward.2.refs_0_, bf16[768,1792]{1,0:T(8,128)(2,1)} %raw_forward.3.refs_1_), custom_call_target="tpu_custom_call" | custom-call | flops 1048576 | bytes 16384 | tf_op jit(solution)/shard_map/spread_tokens/pallas_call | solution.py:120
  52.5 11.8 %backward.3 = (bf16[384,1024]{1,0:T(8,128)(2,1)S(1)}, bf16[384,1024]{1,0:T(8,128)(2,1)S(1)}) custom-call(s32[17]{0:T(128)S(1)} %pad_add_fusion.where, s32[1]{0:T(128)} %bitcast.20.pipe, f32[8,128]{1,0:T(8,128)S(1)} %squeeze.21.gates, bf16[2048,3584]{1,0:T(8,128)(2,1)} %bitcast.32, bf16[64,3584]{1,0:T(8,128)(2,1)S(1)} %copy-done.1, ...), custom_call_target="tpu_custom_call" | custom-call | flops 88080384 | bytes 339968 | tf_op jit(solution)/shard_map/backward/pallas_call | solution.py:120
  64.2 1.4 %collective-permute-done.18 = bf16[64,3584]{1,0:T(8,128)(2,1)} collective-permute-done((bf16[64,3584]{1,0:T(8,128)(2,1)}, bf16[64,3584]{1,0:T(8,128)(2,1)}, u32[]{:S(2)}, u32[]{:S(2)}) %collective-permute-start.18) | collective-permute-done | bytes 458784 | tf_op jit(solution)/shard_map/ppermute | solution.py:89
  65.6 1.1 collective-permute-done.19
  67.3 1.8 %add_convert_fusion.4 = (bf16[64,3584]{1,0:T(8,128)(2,1)S(1)}, bf16[64,3584]{1,0:T(8,128)(2,1)S(1)}) fusion(bf16[64,3584]{1,0:T(8,128)(2,1)} %collective-permute-done.19, bf16[128,3584]{1,0:T(8,128)(2,1)} %collective-permute-done.14, bf16[256,3584]{1,0:T(8,128)(2,1)S(1)} %get-tuple-element.84, bf16[64,3584]{1,0:T(8,128)(2,1)} %collective-permute-done.18), kind=kLoop, calls=%fused_computation.4 | loop fusion | flops 2752512 | bytes 3670016 | tf_op jit(solution)/shard_map/convert_element_type | solution.py:32
  69.0 1.1 collective-permute-start.24
  70.1 1.1 collective-permute-start.25
  71.2 1.5 %collective-permute-start.30 = (bf16[384,1024]{1,0:T(8,128)(2,1)S(1)}, bf16[384,1024]{1,0:T(8,128)(2,1)S(1)}, u32[]{:S(2)}, u32[]{:S(2)}) collective-permute-start(bf16[384,1024]{1,0:T(8,128)(2,1)S(1)} %get-tuple-element.108), channel_id=1, source_target_pairs={{0,16},{16,0},{1,17},{17,1},{2,18},{18,2},{3,19},{19,3},{4,20},{20... | collective-permute-start | bytes 2359304 | tf_op jit(solution)/shard_map/ppermute | solution.py:101
  72.7 9.4 %backward.4 = (bf16[192,1024]{1,0:T(8,128)(2,1)S(1)}, bf16[192,1024]{1,0:T(8,128)(2,1)S(1)}) custom-call(s32[17]{0:T(128)S(1)} %pad_add_fusion.where, s32[1]{0:T(128)} %bitcast.20.pipe, f32[8,128]{1,0:T(8,128)S(1)} %squeeze.21.gates, bf16[2048,3584]{1,0:T(8,128)(2,1)} %bitcast.33, bf16[64,3584]{1,0:T(8,128)(2,1)S(1)} %collective-permute-done.12.refs_0_, ...), custom_call_target="tpu_custom_call" | custom-call | flops 44040192 | bytes 284672 | tf_op jit(solution)/shard_map/backward/pallas_call | solution.py:120
  84.0 1.5 %collective-permute-start.28 = (bf16[64,3584]{1,0:T(8,128)(2,1)S(1)}, bf16[64,3584]{1,0:T(8,128)(2,1)S(1)}, u32[]{:S(2)}, u32[]{:S(2)}) collective-permute-start(bf16[64,3584]{1,0:T(8,128)(2,1)S(1)} %get-tuple-element.106), channel_id=1, source_target_pairs={{0,4},{1,5},{4,8},{5,9},{8,12},{9,13},{12,14},{13,15},{14,10},{15,... | collective-permute-start | bytes 1376264 | tf_op jit(solution)/shard_map/ppermute | solution.py:89
  85.5 1.5 %collective-permute-start.31 = (bf16[192,1024]{1,0:T(8,128)(2,1)S(1)}, bf16[192,1024]{1,0:T(8,128)(2,1)S(1)}, u32[]{:S(2)}, u32[]{:S(2)}) collective-permute-start(bf16[192,1024]{1,0:T(8,128)(2,1)S(1)} %get-tuple-element.109), channel_id=1, source_target_pairs={{0,16},{16,0},{1,17},{17,1},{2,18},{18,2},{3,19},{19,3},{4,20},{20... | collective-permute-start | bytes 1179656 | tf_op jit(solution)/shard_map/ppermute | solution.py:101
  87.0 9.4 %backward.5 = (bf16[192,1024]{1,0:T(8,128)(2,1)S(1)}, bf16[192,1024]{1,0:T(8,128)(2,1)S(1)}) custom-call(s32[17]{0:T(128)S(1)} %pad_add_fusion.where, s32[1]{0:T(128)} %bitcast.20.pipe, f32[8,128]{1,0:T(8,128)S(1)} %squeeze.21.gates, bf16[2048,3584]{1,0:T(8,128)(2,1)} %bitcast.34, bf16[64,3584]{1,0:T(8,128)(2,1)S(1)} %collective-permute-done.16.refs_0_, ...), custom_call_target="tpu_custom_call" | custom-call | flops 44040192 | bytes 284672 | tf_op jit(solution)/shard_map/backward/pallas_call | solution.py:120
  96.4 2.8 %collective-permute-done.31.refs_3_ = bf16[192,1024]{1,0:T(8,128)(2,1)S(1)} collective-permute-done((bf16[192,1024]{1,0:T(8,128)(2,1)S(1)}, bf16[192,1024]{1,0:T(8,128)(2,1)S(1)}, u32[]{:S(2)}, u32[]{:S(2)}) %collective-permute-start.31) | collective-permute-done | bytes 393248 | tf_op jit(solution)/shard_map/ppermute | solution.py:101
  99.5 1.8 %collective-permute-start.32 = (bf16[64,3584]{1,0:T(8,128)(2,1)S(1)}, bf16[64,3584]{1,0:T(8,128)(2,1)S(1)}, u32[]{:S(2)}, u32[]{:S(2)}) collective-permute-start(bf16[64,3584]{1,0:T(8,128)(2,1)S(1)} %get-tuple-element.126), channel_id=1, source_target_pairs={{0,4},{1,5},{4,8},{5,9},{8,12},{9,13},{12,14},{13,15},{14,10},{15,... | collective-permute-start | bytes 1376264 | tf_op jit(solution)/shard_map/ppermute | solution.py:89
  101.6 1.5 %collective-permute-start.34 = (bf16[192,1024]{1,0:T(8,128)(2,1)S(1)}, bf16[192,1024]{1,0:T(8,128)(2,1)S(1)}, u32[]{:S(2)}, u32[]{:S(2)}) collective-permute-start(bf16[192,1024]{1,0:T(8,128)(2,1)S(1)} %get-tuple-element.117), channel_id=1, source_target_pairs={{0,16},{16,0},{1,17},{17,1},{2,18},{18,2},{3,19},{19,3},{4,20},{20... | collective-permute-start | bytes 1179656 | tf_op jit(solution)/shard_map/ppermute | solution.py:101
  103.1 1.6 %collect.2.refs_2_ = bf16[768,1024]{1,0:T(8,128)(2,1)} custom-call(s32[17]{0:T(128)S(1)} %pad_add_fusion.where, bf16[384,1024]{1,0:T(8,128)(2,1)S(1)} %get-tuple-element.113.refs_0_, bf16[384,1024]{1,0:T(8,128)(2,1)S(1)} %collective-permute-done.30.refs_1_, bf16[192,1024]{1,0:T(8,128)(2,1)S(1)} %get-tuple-element.115.refs_2_, ...), custom_call_target="tpu_custom_call" | custom-call | flops 1048576 | bytes 3538944 | tf_op jit(solution)/shard_map/collect/pallas_call | solution.py:451
  104.8 6.7 %collective-permute-done.34.refs_1_ = bf16[192,1024]{1,0:T(8,128)(2,1)S(1)} collective-permute-done((bf16[192,1024]{1,0:T(8,128)(2,1)S(1)}, bf16[192,1024]{1,0:T(8,128)(2,1)S(1)}, u32[]{:S(2)}, u32[]{:S(2)}) %collective-permute-start.34) | collective-permute-done | bytes 393248 | tf_op jit(solution)/shard_map/ppermute | solution.py:101
  111.4 1.3 %collect.3 = bf16[768,1024]{1,0:T(8,128)(2,1)} custom-call(s32[17]{0:T(128)S(1)} %pad_add_fusion.where, bf16[192,1024]{1,0:T(8,128)(2,1)S(1)} %get-tuple-element.112.refs_0_, bf16[192,1024]{1,0:T(8,128)(2,1)S(1)} %collective-permute-done.34.refs_1_, bf16[768,1024]{1,0:T(8,128)(2,1)} %collect.2.refs_2_), custom_call_target="tpu_custom_call", output_to_operand_aliasing={{}: (3, {})} | custom-call | flops 1048576 | bytes 1179648 | tf_op jit(solution)/shard_map/collect/pallas_call | solution.py:451
  112.8 1.0 add_convert_fusion
  (83 shorter events, 10.2 us)
Async XLA Ops:
  1.5 5.3 %collective-permute-start.2 = (f32[16,128]{1,0:T(8,128)S(1)}, f32[16,128]{1,0:T(8,128)S(1)}, u32[]{:S(2)}, u32[]{:S(2)}) collective-permute-start(f32[16,128]{1,0:T(8,128)S(1)} %gates.1), channel_id=1, source_target_pairs={{0,3},{1,2},{2,1},{3,0},{4,7},{5,6},{6,5},{7,4},{8,11},{9,10},{10,... | collective-permute-start | bytes 24584 | tf_op jit(solution)/shard_map/ppermute | solution.py:93
  4.6 3.7 %collective-permute-start.1 = (f32[16,128]{1,0:T(8,128)S(1)}, f32[16,128]{1,0:T(8,128)S(1)}, u32[]{:S(2)}, u32[]{:S(2)}) collective-permute-start(f32[16,128]{1,0:T(8,128)S(1)} %gates.1), channel_id=1, source_target_pairs={{0,2},{1,3},{2,0},{3,1},{4,6},{5,7},{6,4},{7,5},{8,10},{9,11},{10,... | collective-permute-start | bytes 24584 | tf_op jit(solution)/shard_map/ppermute | solution.py:93
  4.7 18.5 %collective-permute-start.6 = (bf16[64,3584]{1,0:T(8,128)(2,1)}, bf16[64,3584]{1,0:T(8,128)(2,1)S(1)}, u32[]{:S(2)}, u32[]{:S(2)}) collective-permute-start(bf16[64,3584]{1,0:T(8,128)(2,1)} %refs_0_.1), channel_id=1, source_target_pairs={{0,4},{1,5},{4,8},{5,9},{8,12},{9,13},{12,14},{13,15},{14,10},{15,... | collective-permute-start | bytes 1376264 | tf_op jit(solution)/shard_map/ppermute | solution.py:89
  6.7 16.5 %collective-permute-start.7 = (bf16[64,3584]{1,0:T(8,128)(2,1)}, bf16[64,3584]{1,0:T(8,128)(2,1)S(1)}, u32[]{:S(2)}, u32[]{:S(2)}) collective-permute-start(bf16[64,3584]{1,0:T(8,128)(2,1)} %refs_0_.1), channel_id=1, source_target_pairs={{0,2},{1,3},{4,0},{5,1},{8,4},{9,5},{12,8},{13,9},{14,12},{15,13},... | collective-permute-start | bytes 1376264 | tf_op jit(solution)/shard_map/ppermute | solution.py:89
  8.3 14.8 %collective-permute-start.3 = (f32[4,4,128]{2,0,1:T(4,128)S(1)}, f32[4,4,128]{2,0,1:T(4,128)S(1)}, u32[]{:S(2)}, u32[]{:S(2)}) collective-permute-start(f32[4,4,128]{2,0,1:T(4,128)S(1)} %bitcast.37), channel_id=1, source_target_pairs={{0,4},{1,5},{2,6},{3,7},{4,0},{5,1},{6,2},{7,3},{8,12},{9,13},{10,... | collective-permute-start | bytes 24584 | tf_op jit(solution)/shard_map/ppermute | solution.py:93
  10.0 13.2 %collective-permute-start.4 = (f32[4,4,128]{2,0,1:T(4,128)S(1)}, f32[4,4,128]{2,0,1:T(4,128)S(1)}, u32[]{:S(2)}, u32[]{:S(2)}) collective-permute-start(f32[4,4,128]{2,0,1:T(4,128)S(1)} %bitcast.38), channel_id=1, source_target_pairs={{0,8},{1,9},{2,10},{3,11},{4,12},{5,13},{6,14},{7,15},{8,0},{9,1},... | collective-permute-start | bytes 24584 | tf_op jit(solution)/shard_map/ppermute | solution.py:93
  12.6 10.7 %collective-permute-start.5 = (f32[4,4,128]{2,0,1:T(4,128)S(1)}, f32[4,4,128]{2,0,1:T(4,128)S(1)}, u32[]{:S(2)}, u32[]{:S(2)}) collective-permute-start(f32[4,4,128]{2,0,1:T(4,128)S(1)} %bitcast.39), channel_id=1, source_target_pairs={{0,12},{1,13},{2,14},{3,15},{4,8},{5,9},{6,10},{7,11},{8,4},{9,5},... | collective-permute-start | bytes 24584 | tf_op jit(solution)/shard_map/ppermute | solution.py:93
  23.1 13.2 %collective-permute-start.8 = (bf16[64,3584]{1,0:T(8,128)(2,1)S(1)}, bf16[64,3584]{1,0:T(8,128)(2,1)S(1)}, u32[]{:S(2)}, u32[]{:S(2)}) collective-permute-start(bf16[64,3584]{1,0:T(8,128)(2,1)S(1)} %copy-done), channel_id=1, source_target_pairs={{0,1},{1,0},{2,3},{3,2},{4,5},{5,4},{6,7},{7,6},{8,9},{9,8},{10,11... | collective-permute-start | bytes 1376264 | tf_op jit(solution)/shard_map/ppermute | solution.py:93
  23.3 14.6 %collective-permute-start.9 = (bf16[64,3584]{1,0:T(8,128)(2,1)S(1)}, bf16[64,3584]{1,0:T(8,128)(2,1)}, u32[]{:S(2)}, u32[]{:S(2)}) collective-permute-start(bf16[64,3584]{1,0:T(8,128)(2,1)S(1)} %collective-permute-done.6.refs_2_), channel_id=1, source_target_pairs={{0,1},{1,0},{2,3},{3,2},{4,5},{5,4},{6,7},{7,6},{8,9},{9,8},{10,11... | collective-permute-start | bytes 1376264 | tf_op jit(solution)/shard_map/ppermute | solution.py:93
  23.8 18.4 %collective-permute-start.11 = (bf16[64,3584]{1,0:T(8,128)(2,1)S(1)}, bf16[64,3584]{1,0:T(8,128)(2,1)}, u32[]{:S(2)}, u32[]{:S(2)}) collective-permute-start(bf16[64,3584]{1,0:T(8,128)(2,1)S(1)} %collective-permute-done.6.refs_2_), channel_id=1, source_target_pairs={{0,4},{1,5},{4,8},{5,9},{8,12},{9,13},{12,14},{13,15},{14,10},{15,... | collective-permute-start | bytes 1376264 | tf_op jit(solution)/shard_map/ppermute | solution.py:89
  24.5 11.9 %collective-permute-start.10 = (bf16[64,3584]{1,0:T(8,128)(2,1)S(1)}, bf16[64,3584]{1,0:T(8,128)(2,1)S(1)}, u32[]{:S(2)}, u32[]{:S(2)}) collective-permute-start(bf16[64,3584]{1,0:T(8,128)(2,1)S(1)} %collective-permute-done.7.refs_4_), channel_id=1, source_target_pairs={{0,1},{1,0},{2,3},{3,2},{4,5},{5,4},{6,7},{7,6},{8,9},{9,8},{10,11... | collective-permute-start | bytes 1376264 | tf_op jit(solution)/shard_map/ppermute | solution.py:93
  24.5 17.8 %collective-permute-start.12 = (bf16[64,3584]{1,0:T(8,128)(2,1)S(1)}, bf16[64,3584]{1,0:T(8,128)(2,1)S(1)}, u32[]{:S(2)}, u32[]{:S(2)}) collective-permute-start(bf16[64,3584]{1,0:T(8,128)(2,1)S(1)} %collective-permute-done.7.refs_4_), channel_id=1, source_target_pairs={{0,2},{1,3},{4,0},{5,1},{8,4},{9,5},{12,8},{13,9},{14,12},{15,13},... | collective-permute-start | bytes 1376264 | tf_op jit(solution)/shard_map/ppermute | solution.py:89
  42.6 4.4 %collective-permute-start.13 = (bf16[64,3584]{1,0:T(8,128)(2,1)}, bf16[64,3584]{1,0:T(8,128)(2,1)S(1)}, u32[]{:S(2)}, u32[]{:S(2)}) collective-permute-start(bf16[64,3584]{1,0:T(8,128)(2,1)} %collective-permute-done.11.refs_6_), channel_id=1, source_target_pairs={{0,1},{1,0},{2,3},{3,2},{4,5},{5,4},{6,7},{7,6},{8,9},{9,8},{10,11... | collective-permute-start | bytes 1376264 | tf_op jit(solution)/shard_map/ppermute | solution.py:93
  42.8 21.4 %collective-permute-start.15 = (bf16[64,3584]{1,0:T(8,128)(2,1)}, bf16[64,3584]{1,0:T(8,128)(2,1)S(1)}, u32[]{:S(2)}, u32[]{:S(2)}) collective-permute-start(bf16[64,3584]{1,0:T(8,128)(2,1)} %collective-permute-done.11.refs_6_), channel_id=1, source_target_pairs={{0,4},{1,5},{4,8},{5,9},{8,12},{9,13},{12,14},{13,15},{14,10},{15,... | collective-permute-start | bytes 1376264 | tf_op jit(solution)/shard_map/ppermute | solution.py:89
  43.5 5.4 %collective-permute-start.14 = (bf16[128,3584]{1,0:T(8,128)(2,1)}, bf16[128,3584]{1,0:T(8,128)(2,1)}, u32[]{:S(2)}, u32[]{:S(2)}) collective-permute-start(bf16[128,3584]{1,0:T(8,128)(2,1)} %get-tuple-element.73), channel_id=1, source_target_pairs={{0,1},{1,0},{2,3},{3,2},{4,5},{5,4},{6,7},{7,6},{8,9},{9,8},{10,11... | collective-permute-start | bytes 2752520 | tf_op jit(solution)/shard_map/ppermute | solution.py:93
  43.5 20.7 %collective-permute-start.16 = (bf16[64,3584]{1,0:T(8,128)(2,1)S(1)}, bf16[64,3584]{1,0:T(8,128)(2,1)S(1)}, u32[]{:S(2)}, u32[]{:S(2)}) collective-permute-start(bf16[64,3584]{1,0:T(8,128)(2,1)S(1)} %collective-permute-done.12.refs_0_), channel_id=1, source_target_pairs={{0,2},{1,3},{4,0},{5,1},{8,4},{9,5},{12,8},{13,9},{14,12},{15,13},... | collective-permute-start | bytes 1376264 | tf_op jit(solution)/shard_map/ppermute | solution.py:89
  46.0 19.6 %collective-permute-start.18 = (bf16[64,3584]{1,0:T(8,128)(2,1)}, bf16[64,3584]{1,0:T(8,128)(2,1)}, u32[]{:S(2)}, u32[]{:S(2)}) collective-permute-start(bf16[64,3584]{1,0:T(8,128)(2,1)} %get-tuple-element.125), channel_id=1, source_target_pairs={{0,4},{1,5},{4,8},{5,9},{8,12},{9,13},{12,14},{13,15},{14,10},{15,... | collective-permute-start | bytes 1376264 | tf_op jit(solution)/shard_map/ppermute | solution.py:89
  47.7 19.1 %collective-permute-start.19 = (bf16[64,3584]{1,0:T(8,128)(2,1)}, bf16[64,3584]{1,0:T(8,128)(2,1)}, u32[]{:S(2)}, u32[]{:S(2)}) collective-permute-start(bf16[64,3584]{1,0:T(8,128)(2,1)} %get-tuple-element.124), channel_id=1, source_target_pairs={{0,2},{1,3},{4,0},{5,1},{8,4},{9,5},{12,8},{13,9},{14,12},{15,13},... | collective-permute-start | bytes 1376264 | tf_op jit(solution)/shard_map/ppermute | solution.py:89
  48.9 23.8 %collective-permute-start.22 = (bf16[64,3584]{1,0:T(8,128)(2,1)S(1)}, bf16[64,3584]{1,0:T(8,128)(2,1)S(1)}, u32[]{:S(2)}, u32[]{:S(2)}) collective-permute-start(bf16[64,3584]{1,0:T(8,128)(2,1)S(1)} %collective-permute-done.12.refs_0_), channel_id=1, source_target_pairs={{0,1},{1,0},{2,3},{3,2},{4,5},{5,4},{6,7},{7,6},{8,9},{9,8},{10,11... | collective-permute-start | bytes 1376264 | tf_op jit(solution)/shard_map/ppermute | solution.py:93
  66.7 3.3 %collective-permute-start.20 = (bf16[128,3584]{1,0:T(8,128)(2,1)S(1)}, bf16[128,3584]{1,0:T(8,128)(2,1)S(1)}, u32[]{:S(2)}, u32[]{:S(2)}) collective-permute-start(bf16[128,3584]{1,0:T(8,128)(2,1)S(1)} %get-tuple-element.88), channel_id=1, source_target_pairs={{0,1},{1,0},{2,3},{3,2},{4,5},{5,4},{6,7},{7,6},{8,9},{9,8},{10,11... | collective-permute-start | bytes 2752520 | tf_op jit(solution)/shard_map/ppermute | solution.py:93
  66.7 4.4 %collective-permute-start.21 = (bf16[128,3584]{1,0:T(8,128)(2,1)S(1)}, bf16[128,3584]{1,0:T(8,128)(2,1)S(1)}, u32[]{:S(2)}, u32[]{:S(2)}) collective-permute-start(bf16[128,3584]{1,0:T(8,128)(2,1)S(1)} %get-tuple-element.89), channel_id=1, source_target_pairs={{0,1},{1,0},{2,3},{3,2},{4,5},{5,4},{6,7},{7,6},{8,9},{9,8},{10,11... | collective-permute-start | bytes 2752520 | tf_op jit(solution)/shard_map/ppermute | solution.py:93
  67.2 5.4 %collective-permute-start.23 = (bf16[64,3584]{1,0:T(8,128)(2,1)S(1)}, bf16[64,3584]{1,0:T(8,128)(2,1)S(1)}, u32[]{:S(2)}, u32[]{:S(2)}) collective-permute-start(bf16[64,3584]{1,0:T(8,128)(2,1)S(1)} %collective-permute-done.15.refs_2_), channel_id=1, source_target_pairs={{0,1},{1,0},{2,3},{3,2},{4,5},{5,4},{6,7},{7,6},{8,9},{9,8},{10,11... | collective-permute-start | bytes 1376264 | tf_op jit(solution)/shard_map/ppermute | solution.py:93
  69.0 13.2 %collective-permute-start.24 = (bf16[64,3584]{1,0:T(8,128)(2,1)S(1)}, bf16[64,3584]{1,0:T(8,128)(2,1)S(1)}, u32[]{:S(2)}, u32[]{:S(2)}) collective-permute-start(bf16[64,3584]{1,0:T(8,128)(2,1)S(1)} %get-tuple-element.100), channel_id=1, source_target_pairs={{0,2},{1,3},{4,0},{5,1},{8,4},{9,5},{12,8},{13,9},{14,12},{15,13},... | collective-permute-start | bytes 1376264 | tf_op jit(solution)/shard_map/ppermute | solution.py:89
  70.1 12.7 %collective-permute-start.25 = (bf16[64,3584]{1,0:T(8,128)(2,1)S(1)}, bf16[64,3584]{1,0:T(8,128)(2,1)S(1)}, u32[]{:S(2)}, u32[]{:S(2)}) collective-permute-start(bf16[64,3584]{1,0:T(8,128)(2,1)S(1)} %collective-permute-done.15.refs_2_), channel_id=1, source_target_pairs={{0,4},{1,5},{4,8},{5,9},{8,12},{9,13},{12,14},{13,15},{14,10},{15,... | collective-permute-start | bytes 1376264 | tf_op jit(solution)/shard_map/ppermute | solution.py:89
  71.2 25.3 %collective-permute-start.30 = (bf16[384,1024]{1,0:T(8,128)(2,1)S(1)}, bf16[384,1024]{1,0:T(8,128)(2,1)S(1)}, u32[]{:S(2)}, u32[]{:S(2)}) collective-permute-start(bf16[384,1024]{1,0:T(8,128)(2,1)S(1)} %get-tuple-element.108), channel_id=1, source_target_pairs={{0,16},{16,0},{1,17},{17,1},{2,18},{18,2},{3,19},{19,3},{4,20},{20... | collective-permute-start | bytes 2359304 | tf_op jit(solution)/shard_map/ppermute | solution.py:101
  82.7 4.3 %collective-permute-start.27 = (bf16[64,3584]{1,0:T(8,128)(2,1)S(1)}, bf16[64,3584]{1,0:T(8,128)(2,1)S(1)}, u32[]{:S(2)}, u32[]{:S(2)}) collective-permute-start(bf16[64,3584]{1,0:T(8,128)(2,1)S(1)} %collective-permute-done.25.refs_2_), channel_id=1, source_target_pairs={{0,1},{1,0},{2,3},{3,2},{4,5},{5,4},{6,7},{7,6},{8,9},{9,8},{10,11... | collective-permute-start | bytes 1376264 | tf_op jit(solution)/shard_map/ppermute | solution.py:93
  83.4 15.8 %collective-permute-start.29 = (bf16[64,3584]{1,0:T(8,128)(2,1)S(1)}, bf16[64,3584]{1,0:T(8,128)(2,1)S(1)}, u32[]{:S(2)}, u32[]{:S(2)}) collective-permute-start(bf16[64,3584]{1,0:T(8,128)(2,1)S(1)} %add_convert_fusion.3), channel_id=1, source_target_pairs={{0,2},{1,3},{4,0},{5,1},{8,4},{9,5},{12,8},{13,9},{14,12},{15,13},... | collective-permute-start | bytes 1376264 | tf_op jit(solution)/shard_map/ppermute | solution.py:89
  84.0 15.2 %collective-permute-start.28 = (bf16[64,3584]{1,0:T(8,128)(2,1)S(1)}, bf16[64,3584]{1,0:T(8,128)(2,1)S(1)}, u32[]{:S(2)}, u32[]{:S(2)}) collective-permute-start(bf16[64,3584]{1,0:T(8,128)(2,1)S(1)} %get-tuple-element.106), channel_id=1, source_target_pairs={{0,4},{1,5},{4,8},{5,9},{8,12},{9,13},{12,14},{13,15},{14,10},{15,... | collective-permute-start | bytes 1376264 | tf_op jit(solution)/shard_map/ppermute | solution.py:89
  85.5 13.7 %collective-permute-start.31 = (bf16[192,1024]{1,0:T(8,128)(2,1)S(1)}, bf16[192,1024]{1,0:T(8,128)(2,1)S(1)}, u32[]{:S(2)}, u32[]{:S(2)}) collective-permute-start(bf16[192,1024]{1,0:T(8,128)(2,1)S(1)} %get-tuple-element.109), channel_id=1, source_target_pairs={{0,16},{16,0},{1,17},{17,1},{2,18},{18,2},{3,19},{19,3},{4,20},{20... | collective-permute-start | bytes 1179656 | tf_op jit(solution)/shard_map/ppermute | solution.py:101
  99.5 13.2 %collective-permute-start.32 = (bf16[64,3584]{1,0:T(8,128)(2,1)S(1)}, bf16[64,3584]{1,0:T(8,128)(2,1)S(1)}, u32[]{:S(2)}, u32[]{:S(2)}) collective-permute-start(bf16[64,3584]{1,0:T(8,128)(2,1)S(1)} %get-tuple-element.126), channel_id=1, source_target_pairs={{0,4},{1,5},{4,8},{5,9},{8,12},{9,13},{12,14},{13,15},{14,10},{15,... | collective-permute-start | bytes 1376264 | tf_op jit(solution)/shard_map/ppermute | solution.py:89
  101.3 11.4 %collective-permute-start.33 = (bf16[64,3584]{1,0:T(8,128)(2,1)S(1)}, bf16[64,3584]{1,0:T(8,128)(2,1)S(1)}, u32[]{:S(2)}, u32[]{:S(2)}) collective-permute-start(bf16[64,3584]{1,0:T(8,128)(2,1)S(1)} %get-tuple-element.127), channel_id=1, source_target_pairs={{0,2},{1,3},{4,0},{5,1},{8,4},{9,5},{12,8},{13,9},{14,12},{15,13},... | collective-permute-start | bytes 1376264 | tf_op jit(solution)/shard_map/ppermute | solution.py:89
  101.6 9.8 %collective-permute-start.34 = (bf16[192,1024]{1,0:T(8,128)(2,1)S(1)}, bf16[192,1024]{1,0:T(8,128)(2,1)S(1)}, u32[]{:S(2)}, u32[]{:S(2)}) collective-permute-start(bf16[192,1024]{1,0:T(8,128)(2,1)S(1)} %get-tuple-element.117), channel_id=1, source_target_pairs={{0,16},{16,0},{1,17},{17,1},{2,18},{18,2},{3,19},{19,3},{4,20},{20... | collective-permute-start | bytes 1179656 | tf_op jit(solution)/shard_map/ppermute | solution.py:101
  (13 other events, 61.2 us)

commit v8 on v6

--- a/solution.py
+++ b/solution.py
@@ -516,21 +516,18 @@
     down = step_ring(add(keep1[tokens : 2 * tokens], other1[tokens:]), -1)
     pair[-2] = core(got[-2])
     gate_a, pair[-2], other2 = tie(gate_a, pair[-2], other2)
-    keep2, other3, other4 = spread((1, -2, -1, 0), 2, gate_a)
+    keep2, other3 = spread((1, -2, -1, 0), 4, gate_a)
     keep2, gate_b = tie(keep2, gate_b)
     groups = (0, -1, 1, -2), (2, -3, 3), (-4,)
     for d in (0, -1, 1):
         pair[d] = pin(pair[d])
     send1, hold1 = bwd(groups[0], share=64)
 
-    def mine(i, other, *more):
+    def mine(i, *more):
         at = slice(i * tokens, (i + 1) * tokens)
-        other_at = slice(i % 2 * tokens, (i % 2 + 1) * tokens)
-        return add(keep2[at], other[other_at], *more)
-
-    send1, got[-3], got[3], up, down, other3, other4 = tie(
-        send1, got[-3], got[3], up, down, other3, other4
-    )
+        return add(keep2[at], other3[at], *more)
+
+    send1, got[-3], got[3], up, down, other3 = tie(send1, got[-3], got[3], up, down, other3)
     got[-4] = step_ring(got[-3], 1)
     up = add(keep1[2 * tokens : 3 * tokens], other2[:tokens], up)
     down = add(keep1[3 * tokens :], other2[tokens:], down)
@@ -538,23 +535,23 @@
     down = step_ring(down, -1)
     recv1 = across(send1)
     pair[2], pair[-3], pair[3] = core(got[2]), core(got[-3]), core(got[3])
-    other3, other4 = core(other3), core(other4)
-    gate_b, other3, other4 = tie(gate_b, other3, other4)
+    other3 = core(other3)
+    gate_b, other3 = tie(gate_b, other3)
     send2, hold2 = bwd(groups[1], share=64)
 
     hold2, send2, up, down, got[-4] = tie(hold2, send2, up, down, got[-4])
-    up, down = step_ring(up, 1), step_ring(mine(1, other3, down), -1)
+    up, down = step_ring(up, 1), step_ring(mine(1, down), -1)
     pair[-4] = core(got[-4])
     recv2 = across(send2)
     send3, hold3 = bwd(groups[2], share=64)
 
     send3, hold3, up, down, recv1 = tie(send3, hold3, up, down, recv1)
-    up, down = step_ring(mine(0, other3, up), 1), step_ring(mine(2, other4, down), -1)
+    up, down = step_ring(mine(0, up), 1), step_ring(mine(2, down), -1)
     recv3 = across(send3)
     hold3, recv2 = tie(hold3, recv2)
     grad = collect(groups[:2], where, (hold1, recv1, hold2, recv2), 8 * rows)
     grad, recv3 = tie(grad, recv3)
-    mixed_a = mine(3, other4, up, down)
+    mixed_a = mine(3, up, down)
     grad = collect(groups[2:], where, (hold3, recv3), 8 * rows, grad)
     return (mixed_a, grad[None])
 

time: 112 us -> 113 us (level)
    ppermute x18 -> x17, starting transfers between devices: 10 us -> 9.93 us  [xor(): return lax.ppermute(value, 'expert', [(i, i ^ bits) for i in range(16)])]
  transfers between devices with their start and end apart: 35 -> 34, of which waited for: 8 -> 8; matrix products, arithmetic and copies ran while one was open for 3% -> 3% of each run, Pallas kernels for 55% -> 55%
where the time goes in v8:
time: 113 us; the launch traced here: 112 us
  Pallas kernels  62.3 us (55%)
  starting transfers between devices  28.4 us (25%)
  waiting for transfers between devices  13.4 us (12%)
  other arithmetic  4.51 us (4%)
  local copies, waits for them, and re-layouts  2.66 us (2%)
    pallas_call x6, Pallas kernels, kernel_call(): pl.pallas_call(kernel, in_specs=in_specs, out_specs=[VMEM] * len(out_shap...  38.8 us
    pallas_call x2, Pallas kernels, raw_forward(): pl.pallas_call(functools.partial(raw_kernel, first), in_specs=[HBM, HBM],...  20.6 us
    ppermute x14, starting transfers between devices, step_ring(): return lax.ppermute(value, 'expert', pairs)  15.2 us
    ppermute x17, starting transfers between devices, xor(): return lax.ppermute(value, 'expert', [(i, i ^ bits) for i in range(16)])  9.93 us
    ppermute x3, waiting for transfers between devices, across(): return lax.ppermute(value, 'pipe', [(0, 1), (1, 0)])  6.04 us
    ppermute x14, waiting for transfers between devices, step_ring(): return lax.ppermute(value, 'expert', pairs)  5.86 us
    convert_element_type x5, other arithmetic, add(): return total.astype(BF16)  4.39 us
    ppermute x3, starting transfers between devices, across(): return lax.ppermute(value, 'pipe', [(0, 1), (1, 0)])  3.22 us
  transfers between devices with their start and end apart: 34, of which 8 were waited for; matrix products, arithmetic and copies ran while one was open for 3% of the time, Pallas kernels for 55%

profile of v8, /device:TPU:0, one launch (start us, length us, event | category | flops | bytes accessed | tf_op | source)
XLA Modules:
  0.0 112.2 jit_solution(15607173181829063341)
XLA Ops:
  1.5 2.5 %collective-permute-start.2 = (f32[16,128]{1,0:T(8,128)S(1)}, f32[16,128]{1,0:T(8,128)S(1)}, u32[]{:S(2)}, u32[]{:S(2)}) collective-permute-start(f32[16,128]{1,0:T(8,128)S(1)} %gates.1), channel_id=1, source_target_pairs={{0,3},{1,2},{2,1},{3,0},{4,7},{5,6},{6,5},{7,4},{8,11},{9,10},{10,... | collective-permute-start | bytes 24584 | tf_op jit(solution)/shard_map/ppermute | solution.py:93
  4.7 2.0 %collective-permute-start.6 = (bf16[64,3584]{1,0:T(8,128)(2,1)}, bf16[64,3584]{1,0:T(8,128)(2,1)S(1)}, u32[]{:S(2)}, u32[]{:S(2)}) collective-permute-start(bf16[64,3584]{1,0:T(8,128)(2,1)} %refs_0_.1), channel_id=1, source_target_pairs={{0,4},{1,5},{4,8},{5,9},{8,12},{9,13},{12,14},{13,15},{14,10},{15,... | collective-permute-start | bytes 1376264 | tf_op jit(solution)/shard_map/ppermute | solution.py:89
  6.8 1.5 %collective-permute-done.1 = f32[16,128]{1,0:T(8,128)S(1)} collective-permute-done((f32[16,128]{1,0:T(8,128)S(1)}, f32[16,128]{1,0:T(8,128)S(1)}, u32[]{:S(2)}, u32[]{:S(2)}) %collective-permute-start.1) | collective-permute-done | bytes 8224 | tf_op jit(solution)/shard_map/ppermute | solution.py:93
  8.3 1.6 %collective-permute-start.3 = (f32[4,4,128]{2,0,1:T(4,128)S(1)}, f32[4,4,128]{2,0,1:T(4,128)S(1)}, u32[]{:S(2)}, u32[]{:S(2)}) collective-permute-start(f32[4,4,128]{2,0,1:T(4,128)S(1)} %bitcast.37), channel_id=1, source_target_pairs={{0,4},{1,5},{2,6},{3,7},{4,0},{5,1},{6,2},{7,3},{8,12},{9,13},{10,... | collective-permute-start | bytes 24584 | tf_op jit(solution)/shard_map/ppermute | solution.py:93
  10.0 2.6 %collective-permute-start.4 = (f32[4,4,128]{2,0,1:T(4,128)S(1)}, f32[4,4,128]{2,0,1:T(4,128)S(1)}, u32[]{:S(2)}, u32[]{:S(2)}) collective-permute-start(f32[4,4,128]{2,0,1:T(4,128)S(1)} %bitcast.38), channel_id=1, source_target_pairs={{0,8},{1,9},{2,10},{3,11},{4,12},{5,13},{6,14},{7,15},{8,0},{9,1},... | collective-permute-start | bytes 24584 | tf_op jit(solution)/shard_map/ppermute | solution.py:93
  12.8 10.3 %raw_forward.2.refs_0_ = bf16[768,1792]{1,0:T(8,128)(2,1)} custom-call(bf16[768,2048]{1,0:T(8,128)(2,1)} %bitcast.51, bf16[2048,3584]{1,0:T(8,128)(2,1)} %bitcast.30), custom_call_target="tpu_custom_call" | custom-call | flops 5637144576 | bytes 13238272 | tf_op jit(solution)/shard_map/raw_forward/pallas_call | solution.py:263
  24.5 1.4 %collective-permute-start.12 = (bf16[64,3584]{1,0:T(8,128)(2,1)S(1)}, bf16[64,3584]{1,0:T(8,128)(2,1)S(1)}, u32[]{:S(2)}, u32[]{:S(2)}) collective-permute-start(bf16[64,3584]{1,0:T(8,128)(2,1)S(1)} %collective-permute-done.7.refs_4_), channel_id=1, source_target_pairs={{0,2},{1,3},{4,0},{5,1},{8,4},{9,5},{12,8},{13,9},{14,12},{15,13},... | collective-permute-start | bytes 1376264 | tf_op jit(solution)/shard_map/ppermute | solution.py:89
  26.1 10.2 %raw_forward.3.refs_1_ = bf16[768,1792]{1,0:T(8,128)(2,1)} custom-call(bf16[768,2048]{1,0:T(8,128)(2,1)} %bitcast.52, bf16[2048,3584]{1,0:T(8,128)(2,1)} %bitcast.31), custom_call_target="tpu_custom_call" | custom-call | flops 5637144576 | bytes 13238272 | tf_op jit(solution)/shard_map/raw_forward/pallas_call | solution.py:263
  38.0 4.4 %spread_tokens.2 = (bf16[256,3584]{1,0:T(8,128)(2,1)S(1)}, bf16[128,3584]{1,0:T(8,128)(2,1)S(1)}, bf16[128,3584]{1,0:T(8,128)(2,1)}) custom-call(s32[17]{0:T(128)S(1)} %pad_add_fusion.where, f32[8,128]{1,0:T(8,128)S(1)} %squeeze.20.gates, bf16[768,1792]{1,0:T(8,128)(2,1)} %raw_forward.2.refs_0_, bf16[768,1792]{1,0:T(8,128)(2,1)} %raw_forward.3.refs_1_), custom_call_target="tpu_custom_call" | custom-call | flops 1048576 | bytes 16384 | tf_op jit(solution)/shard_map/spread_tokens/pallas_call | solution.py:120
  43.6 1.4 %collective-permute-start.16 = (bf16[64,3584]{1,0:T(8,128)(2,1)S(1)}, bf16[64,3584]{1,0:T(8,128)(2,1)S(1)}, u32[]{:S(2)}, u32[]{:S(2)}) collective-permute-start(bf16[64,3584]{1,0:T(8,128)(2,1)S(1)} %collective-permute-done.12.refs_0_), channel_id=1, source_target_pairs={{0,2},{1,3},{4,0},{5,1},{8,4},{9,5},{12,8},{13,9},{14,12},{15,13},... | collective-permute-start | bytes 1376264 | tf_op jit(solution)/shard_map/ppermute | solution.py:89
  45.0 1.1 %add_convert_fusion.6 = (bf16[64,3584]{1,0:T(8,128)(2,1)}, bf16[64,3584]{1,0:T(8,128)(2,1)}) fusion(bf16[128,3584]{1,0:T(8,128)(2,1)S(1)} %collective-permute-done.17, bf16[256,3584]{1,0:T(8,128)(2,1)S(1)} %get-tuple-element.81), kind=kLoop, calls=%fused_computation.6 | loop fusion | flops 1835008 | bytes 2752512 | tf_op jit(solution)/shard_map/convert_element_type | solution.py:32
  47.8 1.1 %collective-permute-start.19 = (bf16[64,3584]{1,0:T(8,128)(2,1)}, bf16[64,3584]{1,0:T(8,128)(2,1)}, u32[]{:S(2)}, u32[]{:S(2)}) collective-permute-start(bf16[64,3584]{1,0:T(8,128)(2,1)} %get-tuple-element.120), channel_id=1, source_target_pairs={{0,2},{1,3},{4,0},{5,1},{8,4},{9,5},{12,8},{13,9},{14,12},{15,13},... | collective-permute-start | bytes 1376264 | tf_op jit(solution)/shard_map/ppermute | solution.py:89
  49.0 3.4 %spread_tokens.3 = (bf16[256,3584]{1,0:T(8,128)(2,1)S(1)}, bf16[256,3584]{1,0:T(8,128)(2,1)S(1)}) custom-call(s32[17]{0:T(128)S(1)} %pad_add_fusion.where, f32[8,128]{1,0:T(8,128)S(1)} %squeeze.20.gates, bf16[768,1792]{1,0:T(8,128)(2,1)} %raw_forward.2.refs_0_, bf16[768,1792]{1,0:T(8,128)(2,1)} %raw_forward.3.refs_1_), custom_call_target="tpu_custom_call" | custom-call | flops 1048576 | bytes 16384 | tf_op jit(solution)/shard_map/spread_tokens/pallas_call | solution.py:120
  52.5 11.8 %backward.3 = (bf16[384,1024]{1,0:T(8,128)(2,1)S(1)}, bf16[384,1024]{1,0:T(8,128)(2,1)S(1)}) custom-call(s32[17]{0:T(128)S(1)} %pad_add_fusion.where, s32[1]{0:T(128)} %bitcast.20.pipe, f32[8,128]{1,0:T(8,128)S(1)} %squeeze.21.gates, bf16[2048,3584]{1,0:T(8,128)(2,1)} %bitcast.32, bf16[64,3584]{1,0:T(8,128)(2,1)S(1)} %copy-done.1, ...), custom_call_target="tpu_custom_call" | custom-call | flops 88080384 | bytes 339968 | tf_op jit(solution)/shard_map/backward/pallas_call | solution.py:120
  64.2 1.5 %collective-permute-done.18 = bf16[64,3584]{1,0:T(8,128)(2,1)} collective-permute-done((bf16[64,3584]{1,0:T(8,128)(2,1)}, bf16[64,3584]{1,0:T(8,128)(2,1)}, u32[]{:S(2)}, u32[]{:S(2)}) %collective-permute-start.18) | collective-permute-done | bytes 458784 | tf_op jit(solution)/shard_map/ppermute | solution.py:89
  65.7 1.1 collective-permute-done.19
  67.8 1.8 %add_convert_fusion.4 = (bf16[64,3584]{1,0:T(8,128)(2,1)S(1)}, bf16[64,3584]{1,0:T(8,128)(2,1)S(1)}) fusion(bf16[64,3584]{1,0:T(8,128)(2,1)} %collective-permute-done.19, bf16[128,3584]{1,0:T(8,128)(2,1)} %collective-permute-done.14, bf16[256,3584]{1,0:T(8,128)(2,1)S(1)} %get-tuple-element.81, bf16[64,3584]{1,0:T(8,128)(2,1)} %collective-permute-done.18), kind=kLoop, calls=%fused_computation.4 | loop fusion | flops 2752512 | bytes 3670016 | tf_op jit(solution)/shard_map/convert_element_type | solution.py:32
  69.6 1.1 collective-permute-start.24
  70.7 1.9 %collective-permute-start.25 = (bf16[64,3584]{1,0:T(8,128)(2,1)S(1)}, bf16[64,3584]{1,0:T(8,128)(2,1)S(1)}, u32[]{:S(2)}, u32[]{:S(2)}) collective-permute-start(bf16[64,3584]{1,0:T(8,128)(2,1)S(1)} %collective-permute-done.15.refs_2_), channel_id=1, source_target_pairs={{0,4},{1,5},{4,8},{5,9},{8,12},{9,13},{12,14},{13,15},{14,10},{15,... | collective-permute-start | bytes 1376264 | tf_op jit(solution)/shard_map/ppermute | solution.py:89
  72.5 1.5 %collective-permute-start.29 = (bf16[384,1024]{1,0:T(8,128)(2,1)S(1)}, bf16[384,1024]{1,0:T(8,128)(2,1)S(1)}, u32[]{:S(2)}, u32[]{:S(2)}) collective-permute-start(bf16[384,1024]{1,0:T(8,128)(2,1)S(1)} %get-tuple-element.101), channel_id=1, source_target_pairs={{0,16},{16,0},{1,17},{17,1},{2,18},{18,2},{3,19},{19,3},{4,20},{20... | collective-permute-start | bytes 2359304 | tf_op jit(solution)/shard_map/ppermute | solution.py:101
  74.0 10.0 %backward.4 = (bf16[288,1024]{1,0:T(8,128)(2,1)S(1)}, bf16[288,1024]{1,0:T(8,128)(2,1)S(1)}) custom-call(s32[17]{0:T(128)S(1)} %pad_add_fusion.where, s32[1]{0:T(128)} %bitcast.20.pipe, f32[8,128]{1,0:T(8,128)S(1)} %squeeze.21.gates, bf16[2048,3584]{1,0:T(8,128)(2,1)} %bitcast.33, bf16[64,3584]{1,0:T(8,128)(2,1)S(1)} %collective-permute-done.12.refs_0_, ...), custom_call_target="tpu_custom_call" | custom-call | flops 66060288 | bytes 312320 | tf_op jit(solution)/shard_map/backward/pallas_call | solution.py:120
  84.5 1.9 %collective-permute-start.27 = (bf16[64,3584]{1,0:T(8,128)(2,1)S(1)}, bf16[64,3584]{1,0:T(8,128)(2,1)S(1)}, u32[]{:S(2)}, u32[]{:S(2)}) collective-permute-start(bf16[64,3584]{1,0:T(8,128)(2,1)S(1)} %get-tuple-element.99), channel_id=1, source_target_pairs={{0,4},{1,5},{4,8},{5,9},{8,12},{9,13},{12,14},{13,15},{14,10},{15,... | collective-permute-start | bytes 1376264 | tf_op jit(solution)/shard_map/ppermute | solution.py:89
  86.9 8.4 %backward.5 = (bf16[96,1024]{1,0:T(8,128)(2,1)S(1)}, bf16[96,1024]{1,0:T(8,128)(2,1)S(1)}) custom-call(s32[17]{0:T(128)S(1)} %pad_add_fusion.where, s32[1]{0:T(128)} %bitcast.20.pipe, f32[8,128]{1,0:T(8,128)S(1)} %squeeze.21.gates, bf16[2048,3584]{1,0:T(8,128)(2,1)} %bitcast.34, bf16[64,3584]{1,0:T(8,128)(2,1)S(1)} %collective-permute-done.25.refs_0_, ...), custom_call_target="tpu_custom_call" | custom-call | flops 22020096 | bytes 257024 | tf_op jit(solution)/shard_map/backward/pallas_call | solution.py:120
  95.3 1.9 %collective-permute-done.28 = bf16[64,3584]{1,0:T(8,128)(2,1)S(1)} collective-permute-done((bf16[64,3584]{1,0:T(8,128)(2,1)S(1)}, bf16[64,3584]{1,0:T(8,128)(2,1)S(1)}, u32[]{:S(2)}, u32[]{:S(2)}) %collective-permute-start.28) | collective-permute-done | bytes 458784 | tf_op jit(solution)/shard_map/ppermute | solution.py:89
  97.7 1.8 %collective-permute-start.30 = (bf16[64,3584]{1,0:T(8,128)(2,1)S(1)}, bf16[64,3584]{1,0:T(8,128)(2,1)S(1)}, u32[]{:S(2)}, u32[]{:S(2)}) collective-permute-start(bf16[64,3584]{1,0:T(8,128)(2,1)S(1)} %get-tuple-element.116), channel_id=1, source_target_pairs={{0,4},{1,5},{4,8},{5,9},{8,12},{9,13},{12,14},{13,15},{14,10},{15,... | collective-permute-start | bytes 1376264 | tf_op jit(solution)/shard_map/ppermute | solution.py:89
  99.8 1.2 %collective-permute-start.33 = (bf16[96,1024]{1,0:T(8,128)(2,1)S(1)}, bf16[96,1024]{1,0:T(8,128)(2,1)S(1)}, u32[]{:S(2)}, u32[]{:S(2)}) collective-permute-start(bf16[96,1024]{1,0:T(8,128)(2,1)S(1)} %get-tuple-element.111), channel_id=1, source_target_pairs={{0,16},{16,0},{1,17},{17,1},{2,18},{18,2},{3,19},{19,3},{4,20},{20... | collective-permute-start | bytes 589832 | tf_op jit(solution)/shard_map/ppermute | solution.py:101
  100.9 4.7 %collective-permute-done.32.refs_3_ = bf16[288,1024]{1,0:T(8,128)(2,1)S(1)} collective-permute-done((bf16[288,1024]{1,0:T(8,128)(2,1)S(1)}, bf16[288,1024]{1,0:T(8,128)(2,1)S(1)}, u32[]{:S(2)}, u32[]{:S(2)}) %collective-permute-start.32) | collective-permute-done | bytes 589856 | tf_op jit(solution)/shard_map/ppermute | solution.py:101
  105.6 1.7 %collect.2.refs_2_ = bf16[768,1024]{1,0:T(8,128)(2,1)} custom-call(s32[17]{0:T(128)S(1)} %pad_add_fusion.where, bf16[384,1024]{1,0:T(8,128)(2,1)S(1)} %get-tuple-element.107.refs_0_, bf16[384,1024]{1,0:T(8,128)(2,1)S(1)} %collective-permute-done.29.refs_1_, bf16[288,1024]{1,0:T(8,128)(2,1)S(1)} %get-tuple-element.109.refs_2_, ...), custom_call_target="tpu_custom_call" | custom-call | flops 1048576 | bytes 4128768 | tf_op jit(solution)/shard_map/collect/pallas_call | solution.py:451
  107.3 1.4 %collective-permute-done.33.refs_1_ = bf16[96,1024]{1,0:T(8,128)(2,1)S(1)} collective-permute-done((bf16[96,1024]{1,0:T(8,128)(2,1)S(1)}, bf16[96,1024]{1,0:T(8,128)(2,1)S(1)}, u32[]{:S(2)}, u32[]{:S(2)}) %collective-permute-start.33) | collective-permute-done | bytes 196640 | tf_op jit(solution)/shard_map/ppermute | solution.py:101
  108.7 1.3 %collect.3 = bf16[768,1024]{1,0:T(8,128)(2,1)} custom-call(s32[17]{0:T(128)S(1)} %pad_add_fusion.where, bf16[96,1024]{1,0:T(8,128)(2,1)S(1)} %get-tuple-element.106.refs_0_, bf16[96,1024]{1,0:T(8,128)(2,1)S(1)} %collective-permute-done.33.refs_1_, bf16[768,1024]{1,0:T(8,128)(2,1)} %collect.2.refs_2_), custom_call_target="tpu_custom_call", output_to_operand_aliasing={{}: (3, {})} | custom-call | flops 1048576 | bytes 589824 | tf_op jit(solution)/shard_map/collect/pallas_call | solution.py:451
  110.0 1.3 %collective-permute-done.31 = bf16[64,3584]{1,0:T(8,128)(2,1)S(1)} collective-permute-done((bf16[64,3584]{1,0:T(8,128)(2,1)S(1)}, bf16[64,3584]{1,0:T(8,128)(2,1)S(1)}, u32[]{:S(2)}, u32[]{:S(2)}) %collective-permute-start.31) | collective-permute-done | bytes 458784 | tf_op jit(solution)/shard_map/ppermute | solution.py:89
  111.2 1.0 add_convert_fusion
  (81 shorter events, 10.8 us)
Async XLA Ops:
  1.5 5.3 %collective-permute-start.2 = (f32[16,128]{1,0:T(8,128)S(1)}, f32[16,128]{1,0:T(8,128)S(1)}, u32[]{:S(2)}, u32[]{:S(2)}) collective-permute-start(f32[16,128]{1,0:T(8,128)S(1)} %gates.1), channel_id=1, source_target_pairs={{0,3},{1,2},{2,1},{3,0},{4,7},{5,6},{6,5},{7,4},{8,11},{9,10},{10,... | collective-permute-start | bytes 24584 | tf_op jit(solution)/shard_map/ppermute | solution.py:93
  4.6 3.7 %collective-permute-start.1 = (f32[16,128]{1,0:T(8,128)S(1)}, f32[16,128]{1,0:T(8,128)S(1)}, u32[]{:S(2)}, u32[]{:S(2)}) collective-permute-start(f32[16,128]{1,0:T(8,128)S(1)} %gates.1), channel_id=1, source_target_pairs={{0,2},{1,3},{2,0},{3,1},{4,6},{5,7},{6,4},{7,5},{8,10},{9,11},{10,... | collective-permute-start | bytes 24584 | tf_op jit(solution)/shard_map/ppermute | solution.py:93
  4.7 18.6 %collective-permute-start.6 = (bf16[64,3584]{1,0:T(8,128)(2,1)}, bf16[64,3584]{1,0:T(8,128)(2,1)S(1)}, u32[]{:S(2)}, u32[]{:S(2)}) collective-permute-start(bf16[64,3584]{1,0:T(8,128)(2,1)} %refs_0_.1), channel_id=1, source_target_pairs={{0,4},{1,5},{4,8},{5,9},{8,12},{9,13},{12,14},{13,15},{14,10},{15,... | collective-permute-start | bytes 1376264 | tf_op jit(solution)/shard_map/ppermute | solution.py:89
  6.7 16.5 %collective-permute-start.7 = (bf16[64,3584]{1,0:T(8,128)(2,1)}, bf16[64,3584]{1,0:T(8,128)(2,1)S(1)}, u32[]{:S(2)}, u32[]{:S(2)}) collective-permute-start(bf16[64,3584]{1,0:T(8,128)(2,1)} %refs_0_.1), channel_id=1, source_target_pairs={{0,2},{1,3},{4,0},{5,1},{8,4},{9,5},{12,8},{13,9},{14,12},{15,13},... | collective-permute-start | bytes 1376264 | tf_op jit(solution)/shard_map/ppermute | solution.py:89
  8.3 14.8 %collective-permute-start.3 = (f32[4,4,128]{2,0,1:T(4,128)S(1)}, f32[4,4,128]{2,0,1:T(4,128)S(1)}, u32[]{:S(2)}, u32[]{:S(2)}) collective-permute-start(f32[4,4,128]{2,0,1:T(4,128)S(1)} %bitcast.37), channel_id=1, source_target_pairs={{0,4},{1,5},{2,6},{3,7},{4,0},{5,1},{6,2},{7,3},{8,12},{9,13},{10,... | collective-permute-start | bytes 24584 | tf_op jit(solution)/shard_map/ppermute | solution.py:93
  10.0 13.2 %collective-permute-start.4 = (f32[4,4,128]{2,0,1:T(4,128)S(1)}, f32[4,4,128]{2,0,1:T(4,128)S(1)}, u32[]{:S(2)}, u32[]{:S(2)}) collective-permute-start(f32[4,4,128]{2,0,1:T(4,128)S(1)} %bitcast.38), channel_id=1, source_target_pairs={{0,8},{1,9},{2,10},{3,11},{4,12},{5,13},{6,14},{7,15},{8,0},{9,1},... | collective-permute-start | bytes 24584 | tf_op jit(solution)/shard_map/ppermute | solution.py:93
  12.6 10.7 %collective-permute-start.5 = (f32[4,4,128]{2,0,1:T(4,128)S(1)}, f32[4,4,128]{2,0,1:T(4,128)S(1)}, u32[]{:S(2)}, u32[]{:S(2)}) collective-permute-start(f32[4,4,128]{2,0,1:T(4,128)S(1)} %bitcast.39), channel_id=1, source_target_pairs={{0,12},{1,13},{2,14},{3,15},{4,8},{5,9},{6,10},{7,11},{8,4},{9,5},... | collective-permute-start | bytes 24584 | tf_op jit(solution)/shard_map/ppermute | solution.py:93
  23.1 13.2 %collective-permute-start.8 = (bf16[64,3584]{1,0:T(8,128)(2,1)S(1)}, bf16[64,3584]{1,0:T(8,128)(2,1)S(1)}, u32[]{:S(2)}, u32[]{:S(2)}) collective-permute-start(bf16[64,3584]{1,0:T(8,128)(2,1)S(1)} %copy-done), channel_id=1, source_target_pairs={{0,1},{1,0},{2,3},{3,2},{4,5},{5,4},{6,7},{7,6},{8,9},{9,8},{10,11... | collective-permute-start | bytes 1376264 | tf_op jit(solution)/shard_map/ppermute | solution.py:93
  23.3 14.7 %collective-permute-start.9 = (bf16[64,3584]{1,0:T(8,128)(2,1)S(1)}, bf16[64,3584]{1,0:T(8,128)(2,1)}, u32[]{:S(2)}, u32[]{:S(2)}) collective-permute-start(bf16[64,3584]{1,0:T(8,128)(2,1)S(1)} %collective-permute-done.6.refs_2_), channel_id=1, source_target_pairs={{0,1},{1,0},{2,3},{3,2},{4,5},{5,4},{6,7},{7,6},{8,9},{9,8},{10,11... | collective-permute-start | bytes 1376264 | tf_op jit(solution)/shard_map/ppermute | solution.py:93
  23.8 18.5 %collective-permute-start.11 = (bf16[64,3584]{1,0:T(8,128)(2,1)S(1)}, bf16[64,3584]{1,0:T(8,128)(2,1)}, u32[]{:S(2)}, u32[]{:S(2)}) collective-permute-start(bf16[64,3584]{1,0:T(8,128)(2,1)S(1)} %collective-permute-done.6.refs_2_), channel_id=1, source_target_pairs={{0,4},{1,5},{4,8},{5,9},{8,12},{9,13},{12,14},{13,15},{14,10},{15,... | collective-permute-start | bytes 1376264 | tf_op jit(solution)/shard_map/ppermute | solution.py:89
  24.5 11.9 %collective-permute-start.10 = (bf16[64,3584]{1,0:T(8,128)(2,1)S(1)}, bf16[64,3584]{1,0:T(8,128)(2,1)S(1)}, u32[]{:S(2)}, u32[]{:S(2)}) collective-permute-start(bf16[64,3584]{1,0:T(8,128)(2,1)S(1)} %collective-permute-done.7.refs_4_), channel_id=1, source_target_pairs={{0,1},{1,0},{2,3},{3,2},{4,5},{5,4},{6,7},{7,6},{8,9},{9,8},{10,11... | collective-permute-start | bytes 1376264 | tf_op jit(solution)/shard_map/ppermute | solution.py:93
  24.5 17.8 %collective-permute-start.12 = (bf16[64,3584]{1,0:T(8,128)(2,1)S(1)}, bf16[64,3584]{1,0:T(8,128)(2,1)S(1)}, u32[]{:S(2)}, u32[]{:S(2)}) collective-permute-start(bf16[64,3584]{1,0:T(8,128)(2,1)S(1)} %collective-permute-done.7.refs_4_), channel_id=1, source_target_pairs={{0,2},{1,3},{4,0},{5,1},{8,4},{9,5},{12,8},{13,9},{14,12},{15,13},... | collective-permute-start | bytes 1376264 | tf_op jit(solution)/shard_map/ppermute | solution.py:89
  42.6 4.4 %collective-permute-start.13 = (bf16[64,3584]{1,0:T(8,128)(2,1)}, bf16[64,3584]{1,0:T(8,128)(2,1)S(1)}, u32[]{:S(2)}, u32[]{:S(2)}) collective-permute-start(bf16[64,3584]{1,0:T(8,128)(2,1)} %collective-permute-done.11.refs_6_), channel_id=1, source_target_pairs={{0,1},{1,0},{2,3},{3,2},{4,5},{5,4},{6,7},{7,6},{8,9},{9,8},{10,11... | collective-permute-start | bytes 1376264 | tf_op jit(solution)/shard_map/ppermute | solution.py:93
  42.9 21.3 %collective-permute-start.15 = (bf16[64,3584]{1,0:T(8,128)(2,1)}, bf16[64,3584]{1,0:T(8,128)(2,1)S(1)}, u32[]{:S(2)}, u32[]{:S(2)}) collective-permute-start(bf16[64,3584]{1,0:T(8,128)(2,1)} %collective-permute-done.11.refs_6_), channel_id=1, source_target_pairs={{0,4},{1,5},{4,8},{5,9},{8,12},{9,13},{12,14},{13,15},{14,10},{15,... | collective-permute-start | bytes 1376264 | tf_op jit(solution)/shard_map/ppermute | solution.py:89
  43.6 5.4 %collective-permute-start.14 = (bf16[128,3584]{1,0:T(8,128)(2,1)}, bf16[128,3584]{1,0:T(8,128)(2,1)}, u32[]{:S(2)}, u32[]{:S(2)}) collective-permute-start(bf16[128,3584]{1,0:T(8,128)(2,1)} %get-tuple-element.70), channel_id=1, source_target_pairs={{0,1},{1,0},{2,3},{3,2},{4,5},{5,4},{6,7},{7,6},{8,9},{9,8},{10,11... | collective-permute-start | bytes 2752520 | tf_op jit(solution)/shard_map/ppermute | solution.py:93
  43.6 20.7 %collective-permute-start.16 = (bf16[64,3584]{1,0:T(8,128)(2,1)S(1)}, bf16[64,3584]{1,0:T(8,128)(2,1)S(1)}, u32[]{:S(2)}, u32[]{:S(2)}) collective-permute-start(bf16[64,3584]{1,0:T(8,128)(2,1)S(1)} %collective-permute-done.12.refs_0_), channel_id=1, source_target_pairs={{0,2},{1,3},{4,0},{5,1},{8,4},{9,5},{12,8},{13,9},{14,12},{15,13},... | collective-permute-start | bytes 1376264 | tf_op jit(solution)/shard_map/ppermute | solution.py:89
  46.1 19.6 %collective-permute-start.18 = (bf16[64,3584]{1,0:T(8,128)(2,1)}, bf16[64,3584]{1,0:T(8,128)(2,1)}, u32[]{:S(2)}, u32[]{:S(2)}) collective-permute-start(bf16[64,3584]{1,0:T(8,128)(2,1)} %get-tuple-element.121), channel_id=1, source_target_pairs={{0,4},{1,5},{4,8},{5,9},{8,12},{9,13},{12,14},{13,15},{14,10},{15,... | collective-permute-start | bytes 1376264 | tf_op jit(solution)/shard_map/ppermute | solution.py:89
  47.8 19.0 %collective-permute-start.19 = (bf16[64,3584]{1,0:T(8,128)(2,1)}, bf16[64,3584]{1,0:T(8,128)(2,1)}, u32[]{:S(2)}, u32[]{:S(2)}) collective-permute-start(bf16[64,3584]{1,0:T(8,128)(2,1)} %get-tuple-element.120), channel_id=1, source_target_pairs={{0,2},{1,3},{4,0},{5,1},{8,4},{9,5},{12,8},{13,9},{14,12},{15,13},... | collective-permute-start | bytes 1376264 | tf_op jit(solution)/shard_map/ppermute | solution.py:89
  66.8 3.9 %collective-permute-start.20 = (bf16[256,3584]{1,0:T(8,128)(2,1)S(1)}, bf16[256,3584]{1,0:T(8,128)(2,1)S(1)}, u32[]{:S(2)}, u32[]{:S(2)}) collective-permute-start(bf16[256,3584]{1,0:T(8,128)(2,1)S(1)} %get-tuple-element.84), channel_id=1, source_target_pairs={{0,1},{1,0},{2,3},{3,2},{4,5},{5,4},{6,7},{7,6},{8,9},{9,8},{10,11... | collective-permute-start | bytes 5505032 | tf_op jit(solution)/shard_map/ppermute | solution.py:93
  66.8 5.7 %collective-permute-start.21 = (bf16[64,3584]{1,0:T(8,128)(2,1)S(1)}, bf16[64,3584]{1,0:T(8,128)(2,1)S(1)}, u32[]{:S(2)}, u32[]{:S(2)}) collective-permute-start(bf16[64,3584]{1,0:T(8,128)(2,1)S(1)} %collective-permute-done.12.refs_0_), channel_id=1, source_target_pairs={{0,1},{1,0},{2,3},{3,2},{4,5},{5,4},{6,7},{7,6},{8,9},{9,8},{10,11... | collective-permute-start | bytes 1376264 | tf_op jit(solution)/shard_map/ppermute | solution.py:93
  67.3 6.7 %collective-permute-start.22 = (bf16[64,3584]{1,0:T(8,128)(2,1)S(1)}, bf16[64,3584]{1,0:T(8,128)(2,1)S(1)}, u32[]{:S(2)}, u32[]{:S(2)}) collective-permute-start(bf16[64,3584]{1,0:T(8,128)(2,1)S(1)} %collective-permute-done.15.refs_2_), channel_id=1, source_target_pairs={{0,1},{1,0},{2,3},{3,2},{4,5},{5,4},{6,7},{7,6},{8,9},{9,8},{10,11... | collective-permute-start | bytes 1376264 | tf_op jit(solution)/shard_map/ppermute | solution.py:93
  67.3 6.7 %collective-permute-start.23 = (bf16[64,3584]{1,0:T(8,128)(2,1)S(1)}, bf16[64,3584]{1,0:T(8,128)(2,1)S(1)}, u32[]{:S(2)}, u32[]{:S(2)}) collective-permute-start(bf16[64,3584]{1,0:T(8,128)(2,1)S(1)} %collective-permute-done.16.refs_4_), channel_id=1, source_target_pairs={{0,1},{1,0},{2,3},{3,2},{4,5},{5,4},{6,7},{7,6},{8,9},{9,8},{10,11... | collective-permute-start | bytes 1376264 | tf_op jit(solution)/shard_map/ppermute | solution.py:93
  69.6 14.4 %collective-permute-start.24 = (bf16[64,3584]{1,0:T(8,128)(2,1)S(1)}, bf16[64,3584]{1,0:T(8,128)(2,1)S(1)}, u32[]{:S(2)}, u32[]{:S(2)}) collective-permute-start(bf16[64,3584]{1,0:T(8,128)(2,1)S(1)} %get-tuple-element.95), channel_id=1, source_target_pairs={{0,2},{1,3},{4,0},{5,1},{8,4},{9,5},{12,8},{13,9},{14,12},{15,13},... | collective-permute-start | bytes 1376264 | tf_op jit(solution)/shard_map/ppermute | solution.py:89
  70.7 13.4 %collective-permute-start.25 = (bf16[64,3584]{1,0:T(8,128)(2,1)S(1)}, bf16[64,3584]{1,0:T(8,128)(2,1)S(1)}, u32[]{:S(2)}, u32[]{:S(2)}) collective-permute-start(bf16[64,3584]{1,0:T(8,128)(2,1)S(1)} %collective-permute-done.15.refs_2_), channel_id=1, source_target_pairs={{0,4},{1,5},{4,8},{5,9},{8,12},{9,13},{12,14},{13,15},{14,10},{15,... | collective-permute-start | bytes 1376264 | tf_op jit(solution)/shard_map/ppermute | solution.py:89
  72.5 22.8 %collective-permute-start.29 = (bf16[384,1024]{1,0:T(8,128)(2,1)S(1)}, bf16[384,1024]{1,0:T(8,128)(2,1)S(1)}, u32[]{:S(2)}, u32[]{:S(2)}) collective-permute-start(bf16[384,1024]{1,0:T(8,128)(2,1)S(1)} %get-tuple-element.101), channel_id=1, source_target_pairs={{0,16},{16,0},{1,17},{17,1},{2,18},{18,2},{3,19},{19,3},{4,20},{20... | collective-permute-start | bytes 2359304 | tf_op jit(solution)/shard_map/ppermute | solution.py:101
  84.0 2.9 %collective-permute-start.26 = (bf16[64,3584]{1,0:T(8,128)(2,1)S(1)}, bf16[64,3584]{1,0:T(8,128)(2,1)S(1)}, u32[]{:S(2)}, u32[]{:S(2)}) collective-permute-start(bf16[64,3584]{1,0:T(8,128)(2,1)S(1)} %collective-permute-done.25.refs_0_), channel_id=1, source_target_pairs={{0,1},{1,0},{2,3},{3,2},{4,5},{5,4},{6,7},{7,6},{8,9},{9,8},{10,11... | collective-permute-start | bytes 1376264 | tf_op jit(solution)/shard_map/ppermute | solution.py:93
  84.3 13.0 %collective-permute-start.28 = (bf16[64,3584]{1,0:T(8,128)(2,1)S(1)}, bf16[64,3584]{1,0:T(8,128)(2,1)S(1)}, u32[]{:S(2)}, u32[]{:S(2)}) collective-permute-start(bf16[64,3584]{1,0:T(8,128)(2,1)S(1)} %add_convert_fusion.3), channel_id=1, source_target_pairs={{0,2},{1,3},{4,0},{5,1},{8,4},{9,5},{12,8},{13,9},{14,12},{15,13},... | collective-permute-start | bytes 1376264 | tf_op jit(solution)/shard_map/ppermute | solution.py:89
  84.5 12.9 %collective-permute-start.27 = (bf16[64,3584]{1,0:T(8,128)(2,1)S(1)}, bf16[64,3584]{1,0:T(8,128)(2,1)S(1)}, u32[]{:S(2)}, u32[]{:S(2)}) collective-permute-start(bf16[64,3584]{1,0:T(8,128)(2,1)S(1)} %get-tuple-element.99), channel_id=1, source_target_pairs={{0,4},{1,5},{4,8},{5,9},{8,12},{9,13},{12,14},{13,15},{14,10},{15,... | collective-permute-start | bytes 1376264 | tf_op jit(solution)/shard_map/ppermute | solution.py:89
  86.4 19.2 %collective-permute-start.32 = (bf16[288,1024]{1,0:T(8,128)(2,1)S(1)}, bf16[288,1024]{1,0:T(8,128)(2,1)S(1)}, u32[]{:S(2)}, u32[]{:S(2)}) collective-permute-start(bf16[288,1024]{1,0:T(8,128)(2,1)S(1)} %get-tuple-element.105), channel_id=1, source_target_pairs={{0,16},{16,0},{1,17},{17,1},{2,18},{18,2},{3,19},{19,3},{4,20},{20... | collective-permute-start | bytes 1769480 | tf_op jit(solution)/shard_map/ppermute | solution.py:101
  97.7 12.3 %collective-permute-start.30 = (bf16[64,3584]{1,0:T(8,128)(2,1)S(1)}, bf16[64,3584]{1,0:T(8,128)(2,1)S(1)}, u32[]{:S(2)}, u32[]{:S(2)}) collective-permute-start(bf16[64,3584]{1,0:T(8,128)(2,1)S(1)} %get-tuple-element.116), channel_id=1, source_target_pairs={{0,4},{1,5},{4,8},{5,9},{8,12},{9,13},{12,14},{13,15},{14,10},{15,... | collective-permute-start | bytes 1376264 | tf_op jit(solution)/shard_map/ppermute | solution.py:89
  99.5 11.8 %collective-permute-start.31 = (bf16[64,3584]{1,0:T(8,128)(2,1)S(1)}, bf16[64,3584]{1,0:T(8,128)(2,1)S(1)}, u32[]{:S(2)}, u32[]{:S(2)}) collective-permute-start(bf16[64,3584]{1,0:T(8,128)(2,1)S(1)} %get-tuple-element.117), channel_id=1, source_target_pairs={{0,2},{1,3},{4,0},{5,1},{8,4},{9,5},{12,8},{13,9},{14,12},{15,13},... | collective-permute-start | bytes 1376264 | tf_op jit(solution)/shard_map/ppermute | solution.py:89
  99.8 8.9 %collective-permute-start.33 = (bf16[96,1024]{1,0:T(8,128)(2,1)S(1)}, bf16[96,1024]{1,0:T(8,128)(2,1)S(1)}, u32[]{:S(2)}, u32[]{:S(2)}) collective-permute-start(bf16[96,1024]{1,0:T(8,128)(2,1)S(1)} %get-tuple-element.111), channel_id=1, source_target_pairs={{0,16},{16,0},{1,17},{17,1},{2,18},{18,2},{3,19},{19,3},{4,20},{20... | collective-permute-start | bytes 589832 | tf_op jit(solution)/shard_map/ppermute | solution.py:101
  (12 other events, 58.2 us)

commit v9 on v8

--- a/solution.py
+++ b/solution.py
@@ -115,7 +115,7 @@
 ANY = pl.BlockSpec(memory_space=pl.ANY)
 
 
-def kernel_call(kernel, name, inputs, out_shape, scratch, flops, moved, limit=12):
+def kernel_call(kernel, name, inputs, out_shape, scratch, flops, moved, limit=9):
     in_specs, arrays = zip(*inputs)
     return pl.pallas_call(
         kernel,
@@ -273,7 +273,7 @@
             pltpu.VMEM((2, rows, RAW_TILE), BF16),
             pltpu.SemaphoreType.DMA((2,)),
         ],
-        compiler_params=pltpu.CompilerParams(vmem_limit_bytes=12 * 2**20),
+        compiler_params=pltpu.CompilerParams(vmem_limit_bytes=9 * 2**20),
         cost_estimate=pl.CostEstimate(
             flops=2 * rows * depth * width,
             bytes_accessed=2 * (depth * width + rows * (depth + width)),
@@ -421,7 +421,7 @@
         ],
         flops=len(sides) * count * rows * depth * width // share,
         moved=2 * (depth * width + count * rows * (depth + 2 * width)) // share,
-        limit=18,
+        limit=16,
     )
 
 
@@ -458,7 +458,7 @@
             pltpu.SemaphoreType.DMA((count,)),
         ],
         input_output_aliases={} if into is None else {len(inputs) - 1: 0},
-        compiler_params=pltpu.CompilerParams(vmem_limit_bytes=12 * 2**20),
+        compiler_params=pltpu.CompilerParams(vmem_limit_bytes=9 * 2**20),
         cost_estimate=pl.CostEstimate(
             flops=2**20, bytes_accessed=6 * count * rows * 128, transcendentals=0
         ),

time: 113 us -> 113 us (level)
  no operation moved by 1% of the time
where the time goes in v9:
time: 113 us; the launch traced here: 112 us
  Pallas kernels  62.3 us (55%)
  starting transfers between devices  28.4 us (25%)
  waiting for transfers between devices  13.4 us (12%)
  other arithmetic  4.51 us (4%)
  local copies, waits for them, and re-layouts  2.66 us (2%)
    pallas_call x6, Pallas kernels, kernel_call(): pl.pallas_call(kernel, in_specs=in_specs, out_specs=[VMEM] * len(out_shap...  38.8 us
    pallas_call x2, Pallas kernels, raw_forward(): pl.pallas_call(functools.partial(raw_kernel, first), in_specs=[HBM, HBM],...  20.6 us
    ppermute x14, starting transfers between devices, step_ring(): return lax.ppermute(value, 'expert', pairs)  15.2 us
    ppermute x17, starting transfers between devices, xor(): return lax.ppermute(value, 'expert', [(i, i ^ bits) for i in range(16)])  9.93 us
    ppermute x3, waiting for transfers between devices, across(): return lax.ppermute(value, 'pipe', [(0, 1), (1, 0)])  6.04 us
    ppermute x14, waiting for transfers between devices, step_ring(): return lax.ppermute(value, 'expert', pairs)  5.86 us
    convert_element_type x5, other arithmetic, add(): return total.astype(BF16)  4.39 us
    ppermute x3, starting transfers between devices, across(): return lax.ppermute(value, 'pipe', [(0, 1), (1, 0)])  3.22 us
  transfers between devices with their start and end apart: 34, of which 8 were waited for; matrix products, arithmetic and copies ran while one was open for 3% of the time, Pallas kernels for 55%

profile of v9, /device:TPU:0, one launch (start us, length us, event | category | flops | bytes accessed | tf_op | source)
XLA Modules:
  0.0 112.2 jit_solution(18025483686644732702)
XLA Ops:
  1.5 2.5 %collective-permute-start.2 = (f32[16,128]{1,0:T(8,128)S(1)}, f32[16,128]{1,0:T(8,128)S(1)}, u32[]{:S(2)}, u32[]{:S(2)}) collective-permute-start(f32[16,128]{1,0:T(8,128)S(1)} %gates.1), channel_id=1, source_target_pairs={{0,3},{1,2},{2,1},{3,0},{4,7},{5,6},{6,5},{7,4},{8,11},{9,10},{10,... | collective-permute-start | bytes 24584 | tf_op jit(solution)/shard_map/ppermute | solution.py:93
  4.7 2.0 %collective-permute-start.6 = (bf16[64,3584]{1,0:T(8,128)(2,1)}, bf16[64,3584]{1,0:T(8,128)(2,1)S(1)}, u32[]{:S(2)}, u32[]{:S(2)}) collective-permute-start(bf16[64,3584]{1,0:T(8,128)(2,1)} %refs_0_.1), channel_id=1, source_target_pairs={{0,4},{1,5},{4,8},{5,9},{8,12},{9,13},{12,14},{13,15},{14,10},{15,... | collective-permute-start | bytes 1376264 | tf_op jit(solution)/shard_map/ppermute | solution.py:89
  6.8 1.5 %collective-permute-done.1 = f32[16,128]{1,0:T(8,128)S(1)} collective-permute-done((f32[16,128]{1,0:T(8,128)S(1)}, f32[16,128]{1,0:T(8,128)S(1)}, u32[]{:S(2)}, u32[]{:S(2)}) %collective-permute-start.1) | collective-permute-done | bytes 8224 | tf_op jit(solution)/shard_map/ppermute | solution.py:93
  8.3 1.6 %collective-permute-start.3 = (f32[4,4,128]{2,0,1:T(4,128)S(1)}, f32[4,4,128]{2,0,1:T(4,128)S(1)}, u32[]{:S(2)}, u32[]{:S(2)}) collective-permute-start(f32[4,4,128]{2,0,1:T(4,128)S(1)} %bitcast.37), channel_id=1, source_target_pairs={{0,4},{1,5},{2,6},{3,7},{4,0},{5,1},{6,2},{7,3},{8,12},{9,13},{10,... | collective-permute-start | bytes 24584 | tf_op jit(solution)/shard_map/ppermute | solution.py:93
  10.0 2.6 %collective-permute-start.4 = (f32[4,4,128]{2,0,1:T(4,128)S(1)}, f32[4,4,128]{2,0,1:T(4,128)S(1)}, u32[]{:S(2)}, u32[]{:S(2)}) collective-permute-start(f32[4,4,128]{2,0,1:T(4,128)S(1)} %bitcast.38), channel_id=1, source_target_pairs={{0,8},{1,9},{2,10},{3,11},{4,12},{5,13},{6,14},{7,15},{8,0},{9,1},... | collective-permute-start | bytes 24584 | tf_op jit(solution)/shard_map/ppermute | solution.py:93
  12.8 10.3 %raw_forward.2.refs_0_ = bf16[768,1792]{1,0:T(8,128)(2,1)} custom-call(bf16[768,2048]{1,0:T(8,128)(2,1)} %bitcast.51, bf16[2048,3584]{1,0:T(8,128)(2,1)} %bitcast.30), custom_call_target="tpu_custom_call" | custom-call | flops 5637144576 | bytes 13238272 | tf_op jit(solution)/shard_map/raw_forward/pallas_call | solution.py:263
  24.5 1.4 %collective-permute-start.12 = (bf16[64,3584]{1,0:T(8,128)(2,1)S(1)}, bf16[64,3584]{1,0:T(8,128)(2,1)S(1)}, u32[]{:S(2)}, u32[]{:S(2)}) collective-permute-start(bf16[64,3584]{1,0:T(8,128)(2,1)S(1)} %collective-permute-done.7.refs_4_), channel_id=1, source_target_pairs={{0,2},{1,3},{4,0},{5,1},{8,4},{9,5},{12,8},{13,9},{14,12},{15,13},... | collective-permute-start | bytes 1376264 | tf_op jit(solution)/shard_map/ppermute | solution.py:89
  26.1 10.2 %raw_forward.3.refs_1_ = bf16[768,1792]{1,0:T(8,128)(2,1)} custom-call(bf16[768,2048]{1,0:T(8,128)(2,1)} %bitcast.52, bf16[2048,3584]{1,0:T(8,128)(2,1)} %bitcast.31), custom_call_target="tpu_custom_call" | custom-call | flops 5637144576 | bytes 13238272 | tf_op jit(solution)/shard_map/raw_forward/pallas_call | solution.py:263
  38.0 4.4 %spread_tokens.2 = (bf16[256,3584]{1,0:T(8,128)(2,1)S(1)}, bf16[128,3584]{1,0:T(8,128)(2,1)S(1)}, bf16[128,3584]{1,0:T(8,128)(2,1)}) custom-call(s32[17]{0:T(128)S(1)} %pad_add_fusion.where, f32[8,128]{1,0:T(8,128)S(1)} %squeeze.20.gates, bf16[768,1792]{1,0:T(8,128)(2,1)} %raw_forward.2.refs_0_, bf16[768,1792]{1,0:T(8,128)(2,1)} %raw_forward.3.refs_1_), custom_call_target="tpu_custom_call" | custom-call | flops 1048576 | bytes 16384 | tf_op jit(solution)/shard_map/spread_tokens/pallas_call | solution.py:120
  43.6 1.4 %collective-permute-start.16 = (bf16[64,3584]{1,0:T(8,128)(2,1)S(1)}, bf16[64,3584]{1,0:T(8,128)(2,1)S(1)}, u32[]{:S(2)}, u32[]{:S(2)}) collective-permute-start(bf16[64,3584]{1,0:T(8,128)(2,1)S(1)} %collective-permute-done.12.refs_0_), channel_id=1, source_target_pairs={{0,2},{1,3},{4,0},{5,1},{8,4},{9,5},{12,8},{13,9},{14,12},{15,13},... | collective-permute-start | bytes 1376264 | tf_op jit(solution)/shard_map/ppermute | solution.py:89
  45.0 1.1 %add_convert_fusion.6 = (bf16[64,3584]{1,0:T(8,128)(2,1)}, bf16[64,3584]{1,0:T(8,128)(2,1)}) fusion(bf16[128,3584]{1,0:T(8,128)(2,1)S(1)} %collective-permute-done.17, bf16[256,3584]{1,0:T(8,128)(2,1)S(1)} %get-tuple-element.81), kind=kLoop, calls=%fused_computation.6 | loop fusion | flops 1835008 | bytes 2752512 | tf_op jit(solution)/shard_map/convert_element_type | solution.py:32
  47.8 1.1 %collective-permute-start.19 = (bf16[64,3584]{1,0:T(8,128)(2,1)}, bf16[64,3584]{1,0:T(8,128)(2,1)}, u32[]{:S(2)}, u32[]{:S(2)}) collective-permute-start(bf16[64,3584]{1,0:T(8,128)(2,1)} %get-tuple-element.120), channel_id=1, source_target_pairs={{0,2},{1,3},{4,0},{5,1},{8,4},{9,5},{12,8},{13,9},{14,12},{15,13},... | collective-permute-start | bytes 1376264 | tf_op jit(solution)/shard_map/ppermute | solution.py:89
  49.0 3.4 %spread_tokens.3 = (bf16[256,3584]{1,0:T(8,128)(2,1)S(1)}, bf16[256,3584]{1,0:T(8,128)(2,1)S(1)}) custom-call(s32[17]{0:T(128)S(1)} %pad_add_fusion.where, f32[8,128]{1,0:T(8,128)S(1)} %squeeze.20.gates, bf16[768,1792]{1,0:T(8,128)(2,1)} %raw_forward.2.refs_0_, bf16[768,1792]{1,0:T(8,128)(2,1)} %raw_forward.3.refs_1_), custom_call_target="tpu_custom_call" | custom-call | flops 1048576 | bytes 16384 | tf_op jit(solution)/shard_map/spread_tokens/pallas_call | solution.py:120
  52.5 11.8 %backward.3 = (bf16[384,1024]{1,0:T(8,128)(2,1)S(1)}, bf16[384,1024]{1,0:T(8,128)(2,1)S(1)}) custom-call(s32[17]{0:T(128)S(1)} %pad_add_fusion.where, s32[1]{0:T(128)} %bitcast.20.pipe, f32[8,128]{1,0:T(8,128)S(1)} %squeeze.21.gates, bf16[2048,3584]{1,0:T(8,128)(2,1)} %bitcast.32, bf16[64,3584]{1,0:T(8,128)(2,1)S(1)} %copy-done.1, ...), custom_call_target="tpu_custom_call" | custom-call | flops 88080384 | bytes 339968 | tf_op jit(solution)/shard_map/backward/pallas_call | solution.py:120
  64.2 1.5 %collective-permute-done.18 = bf16[64,3584]{1,0:T(8,128)(2,1)} collective-permute-done((bf16[64,3584]{1,0:T(8,128)(2,1)}, bf16[64,3584]{1,0:T(8,128)(2,1)}, u32[]{:S(2)}, u32[]{:S(2)}) %collective-permute-start.18) | collective-permute-done | bytes 458784 | tf_op jit(solution)/shard_map/ppermute | solution.py:89
  65.7 1.1 collective-permute-done.19
  67.8 1.8 %add_convert_fusion.4 = (bf16[64,3584]{1,0:T(8,128)(2,1)S(1)}, bf16[64,3584]{1,0:T(8,128)(2,1)S(1)}) fusion(bf16[64,3584]{1,0:T(8,128)(2,1)} %collective-permute-done.19, bf16[128,3584]{1,0:T(8,128)(2,1)} %collective-permute-done.14, bf16[256,3584]{1,0:T(8,128)(2,1)S(1)} %get-tuple-element.81, bf16[64,3584]{1,0:T(8,128)(2,1)} %collective-permute-done.18), kind=kLoop, calls=%fused_computation.4 | loop fusion | flops 2752512 | bytes 3670016 | tf_op jit(solution)/shard_map/convert_element_type | solution.py:32
  69.6 1.1 collective-permute-start.24
  70.7 1.9 %collective-permute-start.25 = (bf16[64,3584]{1,0:T(8,128)(2,1)S(1)}, bf16[64,3584]{1,0:T(8,128)(2,1)S(1)}, u32[]{:S(2)}, u32[]{:S(2)}) collective-permute-start(bf16[64,3584]{1,0:T(8,128)(2,1)S(1)} %collective-permute-done.15.refs_2_), channel_id=1, source_target_pairs={{0,4},{1,5},{4,8},{5,9},{8,12},{9,13},{12,14},{13,15},{14,10},{15,... | collective-permute-start | bytes 1376264 | tf_op jit(solution)/shard_map/ppermute | solution.py:89
  72.5 1.5 %collective-permute-start.29 = (bf16[384,1024]{1,0:T(8,128)(2,1)S(1)}, bf16[384,1024]{1,0:T(8,128)(2,1)S(1)}, u32[]{:S(2)}, u32[]{:S(2)}) collective-permute-start(bf16[384,1024]{1,0:T(8,128)(2,1)S(1)} %get-tuple-element.101), channel_id=1, source_target_pairs={{0,16},{16,0},{1,17},{17,1},{2,18},{18,2},{3,19},{19,3},{4,20},{20... | collective-permute-start | bytes 2359304 | tf_op jit(solution)/shard_map/ppermute | solution.py:101
  74.0 10.0 %backward.4 = (bf16[288,1024]{1,0:T(8,128)(2,1)S(1)}, bf16[288,1024]{1,0:T(8,128)(2,1)S(1)}) custom-call(s32[17]{0:T(128)S(1)} %pad_add_fusion.where, s32[1]{0:T(128)} %bitcast.20.pipe, f32[8,128]{1,0:T(8,128)S(1)} %squeeze.21.gates, bf16[2048,3584]{1,0:T(8,128)(2,1)} %bitcast.33, bf16[64,3584]{1,0:T(8,128)(2,1)S(1)} %collective-permute-done.12.refs_0_, ...), custom_call_target="tpu_custom_call" | custom-call | flops 66060288 | bytes 312320 | tf_op jit(solution)/shard_map/backward/pallas_call | solution.py:120
  84.5 1.9 %collective-permute-start.27 = (bf16[64,3584]{1,0:T(8,128)(2,1)S(1)}, bf16[64,3584]{1,0:T(8,128)(2,1)S(1)}, u32[]{:S(2)}, u32[]{:S(2)}) collective-permute-start(bf16[64,3584]{1,0:T(8,128)(2,1)S(1)} %get-tuple-element.99), channel_id=1, source_target_pairs={{0,4},{1,5},{4,8},{5,9},{8,12},{9,13},{12,14},{13,15},{14,10},{15,... | collective-permute-start | bytes 1376264 | tf_op jit(solution)/shard_map/ppermute | solution.py:89
  86.9 8.4 %backward.5 = (bf16[96,1024]{1,0:T(8,128)(2,1)S(1)}, bf16[96,1024]{1,0:T(8,128)(2,1)S(1)}) custom-call(s32[17]{0:T(128)S(1)} %pad_add_fusion.where, s32[1]{0:T(128)} %bitcast.20.pipe, f32[8,128]{1,0:T(8,128)S(1)} %squeeze.21.gates, bf16[2048,3584]{1,0:T(8,128)(2,1)} %bitcast.34, bf16[64,3584]{1,0:T(8,128)(2,1)S(1)} %collective-permute-done.25.refs_0_, ...), custom_call_target="tpu_custom_call" | custom-call | flops 22020096 | bytes 257024 | tf_op jit(solution)/shard_map/backward/pallas_call | solution.py:120
  95.3 1.9 %collective-permute-done.28 = bf16[64,3584]{1,0:T(8,128)(2,1)S(1)} collective-permute-done((bf16[64,3584]{1,0:T(8,128)(2,1)S(1)}, bf16[64,3584]{1,0:T(8,128)(2,1)S(1)}, u32[]{:S(2)}, u32[]{:S(2)}) %collective-permute-start.28) | collective-permute-done | bytes 458784 | tf_op jit(solution)/shard_map/ppermute | solution.py:89
  97.7 1.8 %collective-permute-start.30 = (bf16[64,3584]{1,0:T(8,128)(2,1)S(1)}, bf16[64,3584]{1,0:T(8,128)(2,1)S(1)}, u32[]{:S(2)}, u32[]{:S(2)}) collective-permute-start(bf16[64,3584]{1,0:T(8,128)(2,1)S(1)} %get-tuple-element.116), channel_id=1, source_target_pairs={{0,4},{1,5},{4,8},{5,9},{8,12},{9,13},{12,14},{13,15},{14,10},{15,... | collective-permute-start | bytes 1376264 | tf_op jit(solution)/shard_map/ppermute | solution.py:89
  99.8 1.2 %collective-permute-start.33 = (bf16[96,1024]{1,0:T(8,128)(2,1)S(1)}, bf16[96,1024]{1,0:T(8,128)(2,1)S(1)}, u32[]{:S(2)}, u32[]{:S(2)}) collective-permute-start(bf16[96,1024]{1,0:T(8,128)(2,1)S(1)} %get-tuple-element.111), channel_id=1, source_target_pairs={{0,16},{16,0},{1,17},{17,1},{2,18},{18,2},{3,19},{19,3},{4,20},{20... | collective-permute-start | bytes 589832 | tf_op jit(solution)/shard_map/ppermute | solution.py:101
  100.9 4.7 %collective-permute-done.32.refs_3_ = bf16[288,1024]{1,0:T(8,128)(2,1)S(1)} collective-permute-done((bf16[288,1024]{1,0:T(8,128)(2,1)S(1)}, bf16[288,1024]{1,0:T(8,128)(2,1)S(1)}, u32[]{:S(2)}, u32[]{:S(2)}) %collective-permute-start.32) | collective-permute-done | bytes 589856 | tf_op jit(solution)/shard_map/ppermute | solution.py:101
  105.6 1.7 %collect.2.refs_2_ = bf16[768,1024]{1,0:T(8,128)(2,1)} custom-call(s32[17]{0:T(128)S(1)} %pad_add_fusion.where, bf16[384,1024]{1,0:T(8,128)(2,1)S(1)} %get-tuple-element.107.refs_0_, bf16[384,1024]{1,0:T(8,128)(2,1)S(1)} %collective-permute-done.29.refs_1_, bf16[288,1024]{1,0:T(8,128)(2,1)S(1)} %get-tuple-element.109.refs_2_, ...), custom_call_target="tpu_custom_call" | custom-call | flops 1048576 | bytes 4128768 | tf_op jit(solution)/shard_map/collect/pallas_call | solution.py:451
  107.3 1.4 %collective-permute-done.33.refs_1_ = bf16[96,1024]{1,0:T(8,128)(2,1)S(1)} collective-permute-done((bf16[96,1024]{1,0:T(8,128)(2,1)S(1)}, bf16[96,1024]{1,0:T(8,128)(2,1)S(1)}, u32[]{:S(2)}, u32[]{:S(2)}) %collective-permute-start.33) | collective-permute-done | bytes 196640 | tf_op jit(solution)/shard_map/ppermute | solution.py:101
  108.7 1.3 %collect.3 = bf16[768,1024]{1,0:T(8,128)(2,1)} custom-call(s32[17]{0:T(128)S(1)} %pad_add_fusion.where, bf16[96,1024]{1,0:T(8,128)(2,1)S(1)} %get-tuple-element.106.refs_0_, bf16[96,1024]{1,0:T(8,128)(2,1)S(1)} %collective-permute-done.33.refs_1_, bf16[768,1024]{1,0:T(8,128)(2,1)} %collect.2.refs_2_), custom_call_target="tpu_custom_call", output_to_operand_aliasing={{}: (3, {})} | custom-call | flops 1048576 | bytes 589824 | tf_op jit(solution)/shard_map/collect/pallas_call | solution.py:451
  110.0 1.3 %collective-permute-done.31 = bf16[64,3584]{1,0:T(8,128)(2,1)S(1)} collective-permute-done((bf16[64,3584]{1,0:T(8,128)(2,1)S(1)}, bf16[64,3584]{1,0:T(8,128)(2,1)S(1)}, u32[]{:S(2)}, u32[]{:S(2)}) %collective-permute-start.31) | collective-permute-done | bytes 458784 | tf_op jit(solution)/shard_map/ppermute | solution.py:89
  111.2 1.0 add_convert_fusion
  (81 shorter events, 10.8 us)
Async XLA Ops:
  1.5 5.3 %collective-permute-start.2 = (f32[16,128]{1,0:T(8,128)S(1)}, f32[16,128]{1,0:T(8,128)S(1)}, u32[]{:S(2)}, u32[]{:S(2)}) collective-permute-start(f32[16,128]{1,0:T(8,128)S(1)} %gates.1), channel_id=1, source_target_pairs={{0,3},{1,2},{2,1},{3,0},{4,7},{5,6},{6,5},{7,4},{8,11},{9,10},{10,... | collective-permute-start | bytes 24584 | tf_op jit(solution)/shard_map/ppermute | solution.py:93
  4.6 3.7 %collective-permute-start.1 = (f32[16,128]{1,0:T(8,128)S(1)}, f32[16,128]{1,0:T(8,128)S(1)}, u32[]{:S(2)}, u32[]{:S(2)}) collective-permute-start(f32[16,128]{1,0:T(8,128)S(1)} %gates.1), channel_id=1, source_target_pairs={{0,2},{1,3},{2,0},{3,1},{4,6},{5,7},{6,4},{7,5},{8,10},{9,11},{10,... | collective-permute-start | bytes 24584 | tf_op jit(solution)/shard_map/ppermute | solution.py:93
  4.7 18.6 %collective-permute-start.6 = (bf16[64,3584]{1,0:T(8,128)(2,1)}, bf16[64,3584]{1,0:T(8,128)(2,1)S(1)}, u32[]{:S(2)}, u32[]{:S(2)}) collective-permute-start(bf16[64,3584]{1,0:T(8,128)(2,1)} %refs_0_.1), channel_id=1, source_target_pairs={{0,4},{1,5},{4,8},{5,9},{8,12},{9,13},{12,14},{13,15},{14,10},{15,... | collective-permute-start | bytes 1376264 | tf_op jit(solution)/shard_map/ppermute | solution.py:89
  6.7 16.5 %collective-permute-start.7 = (bf16[64,3584]{1,0:T(8,128)(2,1)}, bf16[64,3584]{1,0:T(8,128)(2,1)S(1)}, u32[]{:S(2)}, u32[]{:S(2)}) collective-permute-start(bf16[64,3584]{1,0:T(8,128)(2,1)} %refs_0_.1), channel_id=1, source_target_pairs={{0,2},{1,3},{4,0},{5,1},{8,4},{9,5},{12,8},{13,9},{14,12},{15,13},... | collective-permute-start | bytes 1376264 | tf_op jit(solution)/shard_map/ppermute | solution.py:89
  8.3 14.8 %collective-permute-start.3 = (f32[4,4,128]{2,0,1:T(4,128)S(1)}, f32[4,4,128]{2,0,1:T(4,128)S(1)}, u32[]{:S(2)}, u32[]{:S(2)}) collective-permute-start(f32[4,4,128]{2,0,1:T(4,128)S(1)} %bitcast.37), channel_id=1, source_target_pairs={{0,4},{1,5},{2,6},{3,7},{4,0},{5,1},{6,2},{7,3},{8,12},{9,13},{10,... | collective-permute-start | bytes 24584 | tf_op jit(solution)/shard_map/ppermute | solution.py:93
  10.0 13.2 %collective-permute-start.4 = (f32[4,4,128]{2,0,1:T(4,128)S(1)}, f32[4,4,128]{2,0,1:T(4,128)S(1)}, u32[]{:S(2)}, u32[]{:S(2)}) collective-permute-start(f32[4,4,128]{2,0,1:T(4,128)S(1)} %bitcast.38), channel_id=1, source_target_pairs={{0,8},{1,9},{2,10},{3,11},{4,12},{5,13},{6,14},{7,15},{8,0},{9,1},... | collective-permute-start | bytes 24584 | tf_op jit(solution)/shard_map/ppermute | solution.py:93
  12.6 10.7 %collective-permute-start.5 = (f32[4,4,128]{2,0,1:T(4,128)S(1)}, f32[4,4,128]{2,0,1:T(4,128)S(1)}, u32[]{:S(2)}, u32[]{:S(2)}) collective-permute-start(f32[4,4,128]{2,0,1:T(4,128)S(1)} %bitcast.39), channel_id=1, source_target_pairs={{0,12},{1,13},{2,14},{3,15},{4,8},{5,9},{6,10},{7,11},{8,4},{9,5},... | collective-permute-start | bytes 24584 | tf_op jit(solution)/shard_map/ppermute | solution.py:93
  23.1 13.2 %collective-permute-start.8 = (bf16[64,3584]{1,0:T(8,128)(2,1)S(1)}, bf16[64,3584]{1,0:T(8,128)(2,1)S(1)}, u32[]{:S(2)}, u32[]{:S(2)}) collective-permute-start(bf16[64,3584]{1,0:T(8,128)(2,1)S(1)} %copy-done), channel_id=1, source_target_pairs={{0,1},{1,0},{2,3},{3,2},{4,5},{5,4},{6,7},{7,6},{8,9},{9,8},{10,11... | collective-permute-start | bytes 1376264 | tf_op jit(solution)/shard_map/ppermute | solution.py:93
  23.3 14.7 %collective-permute-start.9 = (bf16[64,3584]{1,0:T(8,128)(2,1)S(1)}, bf16[64,3584]{1,0:T(8,128)(2,1)}, u32[]{:S(2)}, u32[]{:S(2)}) collective-permute-start(bf16[64,3584]{1,0:T(8,128)(2,1)S(1)} %collective-permute-done.6.refs_2_), channel_id=1, source_target_pairs={{0,1},{1,0},{2,3},{3,2},{4,5},{5,4},{6,7},{7,6},{8,9},{9,8},{10,11... | collective-permute-start | bytes 1376264 | tf_op jit(solution)/shard_map/ppermute | solution.py:93
  23.8 18.5 %collective-permute-start.11 = (bf16[64,3584]{1,0:T(8,128)(2,1)S(1)}, bf16[64,3584]{1,0:T(8,128)(2,1)}, u32[]{:S(2)}, u32[]{:S(2)}) collective-permute-start(bf16[64,3584]{1,0:T(8,128)(2,1)S(1)} %collective-permute-done.6.refs_2_), channel_id=1, source_target_pairs={{0,4},{1,5},{4,8},{5,9},{8,12},{9,13},{12,14},{13,15},{14,10},{15,... | collective-permute-start | bytes 1376264 | tf_op jit(solution)/shard_map/ppermute | solution.py:89
  24.5 11.9 %collective-permute-start.10 = (bf16[64,3584]{1,0:T(8,128)(2,1)S(1)}, bf16[64,3584]{1,0:T(8,128)(2,1)S(1)}, u32[]{:S(2)}, u32[]{:S(2)}) collective-permute-start(bf16[64,3584]{1,0:T(8,128)(2,1)S(1)} %collective-permute-done.7.refs_4_), channel_id=1, source_target_pairs={{0,1},{1,0},{2,3},{3,2},{4,5},{5,4},{6,7},{7,6},{8,9},{9,8},{10,11... | collective-permute-start | bytes 1376264 | tf_op jit(solution)/shard_map/ppermute | solution.py:93
  24.5 17.8 %collective-permute-start.12 = (bf16[64,3584]{1,0:T(8,128)(2,1)S(1)}, bf16[64,3584]{1,0:T(8,128)(2,1)S(1)}, u32[]{:S(2)}, u32[]{:S(2)}) collective-permute-start(bf16[64,3584]{1,0:T(8,128)(2,1)S(1)} %collective-permute-done.7.refs_4_), channel_id=1, source_target_pairs={{0,2},{1,3},{4,0},{5,1},{8,4},{9,5},{12,8},{13,9},{14,12},{15,13},... | collective-permute-start | bytes 1376264 | tf_op jit(solution)/shard_map/ppermute | solution.py:89
  42.6 4.4 %collective-permute-start.13 = (bf16[64,3584]{1,0:T(8,128)(2,1)}, bf16[64,3584]{1,0:T(8,128)(2,1)S(1)}, u32[]{:S(2)}, u32[]{:S(2)}) collective-permute-start(bf16[64,3584]{1,0:T(8,128)(2,1)} %collective-permute-done.11.refs_6_), channel_id=1, source_target_pairs={{0,1},{1,0},{2,3},{3,2},{4,5},{5,4},{6,7},{7,6},{8,9},{9,8},{10,11... | collective-permute-start | bytes 1376264 | tf_op jit(solution)/shard_map/ppermute | solution.py:93
  42.9 21.3 %collective-permute-start.15 = (bf16[64,3584]{1,0:T(8,128)(2,1)}, bf16[64,3584]{1,0:T(8,128)(2,1)S(1)}, u32[]{:S(2)}, u32[]{:S(2)}) collective-permute-start(bf16[64,3584]{1,0:T(8,128)(2,1)} %collective-permute-done.11.refs_6_), channel_id=1, source_target_pairs={{0,4},{1,5},{4,8},{5,9},{8,12},{9,13},{12,14},{13,15},{14,10},{15,... | collective-permute-start | bytes 1376264 | tf_op jit(solution)/shard_map/ppermute | solution.py:89
  43.6 5.4 %collective-permute-start.14 = (bf16[128,3584]{1,0:T(8,128)(2,1)}, bf16[128,3584]{1,0:T(8,128)(2,1)}, u32[]{:S(2)}, u32[]{:S(2)}) collective-permute-start(bf16[128,3584]{1,0:T(8,128)(2,1)} %get-tuple-element.70), channel_id=1, source_target_pairs={{0,1},{1,0},{2,3},{3,2},{4,5},{5,4},{6,7},{7,6},{8,9},{9,8},{10,11... | collective-permute-start | bytes 2752520 | tf_op jit(solution)/shard_map/ppermute | solution.py:93
  43.6 20.7 %collective-permute-start.16 = (bf16[64,3584]{1,0:T(8,128)(2,1)S(1)}, bf16[64,3584]{1,0:T(8,128)(2,1)S(1)}, u32[]{:S(2)}, u32[]{:S(2)}) collective-permute-start(bf16[64,3584]{1,0:T(8,128)(2,1)S(1)} %collective-permute-done.12.refs_0_), channel_id=1, source_target_pairs={{0,2},{1,3},{4,0},{5,1},{8,4},{9,5},{12,8},{13,9},{14,12},{15,13},... | collective-permute-start | bytes 1376264 | tf_op jit(solution)/shard_map/ppermute | solution.py:89
  46.1 19.6 %collective-permute-start.18 = (bf16[64,3584]{1,0:T(8,128)(2,1)}, bf16[64,3584]{1,0:T(8,128)(2,1)}, u32[]{:S(2)}, u32[]{:S(2)}) collective-permute-start(bf16[64,3584]{1,0:T(8,128)(2,1)} %get-tuple-element.121), channel_id=1, source_target_pairs={{0,4},{1,5},{4,8},{5,9},{8,12},{9,13},{12,14},{13,15},{14,10},{15,... | collective-permute-start | bytes 1376264 | tf_op jit(solution)/shard_map/ppermute | solution.py:89
  47.8 19.0 %collective-permute-start.19 = (bf16[64,3584]{1,0:T(8,128)(2,1)}, bf16[64,3584]{1,0:T(8,128)(2,1)}, u32[]{:S(2)}, u32[]{:S(2)}) collective-permute-start(bf16[64,3584]{1,0:T(8,128)(2,1)} %get-tuple-element.120), channel_id=1, source_target_pairs={{0,2},{1,3},{4,0},{5,1},{8,4},{9,5},{12,8},{13,9},{14,12},{15,13},... | collective-permute-start | bytes 1376264 | tf_op jit(solution)/shard_map/ppermute | solution.py:89
  66.8 3.9 %collective-permute-start.20 = (bf16[256,3584]{1,0:T(8,128)(2,1)S(1)}, bf16[256,3584]{1,0:T(8,128)(2,1)S(1)}, u32[]{:S(2)}, u32[]{:S(2)}) collective-permute-start(bf16[256,3584]{1,0:T(8,128)(2,1)S(1)} %get-tuple-element.84), channel_id=1, source_target_pairs={{0,1},{1,0},{2,3},{3,2},{4,5},{5,4},{6,7},{7,6},{8,9},{9,8},{10,11... | collective-permute-start | bytes 5505032 | tf_op jit(solution)/shard_map/ppermute | solution.py:93
  66.8 5.7 %collective-permute-start.21 = (bf16[64,3584]{1,0:T(8,128)(2,1)S(1)}, bf16[64,3584]{1,0:T(8,128)(2,1)S(1)}, u32[]{:S(2)}, u32[]{:S(2)}) collective-permute-start(bf16[64,3584]{1,0:T(8,128)(2,1)S(1)} %collective-permute-done.12.refs_0_), channel_id=1, source_target_pairs={{0,1},{1,0},{2,3},{3,2},{4,5},{5,4},{6,7},{7,6},{8,9},{9,8},{10,11... | collective-permute-start | bytes 1376264 | tf_op jit(solution)/shard_map/ppermute | solution.py:93
  67.3 6.7 %collective-permute-start.22 = (bf16[64,3584]{1,0:T(8,128)(2,1)S(1)}, bf16[64,3584]{1,0:T(8,128)(2,1)S(1)}, u32[]{:S(2)}, u32[]{:S(2)}) collective-permute-start(bf16[64,3584]{1,0:T(8,128)(2,1)S(1)} %collective-permute-done.15.refs_2_), channel_id=1, source_target_pairs={{0,1},{1,0},{2,3},{3,2},{4,5},{5,4},{6,7},{7,6},{8,9},{9,8},{10,11... | collective-permute-start | bytes 1376264 | tf_op jit(solution)/shard_map/ppermute | solution.py:93
  67.3 6.7 %collective-permute-start.23 = (bf16[64,3584]{1,0:T(8,128)(2,1)S(1)}, bf16[64,3584]{1,0:T(8,128)(2,1)S(1)}, u32[]{:S(2)}, u32[]{:S(2)}) collective-permute-start(bf16[64,3584]{1,0:T(8,128)(2,1)S(1)} %collective-permute-done.16.refs_4_), channel_id=1, source_target_pairs={{0,1},{1,0},{2,3},{3,2},{4,5},{5,4},{6,7},{7,6},{8,9},{9,8},{10,11... | collective-permute-start | bytes 1376264 | tf_op jit(solution)/shard_map/ppermute | solution.py:93
  69.6 14.4 %collective-permute-start.24 = (bf16[64,3584]{1,0:T(8,128)(2,1)S(1)}, bf16[64,3584]{1,0:T(8,128)(2,1)S(1)}, u32[]{:S(2)}, u32[]{:S(2)}) collective-permute-start(bf16[64,3584]{1,0:T(8,128)(2,1)S(1)} %get-tuple-element.95), channel_id=1, source_target_pairs={{0,2},{1,3},{4,0},{5,1},{8,4},{9,5},{12,8},{13,9},{14,12},{15,13},... | collective-permute-start | bytes 1376264 | tf_op jit(solution)/shard_map/ppermute | solution.py:89
  70.7 13.4 %collective-permute-start.25 = (bf16[64,3584]{1,0:T(8,128)(2,1)S(1)}, bf16[64,3584]{1,0:T(8,128)(2,1)S(1)}, u32[]{:S(2)}, u32[]{:S(2)}) collective-permute-start(bf16[64,3584]{1,0:T(8,128)(2,1)S(1)} %collective-permute-done.15.refs_2_), channel_id=1, source_target_pairs={{0,4},{1,5},{4,8},{5,9},{8,12},{9,13},{12,14},{13,15},{14,10},{15,... | collective-permute-start | bytes 1376264 | tf_op jit(solution)/shard_map/ppermute | solution.py:89
  72.5 22.8 %collective-permute-start.29 = (bf16[384,1024]{1,0:T(8,128)(2,1)S(1)}, bf16[384,1024]{1,0:T(8,128)(2,1)S(1)}, u32[]{:S(2)}, u32[]{:S(2)}) collective-permute-start(bf16[384,1024]{1,0:T(8,128)(2,1)S(1)} %get-tuple-element.101), channel_id=1, source_target_pairs={{0,16},{16,0},{1,17},{17,1},{2,18},{18,2},{3,19},{19,3},{4,20},{20... | collective-permute-start | bytes 2359304 | tf_op jit(solution)/shard_map/ppermute | solution.py:101
  84.0 2.9 %collective-permute-start.26 = (bf16[64,3584]{1,0:T(8,128)(2,1)S(1)}, bf16[64,3584]{1,0:T(8,128)(2,1)S(1)}, u32[]{:S(2)}, u32[]{:S(2)}) collective-permute-start(bf16[64,3584]{1,0:T(8,128)(2,1)S(1)} %collective-permute-done.25.refs_0_), channel_id=1, source_target_pairs={{0,1},{1,0},{2,3},{3,2},{4,5},{5,4},{6,7},{7,6},{8,9},{9,8},{10,11... | collective-permute-start | bytes 1376264 | tf_op jit(solution)/shard_map/ppermute | solution.py:93
  84.3 13.0 %collective-permute-start.28 = (bf16[64,3584]{1,0:T(8,128)(2,1)S(1)}, bf16[64,3584]{1,0:T(8,128)(2,1)S(1)}, u32[]{:S(2)}, u32[]{:S(2)}) collective-permute-start(bf16[64,3584]{1,0:T(8,128)(2,1)S(1)} %add_convert_fusion.3), channel_id=1, source_target_pairs={{0,2},{1,3},{4,0},{5,1},{8,4},{9,5},{12,8},{13,9},{14,12},{15,13},... | collective-permute-start | bytes 1376264 | tf_op jit(solution)/shard_map/ppermute | solution.py:89
  84.5 12.9 %collective-permute-start.27 = (bf16[64,3584]{1,0:T(8,128)(2,1)S(1)}, bf16[64,3584]{1,0:T(8,128)(2,1)S(1)}, u32[]{:S(2)}, u32[]{:S(2)}) collective-permute-start(bf16[64,3584]{1,0:T(8,128)(2,1)S(1)} %get-tuple-element.99), channel_id=1, source_target_pairs={{0,4},{1,5},{4,8},{5,9},{8,12},{9,13},{12,14},{13,15},{14,10},{15,... | collective-permute-start | bytes 1376264 | tf_op jit(solution)/shard_map/ppermute | solution.py:89
  86.4 19.2 %collective-permute-start.32 = (bf16[288,1024]{1,0:T(8,128)(2,1)S(1)}, bf16[288,1024]{1,0:T(8,128)(2,1)S(1)}, u32[]{:S(2)}, u32[]{:S(2)}) collective-permute-start(bf16[288,1024]{1,0:T(8,128)(2,1)S(1)} %get-tuple-element.105), channel_id=1, source_target_pairs={{0,16},{16,0},{1,17},{17,1},{2,18},{18,2},{3,19},{19,3},{4,20},{20... | collective-permute-start | bytes 1769480 | tf_op jit(solution)/shard_map/ppermute | solution.py:101
  97.7 12.3 %collective-permute-start.30 = (bf16[64,3584]{1,0:T(8,128)(2,1)S(1)}, bf16[64,3584]{1,0:T(8,128)(2,1)S(1)}, u32[]{:S(2)}, u32[]{:S(2)}) collective-permute-start(bf16[64,3584]{1,0:T(8,128)(2,1)S(1)} %get-tuple-element.116), channel_id=1, source_target_pairs={{0,4},{1,5},{4,8},{5,9},{8,12},{9,13},{12,14},{13,15},{14,10},{15,... | collective-permute-start | bytes 1376264 | tf_op jit(solution)/shard_map/ppermute | solution.py:89
  99.5 11.8 %collective-permute-start.31 = (bf16[64,3584]{1,0:T(8,128)(2,1)S(1)}, bf16[64,3584]{1,0:T(8,128)(2,1)S(1)}, u32[]{:S(2)}, u32[]{:S(2)}) collective-permute-start(bf16[64,3584]{1,0:T(8,128)(2,1)S(1)} %get-tuple-element.117), channel_id=1, source_target_pairs={{0,2},{1,3},{4,0},{5,1},{8,4},{9,5},{12,8},{13,9},{14,12},{15,13},... | collective-permute-start | bytes 1376264 | tf_op jit(solution)/shard_map/ppermute | solution.py:89
  99.8 8.9 %collective-permute-start.33 = (bf16[96,1024]{1,0:T(8,128)(2,1)S(1)}, bf16[96,1024]{1,0:T(8,128)(2,1)S(1)}, u32[]{:S(2)}, u32[]{:S(2)}) collective-permute-start(bf16[96,1024]{1,0:T(8,128)(2,1)S(1)} %get-tuple-element.111), channel_id=1, source_target_pairs={{0,16},{16,0},{1,17},{17,1},{2,18},{18,2},{3,19},{19,3},{4,20},{20... | collective-permute-start | bytes 589832 | tf_op jit(solution)/shard_map/ppermute | solution.py:101
  (12 other events, 58.2 us)

commit v10 on v9

--- a/solution.py
+++ b/solution.py
@@ -519,8 +519,6 @@
     keep2, other3 = spread((1, -2, -1, 0), 4, gate_a)
     keep2, gate_b = tie(keep2, gate_b)
     groups = (0, -1, 1, -2), (2, -3, 3), (-4,)
-    for d in (0, -1, 1):
-        pair[d] = pin(pair[d])
     send1, hold1 = bwd(groups[0], share=64)
 
     def mine(i, *more):

time: 113 us -> 113 us (level)
    unnamed x20 -> x28, local copies, waits for them, and re-layouts: 2.35 us -> 3.14 us
where the time goes in v10:
time: 113 us
  Pallas kernels  63 us (56%)
  starting transfers between devices  28.4 us (25%)
  waiting for transfers between devices  12.5 us (11%)
  other arithmetic  4.54 us (4%)
  local copies, waits for them, and re-layouts  3.45 us (3%)
    pallas_call x6, Pallas kernels, kernel_call(): pl.pallas_call(kernel, in_specs=in_specs, out_specs=[VMEM] * len(out_shap...  39.6 us
    pallas_call x2, Pallas kernels, raw_forward(): pl.pallas_call(functools.partial(raw_kernel, first), in_specs=[HBM, HBM],...  20.5 us
    ppermute x14, starting transfers between devices, step_ring(): return lax.ppermute(value, 'expert', pairs)  15.2 us
    ppermute x17, starting transfers between devices, xor(): return lax.ppermute(value, 'expert', [(i, i ^ bits) for i in range(16)])  9.93 us
    ppermute x3, waiting for transfers between devices, across(): return lax.ppermute(value, 'pipe', [(0, 1), (1, 0)])  6.04 us
    ppermute x14, waiting for transfers between devices, step_ring(): return lax.ppermute(value, 'expert', pairs)  4.96 us
    convert_element_type x5, other arithmetic, add(): return total.astype(BF16)  4.42 us
    ppermute x3, starting transfers between devices, across(): return lax.ppermute(value, 'pipe', [(0, 1), (1, 0)])  3.21 us
  transfers between devices with their start and end apart: 34, of which 8 were waited for; matrix products, arithmetic and copies ran while one was open for 3% of the time, Pallas kernels for 55%

profile of v10, /device:TPU:0, one launch (start us, length us, event | category | flops | bytes accessed | tf_op | source)
XLA Modules:
  0.0 112.9 jit_solution(17765530562471583764)
XLA Ops:
  1.5 2.5 %collective-permute-start.2 = (f32[16,128]{1,0:T(8,128)S(1)}, f32[16,128]{1,0:T(8,128)S(1)}, u32[]{:S(2)}, u32[]{:S(2)}) collective-permute-start(f32[16,128]{1,0:T(8,128)S(1)} %gates.1), channel_id=1, source_target_pairs={{0,3},{1,2},{2,1},{3,0},{4,7},{5,6},{6,5},{7,4},{8,11},{9,10},{10,... | collective-permute-start | bytes 24584 | tf_op jit(solution)/shard_map/ppermute | solution.py:93
  4.7 2.0 %collective-permute-start.6 = (bf16[64,3584]{1,0:T(8,128)(2,1)}, bf16[64,3584]{1,0:T(8,128)(2,1)S(1)}, u32[]{:S(2)}, u32[]{:S(2)}) collective-permute-start(bf16[64,3584]{1,0:T(8,128)(2,1)} %refs_0_.1), channel_id=1, source_target_pairs={{0,4},{1,5},{4,8},{5,9},{8,12},{9,13},{12,14},{13,15},{14,10},{15,... | collective-permute-start | bytes 1376264 | tf_op jit(solution)/shard_map/ppermute | solution.py:89
  6.8 1.5 %collective-permute-done.1 = f32[16,128]{1,0:T(8,128)S(1)} collective-permute-done((f32[16,128]{1,0:T(8,128)S(1)}, f32[16,128]{1,0:T(8,128)S(1)}, u32[]{:S(2)}, u32[]{:S(2)}) %collective-permute-start.1) | collective-permute-done | bytes 8224 | tf_op jit(solution)/shard_map/ppermute | solution.py:93
  8.3 1.6 %collective-permute-start.3 = (f32[4,4,128]{2,0,1:T(4,128)S(1)}, f32[4,4,128]{2,0,1:T(4,128)S(1)}, u32[]{:S(2)}, u32[]{:S(2)}) collective-permute-start(f32[4,4,128]{2,0,1:T(4,128)S(1)} %bitcast.37), channel_id=1, source_target_pairs={{0,4},{1,5},{2,6},{3,7},{4,0},{5,1},{6,2},{7,3},{8,12},{9,13},{10,... | collective-permute-start | bytes 24584 | tf_op jit(solution)/shard_map/ppermute | solution.py:93
  10.0 2.6 %collective-permute-start.4 = (f32[4,4,128]{2,0,1:T(4,128)S(1)}, f32[4,4,128]{2,0,1:T(4,128)S(1)}, u32[]{:S(2)}, u32[]{:S(2)}) collective-permute-start(f32[4,4,128]{2,0,1:T(4,128)S(1)} %bitcast.38), channel_id=1, source_target_pairs={{0,8},{1,9},{2,10},{3,11},{4,12},{5,13},{6,14},{7,15},{8,0},{9,1},... | collective-permute-start | bytes 24584 | tf_op jit(solution)/shard_map/ppermute | solution.py:93
  12.8 10.3 %raw_forward.2.refs_0_ = bf16[768,1792]{1,0:T(8,128)(2,1)} custom-call(bf16[768,2048]{1,0:T(8,128)(2,1)} %bitcast.51, bf16[2048,3584]{1,0:T(8,128)(2,1)} %bitcast.30), custom_call_target="tpu_custom_call" | custom-call | flops 5637144576 | bytes 13238272 | tf_op jit(solution)/shard_map/raw_forward/pallas_call | solution.py:263
  24.5 1.4 %collective-permute-start.12 = (bf16[64,3584]{1,0:T(8,128)(2,1)S(1)}, bf16[64,3584]{1,0:T(8,128)(2,1)S(1)}, u32[]{:S(2)}, u32[]{:S(2)}) collective-permute-start(bf16[64,3584]{1,0:T(8,128)(2,1)S(1)} %collective-permute-done.7.refs_4_), channel_id=1, source_target_pairs={{0,2},{1,3},{4,0},{5,1},{8,4},{9,5},{12,8},{13,9},{14,12},{15,13},... | collective-permute-start | bytes 1376264 | tf_op jit(solution)/shard_map/ppermute | solution.py:89
  26.1 10.2 %raw_forward.3.refs_1_ = bf16[768,1792]{1,0:T(8,128)(2,1)} custom-call(bf16[768,2048]{1,0:T(8,128)(2,1)} %bitcast.52, bf16[2048,3584]{1,0:T(8,128)(2,1)} %bitcast.31), custom_call_target="tpu_custom_call" | custom-call | flops 5637144576 | bytes 13238272 | tf_op jit(solution)/shard_map/raw_forward/pallas_call | solution.py:263
  38.7 4.4 %spread_tokens.2 = (bf16[256,3584]{1,0:T(8,128)(2,1)S(1)}, bf16[128,3584]{1,0:T(8,128)(2,1)S(1)}, bf16[128,3584]{1,0:T(8,128)(2,1)}) custom-call(s32[17]{0:T(128)S(1)} %pad_add_fusion.where, f32[8,128]{1,0:T(8,128)S(1)} %squeeze.20.gates, bf16[768,1792]{1,0:T(8,128)(2,1)} %raw_forward.2.refs_0_, bf16[768,1792]{1,0:T(8,128)(2,1)} %raw_forward.3.refs_1_), custom_call_target="tpu_custom_call" | custom-call | flops 1048576 | bytes 16384 | tf_op jit(solution)/shard_map/spread_tokens/pallas_call | solution.py:120
  44.3 1.4 %collective-permute-start.16 = (bf16[64,3584]{1,0:T(8,128)(2,1)S(1)}, bf16[64,3584]{1,0:T(8,128)(2,1)S(1)}, u32[]{:S(2)}, u32[]{:S(2)}) collective-permute-start(bf16[64,3584]{1,0:T(8,128)(2,1)S(1)} %collective-permute-done.12.refs_0_), channel_id=1, source_target_pairs={{0,2},{1,3},{4,0},{5,1},{8,4},{9,5},{12,8},{13,9},{14,12},{15,13},... | collective-permute-start | bytes 1376264 | tf_op jit(solution)/shard_map/ppermute | solution.py:89
  45.6 1.2 %add_convert_fusion.6 = (bf16[64,3584]{1,0:T(8,128)(2,1)}, bf16[64,3584]{1,0:T(8,128)(2,1)}) fusion(bf16[128,3584]{1,0:T(8,128)(2,1)S(1)} %collective-permute-done.17, bf16[256,3584]{1,0:T(8,128)(2,1)S(1)} %get-tuple-element.81), kind=kLoop, calls=%fused_computation.6 | loop fusion | flops 1835008 | bytes 2752512 | tf_op jit(solution)/shard_map/convert_element_type | solution.py:32
  46.8 0.9 collective-permute-start.18
  48.5 1.1 collective-permute-start.19
  49.7 3.7 %spread_tokens.3 = (bf16[256,3584]{1,0:T(8,128)(2,1)S(1)}, bf16[256,3584]{1,0:T(8,128)(2,1)S(1)}) custom-call(s32[17]{0:T(128)S(1)} %pad_add_fusion.where, f32[8,128]{1,0:T(8,128)S(1)} %squeeze.20.gates, bf16[768,1792]{1,0:T(8,128)(2,1)} %raw_forward.2.refs_0_, bf16[768,1792]{1,0:T(8,128)(2,1)} %raw_forward.3.refs_1_), custom_call_target="tpu_custom_call" | custom-call | flops 1048576 | bytes 16384 | tf_op jit(solution)/shard_map/spread_tokens/pallas_call | solution.py:120
  53.5 12.3 %backward.3 = (bf16[384,1024]{1,0:T(8,128)(2,1)S(1)}, bf16[384,1024]{1,0:T(8,128)(2,1)S(1)}) custom-call(s32[17]{0:T(128)S(1)} %pad_add_fusion.where, s32[1]{0:T(128)} %bitcast.20.pipe, f32[8,128]{1,0:T(8,128)S(1)} %squeeze.21.gates, bf16[2048,3584]{1,0:T(8,128)(2,1)} %bitcast.32, bf16[64,3584]{1,0:T(8,128)(2,1)S(1)} %copy-done.1, ...), custom_call_target="tpu_custom_call" | custom-call | flops 88080384 | bytes 339968 | tf_op jit(solution)/shard_map/backward/pallas_call | solution.py:120
  66.4 1.1 collective-permute-done.19
  68.5 1.8 %add_convert_fusion.4 = (bf16[64,3584]{1,0:T(8,128)(2,1)S(1)}, bf16[64,3584]{1,0:T(8,128)(2,1)S(1)}) fusion(bf16[64,3584]{1,0:T(8,128)(2,1)} %collective-permute-done.19, bf16[128,3584]{1,0:T(8,128)(2,1)} %collective-permute-done.14, bf16[256,3584]{1,0:T(8,128)(2,1)S(1)} %get-tuple-element.81, bf16[64,3584]{1,0:T(8,128)(2,1)} %collective-permute-done.18), kind=kLoop, calls=%fused_computation.4 | loop fusion | flops 2752512 | bytes 3670016 | tf_op jit(solution)/shard_map/convert_element_type | solution.py:32
  70.3 1.1 collective-permute-start.24
  71.4 1.9 %collective-permute-start.25 = (bf16[64,3584]{1,0:T(8,128)(2,1)S(1)}, bf16[64,3584]{1,0:T(8,128)(2,1)S(1)}, u32[]{:S(2)}, u32[]{:S(2)}) collective-permute-start(bf16[64,3584]{1,0:T(8,128)(2,1)S(1)} %collective-permute-done.15.refs_2_), channel_id=1, source_target_pairs={{0,4},{1,5},{4,8},{5,9},{8,12},{9,13},{12,14},{13,15},{14,10},{15,... | collective-permute-start | bytes 1376264 | tf_op jit(solution)/shard_map/ppermute | solution.py:89
  73.2 1.5 %collective-permute-start.29 = (bf16[384,1024]{1,0:T(8,128)(2,1)S(1)}, bf16[384,1024]{1,0:T(8,128)(2,1)S(1)}, u32[]{:S(2)}, u32[]{:S(2)}) collective-permute-start(bf16[384,1024]{1,0:T(8,128)(2,1)S(1)} %get-tuple-element.101), channel_id=1, source_target_pairs={{0,16},{16,0},{1,17},{17,1},{2,18},{18,2},{3,19},{19,3},{4,20},{20... | collective-permute-start | bytes 2359304 | tf_op jit(solution)/shard_map/ppermute | solution.py:101
  74.7 10.0 %backward.4 = (bf16[288,1024]{1,0:T(8,128)(2,1)S(1)}, bf16[288,1024]{1,0:T(8,128)(2,1)S(1)}) custom-call(s32[17]{0:T(128)S(1)} %pad_add_fusion.where, s32[1]{0:T(128)} %bitcast.20.pipe, f32[8,128]{1,0:T(8,128)S(1)} %squeeze.21.gates, bf16[2048,3584]{1,0:T(8,128)(2,1)} %bitcast.33, bf16[64,3584]{1,0:T(8,128)(2,1)S(1)} %collective-permute-done.12.refs_0_, ...), custom_call_target="tpu_custom_call" | custom-call | flops 66060288 | bytes 312320 | tf_op jit(solution)/shard_map/backward/pallas_call | solution.py:120
  85.2 1.9 %collective-permute-start.27 = (bf16[64,3584]{1,0:T(8,128)(2,1)S(1)}, bf16[64,3584]{1,0:T(8,128)(2,1)S(1)}, u32[]{:S(2)}, u32[]{:S(2)}) collective-permute-start(bf16[64,3584]{1,0:T(8,128)(2,1)S(1)} %get-tuple-element.99), channel_id=1, source_target_pairs={{0,4},{1,5},{4,8},{5,9},{8,12},{9,13},{12,14},{13,15},{14,10},{15,... | collective-permute-start | bytes 1376264 | tf_op jit(solution)/shard_map/ppermute | solution.py:89
  87.6 8.4 %backward.5 = (bf16[96,1024]{1,0:T(8,128)(2,1)S(1)}, bf16[96,1024]{1,0:T(8,128)(2,1)S(1)}) custom-call(s32[17]{0:T(128)S(1)} %pad_add_fusion.where, s32[1]{0:T(128)} %bitcast.20.pipe, f32[8,128]{1,0:T(8,128)S(1)} %squeeze.21.gates, bf16[2048,3584]{1,0:T(8,128)(2,1)} %bitcast.34, bf16[64,3584]{1,0:T(8,128)(2,1)S(1)} %collective-permute-done.25.refs_0_, ...), custom_call_target="tpu_custom_call" | custom-call | flops 22020096 | bytes 257024 | tf_op jit(solution)/shard_map/backward/pallas_call | solution.py:120
  96.0 2.0 %collective-permute-done.28 = bf16[64,3584]{1,0:T(8,128)(2,1)S(1)} collective-permute-done((bf16[64,3584]{1,0:T(8,128)(2,1)S(1)}, bf16[64,3584]{1,0:T(8,128)(2,1)S(1)}, u32[]{:S(2)}, u32[]{:S(2)}) %collective-permute-start.28) | collective-permute-done | bytes 458784 | tf_op jit(solution)/shard_map/ppermute | solution.py:89
  98.4 1.8 %collective-permute-start.30 = (bf16[64,3584]{1,0:T(8,128)(2,1)S(1)}, bf16[64,3584]{1,0:T(8,128)(2,1)S(1)}, u32[]{:S(2)}, u32[]{:S(2)}) collective-permute-start(bf16[64,3584]{1,0:T(8,128)(2,1)S(1)} %get-tuple-element.116), channel_id=1, source_target_pairs={{0,4},{1,5},{4,8},{5,9},{8,12},{9,13},{12,14},{13,15},{14,10},{15,... | collective-permute-start | bytes 1376264 | tf_op jit(solution)/shard_map/ppermute | solution.py:89
  100.5 1.2 %collective-permute-start.33 = (bf16[96,1024]{1,0:T(8,128)(2,1)S(1)}, bf16[96,1024]{1,0:T(8,128)(2,1)S(1)}, u32[]{:S(2)}, u32[]{:S(2)}) collective-permute-start(bf16[96,1024]{1,0:T(8,128)(2,1)S(1)} %get-tuple-element.111), channel_id=1, source_target_pairs={{0,16},{16,0},{1,17},{17,1},{2,18},{18,2},{3,19},{19,3},{4,20},{20... | collective-permute-start | bytes 589832 | tf_op jit(solution)/shard_map/ppermute | solution.py:101
  101.6 4.7 %collective-permute-done.32.refs_3_ = bf16[288,1024]{1,0:T(8,128)(2,1)S(1)} collective-permute-done((bf16[288,1024]{1,0:T(8,128)(2,1)S(1)}, bf16[288,1024]{1,0:T(8,128)(2,1)S(1)}, u32[]{:S(2)}, u32[]{:S(2)}) %collective-permute-start.32) | collective-permute-done | bytes 589856 | tf_op jit(solution)/shard_map/ppermute | solution.py:101
  106.3 1.7 %collect.2.refs_2_ = bf16[768,1024]{1,0:T(8,128)(2,1)} custom-call(s32[17]{0:T(128)S(1)} %pad_add_fusion.where, bf16[384,1024]{1,0:T(8,128)(2,1)S(1)} %get-tuple-element.107.refs_0_, bf16[384,1024]{1,0:T(8,128)(2,1)S(1)} %collective-permute-done.29.refs_1_, bf16[288,1024]{1,0:T(8,128)(2,1)S(1)} %get-tuple-element.109.refs_2_, ...), custom_call_target="tpu_custom_call" | custom-call | flops 1048576 | bytes 4128768 | tf_op jit(solution)/shard_map/collect/pallas_call | solution.py:451
  108.0 1.4 %collective-permute-done.33.refs_1_ = bf16[96,1024]{1,0:T(8,128)(2,1)S(1)} collective-permute-done((bf16[96,1024]{1,0:T(8,128)(2,1)S(1)}, bf16[96,1024]{1,0:T(8,128)(2,1)S(1)}, u32[]{:S(2)}, u32[]{:S(2)}) %collective-permute-start.33) | collective-permute-done | bytes 196640 | tf_op jit(solution)/shard_map/ppermute | solution.py:101
  109.4 1.3 %collect.3 = bf16[768,1024]{1,0:T(8,128)(2,1)} custom-call(s32[17]{0:T(128)S(1)} %pad_add_fusion.where, bf16[96,1024]{1,0:T(8,128)(2,1)S(1)} %get-tuple-element.106.refs_0_, bf16[96,1024]{1,0:T(8,128)(2,1)S(1)} %collective-permute-done.33.refs_1_, bf16[768,1024]{1,0:T(8,128)(2,1)} %collect.2.refs_2_), custom_call_target="tpu_custom_call", output_to_operand_aliasing={{}: (3, {})} | custom-call | flops 1048576 | bytes 589824 | tf_op jit(solution)/shard_map/collect/pallas_call | solution.py:451
  110.7 1.2 %collective-permute-done.31 = bf16[64,3584]{1,0:T(8,128)(2,1)S(1)} collective-permute-done((bf16[64,3584]{1,0:T(8,128)(2,1)S(1)}, bf16[64,3584]{1,0:T(8,128)(2,1)S(1)}, u32[]{:S(2)}, u32[]{:S(2)}) %collective-permute-start.31) | collective-permute-done | bytes 458784 | tf_op jit(solution)/shard_map/ppermute | solution.py:89
  111.9 1.0 add_convert_fusion
  (89 shorter events, 11.3 us)
Async XLA Ops:
  1.5 5.3 %collective-permute-start.2 = (f32[16,128]{1,0:T(8,128)S(1)}, f32[16,128]{1,0:T(8,128)S(1)}, u32[]{:S(2)}, u32[]{:S(2)}) collective-permute-start(f32[16,128]{1,0:T(8,128)S(1)} %gates.1), channel_id=1, source_target_pairs={{0,3},{1,2},{2,1},{3,0},{4,7},{5,6},{6,5},{7,4},{8,11},{9,10},{10,... | collective-permute-start | bytes 24584 | tf_op jit(solution)/shard_map/ppermute | solution.py:93
  4.0 2.9 %collective-permute-start = (f32[16,128]{1,0:T(8,128)S(1)}, f32[16,128]{1,0:T(8,128)S(1)}, u32[]{:S(2)}, u32[]{:S(2)}) collective-permute-start(f32[16,128]{1,0:T(8,128)S(1)} %gates.1), channel_id=1, source_target_pairs={{0,1},{1,0},{2,3},{3,2},{4,5},{5,4},{6,7},{7,6},{8,9},{9,8},{10,11... | collective-permute-start | bytes 24584 | tf_op jit(solution)/shard_map/ppermute | solution.py:93
  4.6 3.7 %collective-permute-start.1 = (f32[16,128]{1,0:T(8,128)S(1)}, f32[16,128]{1,0:T(8,128)S(1)}, u32[]{:S(2)}, u32[]{:S(2)}) collective-permute-start(f32[16,128]{1,0:T(8,128)S(1)} %gates.1), channel_id=1, source_target_pairs={{0,2},{1,3},{2,0},{3,1},{4,6},{5,7},{6,4},{7,5},{8,10},{9,11},{10,... | collective-permute-start | bytes 24584 | tf_op jit(solution)/shard_map/ppermute | solution.py:93
  4.7 18.5 %collective-permute-start.6 = (bf16[64,3584]{1,0:T(8,128)(2,1)}, bf16[64,3584]{1,0:T(8,128)(2,1)S(1)}, u32[]{:S(2)}, u32[]{:S(2)}) collective-permute-start(bf16[64,3584]{1,0:T(8,128)(2,1)} %refs_0_.1), channel_id=1, source_target_pairs={{0,4},{1,5},{4,8},{5,9},{8,12},{9,13},{12,14},{13,15},{14,10},{15,... | collective-permute-start | bytes 1376264 | tf_op jit(solution)/shard_map/ppermute | solution.py:89
  6.7 16.5 %collective-permute-start.7 = (bf16[64,3584]{1,0:T(8,128)(2,1)}, bf16[64,3584]{1,0:T(8,128)(2,1)S(1)}, u32[]{:S(2)}, u32[]{:S(2)}) collective-permute-start(bf16[64,3584]{1,0:T(8,128)(2,1)} %refs_0_.1), channel_id=1, source_target_pairs={{0,2},{1,3},{4,0},{5,1},{8,4},{9,5},{12,8},{13,9},{14,12},{15,13},... | collective-permute-start | bytes 1376264 | tf_op jit(solution)/shard_map/ppermute | solution.py:89
  8.3 14.7 %collective-permute-start.3 = (f32[4,4,128]{2,0,1:T(4,128)S(1)}, f32[4,4,128]{2,0,1:T(4,128)S(1)}, u32[]{:S(2)}, u32[]{:S(2)}) collective-permute-start(f32[4,4,128]{2,0,1:T(4,128)S(1)} %bitcast.37), channel_id=1, source_target_pairs={{0,4},{1,5},{2,6},{3,7},{4,0},{5,1},{6,2},{7,3},{8,12},{9,13},{10,... | collective-permute-start | bytes 24584 | tf_op jit(solution)/shard_map/ppermute | solution.py:93
  10.0 13.2 %collective-permute-start.4 = (f32[4,4,128]{2,0,1:T(4,128)S(1)}, f32[4,4,128]{2,0,1:T(4,128)S(1)}, u32[]{:S(2)}, u32[]{:S(2)}) collective-permute-start(f32[4,4,128]{2,0,1:T(4,128)S(1)} %bitcast.38), channel_id=1, source_target_pairs={{0,8},{1,9},{2,10},{3,11},{4,12},{5,13},{6,14},{7,15},{8,0},{9,1},... | collective-permute-start | bytes 24584 | tf_op jit(solution)/shard_map/ppermute | solution.py:93
  12.6 10.6 %collective-permute-start.5 = (f32[4,4,128]{2,0,1:T(4,128)S(1)}, f32[4,4,128]{2,0,1:T(4,128)S(1)}, u32[]{:S(2)}, u32[]{:S(2)}) collective-permute-start(f32[4,4,128]{2,0,1:T(4,128)S(1)} %bitcast.39), channel_id=1, source_target_pairs={{0,12},{1,13},{2,14},{3,15},{4,8},{5,9},{6,10},{7,11},{8,4},{9,5},... | collective-permute-start | bytes 24584 | tf_op jit(solution)/shard_map/ppermute | solution.py:93
  23.1 13.2 %collective-permute-start.8 = (bf16[64,3584]{1,0:T(8,128)(2,1)S(1)}, bf16[64,3584]{1,0:T(8,128)(2,1)S(1)}, u32[]{:S(2)}, u32[]{:S(2)}) collective-permute-start(bf16[64,3584]{1,0:T(8,128)(2,1)S(1)} %copy-done), channel_id=1, source_target_pairs={{0,1},{1,0},{2,3},{3,2},{4,5},{5,4},{6,7},{7,6},{8,9},{9,8},{10,11... | collective-permute-start | bytes 1376264 | tf_op jit(solution)/shard_map/ppermute | solution.py:93
  23.3 14.6 %collective-permute-start.9 = (bf16[64,3584]{1,0:T(8,128)(2,1)S(1)}, bf16[64,3584]{1,0:T(8,128)(2,1)S(1)}, u32[]{:S(2)}, u32[]{:S(2)}) collective-permute-start(bf16[64,3584]{1,0:T(8,128)(2,1)S(1)} %collective-permute-done.6.refs_2_), channel_id=1, source_target_pairs={{0,1},{1,0},{2,3},{3,2},{4,5},{5,4},{6,7},{7,6},{8,9},{9,8},{10,11... | collective-permute-start | bytes 1376264 | tf_op jit(solution)/shard_map/ppermute | solution.py:93
  23.8 19.2 %collective-permute-start.11 = (bf16[64,3584]{1,0:T(8,128)(2,1)S(1)}, bf16[64,3584]{1,0:T(8,128)(2,1)}, u32[]{:S(2)}, u32[]{:S(2)}) collective-permute-start(bf16[64,3584]{1,0:T(8,128)(2,1)S(1)} %collective-permute-done.6.refs_2_), channel_id=1, source_target_pairs={{0,4},{1,5},{4,8},{5,9},{8,12},{9,13},{12,14},{13,15},{14,10},{15,... | collective-permute-start | bytes 1376264 | tf_op jit(solution)/shard_map/ppermute | solution.py:89
  24.5 12.6 %collective-permute-start.10 = (bf16[64,3584]{1,0:T(8,128)(2,1)S(1)}, bf16[64,3584]{1,0:T(8,128)(2,1)S(1)}, u32[]{:S(2)}, u32[]{:S(2)}) collective-permute-start(bf16[64,3584]{1,0:T(8,128)(2,1)S(1)} %collective-permute-done.7.refs_4_), channel_id=1, source_target_pairs={{0,1},{1,0},{2,3},{3,2},{4,5},{5,4},{6,7},{7,6},{8,9},{9,8},{10,11... | collective-permute-start | bytes 1376264 | tf_op jit(solution)/shard_map/ppermute | solution.py:93
  24.5 18.6 %collective-permute-start.12 = (bf16[64,3584]{1,0:T(8,128)(2,1)S(1)}, bf16[64,3584]{1,0:T(8,128)(2,1)S(1)}, u32[]{:S(2)}, u32[]{:S(2)}) collective-permute-start(bf16[64,3584]{1,0:T(8,128)(2,1)S(1)} %collective-permute-done.7.refs_4_), channel_id=1, source_target_pairs={{0,2},{1,3},{4,0},{5,1},{8,4},{9,5},{12,8},{13,9},{14,12},{15,13},... | collective-permute-start | bytes 1376264 | tf_op jit(solution)/shard_map/ppermute | solution.py:89
  43.3 4.4 %collective-permute-start.13 = (bf16[64,3584]{1,0:T(8,128)(2,1)}, bf16[64,3584]{1,0:T(8,128)(2,1)S(1)}, u32[]{:S(2)}, u32[]{:S(2)}) collective-permute-start(bf16[64,3584]{1,0:T(8,128)(2,1)} %collective-permute-done.11.refs_6_), channel_id=1, source_target_pairs={{0,1},{1,0},{2,3},{3,2},{4,5},{5,4},{6,7},{7,6},{8,9},{9,8},{10,11... | collective-permute-start | bytes 1376264 | tf_op jit(solution)/shard_map/ppermute | solution.py:93
  43.6 22.2 %collective-permute-start.15 = (bf16[64,3584]{1,0:T(8,128)(2,1)}, bf16[64,3584]{1,0:T(8,128)(2,1)S(1)}, u32[]{:S(2)}, u32[]{:S(2)}) collective-permute-start(bf16[64,3584]{1,0:T(8,128)(2,1)} %collective-permute-done.11.refs_6_), channel_id=1, source_target_pairs={{0,4},{1,5},{4,8},{5,9},{8,12},{9,13},{12,14},{13,15},{14,10},{15,... | collective-permute-start | bytes 1376264 | tf_op jit(solution)/shard_map/ppermute | solution.py:89
  44.3 5.4 %collective-permute-start.14 = (bf16[128,3584]{1,0:T(8,128)(2,1)}, bf16[128,3584]{1,0:T(8,128)(2,1)}, u32[]{:S(2)}, u32[]{:S(2)}) collective-permute-start(bf16[128,3584]{1,0:T(8,128)(2,1)} %get-tuple-element.70), channel_id=1, source_target_pairs={{0,1},{1,0},{2,3},{3,2},{4,5},{5,4},{6,7},{7,6},{8,9},{9,8},{10,11... | collective-permute-start | bytes 2752520 | tf_op jit(solution)/shard_map/ppermute | solution.py:93
  44.3 21.5 %collective-permute-start.16 = (bf16[64,3584]{1,0:T(8,128)(2,1)S(1)}, bf16[64,3584]{1,0:T(8,128)(2,1)S(1)}, u32[]{:S(2)}, u32[]{:S(2)}) collective-permute-start(bf16[64,3584]{1,0:T(8,128)(2,1)S(1)} %collective-permute-done.12.refs_0_), channel_id=1, source_target_pairs={{0,2},{1,3},{4,0},{5,1},{8,4},{9,5},{12,8},{13,9},{14,12},{15,13},... | collective-permute-start | bytes 1376264 | tf_op jit(solution)/shard_map/ppermute | solution.py:89
  46.8 19.6 %collective-permute-start.18 = (bf16[64,3584]{1,0:T(8,128)(2,1)}, bf16[64,3584]{1,0:T(8,128)(2,1)}, u32[]{:S(2)}, u32[]{:S(2)}) collective-permute-start(bf16[64,3584]{1,0:T(8,128)(2,1)} %get-tuple-element.121), channel_id=1, source_target_pairs={{0,4},{1,5},{4,8},{5,9},{8,12},{9,13},{12,14},{13,15},{14,10},{15,... | collective-permute-start | bytes 1376264 | tf_op jit(solution)/shard_map/ppermute | solution.py:89
  48.5 19.0 %collective-permute-start.19 = (bf16[64,3584]{1,0:T(8,128)(2,1)}, bf16[64,3584]{1,0:T(8,128)(2,1)}, u32[]{:S(2)}, u32[]{:S(2)}) collective-permute-start(bf16[64,3584]{1,0:T(8,128)(2,1)} %get-tuple-element.120), channel_id=1, source_target_pairs={{0,2},{1,3},{4,0},{5,1},{8,4},{9,5},{12,8},{13,9},{14,12},{15,13},... | collective-permute-start | bytes 1376264 | tf_op jit(solution)/shard_map/ppermute | solution.py:89
  67.5 3.9 %collective-permute-start.20 = (bf16[256,3584]{1,0:T(8,128)(2,1)S(1)}, bf16[256,3584]{1,0:T(8,128)(2,1)S(1)}, u32[]{:S(2)}, u32[]{:S(2)}) collective-permute-start(bf16[256,3584]{1,0:T(8,128)(2,1)S(1)} %get-tuple-element.84), channel_id=1, source_target_pairs={{0,1},{1,0},{2,3},{3,2},{4,5},{5,4},{6,7},{7,6},{8,9},{9,8},{10,11... | collective-permute-start | bytes 5505032 | tf_op jit(solution)/shard_map/ppermute | solution.py:93
  67.5 5.7 %collective-permute-start.21 = (bf16[64,3584]{1,0:T(8,128)(2,1)S(1)}, bf16[64,3584]{1,0:T(8,128)(2,1)S(1)}, u32[]{:S(2)}, u32[]{:S(2)}) collective-permute-start(bf16[64,3584]{1,0:T(8,128)(2,1)S(1)} %collective-permute-done.12.refs_0_), channel_id=1, source_target_pairs={{0,1},{1,0},{2,3},{3,2},{4,5},{5,4},{6,7},{7,6},{8,9},{9,8},{10,11... | collective-permute-start | bytes 1376264 | tf_op jit(solution)/shard_map/ppermute | solution.py:93
  68.0 6.7 %collective-permute-start.22 = (bf16[64,3584]{1,0:T(8,128)(2,1)S(1)}, bf16[64,3584]{1,0:T(8,128)(2,1)S(1)}, u32[]{:S(2)}, u32[]{:S(2)}) collective-permute-start(bf16[64,3584]{1,0:T(8,128)(2,1)S(1)} %collective-permute-done.15.refs_2_), channel_id=1, source_target_pairs={{0,1},{1,0},{2,3},{3,2},{4,5},{5,4},{6,7},{7,6},{8,9},{9,8},{10,11... | collective-permute-start | bytes 1376264 | tf_op jit(solution)/shard_map/ppermute | solution.py:93
  68.0 6.7 %collective-permute-start.23 = (bf16[64,3584]{1,0:T(8,128)(2,1)S(1)}, bf16[64,3584]{1,0:T(8,128)(2,1)S(1)}, u32[]{:S(2)}, u32[]{:S(2)}) collective-permute-start(bf16[64,3584]{1,0:T(8,128)(2,1)S(1)} %collective-permute-done.16.refs_4_), channel_id=1, source_target_pairs={{0,1},{1,0},{2,3},{3,2},{4,5},{5,4},{6,7},{7,6},{8,9},{9,8},{10,11... | collective-permute-start | bytes 1376264 | tf_op jit(solution)/shard_map/ppermute | solution.py:93
  70.3 14.4 %collective-permute-start.24 = (bf16[64,3584]{1,0:T(8,128)(2,1)S(1)}, bf16[64,3584]{1,0:T(8,128)(2,1)S(1)}, u32[]{:S(2)}, u32[]{:S(2)}) collective-permute-start(bf16[64,3584]{1,0:T(8,128)(2,1)S(1)} %get-tuple-element.95), channel_id=1, source_target_pairs={{0,2},{1,3},{4,0},{5,1},{8,4},{9,5},{12,8},{13,9},{14,12},{15,13},... | collective-permute-start | bytes 1376264 | tf_op jit(solution)/shard_map/ppermute | solution.py:89
  71.4 13.4 %collective-permute-start.25 = (bf16[64,3584]{1,0:T(8,128)(2,1)S(1)}, bf16[64,3584]{1,0:T(8,128)(2,1)S(1)}, u32[]{:S(2)}, u32[]{:S(2)}) collective-permute-start(bf16[64,3584]{1,0:T(8,128)(2,1)S(1)} %collective-permute-done.15.refs_2_), channel_id=1, source_target_pairs={{0,4},{1,5},{4,8},{5,9},{8,12},{9,13},{12,14},{13,15},{14,10},{15,... | collective-permute-start | bytes 1376264 | tf_op jit(solution)/shard_map/ppermute | solution.py:89
  73.2 22.8 %collective-permute-start.29 = (bf16[384,1024]{1,0:T(8,128)(2,1)S(1)}, bf16[384,1024]{1,0:T(8,128)(2,1)S(1)}, u32[]{:S(2)}, u32[]{:S(2)}) collective-permute-start(bf16[384,1024]{1,0:T(8,128)(2,1)S(1)} %get-tuple-element.101), channel_id=1, source_target_pairs={{0,16},{16,0},{1,17},{17,1},{2,18},{18,2},{3,19},{19,3},{4,20},{20... | collective-permute-start | bytes 2359304 | tf_op jit(solution)/shard_map/ppermute | solution.py:101
  85.0 13.0 %collective-permute-start.28 = (bf16[64,3584]{1,0:T(8,128)(2,1)S(1)}, bf16[64,3584]{1,0:T(8,128)(2,1)S(1)}, u32[]{:S(2)}, u32[]{:S(2)}) collective-permute-start(bf16[64,3584]{1,0:T(8,128)(2,1)S(1)} %add_convert_fusion.3), channel_id=1, source_target_pairs={{0,2},{1,3},{4,0},{5,1},{8,4},{9,5},{12,8},{13,9},{14,12},{15,13},... | collective-permute-start | bytes 1376264 | tf_op jit(solution)/shard_map/ppermute | solution.py:89
  85.2 12.9 %collective-permute-start.27 = (bf16[64,3584]{1,0:T(8,128)(2,1)S(1)}, bf16[64,3584]{1,0:T(8,128)(2,1)S(1)}, u32[]{:S(2)}, u32[]{:S(2)}) collective-permute-start(bf16[64,3584]{1,0:T(8,128)(2,1)S(1)} %get-tuple-element.99), channel_id=1, source_target_pairs={{0,4},{1,5},{4,8},{5,9},{8,12},{9,13},{12,14},{13,15},{14,10},{15,... | collective-permute-start | bytes 1376264 | tf_op jit(solution)/shard_map/ppermute | solution.py:89
  87.1 19.2 %collective-permute-start.32 = (bf16[288,1024]{1,0:T(8,128)(2,1)S(1)}, bf16[288,1024]{1,0:T(8,128)(2,1)S(1)}, u32[]{:S(2)}, u32[]{:S(2)}) collective-permute-start(bf16[288,1024]{1,0:T(8,128)(2,1)S(1)} %get-tuple-element.105), channel_id=1, source_target_pairs={{0,16},{16,0},{1,17},{17,1},{2,18},{18,2},{3,19},{19,3},{4,20},{20... | collective-permute-start | bytes 1769480 | tf_op jit(solution)/shard_map/ppermute | solution.py:101
  98.4 12.3 %collective-permute-start.30 = (bf16[64,3584]{1,0:T(8,128)(2,1)S(1)}, bf16[64,3584]{1,0:T(8,128)(2,1)S(1)}, u32[]{:S(2)}, u32[]{:S(2)}) collective-permute-start(bf16[64,3584]{1,0:T(8,128)(2,1)S(1)} %get-tuple-element.116), channel_id=1, source_target_pairs={{0,4},{1,5},{4,8},{5,9},{8,12},{9,13},{12,14},{13,15},{14,10},{15,... | collective-permute-start | bytes 1376264 | tf_op jit(solution)/shard_map/ppermute | solution.py:89
  100.1 11.8 %collective-permute-start.31 = (bf16[64,3584]{1,0:T(8,128)(2,1)S(1)}, bf16[64,3584]{1,0:T(8,128)(2,1)S(1)}, u32[]{:S(2)}, u32[]{:S(2)}) collective-permute-start(bf16[64,3584]{1,0:T(8,128)(2,1)S(1)} %get-tuple-element.117), channel_id=1, source_target_pairs={{0,2},{1,3},{4,0},{5,1},{8,4},{9,5},{12,8},{13,9},{14,12},{15,13},... | collective-permute-start | bytes 1376264 | tf_op jit(solution)/shard_map/ppermute | solution.py:89
  100.5 8.9 %collective-permute-start.33 = (bf16[96,1024]{1,0:T(8,128)(2,1)S(1)}, bf16[96,1024]{1,0:T(8,128)(2,1)S(1)}, u32[]{:S(2)}, u32[]{:S(2)}) collective-permute-start(bf16[96,1024]{1,0:T(8,128)(2,1)S(1)} %get-tuple-element.111), channel_id=1, source_target_pairs={{0,16},{16,0},{1,17},{17,1},{2,18},{18,2},{3,19},{19,3},{4,20},{20... | collective-permute-start | bytes 589832 | tf_op jit(solution)/shard_map/ppermute | solution.py:101
  (16 other events, 71.1 us)
